TPU v7x, 256 devices: a whole 4x4x8 slice. The times are simulated.
256 devices in a mesh: slab: 16 (over z, core), dom: 16 (over y, x).
Axes of the slice: x: 4, y: 4, z: 8, core: 2. Of those that a mesh axis runs over, the one named last changes fastest.
Arguments:
- a_blocks: bfloat16 [32768, 7, 4096], P(('slab', 'dom')), may hold values from -5 to 5
- p_blocks: bfloat16 [32768, 4096], P(('slab', 'dom')), may hold values from -0.75 to 0.75
- dest_rank: int32 [229376, 1], P(('slab', 'dom')), may hold values from 0 to 15; in each aligned block of 896 rows (0 to 895, 896 to 1791, ...) at most 112 rows name the same one
- dest_block: int32 [32768, 7], P(('slab', 'dom')), may hold values from 0 to 127
Outputs:
- coarse: float32 [32768, 4096], P(('slab', 'dom'))
Inputs may be any that keep to these rules, and one draw needn't show every extreme that they name: `dest_rank`: among the 896 rows of one device no owner index appears more than 112 times, and some owner index appears exactly 112 times.
All inputs are finite; a program needn't handle non-finite values.
Results may differ from a plain program's by a relative error of at most 0.0041.
Values may be sent and summed in bfloat16 or wider, within the bound.
No kernel may reach another device: no remote copies, remote signals or barrier semaphores. Data moves between devices by JAX's collectives and lax.ppermute only.
A program may use at most 128 MiB of HBM per device.

v0:
```python
import jax
import jax.numpy as jnp
from jax import lax
from jax.sharding import PartitionSpec as P

BLOCK = 64
PAIRS = 7
EX = 8
EY = 4
EZ = 4
CB_DEV = 128


def with_halo(x, sides, width):
    for axis, dim in sides:
        size, length = (lax.axis_size(axis), x.shape[dim])
        up = [(i, (i + 1) % size) for i in range(size - 1)]
        down = [(j, i) for i, j in up]
        last = lax.slice_in_dim(x, length - width, length, axis=dim)
        first = lax.slice_in_dim(x, 0, width, axis=dim)
        before = lax.ppermute(last, axis, up)
        after = lax.ppermute(first, axis, down)
        x = jnp.concatenate([before, x, after], axis=dim)
    return x


def neighbour_stack(padded):
    middle = padded[1:-1, 1:-1, 1:-1]
    return jnp.stack(
        [
            middle,
            padded[1:-1, 1:-1, :-2],
            padded[1:-1, 1:-1, 2:],
            padded[1:-1, :-2, 1:-1],
            padded[1:-1, 2:, 1:-1],
            padded[:-2, 1:-1, 1:-1],
            padded[2:, 1:-1, 1:-1],
        ],
        axis=3,
    )


def on_device(a_blocks, p_blocks, dest_rank, dest_block):
    elements = p_blocks.shape[0]
    square = BLOCK * BLOCK
    dom_count = lax.axis_size("dom")
    brick_rows = p_blocks.reshape(EZ, EY, EX, square)
    ghosted = with_halo(brick_rows, (("slab", 0), ("dom", 1)), 1)
    padded = jnp.pad(ghosted, ((0, 0), (0, 0), (1, 1), (0, 0)))
    beside = neighbour_stack(padded).reshape(elements, PAIRS, BLOCK, BLOCK)
    couple = a_blocks.reshape(elements, PAIRS, BLOCK, BLOCK)
    product = jnp.einsum(
        "ekrc,ekcd->ekrd", couple, beside, preferred_element_type=jnp.float32
    ).astype(jnp.bfloat16)
    self_rows = p_blocks.reshape(elements, BLOCK, BLOCK)
    galerkin_terms = jnp.einsum(
        "ecr,ekcd->ekrd", self_rows, product, preferred_element_type=jnp.float32
    ).astype(jnp.bfloat16)
    flat_terms = galerkin_terms.reshape(elements * PAIRS, square)
    owner_rank = dest_rank.reshape(-1)
    target_block = dest_block.reshape(-1)
    capacity = max(2, 2 * PAIRS * elements // dom_count)
    membership = (owner_rank[:, None] == jnp.arange(dom_count, dtype=jnp.int32)[None, :]).astype(
        jnp.int32
    )
    position = jnp.sum((jnp.cumsum(membership, axis=0) - 1) * membership, axis=1)
    slot_index = owner_rank * capacity + position
    slot_match = slot_index[None, :] == jnp.arange(dom_count * capacity, dtype=jnp.int32)[:, None]
    slot_table = slot_match.astype(jnp.bfloat16)
    outgoing = jnp.dot(slot_table, flat_terms, preferred_element_type=jnp.float32).astype(
        jnp.bfloat16
    )
    filled = jnp.sum(slot_match.astype(jnp.int32), axis=1)
    picked = jnp.sum(slot_match.astype(jnp.int32) * target_block[None, :], axis=1)
    labels = (picked + CB_DEV * (1 - filled)).reshape(dom_count, capacity)
    outgoing = outgoing.reshape(dom_count, capacity, square)
    arrived, arrived_labels = (
        lax.all_to_all(outgoing, "dom", split_axis=0, concat_axis=0, tiled=True),
        lax.all_to_all(labels, "dom", split_axis=0, concat_axis=0, tiled=True),
    )
    selector = (
        arrived_labels.reshape(-1)[:, None] == jnp.arange(CB_DEV, dtype=jnp.int32)[None, :]
    ).astype(jnp.bfloat16)
    coarse = jnp.einsum(
        "sc,sv->cv",
        selector,
        arrived.reshape(dom_count * capacity, square),
        preferred_element_type=jnp.float32,
    )
    return coarse


def solution(mesh):
    return jax.shard_map(
        on_device,
        mesh=mesh,
        in_specs=(
            P(("slab", "dom"), None, None),
            P(("slab", "dom"), None),
            P(("slab", "dom"), None),
            P(("slab", "dom"), None),
        ),
        out_specs=P(("slab", "dom"), None),
        check_vma=False,
    )
```

profile of v0, /device:TPU:32, one launch (start us, length us, event | category | flops | bytes accessed | tf_op | source)
XLA Modules:
  0.0 464.2 jit_solution(17591700044320657137)
XLA Ops:
  0.0 1.1 slice_bitcast_fusion.1
  1.1 1.9 collective-permute-start
  3.0 3.6 collective-permute-start.1
  6.6 0.7 reduce
  7.4 2.0 reduce-window.6
  9.8 0.8 copy.19
  10.8 2.1 pad_maximum_fusion.10
  13.0 4.1 collective-permute-start.2
  17.1 1.3 collective-permute-start.3
  18.4 1.8 convert_reduce_fusion
  20.2 0.7 add.28
  20.9 7.8 %all-to-all-start = ((s32[16,1,112]{2,1,0:T(1,128)}), s32[16,1,112]{2,1,0:T(1,128)S(1)}, u32[]{:S(2)}, u32[]{:S(2)}) async-start(s32[16,1,112]{2,1,0:T(1,128)} %add.28), calls=%async_computation | async-start | bytes 16384 | tf_op jit(solution)/shard_map/all_to_all | solution.py:79
  28.7 1.6 copy.20
  30.3 4.4 copy.21
  34.7 3.0 copy.33
  37.7 10.8 %copy.28 = bf16[128,7,4096]{0,2,1:T(8,128)(2,1)} copy(bf16[128,7,4096]{2,0,1:T(8,128)(2,1)} %param.4) | data formatting | bytes 14680064 | tf_op args[0]
  48.5 21.3 %copy.29 = bf16[128,7,64,64]{3,2,1,0:T(8,128)(2,1)} copy(bf16[128,7,64,64]{0,3,2,1:T(8,128)(2,1)} %bitcast.55) | data formatting | bytes 14680064 | tf_op jit(solution)/shard_map/reshape | solution.py:51
  69.8 3.4 constant_dynamic-update-slice_fusion.6
  73.2 3.8 select_maximum_fusion
  77.0 1.7 fusion.19
  78.7 4.2 stack.25
  82.9 4.1 copy.22
  87.0 4.2 stack.26
  91.2 4.1 copy.23
  95.3 3.1 pad_maximum_fusion.2
  98.5 4.2 stack.27
  102.7 4.1 copy.24
  106.8 4.3 stack.28
  111.1 4.1 copy.25
  115.2 4.2 stack.29
  119.4 4.1 copy.26
  123.5 3.2 stack.30
  126.8 4.1 copy.27
  130.9 3.5 constant_dynamic-update-slice_fusion.5
  134.4 3.6 constant_dynamic-update-slice_fusion.4
  138.0 1.8 constant_dynamic-update-slice_fusion.3
  139.8 1.8 constant_dynamic-update-slice_fusion.2
  141.6 1.8 constant_dynamic-update-slice_fusion.1
  143.3 1.8 constant_dynamic-update-slice_fusion
  145.1 19.6 %convert_bitcast_fusion = bf16[128,7,64,64]{2,3,1,0:T(8,128)(2,1)} fusion(bf16[128,64,64,1]{2,1,3,0:T(8,128)(2,1)S(1)} %copy.33, bf16[128,7,64,64]{2,3,1,0:T(8,128)(2,1)} %constant_dynamic-update-slice_fusion, bf16[128,7,64,64]{3,2,1,0:T(8,128)(2,1)} %copy.29), kind=kOutput, calls=%fused_computation.3 | convolution fusion | flops 946864128 | bytes 23068672 | tf_op jit(solution)/shard_map/ecr,ekcd->ekrd/dot_general | solution.py:56
  164.7 19.6 %copy.32 = bf16[128,7,64,64]{3,2,1,0:T(8,128)(2,1)} copy(bf16[128,7,64,64]{2,3,1,0:T(8,128)(2,1)} %convert_bitcast_fusion) | data formatting | bytes 14680064 | tf_op jit(solution)/shard_map/convert_element_type | solution.py:58
  184.3 20.0 %reshape.106 = bf16[896,4096]{1,0:T(8,128)(2,1)} reshape(bf16[128,7,64,64]{3,2,1,0:T(8,128)(2,1)} %copy.32) | data formatting | bytes 14680064 | tf_op jit(solution)/shard_map/reshape | solution.py:59
  204.4 20.9 %convolution_convert_fusion = bf16[1792,4096]{1,0:T(8,128)(2,1)} fusion(bf16[896,4096]{1,0:T(8,128)(2,1)} %reshape.106, s32[896]{0:T(1024)S(1)} %multiply_add_fusion.1), kind=kOutput, calls=%fused_computation | convolution fusion | flops 13162283008 | bytes 22023680 | tf_op jit(solution)/shard_map/dot_general | solution.py:70
  225.2 7.3 %all-to-all-start.1 = ((bf16[16,112,4096]{2,1,0:T(8,128)(2,1)}), bf16[16,112,4096]{2,1,0:T(8,128)(2,1)}, u32[]{:S(2)}, u32[]{:S(2)}) async-start(bf16[16,112,4096]{2,1,0:T(8,128)(2,1)} %bitcast.59), calls=%async_computation.1 | async-start | bytes 29360128 | tf_op jit(solution)/shard_map/all_to_all | solution.py:78
  232.5 0.5 broadcast.118
  233.0 0.7 reduce.7
  233.7 221.7 %all-to-all-done.1 = bf16[16,112,4096]{2,1,0:T(8,128)(2,1)} async-done(((bf16[16,112,4096]{2,1,0:T(8,128)(2,1)}), bf16[16,112,4096]{2,1,0:T(8,128)(2,1)}, u32[]{:S(2)}, u32[]{:S(2)}) %all-to-all-start.1) | async-done | bytes 14680096 | tf_op jit(solution)/shard_map/all_to_all | solution.py:78
  455.5 8.8 %fusion.14 = f32[128,4096]{1,0:T(8,128)} fusion(bf16[1792,4096]{1,0:T(8,128)(2,1)} %bitcast.11, s32[1792]{0:T(1024)S(1)} %eq.61), kind=kOutput, calls=%fused_computation.29 | convolution fusion | flops 1879277568 | bytes 16784384 | tf_op jit(solution)/shard_map/sc,sv->cv/dot_general | solution.py:84
  (27 shorter events, 0.7 us)
Async XLA Ops:
  1.1 9.7 %collective-permute-start = (bf16[1,4,8,4096]{3,2,1,0:T(8,128)(2,1)S(1)}, bf16[1,4,8,4096]{3,2,1,0:T(8,128)(2,1)S(1)}, u32[]{:S(2)}, u32[]{:S(2)}) collective-permute-start(bf16[1,4,8,4096]{3,2,1,0:T(8,128)(2,1)S(1)} %get-tuple-element.15), channel_id=1, source_target_pairs={{0,16},{16,32},{32,48},{48,64},{64,80},{80,96},{96,112},{112,128},... | collective-permute-start | bytes 786440 | tf_op jit(solution)/shard_map/ppermute | solution.py:21
  3.0 7.8 %collective-permute-start.1 = (bf16[1,4,8,4096]{3,2,1,0:T(8,128)(2,1)S(1)}, bf16[1,4,8,4096]{3,2,1,0:T(8,128)(2,1)S(1)}, u32[]{:S(2)}, u32[]{:S(2)}) collective-permute-start(bf16[1,4,8,4096]{3,2,1,0:T(8,128)(2,1)S(1)} %get-tuple-element.16), channel_id=1, source_target_pairs={{16,0},{32,16},{48,32},{64,48},{80,64},{96,80},{112,96},{128,112},... | collective-permute-start | bytes 786440 | tf_op jit(solution)/shard_map/ppermute | solution.py:22
  10.8 10.1 %copy-start.6 = (bf16[1,4,8,4096]{3,2,1,0:T(8,128)(2,1)}, bf16[1,4,8,4096]{3,2,1,0:T(8,128)(2,1)S(1)}, u32[]{:S(2)}) copy-start(bf16[1,4,8,4096]{3,2,1,0:T(8,128)(2,1)S(1)} %collective-permute-done.1) | copy-start | bytes 786436
  13.0 60.2 %collective-permute-start.2 = (bf16[6,1,8,4096]{3,2,1,0:T(8,128)(2,1)}, bf16[6,1,8,4096]{3,2,1,0:T(8,128)(2,1)}, u32[]{:S(2)}, u32[]{:S(2)}) collective-permute-start(bf16[6,1,8,4096]{3,2,1,0:T(8,128)(2,1)} %get-tuple-element.11), channel_id=1, source_target_pairs={{0,1},{1,2},{2,3},{3,4},{4,5},{5,6},{6,7},{7,8},{8,9},{9,10},{10,1... | collective-permute-start | bytes 1179656 | tf_op jit(solution)/shard_map/ppermute | solution.py:21
  17.1 56.1 %collective-permute-start.3 = (bf16[6,1,8,4096]{3,2,1,0:T(8,128)(2,1)}, bf16[6,1,8,4096]{3,2,1,0:T(8,128)(2,1)}, u32[]{:S(2)}, u32[]{:S(2)}) collective-permute-start(bf16[6,1,8,4096]{3,2,1,0:T(8,128)(2,1)} %get-tuple-element.12), channel_id=1, source_target_pairs={{1,0},{2,1},{3,2},{4,3},{5,4},{6,5},{7,6},{8,7},{9,8},{10,9},{11,1... | collective-permute-start | bytes 1179656 | tf_op jit(solution)/shard_map/ppermute | solution.py:22
  20.9 204.3 %all-to-all-start = ((s32[16,1,112]{2,1,0:T(1,128)}), s32[16,1,112]{2,1,0:T(1,128)S(1)}, u32[]{:S(2)}, u32[]{:S(2)}) async-start(s32[16,1,112]{2,1,0:T(1,128)} %add.28), calls=%async_computation | async-start | bytes 16384 | tf_op jit(solution)/shard_map/all_to_all | solution.py:79
  48.5 24.7 %copy-start = (bf16[128,4096]{1,0:T(8,128)(2,1)S(1)}, bf16[128,4096]{1,0:T(8,128)(2,1)}, u32[]{:S(2)}) copy-start(bf16[128,4096]{1,0:T(8,128)(2,1)} %param.5) | copy-start | bytes 3145732
  106.8 16.7 %copy-start.5 = (bf16[4,4,8,4096]{3,2,1,0:T(8,128)(2,1)S(1)}, bf16[4,4,8,4096]{3,2,1,0:T(8,128)(2,1)}, u32[]{:S(2)}) copy-start(bf16[4,4,8,4096]{3,2,1,0:T(8,128)(2,1)} %get-tuple-element.13) | copy-start | bytes 3145732
  130.9 7.1 %copy-start.1 = (bf16[128,1,64,64]{2,3,1,0:T(8,128)(2,1)S(1)}, bf16[128,1,64,64]{2,3,1,0:T(8,128)(2,1)}, u32[]{:S(2)}) copy-start(bf16[128,1,64,64]{2,3,1,0:T(8,128)(2,1)} %copy.24) | copy-start | bytes 3145732
  130.9 8.9 %copy-start.2 = (bf16[128,1,64,64]{2,3,1,0:T(8,128)(2,1)S(1)}, bf16[128,1,64,64]{2,3,1,0:T(8,128)(2,1)}, u32[]{:S(2)}) copy-start(bf16[128,1,64,64]{2,3,1,0:T(8,128)(2,1)} %copy.25) | copy-start | bytes 3145732
  134.4 7.2 %copy-start.3 = (bf16[128,1,64,64]{2,3,1,0:T(8,128)(2,1)S(1)}, bf16[128,1,64,64]{2,3,1,0:T(8,128)(2,1)}, u32[]{:S(2)}) copy-start(bf16[128,1,64,64]{2,3,1,0:T(8,128)(2,1)} %copy.26) | copy-start | bytes 3145732
  138.0 5.4 %copy-start.4 = (bf16[128,1,64,64]{2,3,1,0:T(8,128)(2,1)S(1)}, bf16[128,1,64,64]{2,3,1,0:T(8,128)(2,1)}, u32[]{:S(2)}) copy-start(bf16[128,1,64,64]{2,3,1,0:T(8,128)(2,1)} %copy.27) | copy-start | bytes 3145732
  225.2 230.3 %all-to-all-start.1 = ((bf16[16,112,4096]{2,1,0:T(8,128)(2,1)}), bf16[16,112,4096]{2,1,0:T(8,128)(2,1)}, u32[]{:S(2)}, u32[]{:S(2)}) async-start(bf16[16,112,4096]{2,1,0:T(8,128)(2,1)} %bitcast.59), calls=%async_computation.1 | async-start | bytes 29360128 | tf_op jit(solution)/shard_map/all_to_all | solution.py:78
where the time goes:
time: 467 us; the launch traced here: 464 us
  waiting for transfers between devices  222 us (48%)
  local copies, waits for them, and re-layouts  153 us (33%)
  matrix products  49.2 us (11%)
  starting transfers between devices  26 us (6%)
  other arithmetic  14.4 us (3%)
    all_to_all x1, waiting for transfers between devices, on_device(): lax.all_to_all(outgoing, 'dom', split_axis=0, concat_axis=0, tiled=True)  222 us
    another operation x14, local copies, waits for them, and re-layouts, neighbour_stack(): jnp.stack([middle, padded[1:-1, 1:-1, :-2], padded[1:-1, 1:-1, 2:], padde...  55.2 us
    unnamed x23, local copies, waits for them, and re-layouts  29.1 us
    reshape x1, local copies, waits for them, and re-layouts, on_device(): couple = a_blocks.reshape(elements, PAIRS, BLOCK, BLOCK)  21.3 us
    dot_general x1, matrix products, on_device(): jnp.dot(slot_table, flat_terms, preferred_element_type=jnp.float32)  20.9 us
    reshape x1, local copies, waits for them, and re-layouts, on_device(): flat_terms = galerkin_terms.reshape(elements * PAIRS, square)  20 us
    convert_element_type x1, local copies, waits for them, and re-layouts, on_device(): galerkin_terms = jnp.einsum('ecr,ekcd->ekrd', self_rows, product, preferr...  19.6 us
    dot_general x1, matrix products, on_device(): jnp.einsum('ecr,ekcd->ekrd', self_rows, product, preferred_element_type=j...  19.6 us
  transfers between devices with their start and end apart: 6, of which 1 were waited for; matrix products, arithmetic and copies ran while one was open for 44% of the time, Pallas kernels for 0%

commit v1 on v0

v1 whole, which is shorter than its diff:
```python
import functools

import jax
import jax.numpy as jnp
from jax import lax
from jax.experimental import pallas as pl
from jax.experimental.pallas import tpu as pltpu
from jax.sharding import PartitionSpec as P

BLOCK = 64
PAIRS = 7
EX = 8
EY = 4
EZ = 4
E_DEV = EX * EY * EZ
CB_DEV = 128
SQUARE = BLOCK * BLOCK
ROWS = SQUARE // 128
GROUP = 16
FACE = 32
ZERO_SLOT = E_DEV + 4 * FACE
DRAIN = 64


def spread_rows(flat, scratch, base):
    for t in range(ROWS):
        piece = flat(t).astype(jnp.float32)
        scratch[pl.ds(base + t, GROUP, stride=ROWS), :] = piece


def galerkin_kernel(
    rank_ref, block_ref, a_ref, p_ref, ym_ref, yp_ref, zm_ref, zp_ref, out_ref,
    acc, weights, lefts, rows, stage, sems,
):
    step = pl.program_id(0)
    low = lax.broadcasted_iota(jnp.int32, (ROWS, 128), 1) < BLOCK

    def both_orders(half_rows):
        return jnp.concatenate([half_rows, pltpu.roll(half_rows, BLOCK, 1)], axis=0)

    @pl.when(step == 0)
    def _prepare():
        def clear(i, _):
            acc[pl.ds(i * 8, 8)] = jnp.zeros((8, ROWS, 128), jnp.float32)
            return 0

        lax.fori_loop(0, acc.shape[0] // 8, clear, 0)
        weights[ZERO_SLOT] = jnp.zeros((128, 128), jnp.bfloat16)

        r = lax.broadcasted_iota(jnp.int32, (128, BLOCK), 0)
        c = lax.broadcasted_iota(jnp.int32, (128, BLOCK), 1)
        wanted = (((r % 2) + (r // BLOCK)) % 2) * ROWS + (r % BLOCK) // 2
        place = (c == wanted).astype(jnp.float32).astype(jnp.bfloat16)
        r = lax.broadcasted_iota(jnp.int32, (BLOCK, 128), 0)
        c = lax.broadcasted_iota(jnp.int32, (BLOCK, 128), 1)
        v = r // ROWS
        pick = (c == v * BLOCK + 2 * (r % ROWS) + v).astype(jnp.float32).astype(jnp.bfloat16)
        r = lax.broadcasted_iota(jnp.int32, (128, 128), 0)
        c = lax.broadcasted_iota(jnp.int32, (128, 128), 1)
        diagonal = (r // BLOCK) == (c // BLOCK)

        def prepare(ref, count, slot0, local):
            def group(g, _):
                base = pl.multiple_of(g * GROUP, GROUP)
                spread_rows(
                    lambda t: ref[pl.ds(base, GROUP), t * 128 : (t + 1) * 128], rows, 0
                )
                for i in range(GROUP):
                    own = rows[i * ROWS : (i + 1) * ROWS, :]
                    stacked = both_orders(own).astype(jnp.bfloat16)
                    wide = jnp.dot(place, stacked, preferred_element_type=jnp.float32)
                    wide = jnp.where(diagonal, wide, 0.0).astype(jnp.bfloat16)
                    weights[slot0 + base + i] = wide
                    if local:
                        left = lax.dot_general(
                            pick, stacked, (((1,), (1,)), ((), ())),
                            preferred_element_type=jnp.float32,
                        )
                        lefts[base + i] = left.astype(jnp.bfloat16)
                return 0

            lax.fori_loop(0, count // GROUP, group, 0)

        prepare(p_ref, E_DEV, 0, True)
        prepare(ym_ref, FACE, E_DEV, False)
        prepare(yp_ref, FACE, E_DEV + FACE, False)
        prepare(zm_ref, FACE, E_DEV + 2 * FACE, False)
        prepare(zp_ref, FACE, E_DEV + 3 * FACE, False)

    def relayout(k, _):
        spread_rows(
            lambda t: a_ref[k, :, t * 128 : (t + 1) * 128], rows, k * (GROUP * ROWS)
        )
        return 0

    lax.fori_loop(0, PAIRS, relayout, 0)

    def element(i, _):
        e = step * GROUP + i
        x = e % EX
        y = (e // EX) % EY
        z = e // (EX * EY)
        slots = (
            e,
            jnp.where(x > 0, e - 1, ZERO_SLOT),
            jnp.where(x < EX - 1, e + 1, ZERO_SLOT),
            jnp.where(y > 0, e - EX, E_DEV + z * EX + x),
            jnp.where(y < EY - 1, e + EX, E_DEV + FACE + z * EX + x),
            jnp.where(z > 0, e - EX * EY, E_DEV + 2 * FACE + y * EX + x),
            jnp.where(z < EZ - 1, e + EX * EY, E_DEV + 3 * FACE + y * EX + x),
        )
        stacked = []
        for k in range(PAIRS):
            start = pl.multiple_of((k * GROUP + i) * ROWS, ROWS)
            couple = rows[pl.ds(start, ROWS), :].astype(jnp.bfloat16)
            product = jnp.dot(couple, weights[slots[k]], preferred_element_type=jnp.float32)
            stacked.append(both_orders(product).astype(jnp.bfloat16))
        both = jnp.dot(
            lefts[e], jnp.concatenate(stacked, axis=1), preferred_element_type=jnp.float32
        )
        for k in range(PAIRS):
            own = both[:, k * 128 : (k + 1) * 128]
            term = jnp.where(low, own[:ROWS], own[ROWS:])
            target = rank_ref[e * PAIRS + k] * CB_DEV + block_ref[k, e]
            acc[target] += term.astype(jnp.bfloat16).astype(jnp.float32)
        return 0

    lax.fori_loop(0, GROUP, element, 0)

    @pl.when(step == pl.num_programs(0) - 1)
    def _drain():
        total = acc.shape[0] // DRAIN

        def copy(n, slot):
            return pltpu.make_async_copy(
                stage.at[slot], out_ref.at[pl.ds(n * DRAIN, DRAIN)], sems.at[slot]
            )

        def chunk(n, _):
            slot = n % 2

            @pl.when(n >= 2)
            def _():
                copy(n - 2, slot).wait()

            def cast(i, _):
                stage[slot, pl.ds(i * 8, 8)] = acc[pl.ds(n * DRAIN + i * 8, 8)].astype(
                    jnp.bfloat16
                )
                return 0

            lax.fori_loop(0, DRAIN // 8, cast, 0)
            copy(n, slot).start()
            return 0

        lax.fori_loop(0, total, chunk, 0)
        copy(total - 2, (total - 2) % 2).wait()
        copy(total - 1, (total - 1) % 2).wait()


def local_sums(ranks, blocks, a, p, halos, owners):
    whole = pl.BlockSpec(memory_space=pltpu.VMEM)
    smem = pl.BlockSpec(memory_space=pltpu.SMEM)
    return pl.pallas_call(
        galerkin_kernel,
        grid=(E_DEV // GROUP,),
        in_specs=[
            smem,
            smem,
            pl.BlockSpec((PAIRS, GROUP, SQUARE), lambda i: (0, i, 0)),
            whole, whole, whole, whole, whole,
        ],
        out_specs=pl.BlockSpec(memory_space=pl.ANY),
        out_shape=jax.ShapeDtypeStruct((owners * CB_DEV, ROWS, 128), jnp.bfloat16),
        scratch_shapes=[
            pltpu.VMEM((owners * CB_DEV, ROWS, 128), jnp.float32),
            pltpu.VMEM((ZERO_SLOT + 1, 128, 128), jnp.bfloat16),
            pltpu.VMEM((E_DEV, BLOCK, BLOCK), jnp.bfloat16),
            pltpu.VMEM((PAIRS * GROUP * ROWS, 128), jnp.float32),
            pltpu.VMEM((2, DRAIN, ROWS, 128), jnp.bfloat16),
            pltpu.SemaphoreType.DMA((2,)),
        ],
        compiler_params=pltpu.CompilerParams(
            dimension_semantics=("arbitrary",), vmem_limit_bytes=60 * 1024 * 1024
        ),
        name="galerkin_sums",
    )(ranks, blocks, a, p, *halos)


def faces(p):
    brick = p.reshape(EZ, EY, EX, SQUARE)
    found = []
    for axis, dim in (("dom", 1), ("slab", 0)):
        size = lax.axis_size(axis)
        up = [(i, i + 1) for i in range(size - 1)]
        down = [(j, i) for i, j in up]
        length = brick.shape[dim]
        last = lax.slice_in_dim(brick, length - 1, length, axis=dim).reshape(FACE, SQUARE)
        first = lax.slice_in_dim(brick, 0, 1, axis=dim).reshape(FACE, SQUARE)
        found += [lax.ppermute(last, axis, up), lax.ppermute(first, axis, down)]
    return found


def flat_kernel(in_ref, out_ref, scratch):
    scratch[...] = in_ref[...].reshape(GROUP * ROWS, 128).astype(jnp.float32)
    for t in range(ROWS):
        out_ref[:, t * 128 : (t + 1) * 128] = scratch[pl.ds(t, GROUP, stride=ROWS), :]


def flatten_blocks(x):
    return pl.pallas_call(
        flat_kernel,
        grid=(CB_DEV // GROUP,),
        in_specs=[pl.BlockSpec((GROUP, ROWS, 128), lambda i: (i, 0, 0))],
        out_specs=pl.BlockSpec((GROUP, SQUARE), lambda i: (i, 0)),
        out_shape=jax.ShapeDtypeStruct((CB_DEV, SQUARE), jnp.float32),
        scratch_shapes=[pltpu.VMEM((GROUP * ROWS, 128), jnp.float32)],
        name="flatten_blocks",
    )(x)


def on_device(a_blocks, p_blocks, dest_rank, dest_block):
    owners = lax.axis_size("dom")
    halos = faces(p_blocks)
    sums = local_sums(
        dest_rank.reshape(-1),
        dest_block.T,
        jnp.swapaxes(a_blocks, 0, 1),
        p_blocks,
        halos,
        owners,
    )
    mine = lax.psum_scatter(sums, "dom", scatter_dimension=0, tiled=True)
    return flatten_blocks(mine)


def solution(mesh):
    return jax.shard_map(
        on_device,
        mesh=mesh,
        in_specs=(
            P(("slab", "dom"), None, None),
            P(("slab", "dom"), None),
            P(("slab", "dom"), None),
            P(("slab", "dom"), None),
        ),
        out_specs=P(("slab", "dom"), None),
        check_vma=False,
    )
```

time: 467 us -> 249 us (0.53)
  the two profiles are of different devices: /device:TPU:32 before, /device:TPU:96 now
where the time goes in v1:
time: 249 us; the launch traced here: 247 us
  waiting for transfers between devices  125 us (50%)
  Pallas kernels  95 us (38%)
  between operations  13.5 us (5%)
  starting transfers between devices  10.2 us (4%)
  local copies, waits for them, and re-layouts  2.84 us (1%)
    reduce_scatter x1, waiting for transfers between devices, on_device(): mine = lax.psum_scatter(sums, 'dom', scatter_dimension=0, tiled=True)  121 us
    pallas_call x1, Pallas kernels, local_sums(): pl.pallas_call(galerkin_kernel, grid=(E_DEV // GROUP,), in_specs=[smem, s...  89.1 us
    ppermute x4, starting transfers between devices, faces(): found += [lax.ppermute(last, axis, up), lax.ppermute(first, axis, down)]  10.2 us
    pallas_call x1, Pallas kernels, flatten_blocks(): pl.pallas_call(flat_kernel, grid=(CB_DEV // GROUP,), in_specs=[pl.BlockSp...  5.97 us
  transfers between devices with their start and end apart: 5, of which 3 were waited for; matrix products, arithmetic and copies ran while one was open for 1% of the time, Pallas kernels for 0%

profile of v1, /device:TPU:96, one launch (start us, length us, event | category | flops | bytes accessed | tf_op | source)
XLA Modules:
  0.0 247.4 jit_solution(3793175003027889841)
XLA Ops:
  6.5 0.0 reduce-scatter.2.cloned.1.call-start
  6.5 1.1 slice_bitcast_fusion
  7.6 1.3 collective-permute-start.1
  8.9 4.6 %collective-permute-start = (bf16[32,4096]{1,0:T(8,128)(2,1)S(1)}, bf16[32,4096]{1,0:T(8,128)(2,1)S(1)}, u32[]{:S(2)}, u32[]{:S(2)}) collective-permute-start(bf16[32,4096]{1,0:T(8,128)(2,1)S(1)} %get-tuple-element.8), channel_id=1, source_target_pairs={{0,1},{1,2},{2,3},{3,4},{4,5},{5,6},{6,7},{7,8},{8,9},{9,10},{10,1... | collective-permute-start | bytes 786440 | tf_op jit(solution)/shard_map/ppermute | solution.py:200
  13.5 1.1 fusion
  14.5 1.9 collective-permute-start.3
  16.5 2.4 collective-permute-start.2
  18.9 1.3 reduce.rank_ref
  20.2 0.0 collective-permute-done.1.yp_ref
  20.2 0.0 copy-start
  20.2 0.0 collective-permute-done.ym_ref
  20.2 0.0 copy-start.1
  20.2 0.1 collective-permute-done.3.zp_ref
  20.3 0.0 copy-start.2
  20.3 3.8 %collective-permute-done.2.zm_ref = bf16[32,4096]{1,0:T(8,128)(2,1)S(1)} collective-permute-done((bf16[32,4096]{1,0:T(8,128)(2,1)S(1)}, bf16[32,4096]{1,0:T(8,128)(2,1)S(1)}, u32[]{:S(2)}, u32[]{:S(2)}) %collective-permute-start.2) | collective-permute-done | bytes 262176 | tf_op jit(solution)/shard_map/ppermute | solution.py:200
  24.2 0.0 copy-start.3
  24.2 0.0 copy-done
  24.2 0.0 copy-done.1
  24.2 0.0 copy-done.2
  24.2 0.7 copy-done.3
  24.9 89.1 %galerkin_sums.1 = bf16[2048,32,128]{2,1,0:T(8,128)(2,1)} custom-call(s32[896]{0:T(1024)} %reduce.rank_ref, s32[7,128]{1,0:T(8,128)} %bitcast.13, bf16[7,128,4096]{2,1,0:T(8,128)(2,1)} %bitcast.11, bf16[128,4096]{1,0:T(8,128)(2,1)} %p_ref.1, bf16[32,4096]{1,0:T(8,128)(2,1)} %copy-done.1, bf16[32,4096]{1,0:T(8,128)(2,1)} %copy-done, ...), custom_call_target="tpu_custom_call" | custom-call | tf_op jit(solution)/shard_map/galerkin_sums/pallas_call | solution.py:164
  113.9 0.0 reduce-scatter.2.cloned.1.call-update
  114.0 120.7 %reduce-scatter.2.cloned.1.call-done.in_ref = bf16[128,32,128]{2,1,0:T(8,128)(2,1)} async-done(((bf16[2048,32,128]{2,1,0:T(8,128)(2,1)}), bf16[128,32,128]{2,1,0:T(8,128)(2,1)}) %reduce-scatter.2.cloned.1.call-update) | async-done | bytes 1048592 | tf_op jit(solution)/shard_map/reduce_scatter | solution.py:233
  234.6 6.0 %flatten_blocks.1 = f32[128,4096]{1,0:T(8,128)} custom-call(bf16[128,32,128]{2,1,0:T(8,128)(2,1)} %reduce-scatter.2.cloned.1.call-done.in_ref), custom_call_target="tpu_custom_call" | custom-call | tf_op jit(solution)/shard_map/flatten_blocks/pallas_call | solution.py:211
Async XLA Ops:
  6.5 228.1 %reduce-scatter.2.cloned.1.call-start = ((), (), s32[]{:S(2)}) async-start(), calls=%async_computation.1 | async-start | bytes 17825792 | tf_op jit(solution)/shard_map/reduce_scatter | solution.py:233
  7.6 12.6 %collective-permute-start.1 = (bf16[32,4096]{1,0:T(8,128)(2,1)S(1)}, bf16[32,4096]{1,0:T(8,128)(2,1)S(1)}, u32[]{:S(2)}, u32[]{:S(2)}) collective-permute-start(bf16[32,4096]{1,0:T(8,128)(2,1)S(1)} %get-tuple-element.7), channel_id=1, source_target_pairs={{1,0},{2,1},{3,2},{4,3},{5,4},{6,5},{7,6},{8,7},{9,8},{10,9},{11,1... | collective-permute-start | bytes 786440 | tf_op jit(solution)/shard_map/ppermute | solution.py:200
  8.9 11.3 %collective-permute-start = (bf16[32,4096]{1,0:T(8,128)(2,1)S(1)}, bf16[32,4096]{1,0:T(8,128)(2,1)S(1)}, u32[]{:S(2)}, u32[]{:S(2)}) collective-permute-start(bf16[32,4096]{1,0:T(8,128)(2,1)S(1)} %get-tuple-element.8), channel_id=1, source_target_pairs={{0,1},{1,2},{2,3},{3,4},{4,5},{5,6},{6,7},{7,8},{8,9},{9,10},{10,1... | collective-permute-start | bytes 786440 | tf_op jit(solution)/shard_map/ppermute | solution.py:200
  14.5 5.8 %collective-permute-start.3 = (bf16[32,4096]{1,0:T(8,128)(2,1)S(1)}, bf16[32,4096]{1,0:T(8,128)(2,1)S(1)}, u32[]{:S(2)}, u32[]{:S(2)}) collective-permute-start(bf16[32,4096]{1,0:T(8,128)(2,1)S(1)} %get-tuple-element.5), channel_id=1, source_target_pairs={{16,0},{32,16},{48,32},{64,48},{80,64},{96,80},{112,96},{128,112},... | collective-permute-start | bytes 786440 | tf_op jit(solution)/shard_map/ppermute | solution.py:200
  16.5 7.7 %collective-permute-start.2 = (bf16[32,4096]{1,0:T(8,128)(2,1)S(1)}, bf16[32,4096]{1,0:T(8,128)(2,1)S(1)}, u32[]{:S(2)}, u32[]{:S(2)}) collective-permute-start(bf16[32,4096]{1,0:T(8,128)(2,1)S(1)} %get-tuple-element.6), channel_id=1, source_target_pairs={{0,16},{16,32},{32,48},{48,64},{64,80},{80,96},{96,112},{112,128},... | collective-permute-start | bytes 786440 | tf_op jit(solution)/shard_map/ppermute | solution.py:200
  20.2 4.0 %copy-start = (bf16[32,4096]{1,0:T(8,128)(2,1)}, bf16[32,4096]{1,0:T(8,128)(2,1)S(1)}, u32[]{:S(2)}) copy-start(bf16[32,4096]{1,0:T(8,128)(2,1)S(1)} %collective-permute-done.1.yp_ref) | copy-start | bytes 786436
  20.2 4.0 %copy-start.1 = (bf16[32,4096]{1,0:T(8,128)(2,1)}, bf16[32,4096]{1,0:T(8,128)(2,1)S(1)}, u32[]{:S(2)}) copy-start(bf16[32,4096]{1,0:T(8,128)(2,1)S(1)} %collective-permute-done.ym_ref) | copy-start | bytes 786436
  20.3 3.8 %copy-start.2 = (bf16[32,4096]{1,0:T(8,128)(2,1)}, bf16[32,4096]{1,0:T(8,128)(2,1)S(1)}, u32[]{:S(2)}) copy-start(bf16[32,4096]{1,0:T(8,128)(2,1)S(1)} %collective-permute-done.3.zp_ref) | copy-start | bytes 786436
  24.2 0.7 copy-start.3
Sparse Core Ops, SparseCore 0:
  114.1 120.4 reduce-scatter.1

commit v2 on v1

v2 whole, which is shorter than its diff:
```python
import jax
import jax.numpy as jnp
from jax import lax
from jax.experimental import pallas as pl
from jax.experimental.pallas import tpu as pltpu
from jax.sharding import PartitionSpec as P

BLOCK = 64
PAIRS = 7
EX = 8
EY = 4
EZ = 4
E_DEV = EX * EY * EZ
CB_DEV = 128
SQUARE = BLOCK * BLOCK
ROWS = SQUARE // 128
HALF = ROWS // 2
GROUP = 16
FACE = 32
SIDE = 4
OWNERS = SIDE * SIDE
ZERO_SLOT = E_DEV + 4 * FACE
PART = CB_DEV // 4
SLOT = SIDE * PART
SLOTS = OWNERS * CB_DEV // SLOT
BUFFERS = 4
SLOT_OF = 0x53201476


def spread_rows(flat, scratch, base):
    for t in range(ROWS):
        scratch[pl.ds(base + t, GROUP, stride=ROWS), :] = flat(t).astype(jnp.float32)


def clear(acc):
    def body(i, _):
        acc[pl.ds(i * 16, 16)] = jnp.zeros((16, HALF, 128), jnp.float32)
        return 0

    lax.fori_loop(0, acc.shape[0] // 16, body, 0)


def add_terms(step, half, target_ref, lefts, q_ref, acc):
    low = lax.broadcasted_iota(jnp.int32, (HALF, PAIRS * 128), 1) % 128 < BLOCK

    def element(i, _):
        e = step * GROUP + i
        both = jnp.dot(
            lefts[e, half * ROWS : (half + 1) * ROWS, :], q_ref[i],
            preferred_element_type=jnp.float32,
        )
        terms = jnp.where(low, both[:HALF], both[HALF:])
        terms = terms.astype(jnp.bfloat16).astype(jnp.float32)
        for k in range(PAIRS):
            acc[target_ref[e * PAIRS + k]] += terms[:, k * 128 : (k + 1) * 128]
        return 0

    lax.fori_loop(0, GROUP, element, 0, unroll=4)


def drain(acc, stage, sems, outs):
    places = []
    for out in outs:
        places += [out.at[i] for i in range(out.shape[0])]
    copies = []
    for n in range(SLOTS):
        buffer = n % BUFFERS
        if n >= BUFFERS:
            copies[n - BUFFERS].wait()

        def cast(i, _):
            blocks = acc[pl.ds(n * SLOT + i * 16, 16)]
            stage[buffer, pl.ds(i * 16, 16)] = blocks.astype(jnp.bfloat16)
            return 0

        lax.fori_loop(0, SLOT // 16, cast, 0)
        copy = pltpu.make_async_copy(stage.at[buffer], places[n], sems.at[buffer])
        copy.start()
        copies.append(copy)
    for copy in copies[-BUFFERS:]:
        copy.wait()


def first_kernel(target_ref, a_ref, p_ref, ym_ref, yp_ref, zm_ref, zp_ref, *refs):
    q_ref, left_ref, *outs = refs[:12]
    acc, weights, rows, stage, sems = refs[12:]
    step = pl.program_id(0)

    @pl.when(step == 0)
    def _prepare():
        clear(acc)
        weights[ZERO_SLOT] = jnp.zeros((128, 256), jnp.bfloat16)
        low = lax.broadcasted_iota(jnp.int32, (ROWS, 128), 1) < BLOCK
        low2 = lax.broadcasted_iota(jnp.int32, (BLOCK, 128), 1) < BLOCK
        r = lax.broadcasted_iota(jnp.int32, (BLOCK, BLOCK), 0)
        c = lax.broadcasted_iota(jnp.int32, (BLOCK, BLOCK), 1)
        place = (c == (r % 2) * ROWS + r // 2).astype(jnp.float32).astype(jnp.bfloat16)
        r = lax.broadcasted_iota(jnp.int32, (BLOCK, 128), 0)
        c = lax.broadcasted_iota(jnp.int32, (BLOCK, 128), 1)
        v = (r // HALF) % 2
        lane = v * BLOCK + 2 * ((r // ROWS) * HALF + r % HALF) + v
        pick = (c == lane).astype(jnp.float32).astype(jnp.bfloat16)

        def prepare(ref, count, slot0, local):
            def group(g, _):
                base = pl.multiple_of(g * GROUP, GROUP)
                spread_rows(
                    lambda t: ref[pl.ds(base, GROUP), t * 128 : (t + 1) * 128], rows, 0
                )
                for i in range(0, GROUP, 2):
                    ordered = []
                    for j in (i, i + 1):
                        own = rows[j * ROWS : (j + 1) * ROWS, :]
                        turned = pltpu.roll(own, BLOCK, 1)
                        ordered.append(
                            jnp.concatenate(
                                [jnp.where(low, own, turned), jnp.where(low, turned, own)], axis=0
                            ).astype(jnp.bfloat16)
                        )
                        if local:
                            stacked = jnp.concatenate([own, turned], axis=0)
                            left = lax.dot_general(
                                pick, stacked.astype(jnp.bfloat16), (((1,), (1,)), ((), ())),
                                preferred_element_type=jnp.float32,
                            )
                            left_ref[base + j] = left.astype(jnp.bfloat16)
                    placed = jnp.dot(
                        place, jnp.concatenate(ordered, axis=1), preferred_element_type=jnp.float32
                    )
                    for j in (0, 1):
                        twice = placed[:, j * 128 : (j + 1) * 128]
                        at_low = jnp.where(low2, twice, 0.0).astype(jnp.bfloat16)
                        at_high = jnp.where(low2, 0.0, twice).astype(jnp.bfloat16)
                        slot = slot0 + base + i + j
                        weights[slot, :BLOCK, :128] = at_low
                        weights[slot, :BLOCK, 128:] = at_high
                        weights[slot, BLOCK:, :128] = at_high
                        weights[slot, BLOCK:, 128:] = at_low
                return 0

            lax.fori_loop(0, count // GROUP, group, 0)

        prepare(p_ref, E_DEV, 0, True)
        prepare(ym_ref, FACE, E_DEV, False)
        prepare(yp_ref, FACE, E_DEV + FACE, False)
        prepare(zm_ref, FACE, E_DEV + 2 * FACE, False)
        prepare(zp_ref, FACE, E_DEV + 3 * FACE, False)

    for k in range(PAIRS):
        spread_rows(
            lambda t: a_ref[k, :, t * 128 : (t + 1) * 128], rows, k * (GROUP * ROWS)
        )

    def element(i, _):
        e = step * GROUP + i
        x = e % EX
        y = (e // EX) % EY
        z = e // (EX * EY)
        slots = (
            e,
            jnp.where(x > 0, e - 1, ZERO_SLOT),
            jnp.where(x < EX - 1, e + 1, ZERO_SLOT),
            jnp.where(y > 0, e - EX, E_DEV + z * EX + x),
            jnp.where(y < EY - 1, e + EX, E_DEV + FACE + z * EX + x),
            jnp.where(z > 0, e - EX * EY, E_DEV + 2 * FACE + y * EX + x),
            jnp.where(z < EZ - 1, e + EX * EY, E_DEV + 3 * FACE + y * EX + x),
        )
        for k in range(PAIRS):
            start = pl.multiple_of((k * GROUP + i) * ROWS, ROWS)
            couple = rows[pl.ds(start, ROWS), :].astype(jnp.bfloat16)
            product = jnp.dot(couple, weights[slots[k]], preferred_element_type=jnp.float32)
            product = product.astype(jnp.bfloat16)
            q_ref[i, :ROWS, k * 128 : (k + 1) * 128] = product[:, :128]
            q_ref[i, ROWS:, k * 128 : (k + 1) * 128] = product[:, 128:]
        return 0

    lax.fori_loop(0, GROUP, element, 0, unroll=4)
    add_terms(step, 0, target_ref, left_ref, q_ref, acc)

    @pl.when(step == pl.num_programs(0) - 1)
    def _drain():
        drain(acc, stage, sems, outs)


def second_kernel(target_ref, left_ref, q_ref, *refs):
    outs = refs[:10]
    acc, stage, sems = refs[10:]
    step = pl.program_id(0)

    @pl.when(step == 0)
    def _clear():
        clear(acc)

    add_terms(step, 1, target_ref, left_ref, q_ref, acc)

    @pl.when(step == pl.num_programs(0) - 1)
    def _drain():
        drain(acc, stage, sems, outs)


VMEM = pl.BlockSpec(memory_space=pltpu.VMEM)
SMEM = pl.BlockSpec(memory_space=pltpu.SMEM)
HBM = pl.BlockSpec(memory_space=pl.ANY)
Q_SPEC = pl.BlockSpec((GROUP, BLOCK, PAIRS * 128), lambda i: (i, 0, 0))
PACKS = [
    jax.ShapeDtypeStruct((n, SLOT, HALF, 128), jnp.bfloat16) for n in (2, 2, 1, 1, 2) * 2
]
SUMS = [
    pltpu.VMEM((BUFFERS, SLOT, HALF, 128), jnp.bfloat16),
    pltpu.SemaphoreType.DMA((BUFFERS,)),
]


def params():
    return pltpu.CompilerParams(
        dimension_semantics=("arbitrary",), vmem_limit_bytes=56 * 1024 * 1024
    )


def first_half(target, a, p, halos):
    found = pl.pallas_call(
        first_kernel,
        grid=(E_DEV // GROUP,),
        in_specs=[
            SMEM,
            pl.BlockSpec((PAIRS, GROUP, SQUARE), lambda i: (0, i, 0)),
            VMEM, VMEM, VMEM, VMEM, VMEM,
        ],
        out_specs=[Q_SPEC, VMEM] + [HBM] * len(PACKS),
        out_shape=[
            jax.ShapeDtypeStruct((E_DEV, BLOCK, PAIRS * 128), jnp.bfloat16),
            jax.ShapeDtypeStruct((E_DEV, BLOCK, BLOCK), jnp.bfloat16),
        ]
        + PACKS,
        scratch_shapes=[
            pltpu.VMEM((OWNERS * CB_DEV, HALF, 128), jnp.float32),
            pltpu.VMEM((ZERO_SLOT + 1, 128, 256), jnp.bfloat16),
            pltpu.VMEM((PAIRS * GROUP * ROWS, 128), jnp.float32),
        ]
        + SUMS,
        compiler_params=params(),
        cost_estimate=pl.CostEstimate(
            flops=10**10, bytes_accessed=40 * 10**6, transcendentals=0
        ),
        name="first_half",
    )(target, a, p, *halos)
    return found[0], found[1], found[2:]


def second_half(target, lefts, q):
    return pl.pallas_call(
        second_kernel,
        grid=(E_DEV // GROUP,),
        in_specs=[SMEM, VMEM, Q_SPEC],
        out_specs=[HBM] * len(PACKS),
        out_shape=PACKS,
        scratch_shapes=[pltpu.VMEM((OWNERS * CB_DEV, HALF, 128), jnp.float32)] + SUMS,
        compiler_params=params(),
        cost_estimate=pl.CostEstimate(
            flops=10**10, bytes_accessed=40 * 10**6, transcendentals=0
        ),
        name="second_half",
    )(target, lefts, q)


def faces(p):
    brick = p.reshape(EZ, EY, EX, SQUARE)
    found = []
    for axis, dim in (("dom", 1), ("slab", 0)):
        size = lax.axis_size(axis)
        up = [(i, i + 1) for i in range(size - 1)]
        down = [(j, i) for i, j in up]
        length = brick.shape[dim]
        last = lax.slice_in_dim(brick, length - 1, length, axis=dim).reshape(FACE, SQUARE)
        first = lax.slice_in_dim(brick, 0, 1, axis=dim).reshape(FACE, SQUARE)
        found += [lax.ppermute(last, axis, up), lax.ppermute(first, axis, down)]
    return found


def sum_places(dest_rank, dest_block):
    me = lax.axis_index("dom")
    rank = dest_rank.reshape(-1)
    block = dest_block.reshape(-1)
    dx = (rank - me) % SIDE
    dy = (rank // SIDE - me // SIDE) % SIDE
    which = block // (2 * PART)
    part = (block // PART) % 2
    hops = jnp.where(which == 0, dx, dy)
    other = jnp.where(which == 0, dy, dx)
    slot = (SLOT_OF >> (4 * (2 * hops + part))) & 7
    return ((which * (SLOTS // 2) + slot) * SIDE + other) * PART + block % PART


def ring_perms():
    def moved(dx, dy):
        return [
            (y * SIDE + x, (y + dy) % SIDE * SIDE + (x + dx) % SIDE)
            for y in range(SIDE)
            for x in range(SIDE)
        ]

    return (moved(1, 0), moved(-1, 0)), (moved(0, 1), moved(0, -1))


def added(*parts):
    total = parts[0].astype(jnp.float32)
    for part in parts[1:]:
        total = total + part.astype(jnp.float32)
    return total


def ring_sum(right, left, keep_right, keep_left, own, perms):
    forward, backward = perms
    r1 = lax.ppermute(right, "dom", forward)
    l1 = lax.ppermute(left, "dom", backward)
    r2 = lax.ppermute(added(keep_right, r1[0]).astype(jnp.bfloat16), "dom", forward)
    l2 = lax.ppermute(added(keep_left, l1[0]).astype(jnp.bfloat16), "dom", backward)
    return (own[0], r2, l1[1]), (own[1], r1[1], l2)


def exchange(packs):
    along_x, along_y = ring_perms()
    found = []
    for which, (one, two) in enumerate(((along_x, along_y), (along_y, along_x))):
        right, left, keep_right, keep_left, own = packs[which * 5 : which * 5 + 5]
        first = ring_sum(right, left, keep_right[0], keep_left[0], own, one)
        r, l = (added(*parts).reshape(SIDE, PART, HALF, 128) for parts in first)
        rb, lb = r.astype(jnp.bfloat16), l.astype(jnp.bfloat16)
        found += ring_sum(
            jnp.stack([rb[2], lb[1]]), jnp.stack([lb[2], rb[3]]), rb[1], lb[3], (r[0], l[0]), two
        )
    return found


def finish_kernel(*refs):
    *ins, out_ref, scratch = refs
    for n in range(len(ins) // 3):
        total = ins[3 * n][...] + ins[3 * n + 1][...].astype(jnp.float32)
        total = total + ins[3 * n + 2][...].astype(jnp.float32)
        half, part = divmod(n, 4)
        scratch[...] = total.reshape(PART * HALF, 128)
        for u in range(HALF):
            t = half * HALF + u
            out_ref[part * PART : (part + 1) * PART, t * 128 : (t + 1) * 128] = scratch[
                pl.ds(u, PART, stride=HALF), :
            ]


def finish(parts):
    flat = [array for triple in parts for array in triple]
    return pl.pallas_call(
        finish_kernel,
        in_specs=[VMEM] * len(flat),
        out_specs=VMEM,
        out_shape=jax.ShapeDtypeStruct((CB_DEV, SQUARE), jnp.float32),
        scratch_shapes=[pltpu.VMEM((PART * HALF, 128), jnp.float32)],
        name="finish",
    )(*flat)


def on_device(a_blocks, p_blocks, dest_rank, dest_block):
    halos = faces(p_blocks)
    target = sum_places(dest_rank, dest_block)
    q, lefts, packs = first_half(target, jnp.swapaxes(a_blocks, 0, 1), p_blocks, halos)
    parts = exchange(packs)
    parts += exchange(second_half(target, lefts, q))
    return finish(parts)


def solution(mesh):
    return jax.shard_map(
        on_device,
        mesh=mesh,
        in_specs=(
            P(("slab", "dom"), None, None),
            P(("slab", "dom"), None),
            P(("slab", "dom"), None),
            P(("slab", "dom"), None),
        ),
        out_specs=P(("slab", "dom"), None),
        check_vma=False,
    )
```

time: 249 us -> 193 us (0.78)
  waiting for transfers between devices: 125 us -> 39.5 us
  starting transfers between devices: 10.2 us -> 58.4 us
  Pallas kernels: 95 us -> 72.3 us
  local copies, waits for them, and re-layouts: 2.84 us -> 16.3 us
  between operations: 13.5 us -> 0.6 us
  other arithmetic: 1.29 us -> 5.73 us
    reduce_scatter x1 -> x0, waiting for transfers between devices: 121 us -> none  [on_device(): mine = lax.psum_scatter(sums, 'dom', scatter_dimension=0, tiled=True)]
    ppermute x0 -> x32, starting transfers between devices: none -> 48.3 us  [the longest x8 18.5 us: ring_sum(): l1 = lax.ppermute(left, 'dom', backward)]
    ppermute x0 -> x32, waiting for transfers between devices: none -> 36.6 us  [the longest x8 21.4 us: ring_sum(): r1 = lax.ppermute(right, 'dom', forward)]
    pallas_call x2 -> x3, Pallas kernels: 95 us -> 72.3 us  [the longest x1 50 us: first_half(): pl.pallas_call(first_kernel, grid=(E_DEV // GROUP,), in_specs=[SMEM, pl.B...]
    slice x0 -> x12, local copies, waits for them, and re-layouts: none -> 5.9 us  [the longest x4 2.89 us: exchange(): l[0]]
    squeeze x0 -> x8, local copies, waits for them, and re-layouts: none -> 5.3 us  [ring_sum(): return ((own[0], r2, l1[1]), (own[1], r1[1], l2))]
    convert_element_type x0 -> x20, other arithmetic: none -> 4.19 us  [the longest x8 1.84 us: ring_sum(): added(keep_right, r1[0]).astype(jnp.bfloat16)]
  transfers between devices with their start and end apart: 5 -> 36, of which waited for: 3 -> 12; matrix products, arithmetic and copies ran while one was open for 1% -> 10% of each run, Pallas kernels for 0% -> 9%
where the time goes in v2:
time: 193 us
  Pallas kernels  72.3 us (37%)
  starting transfers between devices  58.4 us (30%)
  waiting for transfers between devices  39.5 us (20%)
  local copies, waits for them, and re-layouts  16.3 us (8%)
  other arithmetic  5.73 us (3%)
    pallas_call x1, Pallas kernels, first_half(): pl.pallas_call(first_kernel, grid=(E_DEV // GROUP,), in_specs=[SMEM, pl.B...  50 us
    ppermute x8, waiting for transfers between devices, ring_sum(): r1 = lax.ppermute(right, 'dom', forward)  21.4 us
    ppermute x8, starting transfers between devices, ring_sum(): l1 = lax.ppermute(left, 'dom', backward)  18.5 us
    pallas_call x1, Pallas kernels, second_half(): pl.pallas_call(second_kernel, grid=(E_DEV // GROUP,), in_specs=[SMEM, VME...  17.9 us
    ppermute x8, starting transfers between devices, ring_sum(): lax.ppermute(added(keep_left, l1[0]).astype(jnp.bfloat16), 'dom', backward)  17.4 us
    ppermute x8, waiting for transfers between devices, ring_sum(): lax.ppermute(added(keep_right, r1[0]).astype(jnp.bfloat16), 'dom', forward)  13.1 us
    ppermute x4, starting transfers between devices, faces(): found += [lax.ppermute(last, axis, up), lax.ppermute(first, axis, down)]  10.2 us
    ppermute x8, starting transfers between devices, ring_sum(): r1 = lax.ppermute(right, 'dom', forward)  7.13 us
  transfers between devices with their start and end apart: 36, of which 12 were waited for; matrix products, arithmetic and copies ran while one was open for 10% of the time, Pallas kernels for 9%

profile of v2, /device:TPU:96, one launch (start us, length us, event | category | flops | bytes accessed | tf_op | source)
XLA Modules:
  0.0 192.9 jit_solution(5643284096926944542)
XLA Ops:
  0.0 1.1 slice_bitcast_fusion.4
  1.1 1.3 collective-permute-start.1
  2.4 4.6 %collective-permute-start = (bf16[32,4096]{1,0:T(8,128)(2,1)S(1)}, bf16[32,4096]{1,0:T(8,128)(2,1)S(1)}, u32[]{:S(2)}, u32[]{:S(2)}) collective-permute-start(bf16[32,4096]{1,0:T(8,128)(2,1)S(1)} %get-tuple-element.76), channel_id=1, source_target_pairs={{0,1},{1,2},{2,3},{3,4},{4,5},{5,6},{6,7},{7,8},{8,9},{9,10},{10,1... | collective-permute-start | bytes 786440 | tf_op jit(solution)/shard_map/ppermute | solution.py:276
  6.9 1.1 fusion.50
  8.0 1.9 collective-permute-start.3
  9.9 2.4 %collective-permute-start.2 = (bf16[32,4096]{1,0:T(8,128)(2,1)S(1)}, bf16[32,4096]{1,0:T(8,128)(2,1)S(1)}, u32[]{:S(2)}, u32[]{:S(2)}) collective-permute-start(bf16[32,4096]{1,0:T(8,128)(2,1)S(1)} %get-tuple-element.74), channel_id=1, source_target_pairs={{0,16},{16,32},{32,48},{48,64},{64,80},{80,96},{96,112},{112,128},... | collective-permute-start | bytes 786440 | tf_op jit(solution)/shard_map/ppermute | solution.py:276
  13.1 0.8 copy.7
  14.7 2.9 %collective-permute-done.2.zm_ref = bf16[32,4096]{1,0:T(8,128)(2,1)S(1)} collective-permute-done((bf16[32,4096]{1,0:T(8,128)(2,1)S(1)}, bf16[32,4096]{1,0:T(8,128)(2,1)S(1)}, u32[]{:S(2)}, u32[]{:S(2)}) %collective-permute-start.2) | collective-permute-done | bytes 262176 | tf_op jit(solution)/shard_map/ppermute | solution.py:276
  18.3 50.0 %first_half.1 = (bf16[128,64,896]{2,1,0:T(8,128)(2,1)}, bf16[128,64,64]{2,1,0:T(8,128)(2,1)}, bf16[2,128,16,128]{3,2,1,0:T(8,128)(2,1)}, bf16[2,128,16,128]{3,2,...) custom-call(s32[896]{0:T(1024)} %fusion.38.target_ref, ...), custom_call_target="tpu_custom_call" | custom-call | flops 10000000000 | bytes 40000000 | tf_op jit(solution)/shard_map/first_half/pallas_call | solution.py:221
  68.3 1.5 collective-permute-start.4
  69.8 3.5 %collective-permute-start.6 = (bf16[2,128,16,128]{3,2,1,0:T(8,128)(2,1)}, bf16[2,128,16,128]{3,2,1,0:T(8,128)(2,1)S(1)}, u32[]{:S(2)}, u32[]{:S(2)}) collective-permute-start(bf16[2,128,16,128]{3,2,1,0:T(8,128)(2,1)} %get-tuple-element.30), channel_id=1, source_target_pairs={{0,3},{1,0},{2,1},{3,2},{4,7},{5,4},{6,5},{7,6},{8,11},{9,8},{10,9... | collective-permute-start | bytes 3145736 | tf_op jit(solution)/shard_map/ppermute | solution.py:315
  73.3 1.6 collective-permute-start.12
  74.9 1.7 collective-permute-start.14
  76.6 17.9 %second_half.1 = (bf16[2,128,16,128]{3,2,1,0:T(8,128)(2,1)}, bf16[2,128,16,128]{3,2,1,0:T(8,128)(2,1)}, bf16[1,128,16,128]{3,2,1,0:T(8,128)(2,1)}, bf16[1,128,16...) custom-call(s32[896]{0:T(1024)} %fusion.38.target_ref, ...), custom_call_target="tpu_custom_call" | custom-call | flops 10000000000 | bytes 40000000 | tf_op jit(solution)/shard_map/second_half/pallas_call | solution.py:251
  94.6 2.8 %collective-permute-done.4 = bf16[2,128,16,128]{3,2,1,0:T(8,128)(2,1)S(1)} collective-permute-done((bf16[2,128,16,128]{3,2,1,0:T(8,128)(2,1)}, bf16[2,128,16,128]{3,2,1,0:T(8,128)(2,1)S(1)}, u32[]{:S(2)}, u32[]{:S(2)}) %collective-permute-start.4) | collective-permute-done | bytes 1048608 | tf_op jit(solution)/shard_map/ppermute | solution.py:314
  97.4 2.1 %collective-permute-start.22 = (bf16[2,128,16,128]{3,2,1,0:T(8,128)(2,1)}, bf16[2,128,16,128]{3,2,1,0:T(8,128)(2,1)S(1)}, u32[]{:S(2)}, u32[]{:S(2)}) collective-permute-start(bf16[2,128,16,128]{3,2,1,0:T(8,128)(2,1)} %get-tuple-element.42), channel_id=1, source_target_pairs={{0,3},{1,0},{2,1},{3,2},{4,7},{5,4},{6,5},{7,6},{8,11},{9,8},{10,9... | collective-permute-start | bytes 3145736 | tf_op jit(solution)/shard_map/ppermute | solution.py:315
  99.6 1.6 collective-permute-start.28
  101.4 1.8 collective-permute-start.30
  103.8 18.3 %collective-permute-done.20 = bf16[2,128,16,128]{3,2,1,0:T(8,128)(2,1)S(1)} collective-permute-done((bf16[2,128,16,128]{3,2,1,0:T(8,128)(2,1)}, bf16[2,128,16,128]{3,2,1,0:T(8,128)(2,1)S(1)}, u32[]{:S(2)}, u32[]{:S(2)}) %collective-permute-start.20) | collective-permute-done | bytes 1048608 | tf_op jit(solution)/shard_map/ppermute | solution.py:314
  122.1 0.8 collective-permute-start.7
  122.9 1.3 fusion.4
  124.1 1.0 collective-permute-start.13
  125.6 2.1 %collective-permute-start.15 = (bf16[128,16,128]{2,1,0:T(8,128)(2,1)S(1)}, bf16[128,16,128]{2,1,0:T(8,128)(2,1)S(1)}, u32[]{:S(2)}, u32[]{:S(2)}) collective-permute-start(bf16[128,16,128]{2,1,0:T(8,128)(2,1)S(1)} %fusion.3), channel_id=1, source_target_pairs={{0,12},{1,13},{2,14},{3,15},{4,0},{5,1},{6,2},{7,3},{8,4},{9,5},{1... | collective-permute-start | bytes 1572872 | tf_op jit(solution)/shard_map/ppermute | solution.py:317
  127.8 1.3 collective-permute-start.21
  129.3 4.0 %collective-permute-done.5 = bf16[128,16,128]{2,1,0:T(8,128)(2,1)S(1)} collective-permute-done((bf16[128,16,128]{2,1,0:T(8,128)(2,1)S(1)}, bf16[128,16,128]{2,1,0:T(8,128)(2,1)S(1)}, u32[]{:S(2)}, u32[]{:S(2)}) %collective-permute-start.5) | collective-permute-done | bytes 524320 | tf_op jit(solution)/shard_map/ppermute | solution.py:316
  133.3 0.8 collective-permute-start.23
  134.2 2.3 %collective-permute-start.29 = (bf16[128,16,128]{2,1,0:T(8,128)(2,1)S(1)}, bf16[128,16,128]{2,1,0:T(8,128)(2,1)S(1)}, u32[]{:S(2)}, u32[]{:S(2)}) collective-permute-start(bf16[128,16,128]{2,1,0:T(8,128)(2,1)S(1)} %fusion.6), channel_id=1, source_target_pairs={{0,4},{1,5},{2,6},{3,7},{4,8},{5,9},{6,10},{7,11},{8,12},{9,13},{1... | collective-permute-start | bytes 1572872 | tf_op jit(solution)/shard_map/ppermute | solution.py:316
  138.9 0.9 collective-permute-start.31
  139.9 1.1 collective-permute-start.8
  141.5 2.0 %collective-permute-done.21 = bf16[128,16,128]{2,1,0:T(8,128)(2,1)S(1)} collective-permute-done((bf16[128,16,128]{2,1,0:T(8,128)(2,1)S(1)}, bf16[128,16,128]{2,1,0:T(8,128)(2,1)S(1)}, u32[]{:S(2)}, u32[]{:S(2)}) %collective-permute-start.21) | collective-permute-done | bytes 524320 | tf_op jit(solution)/shard_map/ppermute | solution.py:316
  143.5 1.0 collective-permute-start.10
  144.5 0.8 collective-permute-done.23
  145.9 4.4 %collective-permute-done.29 = bf16[128,16,128]{2,1,0:T(8,128)(2,1)S(1)} collective-permute-done((bf16[128,16,128]{2,1,0:T(8,128)(2,1)S(1)}, bf16[128,16,128]{2,1,0:T(8,128)(2,1)S(1)}, u32[]{:S(2)}, u32[]{:S(2)}) %collective-permute-start.29) | collective-permute-done | bytes 524320 | tf_op jit(solution)/shard_map/ppermute | solution.py:316
  150.3 1.1 collective-permute-start.24
  151.4 1.1 collective-permute-done.31
  153.1 0.7 slice.416.refs_9_
  154.5 2.9 %collective-permute-start.18 = (bf16[2,32,16,128]{3,2,1,0:T(8,128)(2,1)S(1)}, bf16[2,32,16,128]{3,2,1,0:T(8,128)(2,1)S(1)}, u32[]{:S(2)}, u32[]{:S(2)}) collective-permute-start(bf16[2,32,16,128]{3,2,1,0:T(8,128)(2,1)S(1)} %pad_maximum_fusion.3), channel_id=1, source_target_pairs={{0,3},{1,0},{2,1},{3,2},{4,7},{5,4},{6,5},{7,6},{8,11},{9,8},{10,9... | collective-permute-start | bytes 786440 | tf_op jit(solution)/shard_map/ppermute | solution.py:315
  157.5 0.7 slice.432.refs_15_
  158.2 0.7 slice.422.refs_12_
  159.7 0.7 slice.438.refs_18_
  160.4 2.3 %collective-permute-start.26 = (bf16[2,32,16,128]{3,2,1,0:T(8,128)(2,1)S(1)}, bf16[2,32,16,128]{3,2,1,0:T(8,128)(2,1)S(1)}, u32[]{:S(2)}, u32[]{:S(2)}) collective-permute-start(bf16[2,32,16,128]{3,2,1,0:T(8,128)(2,1)S(1)} %pad_maximum_fusion.5), channel_id=1, source_target_pairs={{0,12},{1,13},{2,14},{3,15},{4,0},{5,1},{6,2},{7,3},{8,4},{9,5},{1... | collective-permute-start | bytes 786440 | tf_op jit(solution)/shard_map/ppermute | solution.py:315
  164.2 3.2 %collective-permute-start.34 = (bf16[2,32,16,128]{3,2,1,0:T(8,128)(2,1)S(1)}, bf16[2,32,16,128]{3,2,1,0:T(8,128)(2,1)S(1)}, u32[]{:S(2)}, u32[]{:S(2)}) collective-permute-start(bf16[2,32,16,128]{3,2,1,0:T(8,128)(2,1)S(1)} %pad_maximum_fusion.7), channel_id=1, source_target_pairs={{0,3},{1,0},{2,1},{3,2},{4,7},{5,4},{6,5},{7,6},{8,11},{9,8},{10,9... | collective-permute-start | bytes 786440 | tf_op jit(solution)/shard_map/ppermute | solution.py:315
  168.9 3.2 %collective-permute-start.11 = (bf16[32,16,128]{2,1,0:T(8,128)(2,1)S(1)}, bf16[32,16,128]{2,1,0:T(8,128)(2,1)S(1)}, u32[]{:S(2)}, u32[]{:S(2)}) collective-permute-start(bf16[32,16,128]{2,1,0:T(8,128)(2,1)S(1)} %fusion.17), channel_id=1, source_target_pairs={{0,12},{1,13},{2,14},{3,15},{4,0},{5,1},{6,2},{7,3},{8,4},{9,5},{1... | collective-permute-start | bytes 393224 | tf_op jit(solution)/shard_map/ppermute | solution.py:317
  173.7 3.2 %collective-permute-start.19 = (bf16[32,16,128]{2,1,0:T(8,128)(2,1)S(1)}, bf16[32,16,128]{2,1,0:T(8,128)(2,1)S(1)}, u32[]{:S(2)}, u32[]{:S(2)}) collective-permute-start(bf16[32,16,128]{2,1,0:T(8,128)(2,1)S(1)} %fusion.19), channel_id=1, source_target_pairs={{0,3},{1,0},{2,1},{3,2},{4,7},{5,4},{6,5},{7,6},{8,11},{9,8},{10,9... | collective-permute-start | bytes 393224 | tf_op jit(solution)/shard_map/ppermute | solution.py:317
  177.7 3.2 %collective-permute-start.27 = (bf16[32,16,128]{2,1,0:T(8,128)(2,1)S(1)}, bf16[32,16,128]{2,1,0:T(8,128)(2,1)S(1)}, u32[]{:S(2)}, u32[]{:S(2)}) collective-permute-start(bf16[32,16,128]{2,1,0:T(8,128)(2,1)S(1)} %fusion.21), channel_id=1, source_target_pairs={{0,12},{1,13},{2,14},{3,15},{4,0},{5,1},{6,2},{7,3},{8,4},{9,5},{1... | collective-permute-start | bytes 393224 | tf_op jit(solution)/shard_map/ppermute | solution.py:317
  181.0 3.2 %collective-permute-start.35 = (bf16[32,16,128]{2,1,0:T(8,128)(2,1)S(1)}, bf16[32,16,128]{2,1,0:T(8,128)(2,1)S(1)}, u32[]{:S(2)}, u32[]{:S(2)}) collective-permute-start(bf16[32,16,128]{2,1,0:T(8,128)(2,1)S(1)} %fusion.23), channel_id=1, source_target_pairs={{0,3},{1,0},{2,1},{3,2},{4,7},{5,4},{6,5},{7,6},{8,11},{9,8},{10,9... | collective-permute-start | bytes 393224 | tf_op jit(solution)/shard_map/ppermute | solution.py:317
  184.9 2.2 %collective-permute-done.33.refs_19_ = bf16[32,16,128]{2,1,0:T(8,128)(2,1)S(1)} collective-permute-done((bf16[32,16,128]{2,1,0:T(8,128)(2,1)S(1)}, bf16[32,16,128]{2,1,0:T(8,128)(2,1)S(1)}, u32[]{:S(2)}, u32[]{:S(2)}) %collective-permute-start.33) | collective-permute-done | bytes 131104 | tf_op jit(solution)/shard_map/ppermute | solution.py:316
  188.4 4.5 %finish.1 = f32[128,4096]{1,0:T(8,128)} custom-call(f32[32,16,128]{2,1,0:T(8,128)} %slice.390.refs_0_, bf16[32,16,128]{2,1,0:T(8,128)(2,1)} %copy-done.11, bf16[32,16,128]{2,1,0:T(8,128)(2,1)} %slice_bitcast_fusion.32.refs_2_, f32[32,16,128]{2,1,0:T(8,128)} %slice.400.refs_3_, bf16[32,16,128]{2,1,0:T(8,128)(2,1)} %slice_bitcast_fusion.31.refs_4_, ...), custom_call_target="tpu_custom_call" | custom-call | tf_op jit(solution)/shard_map/finish/pallas_call | solution.py:351
  (127 shorter events, 16.6 us)
Async XLA Ops:
  1.1 13.6 %collective-permute-start.1 = (bf16[32,4096]{1,0:T(8,128)(2,1)S(1)}, bf16[32,4096]{1,0:T(8,128)(2,1)S(1)}, u32[]{:S(2)}, u32[]{:S(2)}) collective-permute-start(bf16[32,4096]{1,0:T(8,128)(2,1)S(1)} %get-tuple-element.75), channel_id=1, source_target_pairs={{1,0},{2,1},{3,2},{4,3},{5,4},{6,5},{7,6},{8,7},{9,8},{10,9},{11,1... | collective-permute-start | bytes 786440 | tf_op jit(solution)/shard_map/ppermute | solution.py:276
  2.4 12.3 %collective-permute-start = (bf16[32,4096]{1,0:T(8,128)(2,1)S(1)}, bf16[32,4096]{1,0:T(8,128)(2,1)S(1)}, u32[]{:S(2)}, u32[]{:S(2)}) collective-permute-start(bf16[32,4096]{1,0:T(8,128)(2,1)S(1)} %get-tuple-element.76), channel_id=1, source_target_pairs={{0,1},{1,2},{2,3},{3,4},{4,5},{5,6},{6,7},{7,8},{8,9},{9,10},{10,1... | collective-permute-start | bytes 786440 | tf_op jit(solution)/shard_map/ppermute | solution.py:276
  8.0 6.7 %collective-permute-start.3 = (bf16[32,4096]{1,0:T(8,128)(2,1)S(1)}, bf16[32,4096]{1,0:T(8,128)(2,1)S(1)}, u32[]{:S(2)}, u32[]{:S(2)}) collective-permute-start(bf16[32,4096]{1,0:T(8,128)(2,1)S(1)} %get-tuple-element.73), channel_id=1, source_target_pairs={{16,0},{32,16},{48,32},{64,48},{80,64},{96,80},{112,96},{128,112},... | collective-permute-start | bytes 786440 | tf_op jit(solution)/shard_map/ppermute | solution.py:276
  9.9 7.7 %collective-permute-start.2 = (bf16[32,4096]{1,0:T(8,128)(2,1)S(1)}, bf16[32,4096]{1,0:T(8,128)(2,1)S(1)}, u32[]{:S(2)}, u32[]{:S(2)}) collective-permute-start(bf16[32,4096]{1,0:T(8,128)(2,1)S(1)} %get-tuple-element.74), channel_id=1, source_target_pairs={{0,16},{16,32},{32,48},{48,64},{64,80},{80,96},{96,112},{112,128},... | collective-permute-start | bytes 786440 | tf_op jit(solution)/shard_map/ppermute | solution.py:276
  68.3 29.1 %collective-permute-start.4 = (bf16[2,128,16,128]{3,2,1,0:T(8,128)(2,1)}, bf16[2,128,16,128]{3,2,1,0:T(8,128)(2,1)S(1)}, u32[]{:S(2)}, u32[]{:S(2)}) collective-permute-start(bf16[2,128,16,128]{3,2,1,0:T(8,128)(2,1)} %get-tuple-element.29), channel_id=1, source_target_pairs={{0,1},{1,2},{2,3},{3,0},{4,5},{5,6},{6,7},{7,4},{8,9},{9,10},{10,1... | collective-permute-start | bytes 3145736 | tf_op jit(solution)/shard_map/ppermute | solution.py:314
  69.8 29.8 %collective-permute-start.6 = (bf16[2,128,16,128]{3,2,1,0:T(8,128)(2,1)}, bf16[2,128,16,128]{3,2,1,0:T(8,128)(2,1)S(1)}, u32[]{:S(2)}, u32[]{:S(2)}) collective-permute-start(bf16[2,128,16,128]{3,2,1,0:T(8,128)(2,1)} %get-tuple-element.30), channel_id=1, source_target_pairs={{0,3},{1,0},{2,1},{3,2},{4,7},{5,4},{6,5},{7,6},{8,11},{9,8},{10,9... | collective-permute-start | bytes 3145736 | tf_op jit(solution)/shard_map/ppermute | solution.py:315
  73.3 28.1 %collective-permute-start.12 = (bf16[2,128,16,128]{3,2,1,0:T(8,128)(2,1)}, bf16[2,128,16,128]{3,2,1,0:T(8,128)(2,1)S(1)}, u32[]{:S(2)}, u32[]{:S(2)}) collective-permute-start(bf16[2,128,16,128]{3,2,1,0:T(8,128)(2,1)} %get-tuple-element.34), channel_id=1, source_target_pairs={{0,4},{1,5},{2,6},{3,7},{4,8},{5,9},{6,10},{7,11},{8,12},{9,13},{1... | collective-permute-start | bytes 3145736 | tf_op jit(solution)/shard_map/ppermute | solution.py:314
  74.9 28.5 %collective-permute-start.14 = (bf16[2,128,16,128]{3,2,1,0:T(8,128)(2,1)}, bf16[2,128,16,128]{3,2,1,0:T(8,128)(2,1)S(1)}, u32[]{:S(2)}, u32[]{:S(2)}) collective-permute-start(bf16[2,128,16,128]{3,2,1,0:T(8,128)(2,1)} %get-tuple-element.35), channel_id=1, source_target_pairs={{0,12},{1,13},{2,14},{3,15},{4,0},{5,1},{6,2},{7,3},{8,4},{9,5},{1... | collective-permute-start | bytes 3145736 | tf_op jit(solution)/shard_map/ppermute | solution.py:315
  76.6 22.9 %copy-start.10 = (bf16[1,128,16,128]{3,2,1,0:T(8,128)(2,1)S(1)}, bf16[1,128,16,128]{3,2,1,0:T(8,128)(2,1)}, u32[]{:S(2)}) copy-start(bf16[1,128,16,128]{3,2,1,0:T(8,128)(2,1)} %get-tuple-element.28) | copy-start | bytes 1572868
  76.6 24.7 %copy-start.9 = (bf16[1,128,16,128]{3,2,1,0:T(8,128)(2,1)S(1)}, bf16[1,128,16,128]{3,2,1,0:T(8,128)(2,1)}, u32[]{:S(2)}) copy-start(bf16[1,128,16,128]{3,2,1,0:T(8,128)(2,1)} %get-tuple-element.31) | copy-start | bytes 1572868
  76.6 26.6 %copy-start.8 = (bf16[1,128,16,128]{3,2,1,0:T(8,128)(2,1)S(1)}, bf16[1,128,16,128]{3,2,1,0:T(8,128)(2,1)}, u32[]{:S(2)}) copy-start(bf16[1,128,16,128]{3,2,1,0:T(8,128)(2,1)} %get-tuple-element.33) | copy-start | bytes 1572868
  76.6 27.0 %copy-start.6 = (bf16[1,128,16,128]{3,2,1,0:T(8,128)(2,1)S(1)}, bf16[1,128,16,128]{3,2,1,0:T(8,128)(2,1)}, u32[]{:S(2)}) copy-start(bf16[1,128,16,128]{3,2,1,0:T(8,128)(2,1)} %get-tuple-element.36) | copy-start | bytes 1572868
  94.5 30.7 %copy-start.7 = (bf16[1,128,16,128]{3,2,1,0:T(8,128)(2,1)S(1)}, bf16[1,128,16,128]{3,2,1,0:T(8,128)(2,1)}, u32[]{:S(2)}) copy-start(bf16[1,128,16,128]{3,2,1,0:T(8,128)(2,1)} %get-tuple-element.43) | copy-start | bytes 1572868
  94.5 33.2 %copy-start.5 = (bf16[1,128,16,128]{3,2,1,0:T(8,128)(2,1)S(1)}, bf16[1,128,16,128]{3,2,1,0:T(8,128)(2,1)}, u32[]{:S(2)}) copy-start(bf16[1,128,16,128]{3,2,1,0:T(8,128)(2,1)} %get-tuple-element.45) | copy-start | bytes 1572868
  94.5 34.6 %copy-start.4 = (bf16[1,128,16,128]{3,2,1,0:T(8,128)(2,1)S(1)}, bf16[1,128,16,128]{3,2,1,0:T(8,128)(2,1)}, u32[]{:S(2)}) copy-start(bf16[1,128,16,128]{3,2,1,0:T(8,128)(2,1)} %get-tuple-element.48) | copy-start | bytes 1572868
  94.5 42.1 %copy-start.3 = (bf16[2,128,16,128]{3,2,1,0:T(8,128)(2,1)S(1)}, bf16[2,128,16,128]{3,2,1,0:T(8,128)(2,1)}, u32[]{:S(2)}) copy-start(bf16[2,128,16,128]{3,2,1,0:T(8,128)(2,1)} %get-tuple-element.27) | copy-start | bytes 3145732
  94.5 27.5 %collective-permute-start.20 = (bf16[2,128,16,128]{3,2,1,0:T(8,128)(2,1)}, bf16[2,128,16,128]{3,2,1,0:T(8,128)(2,1)S(1)}, u32[]{:S(2)}, u32[]{:S(2)}) collective-permute-start(bf16[2,128,16,128]{3,2,1,0:T(8,128)(2,1)} %get-tuple-element.41), channel_id=1, source_target_pairs={{0,1},{1,2},{2,3},{3,0},{4,5},{5,6},{6,7},{7,4},{8,9},{9,10},{10,1... | collective-permute-start | bytes 3145736 | tf_op jit(solution)/shard_map/ppermute | solution.py:314
  97.4 26.7 %collective-permute-start.22 = (bf16[2,128,16,128]{3,2,1,0:T(8,128)(2,1)}, bf16[2,128,16,128]{3,2,1,0:T(8,128)(2,1)S(1)}, u32[]{:S(2)}, u32[]{:S(2)}) collective-permute-start(bf16[2,128,16,128]{3,2,1,0:T(8,128)(2,1)} %get-tuple-element.42), channel_id=1, source_target_pairs={{0,3},{1,0},{2,1},{3,2},{4,7},{5,4},{6,5},{7,6},{8,11},{9,8},{10,9... | collective-permute-start | bytes 3145736 | tf_op jit(solution)/shard_map/ppermute | solution.py:315
  99.6 26.0 %collective-permute-start.28 = (bf16[2,128,16,128]{3,2,1,0:T(8,128)(2,1)}, bf16[2,128,16,128]{3,2,1,0:T(8,128)(2,1)S(1)}, u32[]{:S(2)}, u32[]{:S(2)}) collective-permute-start(bf16[2,128,16,128]{3,2,1,0:T(8,128)(2,1)} %get-tuple-element.46), channel_id=1, source_target_pairs={{0,4},{1,5},{2,6},{3,7},{4,8},{5,9},{6,10},{7,11},{8,12},{9,13},{1... | collective-permute-start | bytes 3145736 | tf_op jit(solution)/shard_map/ppermute | solution.py:314
  101.4 26.4 %collective-permute-start.30 = (bf16[2,128,16,128]{3,2,1,0:T(8,128)(2,1)}, bf16[2,128,16,128]{3,2,1,0:T(8,128)(2,1)S(1)}, u32[]{:S(2)}, u32[]{:S(2)}) collective-permute-start(bf16[2,128,16,128]{3,2,1,0:T(8,128)(2,1)} %get-tuple-element.47), channel_id=1, source_target_pairs={{0,12},{1,13},{2,14},{3,15},{4,0},{5,1},{6,2},{7,3},{8,4},{9,5},{1... | collective-permute-start | bytes 3145736 | tf_op jit(solution)/shard_map/ppermute | solution.py:315
  103.3 30.0 %collective-permute-start.5 = (bf16[128,16,128]{2,1,0:T(8,128)(2,1)S(1)}, bf16[128,16,128]{2,1,0:T(8,128)(2,1)S(1)}, u32[]{:S(2)}, u32[]{:S(2)}) collective-permute-start(bf16[128,16,128]{2,1,0:T(8,128)(2,1)S(1)} %fusion), channel_id=1, source_target_pairs={{0,1},{1,2},{2,3},{3,0},{4,5},{5,6},{6,7},{7,4},{8,9},{9,10},{10,1... | collective-permute-start | bytes 1572872 | tf_op jit(solution)/shard_map/ppermute | solution.py:316
  122.1 12.2 %collective-permute-start.7 = (bf16[128,16,128]{2,1,0:T(8,128)(2,1)S(1)}, bf16[128,16,128]{2,1,0:T(8,128)(2,1)S(1)}, u32[]{:S(2)}, u32[]{:S(2)}) collective-permute-start(bf16[128,16,128]{2,1,0:T(8,128)(2,1)S(1)} %fusion.1), channel_id=1, source_target_pairs={{0,3},{1,0},{2,1},{3,2},{4,7},{5,4},{6,5},{7,6},{8,11},{9,8},{10,9... | collective-permute-start | bytes 1572872 | tf_op jit(solution)/shard_map/ppermute | solution.py:317
  122.9 18.1 %copy-start.2 = (bf16[2,128,16,128]{3,2,1,0:T(8,128)(2,1)S(1)}, bf16[2,128,16,128]{3,2,1,0:T(8,128)(2,1)}, u32[]{:S(2)}) copy-start(bf16[2,128,16,128]{3,2,1,0:T(8,128)(2,1)} %get-tuple-element.32) | copy-start | bytes 3145732
  124.1 14.8 %collective-permute-start.13 = (bf16[128,16,128]{2,1,0:T(8,128)(2,1)S(1)}, bf16[128,16,128]{2,1,0:T(8,128)(2,1)S(1)}, u32[]{:S(2)}, u32[]{:S(2)}) collective-permute-start(bf16[128,16,128]{2,1,0:T(8,128)(2,1)S(1)} %fusion.2), channel_id=1, source_target_pairs={{0,4},{1,5},{2,6},{3,7},{4,8},{5,9},{6,10},{7,11},{8,12},{9,13},{1... | collective-permute-start | bytes 1572872 | tf_op jit(solution)/shard_map/ppermute | solution.py:316
  125.6 14.3 %collective-permute-start.15 = (bf16[128,16,128]{2,1,0:T(8,128)(2,1)S(1)}, bf16[128,16,128]{2,1,0:T(8,128)(2,1)S(1)}, u32[]{:S(2)}, u32[]{:S(2)}) collective-permute-start(bf16[128,16,128]{2,1,0:T(8,128)(2,1)S(1)} %fusion.3), channel_id=1, source_target_pairs={{0,12},{1,13},{2,14},{3,15},{4,0},{5,1},{6,2},{7,3},{8,4},{9,5},{1... | collective-permute-start | bytes 1572872 | tf_op jit(solution)/shard_map/ppermute | solution.py:317
  127.8 15.6 %collective-permute-start.21 = (bf16[128,16,128]{2,1,0:T(8,128)(2,1)S(1)}, bf16[128,16,128]{2,1,0:T(8,128)(2,1)S(1)}, u32[]{:S(2)}, u32[]{:S(2)}) collective-permute-start(bf16[128,16,128]{2,1,0:T(8,128)(2,1)S(1)} %fusion.4), channel_id=1, source_target_pairs={{0,1},{1,2},{2,3},{3,0},{4,5},{5,6},{6,7},{7,4},{8,9},{9,10},{10,1... | collective-permute-start | bytes 1572872 | tf_op jit(solution)/shard_map/ppermute | solution.py:316
  133.3 12.0 %collective-permute-start.23 = (bf16[128,16,128]{2,1,0:T(8,128)(2,1)S(1)}, bf16[128,16,128]{2,1,0:T(8,128)(2,1)S(1)}, u32[]{:S(2)}, u32[]{:S(2)}) collective-permute-start(bf16[128,16,128]{2,1,0:T(8,128)(2,1)S(1)} %fusion.5), channel_id=1, source_target_pairs={{0,3},{1,0},{2,1},{3,2},{4,7},{5,4},{6,5},{7,6},{8,11},{9,8},{10,9... | collective-permute-start | bytes 1572872 | tf_op jit(solution)/shard_map/ppermute | solution.py:317
  134.2 16.1 %collective-permute-start.29 = (bf16[128,16,128]{2,1,0:T(8,128)(2,1)S(1)}, bf16[128,16,128]{2,1,0:T(8,128)(2,1)S(1)}, u32[]{:S(2)}, u32[]{:S(2)}) collective-permute-start(bf16[128,16,128]{2,1,0:T(8,128)(2,1)S(1)} %fusion.6), channel_id=1, source_target_pairs={{0,4},{1,5},{2,6},{3,7},{4,8},{5,9},{6,10},{7,11},{8,12},{9,13},{1... | collective-permute-start | bytes 1572872 | tf_op jit(solution)/shard_map/ppermute | solution.py:316
  136.6 8.7 %copy-start.1 = (bf16[2,128,16,128]{3,2,1,0:T(8,128)(2,1)S(1)}, bf16[2,128,16,128]{3,2,1,0:T(8,128)(2,1)}, u32[]{:S(2)}) copy-start(bf16[2,128,16,128]{3,2,1,0:T(8,128)(2,1)} %get-tuple-element.39) | copy-start | bytes 3145732
  138.9 13.6 %collective-permute-start.31 = (bf16[128,16,128]{2,1,0:T(8,128)(2,1)S(1)}, bf16[128,16,128]{2,1,0:T(8,128)(2,1)S(1)}, u32[]{:S(2)}, u32[]{:S(2)}) collective-permute-start(bf16[128,16,128]{2,1,0:T(8,128)(2,1)S(1)} %fusion.7), channel_id=1, source_target_pairs={{0,12},{1,13},{2,14},{3,15},{4,0},{5,1},{6,2},{7,3},{8,4},{9,5},{1... | collective-permute-start | bytes 1572872 | tf_op jit(solution)/shard_map/ppermute | solution.py:317
  139.9 20.5 %collective-permute-start.8 = (bf16[2,32,16,128]{3,2,1,0:T(8,128)(2,1)S(1)}, bf16[2,32,16,128]{3,2,1,0:T(8,128)(2,1)S(1)}, u32[]{:S(2)}, u32[]{:S(2)}) collective-permute-start(bf16[2,32,16,128]{3,2,1,0:T(8,128)(2,1)S(1)} %pad_maximum_fusion), channel_id=1, source_target_pairs={{0,4},{1,5},{2,6},{3,7},{4,8},{5,9},{6,10},{7,11},{8,12},{9,13},{1... | collective-permute-start | bytes 786440 | tf_op jit(solution)/shard_map/ppermute | solution.py:314
  141.0 11.6 %copy-start = (bf16[2,128,16,128]{3,2,1,0:T(8,128)(2,1)S(1)}, bf16[2,128,16,128]{3,2,1,0:T(8,128)(2,1)}, u32[]{:S(2)}) copy-start(bf16[2,128,16,128]{3,2,1,0:T(8,128)(2,1)} %get-tuple-element.44) | copy-start | bytes 3145732
  143.5 19.2 %collective-permute-start.10 = (bf16[2,32,16,128]{3,2,1,0:T(8,128)(2,1)S(1)}, bf16[2,32,16,128]{3,2,1,0:T(8,128)(2,1)S(1)}, u32[]{:S(2)}, u32[]{:S(2)}) collective-permute-start(bf16[2,32,16,128]{3,2,1,0:T(8,128)(2,1)S(1)} %pad_maximum_fusion.1), channel_id=1, source_target_pairs={{0,12},{1,13},{2,14},{3,15},{4,0},{5,1},{6,2},{7,3},{8,4},{9,5},{1... | collective-permute-start | bytes 786440 | tf_op jit(solution)/shard_map/ppermute | solution.py:315
  145.3 18.9 %collective-permute-start.16 = (bf16[2,32,16,128]{3,2,1,0:T(8,128)(2,1)S(1)}, bf16[2,32,16,128]{3,2,1,0:T(8,128)(2,1)S(1)}, u32[]{:S(2)}, u32[]{:S(2)}) collective-permute-start(bf16[2,32,16,128]{3,2,1,0:T(8,128)(2,1)S(1)} %pad_maximum_fusion.2), channel_id=1, source_target_pairs={{0,1},{1,2},{2,3},{3,0},{4,5},{5,6},{6,7},{7,4},{8,9},{9,10},{10,1... | collective-permute-start | bytes 786440 | tf_op jit(solution)/shard_map/ppermute | solution.py:314
  150.3 18.6 %collective-permute-start.24 = (bf16[2,32,16,128]{3,2,1,0:T(8,128)(2,1)S(1)}, bf16[2,32,16,128]{3,2,1,0:T(8,128)(2,1)S(1)}, u32[]{:S(2)}, u32[]{:S(2)}) collective-permute-start(bf16[2,32,16,128]{3,2,1,0:T(8,128)(2,1)S(1)} %pad_maximum_fusion.4), channel_id=1, source_target_pairs={{0,4},{1,5},{2,6},{3,7},{4,8},{5,9},{6,10},{7,11},{8,12},{9,13},{1... | collective-permute-start | bytes 786440 | tf_op jit(solution)/shard_map/ppermute | solution.py:314
  154.5 12.9 %collective-permute-start.18 = (bf16[2,32,16,128]{3,2,1,0:T(8,128)(2,1)S(1)}, bf16[2,32,16,128]{3,2,1,0:T(8,128)(2,1)S(1)}, u32[]{:S(2)}, u32[]{:S(2)}) collective-permute-start(bf16[2,32,16,128]{3,2,1,0:T(8,128)(2,1)S(1)} %pad_maximum_fusion.3), channel_id=1, source_target_pairs={{0,3},{1,0},{2,1},{3,2},{4,7},{5,4},{6,5},{7,6},{8,11},{9,8},{10,9... | collective-permute-start | bytes 786440 | tf_op jit(solution)/shard_map/ppermute | solution.py:315
  160.4 11.8 %collective-permute-start.26 = (bf16[2,32,16,128]{3,2,1,0:T(8,128)(2,1)S(1)}, bf16[2,32,16,128]{3,2,1,0:T(8,128)(2,1)S(1)}, u32[]{:S(2)}, u32[]{:S(2)}) collective-permute-start(bf16[2,32,16,128]{3,2,1,0:T(8,128)(2,1)S(1)} %pad_maximum_fusion.5), channel_id=1, source_target_pairs={{0,12},{1,13},{2,14},{3,15},{4,0},{5,1},{6,2},{7,3},{8,4},{9,5},{1... | collective-permute-start | bytes 786440 | tf_op jit(solution)/shard_map/ppermute | solution.py:315
  162.7 10.9 %collective-permute-start.32 = (bf16[2,32,16,128]{3,2,1,0:T(8,128)(2,1)S(1)}, bf16[2,32,16,128]{3,2,1,0:T(8,128)(2,1)S(1)}, u32[]{:S(2)}, u32[]{:S(2)}) collective-permute-start(bf16[2,32,16,128]{3,2,1,0:T(8,128)(2,1)S(1)} %pad_maximum_fusion.6), channel_id=1, source_target_pairs={{0,1},{1,2},{2,3},{3,0},{4,5},{5,6},{6,7},{7,4},{8,9},{9,10},{10,1... | collective-permute-start | bytes 786440 | tf_op jit(solution)/shard_map/ppermute | solution.py:314
  164.2 12.7 %collective-permute-start.34 = (bf16[2,32,16,128]{3,2,1,0:T(8,128)(2,1)S(1)}, bf16[2,32,16,128]{3,2,1,0:T(8,128)(2,1)S(1)}, u32[]{:S(2)}, u32[]{:S(2)}) collective-permute-start(bf16[2,32,16,128]{3,2,1,0:T(8,128)(2,1)S(1)} %pad_maximum_fusion.7), channel_id=1, source_target_pairs={{0,3},{1,0},{2,1},{3,2},{4,7},{5,4},{6,5},{7,6},{8,11},{9,8},{10,9... | collective-permute-start | bytes 786440 | tf_op jit(solution)/shard_map/ppermute | solution.py:315
  167.5 10.3 %collective-permute-start.9 = (bf16[32,16,128]{2,1,0:T(8,128)(2,1)S(1)}, bf16[32,16,128]{2,1,0:T(8,128)(2,1)S(1)}, u32[]{:S(2)}, u32[]{:S(2)}) collective-permute-start(bf16[32,16,128]{2,1,0:T(8,128)(2,1)S(1)} %fusion.16), channel_id=1, source_target_pairs={{0,4},{1,5},{2,6},{3,7},{4,8},{5,9},{6,10},{7,11},{8,12},{9,13},{1... | collective-permute-start | bytes 393224 | tf_op jit(solution)/shard_map/ppermute | solution.py:316
  168.9 12.0 %collective-permute-start.11 = (bf16[32,16,128]{2,1,0:T(8,128)(2,1)S(1)}, bf16[32,16,128]{2,1,0:T(8,128)(2,1)S(1)}, u32[]{:S(2)}, u32[]{:S(2)}) collective-permute-start(bf16[32,16,128]{2,1,0:T(8,128)(2,1)S(1)} %fusion.17), channel_id=1, source_target_pairs={{0,12},{1,13},{2,14},{3,15},{4,0},{5,1},{6,2},{7,3},{8,4},{9,5},{1... | collective-permute-start | bytes 393224 | tf_op jit(solution)/shard_map/ppermute | solution.py:317
  172.2 8.8 %collective-permute-start.17 = (bf16[32,16,128]{2,1,0:T(8,128)(2,1)S(1)}, bf16[32,16,128]{2,1,0:T(8,128)(2,1)S(1)}, u32[]{:S(2)}, u32[]{:S(2)}) collective-permute-start(bf16[32,16,128]{2,1,0:T(8,128)(2,1)S(1)} %fusion.18), channel_id=1, source_target_pairs={{0,1},{1,2},{2,3},{3,0},{4,5},{5,6},{6,7},{7,4},{8,9},{9,10},{10,1... | collective-permute-start | bytes 393224 | tf_op jit(solution)/shard_map/ppermute | solution.py:316
  173.7 11.2 %collective-permute-start.19 = (bf16[32,16,128]{2,1,0:T(8,128)(2,1)S(1)}, bf16[32,16,128]{2,1,0:T(8,128)(2,1)S(1)}, u32[]{:S(2)}, u32[]{:S(2)}) collective-permute-start(bf16[32,16,128]{2,1,0:T(8,128)(2,1)S(1)} %fusion.19), channel_id=1, source_target_pairs={{0,3},{1,0},{2,1},{3,2},{4,7},{5,4},{6,5},{7,6},{8,11},{9,8},{10,9... | collective-permute-start | bytes 393224 | tf_op jit(solution)/shard_map/ppermute | solution.py:317
  176.9 7.9 %collective-permute-start.25 = (bf16[32,16,128]{2,1,0:T(8,128)(2,1)S(1)}, bf16[32,16,128]{2,1,0:T(8,128)(2,1)S(1)}, u32[]{:S(2)}, u32[]{:S(2)}) collective-permute-start(bf16[32,16,128]{2,1,0:T(8,128)(2,1)S(1)} %fusion.20), channel_id=1, source_target_pairs={{0,4},{1,5},{2,6},{3,7},{4,8},{5,9},{6,10},{7,11},{8,12},{9,13},{1... | collective-permute-start | bytes 393224 | tf_op jit(solution)/shard_map/ppermute | solution.py:316
  177.7 9.4 %copy-start.11 = (bf16[32,16,128]{2,1,0:T(8,128)(2,1)}, bf16[32,16,128]{2,1,0:T(8,128)(2,1)S(1)}, u32[]{:S(2)}) copy-start(bf16[32,16,128]{2,1,0:T(8,128)(2,1)S(1)} %collective-permute-done.9.refs_1_) | copy-start | bytes 393220
  177.7 7.2 %collective-permute-start.27 = (bf16[32,16,128]{2,1,0:T(8,128)(2,1)S(1)}, bf16[32,16,128]{2,1,0:T(8,128)(2,1)S(1)}, u32[]{:S(2)}, u32[]{:S(2)}) collective-permute-start(bf16[32,16,128]{2,1,0:T(8,128)(2,1)S(1)} %fusion.21), channel_id=1, source_target_pairs={{0,12},{1,13},{2,14},{3,15},{4,0},{5,1},{6,2},{7,3},{8,4},{9,5},{1... | collective-permute-start | bytes 393224 | tf_op jit(solution)/shard_map/ppermute | solution.py:317
  181.0 6.2 %collective-permute-start.33 = (bf16[32,16,128]{2,1,0:T(8,128)(2,1)S(1)}, bf16[32,16,128]{2,1,0:T(8,128)(2,1)S(1)}, u32[]{:S(2)}, u32[]{:S(2)}) collective-permute-start(bf16[32,16,128]{2,1,0:T(8,128)(2,1)S(1)} %fusion.22), channel_id=1, source_target_pairs={{0,1},{1,2},{2,3},{3,0},{4,5},{5,6},{6,7},{7,4},{8,9},{9,10},{10,1... | collective-permute-start | bytes 393224 | tf_op jit(solution)/shard_map/ppermute | solution.py:316
  181.0 6.2 %collective-permute-start.35 = (bf16[32,16,128]{2,1,0:T(8,128)(2,1)S(1)}, bf16[32,16,128]{2,1,0:T(8,128)(2,1)S(1)}, u32[]{:S(2)}, u32[]{:S(2)}) collective-permute-start(bf16[32,16,128]{2,1,0:T(8,128)(2,1)S(1)} %fusion.23), channel_id=1, source_target_pairs={{0,3},{1,0},{2,1},{3,2},{4,7},{5,4},{6,5},{7,6},{8,11},{9,8},{10,9... | collective-permute-start | bytes 393224 | tf_op jit(solution)/shard_map/ppermute | solution.py:317
  (11 other events, 30.0 us)

commit v3 on v2

v3 whole, which is shorter than its diff:
```python
import jax
import jax.numpy as jnp
from jax import lax
from jax.experimental import pallas as pl
from jax.experimental.pallas import tpu as pltpu
from jax.sharding import PartitionSpec as P

BLOCK = 64
PAIRS = 7
EX = 8
EY = 4
EZ = 4
E_DEV = EX * EY * EZ
CB_DEV = 128
SQUARE = BLOCK * BLOCK
ROWS = SQUARE // 128
HALF = ROWS // 2
PITCH = 33
FLAT_PITCH = 17
GROUP = 16
FACE = 32
SIDE = 4
OWNERS = SIDE * SIDE
PART = CB_DEV // 4
SLOT = SIDE * PART
SLOTS = OWNERS * CB_DEV // SLOT
BUFFERS = 4
SLOT_OF = 0x53201476


def spread_rows(flat, scratch, base):
    for t in range(ROWS):
        scratch[pl.ds(base + t, GROUP, stride=PITCH), :] = flat(t).astype(jnp.float32)


def piece(scratch, index):
    return scratch[pl.ds(index * PITCH, ROWS), :]


def clear(acc):
    def body(i, _):
        acc[pl.ds(i * 16, 16)] = jnp.zeros((16, HALF, 128), jnp.float32)
        return 0

    lax.fori_loop(0, OWNERS * CB_DEV // 16, body, 0)


def spread_weights(ref, base, rows, weights, slot0, lefts):
    low = lax.broadcasted_iota(jnp.int32, (ROWS, 128), 1) < BLOCK
    low2 = lax.broadcasted_iota(jnp.int32, (BLOCK, 128), 1) < BLOCK
    r = lax.broadcasted_iota(jnp.int32, (BLOCK, BLOCK), 0)
    c = lax.broadcasted_iota(jnp.int32, (BLOCK, BLOCK), 1)
    place = (c == (r % 2) * ROWS + r // 2).astype(jnp.float32).astype(jnp.bfloat16)
    r = lax.broadcasted_iota(jnp.int32, (BLOCK, 128), 0)
    c = lax.broadcasted_iota(jnp.int32, (BLOCK, 128), 1)
    v = (r // HALF) % 2
    lane = v * BLOCK + 2 * ((r // ROWS) * HALF + r % HALF) + v
    pick = (c == lane).astype(jnp.float32).astype(jnp.bfloat16)
    spread_rows(lambda t: ref[pl.ds(base, GROUP), t * 128 : (t + 1) * 128], rows, 0)
    for i in range(0, GROUP, 2):
        ordered = []
        for j in (i, i + 1):
            own = piece(rows, j)
            turned = pltpu.roll(own, BLOCK, 1)
            ordered.append(
                jnp.concatenate(
                    [jnp.where(low, own, turned), jnp.where(low, turned, own)], axis=0
                ).astype(jnp.bfloat16)
            )
            if lefts is not None:
                stacked = jnp.concatenate([own, turned], axis=0)
                left = lax.dot_general(
                    pick, stacked.astype(jnp.bfloat16), (((1,), (1,)), ((), ())),
                    preferred_element_type=jnp.float32,
                )
                lefts[base + j] = left.astype(jnp.bfloat16)
        placed = jnp.dot(
            place, jnp.concatenate(ordered, axis=1), preferred_element_type=jnp.float32
        )
        for j in (0, 1):
            twice = placed[:, j * 128 : (j + 1) * 128]
            at_low = jnp.where(low2, twice, 0.0).astype(jnp.bfloat16)
            at_high = jnp.where(low2, 0.0, twice).astype(jnp.bfloat16)
            weights[slot0 + i + j, :BLOCK, :128] = at_low
            weights[slot0 + i + j, :BLOCK, 128:] = at_high
            weights[slot0 + i + j, BLOCK:, :128] = at_high
            weights[slot0 + i + j, BLOCK:, 128:] = at_low


def product_kernel(a_ref, p_ref, q_out, left_ref, face_ref, couples, q, rows, weights, sems):
    step = pl.program_id(0)
    start = pl.multiple_of(step * GROUP, GROUP)
    spread_weights(p_ref, start, rows, weights, start, left_ref)
    for k in range(PAIRS):
        spread_rows(
            lambda t: a_ref[k, :, t * 128 : (t + 1) * 128], rows, k * (GROUP * PITCH)
        )

    def lay(i, _):
        for k in range(PAIRS):
            couples[k, step * GROUP + i] = piece(rows, k * GROUP + i).astype(jnp.bfloat16)
        return 0

    lax.fori_loop(0, GROUP, lay, 0, unroll=4)

    @pl.when(step == pl.num_programs(0) - 1)
    def _multiply():
        plane = EX * EY

        def copy(n):
            span = pl.ds(n * GROUP, GROUP)
            return pltpu.make_async_copy(q.at[span], q_out.at[span], sems.at[n])

        behind = plane // GROUP

        for z in range(EZ):
            for g in range(plane // GROUP):
                base = z * plane + g * GROUP
                def neighbour(i, _):
                    j = base + i
                    x = j % EX
                    y = (j // EX) % EY
                    inside = (
                        None, x < EX - 1, x > 0, y < EY - 1, y > 0,
                        z < EZ - 1 or None, z > 0 or None,
                    )
                    away = (0, 1, -1, EX, -EX, plane, -plane)
                    here = [k for k in range(PAIRS) if k < 5 or inside[k]]
                    owners = [
                        j + away[k] if inside[k] is None or k >= 5
                        else jnp.where(inside[k], j + away[k], E_DEV)
                        for k in here
                    ]
                    left = jnp.concatenate(
                        [couples[k, e] for k, e in zip(here, owners)], axis=0
                    )
                    found = jnp.dot(left, weights[j], preferred_element_type=jnp.float32)
                    found = found.astype(jnp.bfloat16)
                    for n, (k, e) in enumerate(zip(here, owners)):
                        own = found[n * ROWS : (n + 1) * ROWS]
                        q[e, :ROWS, k * 128 : (k + 1) * 128] = own[:, :128]
                        q[e, ROWS:, k * 128 : (k + 1) * 128] = own[:, 128:]
                    return 0

                lax.fori_loop(0, GROUP, neighbour, 0, unroll=4)
                if base // GROUP >= behind:
                    copy(base // GROUP - behind).start()
        for n in range(E_DEV // GROUP - behind, E_DEV // GROUP):
            copy(n).start()
        for n in range(FACE):
            outer, x = divmod(n, EX)
            face_ref[n] = couples[3, outer * plane + x]
            face_ref[FACE + n] = couples[4, outer * plane + plane - EX + x]
            face_ref[2 * FACE + n] = couples[5, n]
            face_ref[3 * FACE + n] = couples[6, E_DEV - plane + n]
        for n in range(E_DEV // GROUP):
            copy(n).wait()


def add_terms(step, half, target_ref, lefts, q_ref, acc):
    low = lax.broadcasted_iota(jnp.int32, (HALF, PAIRS * 128), 1) % 128 < BLOCK

    def element(i, _):
        e = step * GROUP + i
        x = e % EX
        y = (e // EX) % EY
        z = e // (EX * EY)
        inside = (None, x > 0, x < EX - 1, y > 0, y < EY - 1, z > 0, z < EZ - 1)
        both = jnp.dot(
            lefts[e, half * ROWS : (half + 1) * ROWS, :], q_ref[i],
            preferred_element_type=jnp.float32,
        )
        terms = jnp.where(low, both[:HALF], both[HALF:])
        terms = terms.astype(jnp.bfloat16).astype(jnp.float32)
        for k in range(PAIRS):
            target = target_ref[e * PAIRS + k]
            if inside[k] is not None:
                target = jnp.where(inside[k], target, OWNERS * CB_DEV)
            acc[target] += terms[:, k * 128 : (k + 1) * 128]
        return 0

    lax.fori_loop(0, GROUP, element, 0, unroll=4)


def add_face_terms(step, half, target_ref, lefts, qh_ref, acc):
    low = lax.broadcasted_iota(jnp.int32, (HALF, 128), 1) < BLOCK
    plane = EX * EY
    face = step // (FACE // GROUP)

    def pair(i, _):
        n = step % (FACE // GROUP) * GROUP + i
        column = n // EX * plane + n % EX
        e = jnp.where(
            face < 2, column + face * (plane - EX), n + (face - 2) * (E_DEV - plane)
        )
        both = jnp.dot(
            lefts[e, half * ROWS : (half + 1) * ROWS, :], qh_ref[step * GROUP + i],
            preferred_element_type=jnp.float32,
        )
        term = jnp.where(low, both[:HALF], both[HALF:])
        acc[target_ref[e * PAIRS + 3 + face]] += term.astype(jnp.bfloat16).astype(jnp.float32)
        return 0

    lax.fori_loop(0, GROUP, pair, 0, unroll=8)


def drain(acc, stage, sems, outs):
    places = []
    for out in outs:
        places += [out.at[i] for i in range(out.shape[0])]
    copies = []
    for n in range(SLOTS):
        buffer = n % BUFFERS
        if n >= BUFFERS:
            copies[n - BUFFERS].wait()

        def cast(i, _):
            blocks = acc[pl.ds(n * SLOT + i * 16, 16)]
            stage[buffer, pl.ds(i * 16, 16)] = blocks.astype(jnp.bfloat16)
            return 0

        lax.fori_loop(0, SLOT // 16, cast, 0)
        copy = pltpu.make_async_copy(stage.at[buffer], places[n], sems.at[buffer])
        copy.start()
        copies.append(copy)
    for copy in copies[-BUFFERS:]:
        copy.wait()


def first_kernel(target_ref, left_ref, q_ref, face_ref, ym_ref, yp_ref, zm_ref, zp_ref, *refs):
    qh_ref, *outs = refs[:11]
    acc, stage, sems, weights, rows = refs[11:]
    step = pl.program_id(0)

    @pl.when(step == 0)
    def _clear():
        clear(acc)

    groups = FACE // GROUP
    for f, ref in enumerate((ym_ref, yp_ref, zm_ref, zp_ref)):

        @pl.when(step // groups == f)
        def _weights():
            base = pl.multiple_of(step % groups * GROUP, GROUP)
            spread_weights(ref, base, rows, weights, 0, None)

    def multiply(i, _):
        n = step * GROUP + i
        found = jnp.dot(face_ref[n], weights[i], preferred_element_type=jnp.float32)
        found = found.astype(jnp.bfloat16)
        qh_ref[n, :ROWS, :] = found[:, :128]
        qh_ref[n, ROWS:, :] = found[:, 128:]
        return 0

    lax.fori_loop(0, GROUP, multiply, 0, unroll=8)
    add_face_terms(step, 0, target_ref, left_ref, qh_ref, acc)
    add_terms(step, 0, target_ref, left_ref, q_ref, acc)

    @pl.when(step == pl.num_programs(0) - 1)
    def _drain():
        drain(acc, stage, sems, outs)


def second_kernel(target_ref, left_ref, q_ref, qh_ref, *refs):
    outs = refs[:10]
    acc, stage, sems = refs[10:]
    step = pl.program_id(0)

    @pl.when(step == 0)
    def _clear():
        clear(acc)

    add_face_terms(step, 1, target_ref, left_ref, qh_ref, acc)
    add_terms(step, 1, target_ref, left_ref, q_ref, acc)

    @pl.when(step == pl.num_programs(0) - 1)
    def _drain():
        drain(acc, stage, sems, outs)


VMEM = pl.BlockSpec(memory_space=pltpu.VMEM)
SMEM = pl.BlockSpec(memory_space=pltpu.SMEM)
HBM = pl.BlockSpec(memory_space=pl.ANY)
Q_SPEC = pl.BlockSpec((GROUP, BLOCK, PAIRS * 128), lambda i: (i, 0, 0))
PACKS = [
    jax.ShapeDtypeStruct((n, SLOT, HALF, 128), jnp.bfloat16) for n in (2, 2, 1, 1, 2) * 2
]
SUMS = [
    pltpu.VMEM((OWNERS * CB_DEV + 1, HALF, 128), jnp.float32),
    pltpu.VMEM((BUFFERS, SLOT, HALF, 128), jnp.bfloat16),
    pltpu.SemaphoreType.DMA((BUFFERS,)),
]
WEIGHTS = pltpu.VMEM((GROUP, 128, 256), jnp.bfloat16)


def params():
    return pltpu.CompilerParams(
        dimension_semantics=("arbitrary",), vmem_limit_bytes=48 * 1024 * 1024
    )


def cost(megabytes):
    return pl.CostEstimate(flops=10**10, bytes_accessed=megabytes * 10**6, transcendentals=0)


def local_products(a, p):
    return pl.pallas_call(
        product_kernel,
        grid=(E_DEV // GROUP,),
        in_specs=[pl.BlockSpec((PAIRS, GROUP, SQUARE), lambda i: (0, i, 0)), VMEM],
        out_specs=[HBM, VMEM, VMEM],
        out_shape=[
            jax.ShapeDtypeStruct((E_DEV, BLOCK, PAIRS * 128), jnp.bfloat16),
            jax.ShapeDtypeStruct((E_DEV, BLOCK, BLOCK), jnp.bfloat16),
            jax.ShapeDtypeStruct((4 * FACE, ROWS, 128), jnp.bfloat16),
        ],
        scratch_shapes=[
            pltpu.VMEM((PAIRS, E_DEV + 1, ROWS, 128), jnp.bfloat16),
            pltpu.VMEM((E_DEV + 1, BLOCK, PAIRS * 128), jnp.bfloat16),
            pltpu.VMEM((PAIRS * GROUP * PITCH + 8, 128), jnp.float32),
            pltpu.VMEM((E_DEV, 128, 256), jnp.bfloat16),
            pltpu.SemaphoreType.DMA((E_DEV // GROUP,)),
        ],
        compiler_params=params(),
        cost_estimate=cost(60),
        name="local_products",
    )(a, p)


def first_half(target, lefts, q, face, halos):
    found = pl.pallas_call(
        first_kernel,
        grid=(E_DEV // GROUP,),
        in_specs=[SMEM, VMEM, Q_SPEC, VMEM, VMEM, VMEM, VMEM, VMEM],
        out_specs=[VMEM] + [HBM] * len(PACKS),
        out_shape=[jax.ShapeDtypeStruct((4 * FACE, BLOCK, 128), jnp.bfloat16)] + PACKS,
        scratch_shapes=SUMS + [WEIGHTS, pltpu.VMEM((GROUP * PITCH + 8, 128), jnp.float32)],
        compiler_params=params(),
        cost_estimate=cost(60),
        name="first_half",
    )(target, lefts, q, face, *halos)
    return found[0], found[1:]


def second_half(target, lefts, q, qh):
    return pl.pallas_call(
        second_kernel,
        grid=(E_DEV // GROUP,),
        in_specs=[SMEM, VMEM, Q_SPEC, VMEM],
        out_specs=[HBM] * len(PACKS),
        out_shape=PACKS,
        scratch_shapes=SUMS,
        compiler_params=params(),
        cost_estimate=cost(60),
        name="second_half",
    )(target, lefts, q, qh)


def faces(p):
    brick = p.reshape(EZ, EY, EX, SQUARE)
    found = []
    for axis, dim in (("dom", 1), ("slab", 0)):
        size = lax.axis_size(axis)
        up = [(i, i + 1) for i in range(size - 1)]
        down = [(j, i) for i, j in up]
        length = brick.shape[dim]
        last = lax.slice_in_dim(brick, length - 1, length, axis=dim).reshape(FACE, SQUARE)
        first = lax.slice_in_dim(brick, 0, 1, axis=dim).reshape(FACE, SQUARE)
        found += [lax.ppermute(last, axis, up), lax.ppermute(first, axis, down)]
    return found


def sum_places(dest_rank, dest_block):
    me = lax.axis_index("dom")
    rank = dest_rank.reshape(-1)
    block = dest_block.reshape(-1)
    dx = (rank - me) % SIDE
    dy = (rank // SIDE - me // SIDE) % SIDE
    which = block // (2 * PART)
    part = (block // PART) % 2
    hops = jnp.where(which == 0, dx, dy)
    other = jnp.where(which == 0, dy, dx)
    slot = (SLOT_OF >> (4 * (2 * hops + part))) & 7
    return ((which * (SLOTS // 2) + slot) * SIDE + other) * PART + block % PART


def ring_perms():
    def moved(dx, dy):
        return [
            (y * SIDE + x, (y + dy) % SIDE * SIDE + (x + dx) % SIDE)
            for y in range(SIDE)
            for x in range(SIDE)
        ]

    return (moved(1, 0), moved(-1, 0)), (moved(0, 1), moved(0, -1))


def added(*parts):
    total = parts[0].astype(jnp.float32)
    for part in parts[1:]:
        total = total + part.astype(jnp.float32)
    return total


def join(keep, arrived):
    return added(keep, arrived).astype(jnp.bfloat16)


def sum_of_rows(packs, perms):
    right, left, keep_right, keep_left, own = packs
    forward, backward = perms
    r1 = lax.ppermute(right, "dom", forward)
    l1 = lax.ppermute(left, "dom", backward)
    r2 = lax.ppermute(join(keep_right[0], r1[0]), "dom", forward)
    l2 = lax.ppermute(join(keep_left[0], l1[0]), "dom", backward)
    shape = (SIDE, PART, HALF, 128)
    return added(own[0], r2, l1[1]).reshape(shape), added(own[1], r1[1], l2).reshape(shape)


def exchange(halves):
    along_x, along_y = ring_perms()
    found = []
    for which, (one, two) in enumerate(((along_x, along_y), (along_y, along_x))):
        sums = [sum_of_rows(packs[which * 5 : which * 5 + 5], one) for packs in halves]
        r = [jnp.stack([s[0][n] for s in sums]) for n in range(3)]
        l = [jnp.stack([s[1][n] for s in sums]) for n in (0, 1, 2, 3)]
        r16 = [v.astype(jnp.bfloat16) for v in r]
        l16 = [v.astype(jnp.bfloat16) for v in l]
        r3 = jnp.stack([s[0][3] for s in sums]).astype(jnp.bfloat16)
        forward, backward = two
        r1 = lax.ppermute(jnp.stack([r16[2], l16[1]]), "dom", forward)
        l1 = lax.ppermute(jnp.stack([l16[2], r3]), "dom", backward)
        r2 = lax.ppermute(join(r16[1], r1[0]), "dom", forward)
        l2 = lax.ppermute(join(l16[3], l1[0]), "dom", backward)
        found += [r[0], l[0], r1, l1, r2, l2]
    return found


def finish_kernel(*refs):
    *ins, out_ref, scratch = refs
    for which in range(2):
        own_right, own_left, r1, l1, r2, l2 = ins[6 * which : 6 * which + 6]
        for half in range(2):
            parts = (
                (own_right[half], r2[half], l1[1, half]),
                (own_left[half], r1[1, half], l2[half]),
            )
            for part, pieces in enumerate(parts):
                total = added(*pieces)
                for c in range(PART):
                    scratch[c * FLAT_PITCH : c * FLAT_PITCH + HALF, :] = total[c]
                rows = pl.ds((2 * which + part) * PART, PART)
                for u in range(HALF):
                    t = half * HALF + u
                    out_ref[rows, t * 128 : (t + 1) * 128] = scratch[
                        pl.ds(u, PART, stride=FLAT_PITCH), :
                    ]


def finish(parts):
    return pl.pallas_call(
        finish_kernel,
        in_specs=[VMEM] * len(parts),
        out_specs=VMEM,
        out_shape=jax.ShapeDtypeStruct((CB_DEV, SQUARE), jnp.float32),
        scratch_shapes=[pltpu.VMEM((PART * FLAT_PITCH + 8, 128), jnp.float32)],
        name="finish",
    )(*parts)


def on_device(a_blocks, p_blocks, dest_rank, dest_block):
    halos = faces(p_blocks)
    target = sum_places(dest_rank, dest_block)
    q, lefts, face = local_products(jnp.swapaxes(a_blocks, 0, 1), p_blocks)
    qh, first = first_half(target, lefts, q, face, halos)
    second = second_half(target, lefts, q, qh)
    return finish(exchange((first, second)))


def solution(mesh):
    return jax.shard_map(
        on_device,
        mesh=mesh,
        in_specs=(
            P(("slab", "dom"), None, None),
            P(("slab", "dom"), None),
            P(("slab", "dom"), None),
            P(("slab", "dom"), None),
        ),
        out_specs=P(("slab", "dom"), None),
        check_vma=False,
    )
```

time: 193 us -> 197 us (1.021)
  waiting for transfers between devices: 39.5 us -> 70.7 us
  starting transfers between devices: 58.4 us -> 42.5 us
  local copies, waits for them, and re-layouts: 16.3 us -> 6.28 us
  Pallas kernels: 72.3 us -> 69.8 us
    ppermute x32 -> x24, waiting for transfers between devices: 36.6 us -> 70.6 us  [the longest x4 42 us: sum_of_rows(): r1 = lax.ppermute(right, 'dom', forward)]
    ppermute x32 -> x24, starting transfers between devices: 48.3 us -> 32.3 us  [the longest x4 8.37 us: sum_of_rows(): l2 = lax.ppermute(join(keep_left[0], l1[0]), 'dom', backward)]
    squeeze x8 -> x0, local copies, waits for them, and re-layouts: 5.3 us -> none  [ring_sum(): return ((own[0], r2, l1[1]), (own[1], r1[1], l2))]
    slice x12 -> x8, local copies, waits for them, and re-layouts: 5.9 us -> 0.7 us  [exchange(): l = [jnp.stack([s[1][n] for s in sums]) for n in (0, 1, 2, 3)]]
    another operation x8 -> x12, other arithmetic: 0.22 us -> 5.21 us  [the longest x2 1.69 us: exchange(): l = [jnp.stack([s[1][n] for s in sums]) for n in (0, 1, 2, 3)]]
    pallas_call x2 -> x3, Pallas kernels: 54.4 us -> 50.6 us  [the longest x1 26.9 us: first_half(): pl.pallas_call(first_kernel, grid=(E_DEV // GROUP,), in_specs=[SMEM, VMEM...]
    ppermute x4, waiting for transfers between devices: 2.89 us -> 0.01 us  [faces(): found += [lax.ppermute(last, axis, up), lax.ppermute(first, axis, down)]]
    convert_element_type x20 -> x12, other arithmetic: 4.19 us -> 1.41 us  [join(): return added(keep, arrived).astype(jnp.bfloat16)]
  transfers between devices with their start and end apart: 36 -> 28, of which waited for: 12 -> 10; matrix products, arithmetic and copies ran while one was open for 10% -> 4% of each run, Pallas kernels for 9% -> 20%
where the time goes in v3:
time: 197 us; the launch traced here: 196 us
  waiting for transfers between devices  70.7 us (36%)
  Pallas kernels  69.8 us (35%)
  starting transfers between devices  42.5 us (22%)
  other arithmetic  6.67 us (3%)
  local copies, waits for them, and re-layouts  6.28 us (3%)
    ppermute x4, waiting for transfers between devices, sum_of_rows(): r1 = lax.ppermute(right, 'dom', forward)  42 us
    pallas_call x1, Pallas kernels, first_half(): pl.pallas_call(first_kernel, grid=(E_DEV // GROUP,), in_specs=[SMEM, VMEM...  26.9 us
    pallas_call x1, Pallas kernels, local_products(): pl.pallas_call(product_kernel, grid=(E_DEV // GROUP,), in_specs=[pl.Block...  19.4 us
    pallas_call x1, Pallas kernels, second_half(): pl.pallas_call(second_kernel, grid=(E_DEV // GROUP,), in_specs=[SMEM, VME...  19.2 us
    ppermute x4, waiting for transfers between devices, sum_of_rows(): r2 = lax.ppermute(join(keep_right[0], r1[0]), 'dom', forward)  12.8 us
    ppermute x4, starting transfers between devices, faces(): found += [lax.ppermute(last, axis, up), lax.ppermute(first, axis, down)]  10.3 us
    ppermute x4, starting transfers between devices, sum_of_rows(): l2 = lax.ppermute(join(keep_left[0], l1[0]), 'dom', backward)  8.37 us
    ppermute x4, starting transfers between devices, sum_of_rows(): l1 = lax.ppermute(left, 'dom', backward)  7.62 us
  transfers between devices with their start and end apart: 28, of which 10 were waited for; matrix products, arithmetic and copies ran while one was open for 4% of the time, Pallas kernels for 20%

profile of v3, /device:TPU:96, one launch (start us, length us, event | category | flops | bytes accessed | tf_op | source)
XLA Modules:
  0.0 196.4 jit_solution(619889732968988855)
XLA Ops:
  0.0 1.2 slice_bitcast_fusion.16
  1.2 3.4 %collective-permute-start = (bf16[32,4096]{1,0:T(8,128)(2,1)S(1)}, bf16[32,4096]{1,0:T(8,128)(2,1)S(1)}, u32[]{:S(2)}, u32[]{:S(2)}) collective-permute-start(bf16[32,4096]{1,0:T(8,128)(2,1)S(1)} %get-tuple-element.80), channel_id=1, source_target_pairs={{0,1},{1,2},{2,3},{3,4},{4,5},{5,6},{6,7},{7,8},{8,9},{9,10},{10,1... | collective-permute-start | bytes 786440 | tf_op jit(solution)/shard_map/ppermute | solution.py:369
  4.6 1.3 collective-permute-start.1
  5.9 1.1 fusion.38
  6.9 1.9 collective-permute-start.2
  8.9 3.6 %collective-permute-start.3 = (bf16[32,4096]{1,0:T(8,128)(2,1)S(1)}, bf16[32,4096]{1,0:T(8,128)(2,1)S(1)}, u32[]{:S(2)}, u32[]{:S(2)}) collective-permute-start(bf16[32,4096]{1,0:T(8,128)(2,1)S(1)} %get-tuple-element.77), channel_id=1, source_target_pairs={{16,0},{32,16},{48,32},{64,48},{80,64},{96,80},{112,96},{128,112},... | collective-permute-start | bytes 786440 | tf_op jit(solution)/shard_map/ppermute | solution.py:369
  12.6 19.4 %local_products.1 = (bf16[128,64,896]{2,1,0:T(8,128)(2,1)}, bf16[128,64,64]{2,1,0:T(8,128)(2,1)S(1)}, bf16[128,32,128]{2,1,0:T(8,128)(2,1)S(1)}) custom-call(bf16[7,128,4096]{2,1,0:T(8,128)(2,1)} %bitcast.163, bf16[128,4096]{1,0:T(8,128)(2,1)S(1)} %copy-done), custom_call_target="tpu_custom_call" | custom-call | flops 10000000000 | bytes 60000000 | tf_op jit(solution)/shard_map/local_products/pallas_call | solution.py:307
  32.0 1.3 copy-done.1
  33.3 1.0 copy-done.2
  34.4 0.2 reshape.401
  34.8 26.9 %first_half.1 = (bf16[128,64,128]{2,1,0:T(8,128)(2,1)}, bf16[2,128,16,128]{3,2,1,0:T(8,128)(2,1)S(1)}, bf16[2,128,16,128]{3,2,1,0:T(8,128)(2,1)S(1)}, bf16[1,128...) custom-call(s32[896]{0:T(1024)S(1)} %fusion.26.target_ref, ...), custom_call_target="tpu_custom_call" | custom-call | flops 10000000000 | bytes 60000000 | tf_op jit(solution)/shard_map/first_half/pallas_call | solution.py:331
  61.6 4.9 %collective-permute-start.16 = (bf16[2,128,16,128]{3,2,1,0:T(8,128)(2,1)}, bf16[2,128,16,128]{3,2,1,0:T(8,128)(2,1)S(1)}, u32[]{:S(2)}, u32[]{:S(2)}) collective-permute-start(bf16[2,128,16,128]{3,2,1,0:T(8,128)(2,1)} %get-tuple-element.45), channel_id=1, source_target_pairs={{0,4},{1,5},{2,6},{3,7},{4,8},{5,9},{6,10},{7,11},{8,12},{9,13},{1... | collective-permute-start | bytes 3145736 | tf_op jit(solution)/shard_map/ppermute | solution.py:412
  66.5 1.5 collective-permute-start.18
  68.1 19.2 %second_half.1 = (bf16[2,128,16,128]{3,2,1,0:T(8,128)(2,1)S(1)}, bf16[2,128,16,128]{3,2,1,0:T(8,128)(2,1)S(1)}, bf16[1,128,16,128]{3,2,1,0:T(8,128)(2,1)S(1)}, b...) custom-call(s32[896]{0:T(1024)S(1)} %fusion.26.target_ref, ...), custom_call_target="tpu_custom_call" | custom-call | flops 10000000000 | bytes 60000000 | tf_op jit(solution)/shard_map/second_half/pallas_call | solution.py:346
  87.3 0.6 collective-permute-start.19
  87.8 2.7 %collective-permute-start.21 = (bf16[2,128,16,128]{3,2,1,0:T(8,128)(2,1)}, bf16[2,128,16,128]{3,2,1,0:T(8,128)(2,1)S(1)}, u32[]{:S(2)}, u32[]{:S(2)}) collective-permute-start(bf16[2,128,16,128]{3,2,1,0:T(8,128)(2,1)} %get-tuple-element.50), channel_id=1, source_target_pairs={{0,12},{1,13},{2,14},{3,15},{4,0},{5,1},{6,2},{7,3},{8,4},{9,5},{1... | collective-permute-start | bytes 3145736 | tf_op jit(solution)/shard_map/ppermute | solution.py:413
  90.6 0.8 collective-permute-done.16
  91.4 2.4 %collective-permute-start.6 = (bf16[2,128,16,128]{3,2,1,0:T(8,128)(2,1)S(1)}, bf16[2,128,16,128]{3,2,1,0:T(8,128)(2,1)S(1)}, u32[]{:S(2)}, u32[]{:S(2)}) collective-permute-start(bf16[2,128,16,128]{3,2,1,0:T(8,128)(2,1)S(1)} %get-tuple-element.35), channel_id=1, source_target_pairs={{0,3},{1,0},{2,1},{3,2},{4,7},{5,4},{6,5},{7,6},{8,11},{9,8},{10,9... | collective-permute-start | bytes 3145736 | tf_op jit(solution)/shard_map/ppermute | solution.py:413
  94.2 20.3 %collective-permute-done.19 = bf16[2,128,16,128]{3,2,1,0:T(8,128)(2,1)S(1)} collective-permute-done((bf16[2,128,16,128]{3,2,1,0:T(8,128)(2,1)}, bf16[2,128,16,128]{3,2,1,0:T(8,128)(2,1)S(1)}, u32[]{:S(2)}, u32[]{:S(2)}) %collective-permute-start.19) | collective-permute-done | bytes 1048608 | tf_op jit(solution)/shard_map/ppermute | solution.py:412
  114.5 0.9 collective-permute-start.9
  115.6 1.0 collective-permute-start.17
  116.7 1.1 collective-permute-done.4
  117.8 1.3 collective-permute-start.22
  119.3 0.8 collective-permute-start.20
  120.2 19.8 %collective-permute-done.7 = bf16[2,128,16,128]{3,2,1,0:T(8,128)(2,1)S(1)} collective-permute-done((bf16[2,128,16,128]{3,2,1,0:T(8,128)(2,1)S(1)}, bf16[2,128,16,128]{3,2,1,0:T(8,128)(2,1)S(1)}, u32[]{:S(2)}, u32[]{:S(2)}) %collective-permute-start.7) | collective-permute-done | bytes 1048608 | tf_op jit(solution)/shard_map/ppermute | solution.py:412
  140.0 0.4 collective-permute-start.23
  140.8 3.3 %collective-permute-start.10 = (bf16[128,16,128]{2,1,0:T(8,128)(2,1)S(1)}, bf16[128,16,128]{2,1,0:T(8,128)(2,1)S(1)}, u32[]{:S(2)}, u32[]{:S(2)}) collective-permute-start(bf16[128,16,128]{2,1,0:T(8,128)(2,1)S(1)} %fusion.2), channel_id=1, source_target_pairs={{0,3},{1,0},{2,1},{3,2},{4,7},{5,4},{6,5},{7,6},{8,11},{9,8},{10,9... | collective-permute-start | bytes 1572872 | tf_op jit(solution)/shard_map/ppermute | solution.py:415
  144.2 0.4 fusion.32
  144.6 3.3 %collective-permute-start.11 = (bf16[128,16,128]{2,1,0:T(8,128)(2,1)S(1)}, bf16[128,16,128]{2,1,0:T(8,128)(2,1)S(1)}, u32[]{:S(2)}, u32[]{:S(2)}) collective-permute-start(bf16[128,16,128]{2,1,0:T(8,128)(2,1)S(1)} %fusion.3), channel_id=1, source_target_pairs={{0,3},{1,0},{2,1},{3,2},{4,7},{5,4},{6,5},{7,6},{8,11},{9,8},{10,9... | collective-permute-start | bytes 1572872 | tf_op jit(solution)/shard_map/ppermute | solution.py:415
  147.9 5.8 %collective-permute-done.23 = bf16[128,16,128]{2,1,0:T(8,128)(2,1)S(1)} collective-permute-done((bf16[128,16,128]{2,1,0:T(8,128)(2,1)S(1)}, bf16[128,16,128]{2,1,0:T(8,128)(2,1)S(1)}, u32[]{:S(2)}, u32[]{:S(2)}) %collective-permute-start.23) | collective-permute-done | bytes 524320 | tf_op jit(solution)/shard_map/ppermute | solution.py:415
  153.7 0.4 fusion.33
  154.6 2.2 %collective-permute-done.5 = bf16[128,16,128]{2,1,0:T(8,128)(2,1)S(1)} collective-permute-done((bf16[128,16,128]{2,1,0:T(8,128)(2,1)S(1)}, bf16[128,16,128]{2,1,0:T(8,128)(2,1)S(1)}, u32[]{:S(2)}, u32[]{:S(2)}) %collective-permute-start.5) | collective-permute-done | bytes 524320 | tf_op jit(solution)/shard_map/ppermute | solution.py:414
  156.8 0.4 fusion.36
  157.3 10.7 %collective-permute-done.8 = bf16[128,16,128]{2,1,0:T(8,128)(2,1)S(1)} collective-permute-done((bf16[128,16,128]{2,1,0:T(8,128)(2,1)S(1)}, bf16[128,16,128]{2,1,0:T(8,128)(2,1)S(1)}, u32[]{:S(2)}, u32[]{:S(2)}) %collective-permute-start.8) | collective-permute-done | bytes 524320 | tf_op jit(solution)/shard_map/ppermute | solution.py:414
  168.0 0.4 fusion.37
  168.6 1.6 collective-permute-start.13
  170.2 0.8 collective-permute-start.12
  171.2 0.8 pad_maximum_fusion.3.refs_7_
  172.1 5.0 %collective-permute-done.25.refs_9_ = bf16[2,2,32,16,128]{4,3,2,1,0:T(8,128)(2,1)S(1)} collective-permute-done((bf16[2,2,32,16,128]{4,3,2,1,0:T(8,128)(2,1)S(1)}, bf16[2,2,32,16,128]{4,3,2,1,0:T(8,128)(2,1)S(1)}, u32[]{:S(2)}, u32[]{:S(2)}) %collective-permute-start.25) | collective-permute-done | bytes 524320 | tf_op jit(solution)/shard_map/ppermute | solution.py:432
  177.1 3.8 %collective-permute-start.27 = (bf16[2,32,16,128]{3,2,1,0:T(8,128)(2,1)S(1)}, bf16[2,32,16,128]{3,2,1,0:T(8,128)(2,1)S(1)}, u32[]{:S(2)}, u32[]{:S(2)}) collective-permute-start(bf16[2,32,16,128]{3,2,1,0:T(8,128)(2,1)S(1)} %fusion.8), channel_id=1, source_target_pairs={{0,3},{1,0},{2,1},{3,2},{4,7},{5,4},{6,5},{7,6},{8,11},{9,8},{10,9... | collective-permute-start | bytes 786440 | tf_op jit(solution)/shard_map/ppermute | solution.py:434
  181.2 2.5 %collective-permute-start.15 = (bf16[2,32,16,128]{3,2,1,0:T(8,128)(2,1)S(1)}, bf16[2,32,16,128]{3,2,1,0:T(8,128)(2,1)S(1)}, u32[]{:S(2)}, u32[]{:S(2)}) collective-permute-start(bf16[2,32,16,128]{3,2,1,0:T(8,128)(2,1)S(1)} %fusion.10), channel_id=1, source_target_pairs={{0,12},{1,13},{2,14},{3,15},{4,0},{5,1},{6,2},{7,3},{8,4},{9,5},{1... | collective-permute-start | bytes 786440 | tf_op jit(solution)/shard_map/ppermute | solution.py:434
  183.8 0.8 pad_maximum_fusion.2.refs_6_
  184.7 0.9 pad_maximum_fusion.1.refs_1_
  185.5 0.8 pad_maximum_fusion.refs_0_
  186.4 2.3 %collective-permute-done.26.refs_10_ = bf16[2,32,16,128]{3,2,1,0:T(8,128)(2,1)S(1)} collective-permute-done((bf16[2,32,16,128]{3,2,1,0:T(8,128)(2,1)S(1)}, bf16[2,32,16,128]{3,2,1,0:T(8,128)(2,1)S(1)}, u32[]{:S(2)}, u32[]{:S(2)}) %collective-permute-start.26) | collective-permute-done | bytes 262176 | tf_op jit(solution)/shard_map/ppermute | solution.py:433
  188.7 2.7 %collective-permute-done.14.refs_4_ = bf16[2,32,16,128]{3,2,1,0:T(8,128)(2,1)S(1)} collective-permute-done((bf16[2,32,16,128]{3,2,1,0:T(8,128)(2,1)S(1)}, bf16[2,32,16,128]{3,2,1,0:T(8,128)(2,1)S(1)}, u32[]{:S(2)}, u32[]{:S(2)}) %collective-permute-start.14) | collective-permute-done | bytes 262176 | tf_op jit(solution)/shard_map/ppermute | solution.py:433
  191.4 0.7 copy-done.13
  192.1 4.3 %finish.1 = f32[128,4096]{1,0:T(8,128)} custom-call(f32[2,32,16,128]{3,2,1,0:T(8,128)} %pad_maximum_fusion.refs_0_, f32[2,32,16,128]{3,2,1,0:T(8,128)} %pad_maximum_fusion.1.refs_1_, bf16[2,2,32,16,128]{4,3,2,1,0:T(8,128)(2,1)} %copy-done.6, bf16[2,2,32,16,128]{4,3,2,1,0:T(8,128)(2,1)} %copy-done.5, bf16[2,32,16,128]{3,2,1,0:T(8,128)(2,1)} %copy-done.13, ...), custom_call_target="tpu_custom_call" | custom-call | tf_op jit(solution)/shard_map/finish/pallas_call | solution.py:461
  (82 shorter events, 3.0 us)
Async XLA Ops:
  0.0 12.5 %copy-start = (bf16[128,4096]{1,0:T(8,128)(2,1)S(1)}, bf16[128,4096]{1,0:T(8,128)(2,1)}, u32[]{:S(2)}) copy-start(bf16[128,4096]{1,0:T(8,128)(2,1)} %p_ref.1) | copy-start | bytes 3145732
  1.2 33.6 %collective-permute-start = (bf16[32,4096]{1,0:T(8,128)(2,1)S(1)}, bf16[32,4096]{1,0:T(8,128)(2,1)S(1)}, u32[]{:S(2)}, u32[]{:S(2)}) collective-permute-start(bf16[32,4096]{1,0:T(8,128)(2,1)S(1)} %get-tuple-element.80), channel_id=1, source_target_pairs={{0,1},{1,2},{2,3},{3,4},{4,5},{5,6},{6,7},{7,8},{8,9},{9,10},{10,1... | collective-permute-start | bytes 786440 | tf_op jit(solution)/shard_map/ppermute | solution.py:369
  4.6 30.2 %collective-permute-start.1 = (bf16[32,4096]{1,0:T(8,128)(2,1)S(1)}, bf16[32,4096]{1,0:T(8,128)(2,1)S(1)}, u32[]{:S(2)}, u32[]{:S(2)}) collective-permute-start(bf16[32,4096]{1,0:T(8,128)(2,1)S(1)} %get-tuple-element.79), channel_id=1, source_target_pairs={{1,0},{2,1},{3,2},{4,3},{5,4},{6,5},{7,6},{8,7},{9,8},{10,9},{11,1... | collective-permute-start | bytes 786440 | tf_op jit(solution)/shard_map/ppermute | solution.py:369
  6.9 27.8 %collective-permute-start.2 = (bf16[32,4096]{1,0:T(8,128)(2,1)S(1)}, bf16[32,4096]{1,0:T(8,128)(2,1)S(1)}, u32[]{:S(2)}, u32[]{:S(2)}) collective-permute-start(bf16[32,4096]{1,0:T(8,128)(2,1)S(1)} %get-tuple-element.78), channel_id=1, source_target_pairs={{0,16},{16,32},{32,48},{48,64},{64,80},{80,96},{96,112},{112,128},... | collective-permute-start | bytes 786440 | tf_op jit(solution)/shard_map/ppermute | solution.py:369
  8.9 25.9 %collective-permute-start.3 = (bf16[32,4096]{1,0:T(8,128)(2,1)S(1)}, bf16[32,4096]{1,0:T(8,128)(2,1)S(1)}, u32[]{:S(2)}, u32[]{:S(2)}) collective-permute-start(bf16[32,4096]{1,0:T(8,128)(2,1)S(1)} %get-tuple-element.77), channel_id=1, source_target_pairs={{16,0},{32,16},{48,32},{64,48},{80,64},{96,80},{112,96},{128,112},... | collective-permute-start | bytes 786440 | tf_op jit(solution)/shard_map/ppermute | solution.py:369
  12.5 21.8 %copy-start.14 = (s32[128,7]{0,1:T(8,128)S(1)}, s32[128,7]{0,1:T(8,128)}, u32[]{:S(2)}) copy-start(s32[128,7]{0,1:T(8,128)} %param.7) | copy-start | bytes 10756
  12.5 22.1 %copy-start.15 = (s32[896,1]{0,1:T(1,128)S(1)}, s32[896,1]{0,1:T(1,128)}, u32[]{:S(2)}) copy-start(s32[896,1]{0,1:T(1,128)} %param.6) | copy-start | bytes 10756
  32.0 1.3 copy-start.1
  33.3 1.0 copy-start.2
  61.6 29.8 %collective-permute-start.16 = (bf16[2,128,16,128]{3,2,1,0:T(8,128)(2,1)}, bf16[2,128,16,128]{3,2,1,0:T(8,128)(2,1)S(1)}, u32[]{:S(2)}, u32[]{:S(2)}) collective-permute-start(bf16[2,128,16,128]{3,2,1,0:T(8,128)(2,1)} %get-tuple-element.45), channel_id=1, source_target_pairs={{0,4},{1,5},{2,6},{3,7},{4,8},{5,9},{6,10},{7,11},{8,12},{9,13},{1... | collective-permute-start | bytes 3145736 | tf_op jit(solution)/shard_map/ppermute | solution.py:412
  66.5 27.4 %collective-permute-start.18 = (bf16[2,128,16,128]{3,2,1,0:T(8,128)(2,1)}, bf16[2,128,16,128]{3,2,1,0:T(8,128)(2,1)S(1)}, u32[]{:S(2)}, u32[]{:S(2)}) collective-permute-start(bf16[2,128,16,128]{3,2,1,0:T(8,128)(2,1)} %get-tuple-element.46), channel_id=1, source_target_pairs={{0,12},{1,13},{2,14},{3,15},{4,0},{5,1},{6,2},{7,3},{8,4},{9,5},{1... | collective-permute-start | bytes 3145736 | tf_op jit(solution)/shard_map/ppermute | solution.py:413
  87.3 27.3 %collective-permute-start.19 = (bf16[2,128,16,128]{3,2,1,0:T(8,128)(2,1)}, bf16[2,128,16,128]{3,2,1,0:T(8,128)(2,1)S(1)}, u32[]{:S(2)}, u32[]{:S(2)}) collective-permute-start(bf16[2,128,16,128]{3,2,1,0:T(8,128)(2,1)} %get-tuple-element.49), channel_id=1, source_target_pairs={{0,4},{1,5},{2,6},{3,7},{4,8},{5,9},{6,10},{7,11},{8,12},{9,13},{1... | collective-permute-start | bytes 3145736 | tf_op jit(solution)/shard_map/ppermute | solution.py:412
  87.8 27.8 %collective-permute-start.21 = (bf16[2,128,16,128]{3,2,1,0:T(8,128)(2,1)}, bf16[2,128,16,128]{3,2,1,0:T(8,128)(2,1)S(1)}, u32[]{:S(2)}, u32[]{:S(2)}) collective-permute-start(bf16[2,128,16,128]{3,2,1,0:T(8,128)(2,1)} %get-tuple-element.50), channel_id=1, source_target_pairs={{0,12},{1,13},{2,14},{3,15},{4,0},{5,1},{6,2},{7,3},{8,4},{9,5},{1... | collective-permute-start | bytes 3145736 | tf_op jit(solution)/shard_map/ppermute | solution.py:413
  90.6 27.2 %collective-permute-start.4 = (bf16[2,128,16,128]{3,2,1,0:T(8,128)(2,1)S(1)}, bf16[2,128,16,128]{3,2,1,0:T(8,128)(2,1)S(1)}, u32[]{:S(2)}, u32[]{:S(2)}) collective-permute-start(bf16[2,128,16,128]{3,2,1,0:T(8,128)(2,1)S(1)} %get-tuple-element.34), channel_id=1, source_target_pairs={{0,1},{1,2},{2,3},{3,0},{4,5},{5,6},{6,7},{7,4},{8,9},{9,10},{10,1... | collective-permute-start | bytes 3145736 | tf_op jit(solution)/shard_map/ppermute | solution.py:412
  91.4 27.9 %collective-permute-start.6 = (bf16[2,128,16,128]{3,2,1,0:T(8,128)(2,1)S(1)}, bf16[2,128,16,128]{3,2,1,0:T(8,128)(2,1)S(1)}, u32[]{:S(2)}, u32[]{:S(2)}) collective-permute-start(bf16[2,128,16,128]{3,2,1,0:T(8,128)(2,1)S(1)} %get-tuple-element.35), channel_id=1, source_target_pairs={{0,3},{1,0},{2,1},{3,2},{4,7},{5,4},{6,5},{7,6},{8,11},{9,8},{10,9... | collective-permute-start | bytes 3145736 | tf_op jit(solution)/shard_map/ppermute | solution.py:413
  94.0 46.0 %collective-permute-start.7 = (bf16[2,128,16,128]{3,2,1,0:T(8,128)(2,1)S(1)}, bf16[2,128,16,128]{3,2,1,0:T(8,128)(2,1)S(1)}, u32[]{:S(2)}, u32[]{:S(2)}) collective-permute-start(bf16[2,128,16,128]{3,2,1,0:T(8,128)(2,1)S(1)} %get-tuple-element.39), channel_id=1, source_target_pairs={{0,1},{1,2},{2,3},{3,0},{4,5},{5,6},{6,7},{7,4},{8,9},{9,10},{10,1... | collective-permute-start | bytes 3145736 | tf_op jit(solution)/shard_map/ppermute | solution.py:412
  114.5 26.1 %collective-permute-start.9 = (bf16[2,128,16,128]{3,2,1,0:T(8,128)(2,1)S(1)}, bf16[2,128,16,128]{3,2,1,0:T(8,128)(2,1)S(1)}, u32[]{:S(2)}, u32[]{:S(2)}) collective-permute-start(bf16[2,128,16,128]{3,2,1,0:T(8,128)(2,1)S(1)} %get-tuple-element.40), channel_id=1, source_target_pairs={{0,3},{1,0},{2,1},{3,2},{4,7},{5,4},{6,5},{7,6},{8,11},{9,8},{10,9... | collective-permute-start | bytes 3145736 | tf_op jit(solution)/shard_map/ppermute | solution.py:413
  115.6 25.2 %collective-permute-start.17 = (bf16[128,16,128]{2,1,0:T(8,128)(2,1)S(1)}, bf16[128,16,128]{2,1,0:T(8,128)(2,1)S(1)}, u32[]{:S(2)}, u32[]{:S(2)}) collective-permute-start(bf16[128,16,128]{2,1,0:T(8,128)(2,1)S(1)} %fusion.4), channel_id=1, source_target_pairs={{0,4},{1,5},{2,6},{3,7},{4,8},{5,9},{6,10},{7,11},{8,12},{9,13},{1... | collective-permute-start | bytes 1572872 | tf_op jit(solution)/shard_map/ppermute | solution.py:414
  117.8 26.3 %collective-permute-start.22 = (bf16[128,16,128]{2,1,0:T(8,128)(2,1)S(1)}, bf16[128,16,128]{2,1,0:T(8,128)(2,1)S(1)}, u32[]{:S(2)}, u32[]{:S(2)}) collective-permute-start(bf16[128,16,128]{2,1,0:T(8,128)(2,1)S(1)} %fusion.6), channel_id=1, source_target_pairs={{0,12},{1,13},{2,14},{3,15},{4,0},{5,1},{6,2},{7,3},{8,4},{9,5},{1... | collective-permute-start | bytes 1572872 | tf_op jit(solution)/shard_map/ppermute | solution.py:415
  119.3 25.3 %collective-permute-start.20 = (bf16[128,16,128]{2,1,0:T(8,128)(2,1)S(1)}, bf16[128,16,128]{2,1,0:T(8,128)(2,1)S(1)}, u32[]{:S(2)}, u32[]{:S(2)}) collective-permute-start(bf16[128,16,128]{2,1,0:T(8,128)(2,1)S(1)} %fusion.5), channel_id=1, source_target_pairs={{0,4},{1,5},{2,6},{3,7},{4,8},{5,9},{6,10},{7,11},{8,12},{9,13},{1... | collective-permute-start | bytes 1572872 | tf_op jit(solution)/shard_map/ppermute | solution.py:414
  120.1 24.1 %copy-start.8 = (bf16[2,128,16,128]{3,2,1,0:T(8,128)(2,1)S(1)}, bf16[2,128,16,128]{3,2,1,0:T(8,128)(2,1)}, u32[]{:S(2)}) copy-start(bf16[2,128,16,128]{3,2,1,0:T(8,128)(2,1)} %get-tuple-element.43) | copy-start | bytes 3145732
  140.0 13.7 %collective-permute-start.23 = (bf16[128,16,128]{2,1,0:T(8,128)(2,1)S(1)}, bf16[128,16,128]{2,1,0:T(8,128)(2,1)S(1)}, u32[]{:S(2)}, u32[]{:S(2)}) collective-permute-start(bf16[128,16,128]{2,1,0:T(8,128)(2,1)S(1)} %fusion.7), channel_id=1, source_target_pairs={{0,12},{1,13},{2,14},{3,15},{4,0},{5,1},{6,2},{7,3},{8,4},{9,5},{1... | collective-permute-start | bytes 1572872 | tf_op jit(solution)/shard_map/ppermute | solution.py:415
  140.6 16.1 %collective-permute-start.5 = (bf16[128,16,128]{2,1,0:T(8,128)(2,1)S(1)}, bf16[128,16,128]{2,1,0:T(8,128)(2,1)S(1)}, u32[]{:S(2)}, u32[]{:S(2)}) collective-permute-start(bf16[128,16,128]{2,1,0:T(8,128)(2,1)S(1)} %fusion), channel_id=1, source_target_pairs={{0,1},{1,2},{2,3},{3,0},{4,5},{5,6},{6,7},{7,4},{8,9},{9,10},{10,1... | collective-permute-start | bytes 1572872 | tf_op jit(solution)/shard_map/ppermute | solution.py:414
  140.8 15.9 %collective-permute-start.10 = (bf16[128,16,128]{2,1,0:T(8,128)(2,1)S(1)}, bf16[128,16,128]{2,1,0:T(8,128)(2,1)S(1)}, u32[]{:S(2)}, u32[]{:S(2)}) collective-permute-start(bf16[128,16,128]{2,1,0:T(8,128)(2,1)S(1)} %fusion.2), channel_id=1, source_target_pairs={{0,3},{1,0},{2,1},{3,2},{4,7},{5,4},{6,5},{7,6},{8,11},{9,8},{10,9... | collective-permute-start | bytes 1572872 | tf_op jit(solution)/shard_map/ppermute | solution.py:415
  144.1 23.8 %collective-permute-start.8 = (bf16[128,16,128]{2,1,0:T(8,128)(2,1)S(1)}, bf16[128,16,128]{2,1,0:T(8,128)(2,1)S(1)}, u32[]{:S(2)}, u32[]{:S(2)}) collective-permute-start(bf16[128,16,128]{2,1,0:T(8,128)(2,1)S(1)} %fusion.1), channel_id=1, source_target_pairs={{0,1},{1,2},{2,3},{3,0},{4,5},{5,6},{6,7},{7,4},{8,9},{9,10},{10,1... | collective-permute-start | bytes 1572872 | tf_op jit(solution)/shard_map/ppermute | solution.py:414
  144.1 9.5 %copy-start.9 = (bf16[2,128,16,128]{3,2,1,0:T(8,128)(2,1)S(1)}, bf16[2,128,16,128]{3,2,1,0:T(8,128)(2,1)}, u32[]{:S(2)}) copy-start(bf16[2,128,16,128]{3,2,1,0:T(8,128)(2,1)} %get-tuple-element.47) | copy-start | bytes 3145732
  144.6 23.4 %collective-permute-start.11 = (bf16[128,16,128]{2,1,0:T(8,128)(2,1)S(1)}, bf16[128,16,128]{2,1,0:T(8,128)(2,1)S(1)}, u32[]{:S(2)}, u32[]{:S(2)}) collective-permute-start(bf16[128,16,128]{2,1,0:T(8,128)(2,1)S(1)} %fusion.3), channel_id=1, source_target_pairs={{0,3},{1,0},{2,1},{3,2},{4,7},{5,4},{6,5},{7,6},{8,11},{9,8},{10,9... | collective-permute-start | bytes 1572872 | tf_op jit(solution)/shard_map/ppermute | solution.py:415
  154.2 2.5 %copy-start.7 = (bf16[2,128,16,128]{3,2,1,0:T(8,128)(2,1)S(1)}, bf16[2,128,16,128]{3,2,1,0:T(8,128)(2,1)}, u32[]{:S(2)}) copy-start(bf16[2,128,16,128]{3,2,1,0:T(8,128)(2,1)} %get-tuple-element.32) | copy-start | bytes 3145732
  154.4 22.6 %collective-permute-start.25 = (bf16[2,2,32,16,128]{4,3,2,1,0:T(8,128)(2,1)S(1)}, bf16[2,2,32,16,128]{4,3,2,1,0:T(8,128)(2,1)S(1)}, u32[]{:S(2)}, u32[]{:S(2)}) collective-permute-start(bf16[2,2,32,16,128]{4,3,2,1,0:T(8,128)(2,1)S(1)} %maximum_maximum_fusion.3), channel_id=1, source_target_pairs={{0,3},{1,0},{2,1},{3,2},{4,7},{5,4},{6,5},{7,6},{8,11},{9,8},{10,9... | collective-permute-start | bytes 1572872 | tf_op jit(solution)/shard_map/ppermute | solution.py:432
  156.7 24.2 %collective-permute-start.24 = (bf16[2,2,32,16,128]{4,3,2,1,0:T(8,128)(2,1)S(1)}, bf16[2,2,32,16,128]{4,3,2,1,0:T(8,128)(2,1)S(1)}, u32[]{:S(2)}, u32[]{:S(2)}) collective-permute-start(bf16[2,2,32,16,128]{4,3,2,1,0:T(8,128)(2,1)S(1)} %maximum_maximum_fusion.2), channel_id=1, source_target_pairs={{0,1},{1,2},{2,3},{3,0},{4,5},{5,6},{6,7},{7,4},{8,9},{9,10},{10,1... | collective-permute-start | bytes 1572872 | tf_op jit(solution)/shard_map/ppermute | solution.py:431
  168.6 12.5 %collective-permute-start.13 = (bf16[2,2,32,16,128]{4,3,2,1,0:T(8,128)(2,1)S(1)}, bf16[2,2,32,16,128]{4,3,2,1,0:T(8,128)(2,1)S(1)}, u32[]{:S(2)}, u32[]{:S(2)}) collective-permute-start(bf16[2,2,32,16,128]{4,3,2,1,0:T(8,128)(2,1)S(1)} %maximum_maximum_fusion.1), channel_id=1, source_target_pairs={{0,12},{1,13},{2,14},{3,15},{4,0},{5,1},{6,2},{7,3},{8,4},{9,5},{1... | collective-permute-start | bytes 1572872 | tf_op jit(solution)/shard_map/ppermute | solution.py:432
  170.2 13.4 %collective-permute-start.12 = (bf16[2,2,32,16,128]{4,3,2,1,0:T(8,128)(2,1)S(1)}, bf16[2,2,32,16,128]{4,3,2,1,0:T(8,128)(2,1)S(1)}, u32[]{:S(2)}, u32[]{:S(2)}) collective-permute-start(bf16[2,2,32,16,128]{4,3,2,1,0:T(8,128)(2,1)S(1)} %maximum_maximum_fusion), channel_id=1, source_target_pairs={{0,4},{1,5},{2,6},{3,7},{4,8},{5,9},{6,10},{7,11},{8,12},{9,13},{1... | collective-permute-start | bytes 1572872 | tf_op jit(solution)/shard_map/ppermute | solution.py:431
  177.1 7.6 %copy-start.3 = (bf16[2,2,32,16,128]{4,3,2,1,0:T(8,128)(2,1)}, bf16[2,2,32,16,128]{4,3,2,1,0:T(8,128)(2,1)S(1)}, u32[]{:S(2)}) copy-start(bf16[2,2,32,16,128]{4,3,2,1,0:T(8,128)(2,1)S(1)} %collective-permute-done.25.refs_9_) | copy-start | bytes 1572868
  177.1 9.2 %collective-permute-start.27 = (bf16[2,32,16,128]{3,2,1,0:T(8,128)(2,1)S(1)}, bf16[2,32,16,128]{3,2,1,0:T(8,128)(2,1)S(1)}, u32[]{:S(2)}, u32[]{:S(2)}) collective-permute-start(bf16[2,32,16,128]{3,2,1,0:T(8,128)(2,1)S(1)} %fusion.8), channel_id=1, source_target_pairs={{0,3},{1,0},{2,1},{3,2},{4,7},{5,4},{6,5},{7,6},{8,11},{9,8},{10,9... | collective-permute-start | bytes 786440 | tf_op jit(solution)/shard_map/ppermute | solution.py:434
  180.9 4.6 %copy-start.4 = (bf16[2,2,32,16,128]{4,3,2,1,0:T(8,128)(2,1)}, bf16[2,2,32,16,128]{4,3,2,1,0:T(8,128)(2,1)S(1)}, u32[]{:S(2)}) copy-start(bf16[2,2,32,16,128]{4,3,2,1,0:T(8,128)(2,1)S(1)} %collective-permute-done.24.refs_8_) | copy-start | bytes 1572868
  181.0 7.7 %collective-permute-start.26 = (bf16[2,32,16,128]{3,2,1,0:T(8,128)(2,1)S(1)}, bf16[2,32,16,128]{3,2,1,0:T(8,128)(2,1)S(1)}, u32[]{:S(2)}, u32[]{:S(2)}) collective-permute-start(bf16[2,32,16,128]{3,2,1,0:T(8,128)(2,1)S(1)} %fusion.9), channel_id=1, source_target_pairs={{0,1},{1,2},{2,3},{3,0},{4,5},{5,6},{6,7},{7,4},{8,9},{9,10},{10,1... | collective-permute-start | bytes 786440 | tf_op jit(solution)/shard_map/ppermute | solution.py:433
  181.1 5.3 %copy-start.5 = (bf16[2,2,32,16,128]{4,3,2,1,0:T(8,128)(2,1)}, bf16[2,2,32,16,128]{4,3,2,1,0:T(8,128)(2,1)S(1)}, u32[]{:S(2)}) copy-start(bf16[2,2,32,16,128]{4,3,2,1,0:T(8,128)(2,1)S(1)} %collective-permute-done.13.refs_3_) | copy-start | bytes 1572868
  181.2 7.5 %collective-permute-start.15 = (bf16[2,32,16,128]{3,2,1,0:T(8,128)(2,1)S(1)}, bf16[2,32,16,128]{3,2,1,0:T(8,128)(2,1)S(1)}, u32[]{:S(2)}, u32[]{:S(2)}) collective-permute-start(bf16[2,32,16,128]{3,2,1,0:T(8,128)(2,1)S(1)} %fusion.10), channel_id=1, source_target_pairs={{0,12},{1,13},{2,14},{3,15},{4,0},{5,1},{6,2},{7,3},{8,4},{9,5},{1... | collective-permute-start | bytes 786440 | tf_op jit(solution)/shard_map/ppermute | solution.py:434
  183.7 7.7 %copy-start.6 = (bf16[2,2,32,16,128]{4,3,2,1,0:T(8,128)(2,1)}, bf16[2,2,32,16,128]{4,3,2,1,0:T(8,128)(2,1)S(1)}, u32[]{:S(2)}) copy-start(bf16[2,2,32,16,128]{4,3,2,1,0:T(8,128)(2,1)S(1)} %collective-permute-done.12.refs_2_) | copy-start | bytes 1572868
  183.7 7.7 %collective-permute-start.14 = (bf16[2,32,16,128]{3,2,1,0:T(8,128)(2,1)S(1)}, bf16[2,32,16,128]{3,2,1,0:T(8,128)(2,1)S(1)}, u32[]{:S(2)}, u32[]{:S(2)}) collective-permute-start(bf16[2,32,16,128]{3,2,1,0:T(8,128)(2,1)S(1)} %fusion.11), channel_id=1, source_target_pairs={{0,4},{1,5},{2,6},{3,7},{4,8},{5,9},{6,10},{7,11},{8,12},{9,13},{1... | collective-permute-start | bytes 786440 | tf_op jit(solution)/shard_map/ppermute | solution.py:433
  186.4 5.0 %copy-start.10 = (bf16[2,32,16,128]{3,2,1,0:T(8,128)(2,1)}, bf16[2,32,16,128]{3,2,1,0:T(8,128)(2,1)S(1)}, u32[]{:S(2)}) copy-start(bf16[2,32,16,128]{3,2,1,0:T(8,128)(2,1)S(1)} %collective-permute-done.27.refs_11_) | copy-start | bytes 786436
  188.7 2.7 %copy-start.11 = (bf16[2,32,16,128]{3,2,1,0:T(8,128)(2,1)}, bf16[2,32,16,128]{3,2,1,0:T(8,128)(2,1)S(1)}, u32[]{:S(2)}) copy-start(bf16[2,32,16,128]{3,2,1,0:T(8,128)(2,1)S(1)} %collective-permute-done.26.refs_10_) | copy-start | bytes 786436
  188.7 2.7 %copy-start.12 = (bf16[2,32,16,128]{3,2,1,0:T(8,128)(2,1)}, bf16[2,32,16,128]{3,2,1,0:T(8,128)(2,1)S(1)}, u32[]{:S(2)}) copy-start(bf16[2,32,16,128]{3,2,1,0:T(8,128)(2,1)S(1)} %collective-permute-done.15.refs_5_) | copy-start | bytes 786436
  191.4 0.7 copy-start.13

commit v4 on v3

--- a/solution.py
+++ b/solution.py
@@ -406,33 +406,42 @@
     return added(keep, arrived).astype(jnp.bfloat16)
 
 
-def sum_of_rows(packs, perms):
-    right, left, keep_right, keep_left, own = packs
-    forward, backward = perms
-    r1 = lax.ppermute(right, "dom", forward)
-    l1 = lax.ppermute(left, "dom", backward)
-    r2 = lax.ppermute(join(keep_right[0], r1[0]), "dom", forward)
-    l2 = lax.ppermute(join(keep_left[0], l1[0]), "dom", backward)
-    shape = (SIDE, PART, HALF, 128)
-    return added(own[0], r2, l1[1]).reshape(shape), added(own[1], r1[1], l2).reshape(shape)
-
-
 def exchange(halves):
     along_x, along_y = ring_perms()
+    sets = ((0, along_x, along_y), (5, along_y, along_x))
+
+    def send(pair, perms):
+        return [lax.ppermute(v, "dom", perm) for v, perm in zip(pair, perms)]
+
+    first = [
+        lax.optimization_barrier([send(packs[at : at + 2], one) for at, one, _ in sets])
+        for packs in halves
+    ]
+    second = []
+    for packs, arrived in zip(halves, first):
+        row = []
+        for (at, one, _), (r1, l1) in zip(sets, arrived):
+            row.append(send((join(packs[at + 2][0], r1[0]), join(packs[at + 3][0], l1[0])), one))
+        second.append(lax.optimization_barrier(row))
+    shape = (SIDE, PART, HALF, 128)
+    sums = [[], []]
+    for packs, one, two in zip(halves, first, second):
+        for n, ((at, _, _), (r1, l1), (r2, l2)) in enumerate(zip(sets, one, two)):
+            own = packs[at + 4]
+            sums[n].append(
+                (added(own[0], r2, l1[1]).reshape(shape), added(own[1], r1[1], l2).reshape(shape))
+            )
+    third, kept = [], []
+    for (_, _, two), parts in zip(sets, sums):
+        r, l = ([jnp.stack([h[p][n] for h in parts]) for n in range(SIDE)] for p in range(2))
+        r16, l16 = ([v.astype(jnp.bfloat16) for v in w] for w in (r, l))
+        kept.append((r[0], l[0], r16[1], l16[3]))
+        third.append(send((jnp.stack([r16[2], l16[1]]), jnp.stack([l16[2], r16[3]])), two))
+    third = lax.optimization_barrier(third)
     found = []
-    for which, (one, two) in enumerate(((along_x, along_y), (along_y, along_x))):
-        sums = [sum_of_rows(packs[which * 5 : which * 5 + 5], one) for packs in halves]
-        r = [jnp.stack([s[0][n] for s in sums]) for n in range(3)]
-        l = [jnp.stack([s[1][n] for s in sums]) for n in (0, 1, 2, 3)]
-        r16 = [v.astype(jnp.bfloat16) for v in r]
-        l16 = [v.astype(jnp.bfloat16) for v in l]
-        r3 = jnp.stack([s[0][3] for s in sums]).astype(jnp.bfloat16)
-        forward, backward = two
-        r1 = lax.ppermute(jnp.stack([r16[2], l16[1]]), "dom", forward)
-        l1 = lax.ppermute(jnp.stack([l16[2], r3]), "dom", backward)
-        r2 = lax.ppermute(join(r16[1], r1[0]), "dom", forward)
-        l2 = lax.ppermute(join(l16[3], l1[0]), "dom", backward)
-        found += [r[0], l[0], r1, l1, r2, l2]
+    for (_, _, two), (right, left, keep_right, keep_left), (r1, l1) in zip(sets, kept, third):
+        fourth = send((join(keep_right, r1[0]), join(keep_left, l1[0])), two)
+        found += [right, left, r1, l1, *fourth]
     return found
 
 

time: 197 us -> 183 us (0.929)
  waiting for transfers between devices: 70.7 us -> 52 us
  starting transfers between devices: 42.5 us -> 46.9 us
    ppermute x24, waiting for transfers between devices: 70.6 us -> 52 us  [send(): return [lax.ppermute(v, 'dom', perm) for v, perm in zip(pair, perms)]]
    ppermute x24, starting transfers between devices: 32.3 us -> 36.6 us  [send(): return [lax.ppermute(v, 'dom', perm) for v, perm in zip(pair, perms)]]
    another operation x12 -> x10, other arithmetic: 5.21 us -> 5.2 us  [the longest x4 3.34 us: exchange(): jnp.stack([h[p][n] for h in parts])]
  transfers between devices with their start and end apart: 28 -> 28, of which waited for: 10 -> 13; matrix products, arithmetic and copies ran while one was open for 4% -> 4% of each run, Pallas kernels for 20% -> 21%
where the time goes in v4:
time: 183 us; the launch traced here: 182 us
  Pallas kernels  69.8 us (38%)
  waiting for transfers between devices  52 us (28%)
  starting transfers between devices  46.9 us (26%)
  other arithmetic  6.66 us (4%)
  local copies, waits for them, and re-layouts  5.95 us (3%)
    ppermute x24, waiting for transfers between devices, send(): return [lax.ppermute(v, 'dom', perm) for v, perm in zip(pair, perms)]  52 us
    ppermute x24, starting transfers between devices, send(): return [lax.ppermute(v, 'dom', perm) for v, perm in zip(pair, perms)]  36.6 us
    pallas_call x1, Pallas kernels, first_half(): pl.pallas_call(first_kernel, grid=(E_DEV // GROUP,), in_specs=[SMEM, VMEM...  26.8 us
    pallas_call x1, Pallas kernels, local_products(): pl.pallas_call(product_kernel, grid=(E_DEV // GROUP,), in_specs=[pl.Block...  19.4 us
    pallas_call x1, Pallas kernels, second_half(): pl.pallas_call(second_kernel, grid=(E_DEV // GROUP,), in_specs=[SMEM, VME...  19.2 us
    ppermute x4, starting transfers between devices, faces(): found += [lax.ppermute(last, axis, up), lax.ppermute(first, axis, down)]  10.3 us
    pallas_call x1, Pallas kernels, finish(): pl.pallas_call(finish_kernel, in_specs=[VMEM] * len(parts), out_specs=VME...  4.31 us
  transfers between devices with their start and end apart: 28, of which 13 were waited for; matrix products, arithmetic and copies ran while one was open for 4% of the time, Pallas kernels for 21%

profile of v4, /device:TPU:96, one launch (start us, length us, event | category | flops | bytes accessed | tf_op | source)
XLA Modules:
  0.0 181.8 jit_solution(17234222861953157953)
XLA Ops:
  0.0 1.2 slice_bitcast_fusion.8
  1.2 3.4 %collective-permute-start = (bf16[32,4096]{1,0:T(8,128)(2,1)S(1)}, bf16[32,4096]{1,0:T(8,128)(2,1)S(1)}, u32[]{:S(2)}, u32[]{:S(2)}) collective-permute-start(bf16[32,4096]{1,0:T(8,128)(2,1)S(1)} %get-tuple-element.120), channel_id=1, source_target_pairs={{0,1},{1,2},{2,3},{3,4},{4,5},{5,6},{6,7},{7,8},{8,9},{9,10},{10,1... | collective-permute-start | bytes 786440 | tf_op jit(solution)/shard_map/ppermute | solution.py:369
  4.6 1.3 collective-permute-start.1
  5.9 1.1 fusion.38
  6.9 1.9 %collective-permute-start.2 = (bf16[32,4096]{1,0:T(8,128)(2,1)S(1)}, bf16[32,4096]{1,0:T(8,128)(2,1)S(1)}, u32[]{:S(2)}, u32[]{:S(2)}) collective-permute-start(bf16[32,4096]{1,0:T(8,128)(2,1)S(1)} %get-tuple-element.118), channel_id=1, source_target_pairs={{0,16},{16,32},{32,48},{48,64},{64,80},{80,96},{96,112},{112,128},... | collective-permute-start | bytes 786440 | tf_op jit(solution)/shard_map/ppermute | solution.py:369
  8.9 3.6 %collective-permute-start.3 = (bf16[32,4096]{1,0:T(8,128)(2,1)S(1)}, bf16[32,4096]{1,0:T(8,128)(2,1)S(1)}, u32[]{:S(2)}, u32[]{:S(2)}) collective-permute-start(bf16[32,4096]{1,0:T(8,128)(2,1)S(1)} %get-tuple-element.117), channel_id=1, source_target_pairs={{16,0},{32,16},{48,32},{64,48},{80,64},{96,80},{112,96},{128,112},... | collective-permute-start | bytes 786440 | tf_op jit(solution)/shard_map/ppermute | solution.py:369
  12.6 19.4 %local_products.1 = (bf16[128,64,896]{2,1,0:T(8,128)(2,1)}, bf16[128,64,64]{2,1,0:T(8,128)(2,1)S(1)}, bf16[128,32,128]{2,1,0:T(8,128)(2,1)S(1)}) custom-call(bf16[7,128,4096]{2,1,0:T(8,128)(2,1)} %bitcast.147, bf16[128,4096]{1,0:T(8,128)(2,1)S(1)} %copy-done), custom_call_target="tpu_custom_call" | custom-call | flops 10000000000 | bytes 60000000 | tf_op jit(solution)/shard_map/local_products/pallas_call | solution.py:307
  32.0 1.3 copy-done.1
  33.3 1.0 copy-done.2
  34.8 26.8 %first_half.1 = (bf16[128,64,128]{2,1,0:T(8,128)(2,1)}, bf16[2,128,16,128]{3,2,1,0:T(8,128)(2,1)S(1)}, bf16[2,128,16,128]{3,2,1,0:T(8,128)(2,1)S(1)}, bf16[1,128...) custom-call(s32[896]{0:T(1024)S(1)} %fusion.26.target_ref, ...), custom_call_target="tpu_custom_call" | custom-call | flops 10000000000 | bytes 60000000 | tf_op jit(solution)/shard_map/first_half/pallas_call | solution.py:331
  61.6 2.7 %collective-permute-start.4 = (bf16[2,128,16,128]{3,2,1,0:T(8,128)(2,1)S(1)}, bf16[2,128,16,128]{3,2,1,0:T(8,128)(2,1)S(1)}, u32[]{:S(2)}, u32[]{:S(2)}) collective-permute-start(bf16[2,128,16,128]{3,2,1,0:T(8,128)(2,1)S(1)} %get-tuple-element.54), channel_id=1, source_target_pairs={{0,1},{1,2},{2,3},{3,0},{4,5},{5,6},{6,7},{7,4},{8,9},{9,10},{10,1... | collective-permute-start | bytes 3145736 | tf_op jit(solution)/shard_map/ppermute | solution.py:414
  64.3 1.4 collective-permute-start.5
  65.7 4.1 %collective-permute-start.6 = (bf16[2,128,16,128]{3,2,1,0:T(8,128)(2,1)}, bf16[2,128,16,128]{3,2,1,0:T(8,128)(2,1)S(1)}, u32[]{:S(2)}, u32[]{:S(2)}) collective-permute-start(bf16[2,128,16,128]{3,2,1,0:T(8,128)(2,1)} %get-tuple-element.56), channel_id=1, source_target_pairs={{0,4},{1,5},{2,6},{3,7},{4,8},{5,9},{6,10},{7,11},{8,12},{9,13},{1... | collective-permute-start | bytes 3145736 | tf_op jit(solution)/shard_map/ppermute | solution.py:414
  69.7 1.4 collective-permute-start.7
  71.2 19.2 %second_half.1 = (bf16[2,128,16,128]{3,2,1,0:T(8,128)(2,1)S(1)}, bf16[2,128,16,128]{3,2,1,0:T(8,128)(2,1)S(1)}, bf16[1,128,16,128]{3,2,1,0:T(8,128)(2,1)S(1)}, b...) custom-call(s32[896]{0:T(1024)S(1)} %fusion.26.target_ref, ...), custom_call_target="tpu_custom_call" | custom-call | flops 10000000000 | bytes 60000000 | tf_op jit(solution)/shard_map/second_half/pallas_call | solution.py:346
  90.5 3.2 %collective-permute-start.13 = (bf16[2,128,16,128]{3,2,1,0:T(8,128)(2,1)S(1)}, bf16[2,128,16,128]{3,2,1,0:T(8,128)(2,1)S(1)}, u32[]{:S(2)}, u32[]{:S(2)}) collective-permute-start(bf16[2,128,16,128]{3,2,1,0:T(8,128)(2,1)S(1)} %get-tuple-element.70), channel_id=1, source_target_pairs={{0,3},{1,0},{2,1},{3,2},{4,7},{5,4},{6,5},{7,6},{8,11},{9,8},{10,9... | collective-permute-start | bytes 3145736 | tf_op jit(solution)/shard_map/ppermute | solution.py:414
  93.7 0.6 collective-permute-start.14
  94.3 0.8 collective-permute-done.6
  95.1 2.3 %collective-permute-start.15 = (bf16[2,128,16,128]{3,2,1,0:T(8,128)(2,1)}, bf16[2,128,16,128]{3,2,1,0:T(8,128)(2,1)S(1)}, u32[]{:S(2)}, u32[]{:S(2)}) collective-permute-start(bf16[2,128,16,128]{3,2,1,0:T(8,128)(2,1)} %get-tuple-element.72), channel_id=1, source_target_pairs={{0,12},{1,13},{2,14},{3,15},{4,0},{5,1},{6,2},{7,3},{8,4},{9,5},{1... | collective-permute-start | bytes 3145736 | tf_op jit(solution)/shard_map/ppermute | solution.py:414
  97.6 1.5 collective-permute-start.11
  99.5 18.0 %collective-permute-done.12 = bf16[2,128,16,128]{3,2,1,0:T(8,128)(2,1)S(1)} collective-permute-done((bf16[2,128,16,128]{3,2,1,0:T(8,128)(2,1)S(1)}, bf16[2,128,16,128]{3,2,1,0:T(8,128)(2,1)S(1)}, u32[]{:S(2)}, u32[]{:S(2)}) %collective-permute-start.12) | collective-permute-done | bytes 1048608 | tf_op jit(solution)/shard_map/ppermute | solution.py:414
  117.8 2.7 %collective-permute-start.9 = (bf16[128,16,128]{2,1,0:T(8,128)(2,1)S(1)}, bf16[128,16,128]{2,1,0:T(8,128)(2,1)S(1)}, u32[]{:S(2)}, u32[]{:S(2)}) collective-permute-start(bf16[128,16,128]{2,1,0:T(8,128)(2,1)S(1)} %fusion.1), channel_id=1, source_target_pairs={{0,3},{1,0},{2,1},{3,2},{4,7},{5,4},{6,5},{7,6},{8,11},{9,8},{10,9... | collective-permute-start | bytes 1572872 | tf_op jit(solution)/shard_map/ppermute | solution.py:414
  120.7 0.6 collective-permute-done.15
  121.5 3.6 %collective-permute-start.19 = (bf16[128,16,128]{2,1,0:T(8,128)(2,1)S(1)}, bf16[128,16,128]{2,1,0:T(8,128)(2,1)S(1)}, u32[]{:S(2)}, u32[]{:S(2)}) collective-permute-start(bf16[128,16,128]{2,1,0:T(8,128)(2,1)S(1)} %fusion.7), channel_id=1, source_target_pairs={{0,12},{1,13},{2,14},{3,15},{4,0},{5,1},{6,2},{7,3},{8,4},{9,5},{1... | collective-permute-start | bytes 1572872 | tf_op jit(solution)/shard_map/ppermute | solution.py:414
  125.5 7.1 %collective-permute-done.11 = bf16[128,16,128]{2,1,0:T(8,128)(2,1)S(1)} collective-permute-done((bf16[128,16,128]{2,1,0:T(8,128)(2,1)S(1)}, bf16[128,16,128]{2,1,0:T(8,128)(2,1)S(1)}, u32[]{:S(2)}, u32[]{:S(2)}) %collective-permute-start.11) | collective-permute-done | bytes 524320 | tf_op jit(solution)/shard_map/ppermute | solution.py:414
  132.6 0.9 collective-permute-start.18
  133.4 2.4 %collective-permute-start.17 = (bf16[128,16,128]{2,1,0:T(8,128)(2,1)S(1)}, bf16[128,16,128]{2,1,0:T(8,128)(2,1)S(1)}, u32[]{:S(2)}, u32[]{:S(2)}) collective-permute-start(bf16[128,16,128]{2,1,0:T(8,128)(2,1)S(1)} %fusion.5), channel_id=1, source_target_pairs={{0,3},{1,0},{2,1},{3,2},{4,7},{5,4},{6,5},{7,6},{8,11},{9,8},{10,9... | collective-permute-start | bytes 1572872 | tf_op jit(solution)/shard_map/ppermute | solution.py:414
  135.8 0.8 fusion.30
  136.8 6.5 %collective-permute-done.19 = bf16[128,16,128]{2,1,0:T(8,128)(2,1)S(1)} collective-permute-done((bf16[128,16,128]{2,1,0:T(8,128)(2,1)S(1)}, bf16[128,16,128]{2,1,0:T(8,128)(2,1)S(1)}, u32[]{:S(2)}, u32[]{:S(2)}) %collective-permute-start.19) | collective-permute-done | bytes 524320 | tf_op jit(solution)/shard_map/ppermute | solution.py:414
  143.3 3.4 %collective-permute-done.18 = bf16[128,16,128]{2,1,0:T(8,128)(2,1)S(1)} collective-permute-done((bf16[128,16,128]{2,1,0:T(8,128)(2,1)S(1)}, bf16[128,16,128]{2,1,0:T(8,128)(2,1)S(1)}, u32[]{:S(2)}, u32[]{:S(2)}) %collective-permute-start.18) | collective-permute-done | bytes 524320 | tf_op jit(solution)/shard_map/ppermute | solution.py:414
  146.6 1.5 collective-permute-done.16
  148.1 0.8 fusion.31
  149.5 1.8 %collective-permute-start.22 = (bf16[2,2,32,16,128]{4,3,2,1,0:T(8,128)(2,1)S(1)}, bf16[2,2,32,16,128]{4,3,2,1,0:T(8,128)(2,1)S(1)}, u32[]{:S(2)}, u32[]{:S(2)}) collective-permute-start(bf16[2,2,32,16,128]{4,3,2,1,0:T(8,128)(2,1)S(1)} %maximum_maximum_fusion.2), channel_id=1, source_target_pairs={{0,1},{1,2},{2,3},{3,0},{4,5},{5,6},{6,7},{7,4},{8,9},{9,10},{10,1... | collective-permute-start | bytes 1572872 | tf_op jit(solution)/shard_map/ppermute | solution.py:414
  151.5 2.5 %collective-permute-start.21 = (bf16[2,2,32,16,128]{4,3,2,1,0:T(8,128)(2,1)S(1)}, bf16[2,2,32,16,128]{4,3,2,1,0:T(8,128)(2,1)S(1)}, u32[]{:S(2)}, u32[]{:S(2)}) collective-permute-start(bf16[2,2,32,16,128]{4,3,2,1,0:T(8,128)(2,1)S(1)} %maximum_maximum_fusion.1), channel_id=1, source_target_pairs={{0,12},{1,13},{2,14},{3,15},{4,0},{5,1},{6,2},{7,3},{8,4},{9,5},{1... | collective-permute-start | bytes 1572872 | tf_op jit(solution)/shard_map/ppermute | solution.py:414
  154.5 0.8 pad_maximum_fusion.3.refs_7_
  155.4 3.9 %collective-permute-done.23.refs_9_ = bf16[2,2,32,16,128]{4,3,2,1,0:T(8,128)(2,1)S(1)} collective-permute-done((bf16[2,2,32,16,128]{4,3,2,1,0:T(8,128)(2,1)S(1)}, bf16[2,2,32,16,128]{4,3,2,1,0:T(8,128)(2,1)S(1)}, u32[]{:S(2)}, u32[]{:S(2)}) %collective-permute-start.23) | collective-permute-done | bytes 524320 | tf_op jit(solution)/shard_map/ppermute | solution.py:414
  159.3 2.1 %collective-permute-done.22.refs_8_ = bf16[2,2,32,16,128]{4,3,2,1,0:T(8,128)(2,1)S(1)} collective-permute-done((bf16[2,2,32,16,128]{4,3,2,1,0:T(8,128)(2,1)S(1)}, bf16[2,2,32,16,128]{4,3,2,1,0:T(8,128)(2,1)S(1)}, u32[]{:S(2)}, u32[]{:S(2)}) %collective-permute-start.22) | collective-permute-done | bytes 524320 | tf_op jit(solution)/shard_map/ppermute | solution.py:414
  161.9 3.8 %collective-permute-done.20.refs_2_ = bf16[2,2,32,16,128]{4,3,2,1,0:T(8,128)(2,1)S(1)} collective-permute-done((bf16[2,2,32,16,128]{4,3,2,1,0:T(8,128)(2,1)S(1)}, bf16[2,2,32,16,128]{4,3,2,1,0:T(8,128)(2,1)S(1)}, u32[]{:S(2)}, u32[]{:S(2)}) %collective-permute-start.20) | collective-permute-done | bytes 524320 | tf_op jit(solution)/shard_map/ppermute | solution.py:414
  165.7 1.8 %collective-permute-start.27 = (bf16[2,32,16,128]{3,2,1,0:T(8,128)(2,1)S(1)}, bf16[2,32,16,128]{3,2,1,0:T(8,128)(2,1)S(1)}, u32[]{:S(2)}, u32[]{:S(2)}) collective-permute-start(bf16[2,32,16,128]{3,2,1,0:T(8,128)(2,1)S(1)} %fusion.8), channel_id=1, source_target_pairs={{0,3},{1,0},{2,1},{3,2},{4,7},{5,4},{6,5},{7,6},{8,11},{9,8},{10,9... | collective-permute-start | bytes 786440 | tf_op jit(solution)/shard_map/ppermute | solution.py:414
  168.0 1.0 collective-permute-start.25
  169.1 1.2 collective-permute-start.24
  170.3 0.8 pad_maximum_fusion.2.refs_6_
  171.1 0.8 pad_maximum_fusion.1.refs_1_
  172.0 0.8 pad_maximum_fusion.refs_0_
  172.8 2.5 %collective-permute-done.26.refs_10_ = bf16[2,32,16,128]{3,2,1,0:T(8,128)(2,1)S(1)} collective-permute-done((bf16[2,32,16,128]{3,2,1,0:T(8,128)(2,1)S(1)}, bf16[2,32,16,128]{3,2,1,0:T(8,128)(2,1)S(1)}, u32[]{:S(2)}, u32[]{:S(2)}) %collective-permute-start.26) | collective-permute-done | bytes 262176 | tf_op jit(solution)/shard_map/ppermute | solution.py:414
  175.3 1.5 collective-permute-done.24.refs_4_
  176.8 0.7 copy-done.13
  177.5 4.3 %finish.1 = f32[128,4096]{1,0:T(8,128)} custom-call(f32[2,32,16,128]{3,2,1,0:T(8,128)} %pad_maximum_fusion.refs_0_, f32[2,32,16,128]{3,2,1,0:T(8,128)} %pad_maximum_fusion.1.refs_1_, bf16[2,2,32,16,128]{4,3,2,1,0:T(8,128)(2,1)} %copy-done.6, bf16[2,2,32,16,128]{4,3,2,1,0:T(8,128)(2,1)} %copy-done.5, bf16[2,32,16,128]{3,2,1,0:T(8,128)(2,1)} %copy-done.13, ...), custom_call_target="tpu_custom_call" | custom-call | tf_op jit(solution)/shard_map/finish/pallas_call | solution.py:470
  (88 shorter events, 4.6 us)
Async XLA Ops:
  0.0 12.5 %copy-start = (bf16[128,4096]{1,0:T(8,128)(2,1)S(1)}, bf16[128,4096]{1,0:T(8,128)(2,1)}, u32[]{:S(2)}) copy-start(bf16[128,4096]{1,0:T(8,128)(2,1)} %p_ref.1) | copy-start | bytes 3145732
  1.2 33.6 %collective-permute-start = (bf16[32,4096]{1,0:T(8,128)(2,1)S(1)}, bf16[32,4096]{1,0:T(8,128)(2,1)S(1)}, u32[]{:S(2)}, u32[]{:S(2)}) collective-permute-start(bf16[32,4096]{1,0:T(8,128)(2,1)S(1)} %get-tuple-element.120), channel_id=1, source_target_pairs={{0,1},{1,2},{2,3},{3,4},{4,5},{5,6},{6,7},{7,8},{8,9},{9,10},{10,1... | collective-permute-start | bytes 786440 | tf_op jit(solution)/shard_map/ppermute | solution.py:369
  4.6 30.2 %collective-permute-start.1 = (bf16[32,4096]{1,0:T(8,128)(2,1)S(1)}, bf16[32,4096]{1,0:T(8,128)(2,1)S(1)}, u32[]{:S(2)}, u32[]{:S(2)}) collective-permute-start(bf16[32,4096]{1,0:T(8,128)(2,1)S(1)} %get-tuple-element.119), channel_id=1, source_target_pairs={{1,0},{2,1},{3,2},{4,3},{5,4},{6,5},{7,6},{8,7},{9,8},{10,9},{11,1... | collective-permute-start | bytes 786440 | tf_op jit(solution)/shard_map/ppermute | solution.py:369
  6.9 27.8 %collective-permute-start.2 = (bf16[32,4096]{1,0:T(8,128)(2,1)S(1)}, bf16[32,4096]{1,0:T(8,128)(2,1)S(1)}, u32[]{:S(2)}, u32[]{:S(2)}) collective-permute-start(bf16[32,4096]{1,0:T(8,128)(2,1)S(1)} %get-tuple-element.118), channel_id=1, source_target_pairs={{0,16},{16,32},{32,48},{48,64},{64,80},{80,96},{96,112},{112,128},... | collective-permute-start | bytes 786440 | tf_op jit(solution)/shard_map/ppermute | solution.py:369
  8.9 25.9 %collective-permute-start.3 = (bf16[32,4096]{1,0:T(8,128)(2,1)S(1)}, bf16[32,4096]{1,0:T(8,128)(2,1)S(1)}, u32[]{:S(2)}, u32[]{:S(2)}) collective-permute-start(bf16[32,4096]{1,0:T(8,128)(2,1)S(1)} %get-tuple-element.117), channel_id=1, source_target_pairs={{16,0},{32,16},{48,32},{64,48},{80,64},{96,80},{112,96},{128,112},... | collective-permute-start | bytes 786440 | tf_op jit(solution)/shard_map/ppermute | solution.py:369
  12.5 21.8 %copy-start.14 = (s32[128,7]{0,1:T(8,128)S(1)}, s32[128,7]{0,1:T(8,128)}, u32[]{:S(2)}) copy-start(s32[128,7]{0,1:T(8,128)} %param.7) | copy-start | bytes 10756
  12.5 22.1 %copy-start.15 = (s32[896,1]{0,1:T(1,128)S(1)}, s32[896,1]{0,1:T(1,128)}, u32[]{:S(2)}) copy-start(s32[896,1]{0,1:T(1,128)} %param.6) | copy-start | bytes 10756
  32.0 1.3 copy-start.1
  33.3 1.0 copy-start.2
  61.6 28.9 %collective-permute-start.4 = (bf16[2,128,16,128]{3,2,1,0:T(8,128)(2,1)S(1)}, bf16[2,128,16,128]{3,2,1,0:T(8,128)(2,1)S(1)}, u32[]{:S(2)}, u32[]{:S(2)}) collective-permute-start(bf16[2,128,16,128]{3,2,1,0:T(8,128)(2,1)S(1)} %get-tuple-element.54), channel_id=1, source_target_pairs={{0,1},{1,2},{2,3},{3,0},{4,5},{5,6},{6,7},{7,4},{8,9},{9,10},{10,1... | collective-permute-start | bytes 3145736 | tf_op jit(solution)/shard_map/ppermute | solution.py:414
  64.3 29.4 %collective-permute-start.5 = (bf16[2,128,16,128]{3,2,1,0:T(8,128)(2,1)S(1)}, bf16[2,128,16,128]{3,2,1,0:T(8,128)(2,1)S(1)}, u32[]{:S(2)}, u32[]{:S(2)}) collective-permute-start(bf16[2,128,16,128]{3,2,1,0:T(8,128)(2,1)S(1)} %get-tuple-element.55), channel_id=1, source_target_pairs={{0,3},{1,0},{2,1},{3,2},{4,7},{5,4},{6,5},{7,6},{8,11},{9,8},{10,9... | collective-permute-start | bytes 3145736 | tf_op jit(solution)/shard_map/ppermute | solution.py:414
  65.7 29.4 %collective-permute-start.6 = (bf16[2,128,16,128]{3,2,1,0:T(8,128)(2,1)}, bf16[2,128,16,128]{3,2,1,0:T(8,128)(2,1)S(1)}, u32[]{:S(2)}, u32[]{:S(2)}) collective-permute-start(bf16[2,128,16,128]{3,2,1,0:T(8,128)(2,1)} %get-tuple-element.56), channel_id=1, source_target_pairs={{0,4},{1,5},{2,6},{3,7},{4,8},{5,9},{6,10},{7,11},{8,12},{9,13},{1... | collective-permute-start | bytes 3145736 | tf_op jit(solution)/shard_map/ppermute | solution.py:414
  69.7 27.7 %collective-permute-start.7 = (bf16[2,128,16,128]{3,2,1,0:T(8,128)(2,1)}, bf16[2,128,16,128]{3,2,1,0:T(8,128)(2,1)S(1)}, u32[]{:S(2)}, u32[]{:S(2)}) collective-permute-start(bf16[2,128,16,128]{3,2,1,0:T(8,128)(2,1)} %get-tuple-element.57), channel_id=1, source_target_pairs={{0,12},{1,13},{2,14},{3,15},{4,0},{5,1},{6,2},{7,3},{8,4},{9,5},{1... | collective-permute-start | bytes 3145736 | tf_op jit(solution)/shard_map/ppermute | solution.py:414
  90.4 27.0 %collective-permute-start.12 = (bf16[2,128,16,128]{3,2,1,0:T(8,128)(2,1)S(1)}, bf16[2,128,16,128]{3,2,1,0:T(8,128)(2,1)S(1)}, u32[]{:S(2)}, u32[]{:S(2)}) collective-permute-start(bf16[2,128,16,128]{3,2,1,0:T(8,128)(2,1)S(1)} %get-tuple-element.69), channel_id=1, source_target_pairs={{0,1},{1,2},{2,3},{3,0},{4,5},{5,6},{6,7},{7,4},{8,9},{9,10},{10,1... | collective-permute-start | bytes 3145736 | tf_op jit(solution)/shard_map/ppermute | solution.py:414
  90.5 27.3 %collective-permute-start.13 = (bf16[2,128,16,128]{3,2,1,0:T(8,128)(2,1)S(1)}, bf16[2,128,16,128]{3,2,1,0:T(8,128)(2,1)S(1)}, u32[]{:S(2)}, u32[]{:S(2)}) collective-permute-start(bf16[2,128,16,128]{3,2,1,0:T(8,128)(2,1)S(1)} %get-tuple-element.70), channel_id=1, source_target_pairs={{0,3},{1,0},{2,1},{3,2},{4,7},{5,4},{6,5},{7,6},{8,11},{9,8},{10,9... | collective-permute-start | bytes 3145736 | tf_op jit(solution)/shard_map/ppermute | solution.py:414
  93.7 26.7 %collective-permute-start.14 = (bf16[2,128,16,128]{3,2,1,0:T(8,128)(2,1)}, bf16[2,128,16,128]{3,2,1,0:T(8,128)(2,1)S(1)}, u32[]{:S(2)}, u32[]{:S(2)}) collective-permute-start(bf16[2,128,16,128]{3,2,1,0:T(8,128)(2,1)} %get-tuple-element.71), channel_id=1, source_target_pairs={{0,4},{1,5},{2,6},{3,7},{4,8},{5,9},{6,10},{7,11},{8,12},{9,13},{1... | collective-permute-start | bytes 3145736 | tf_op jit(solution)/shard_map/ppermute | solution.py:414
  95.1 26.2 %collective-permute-start.15 = (bf16[2,128,16,128]{3,2,1,0:T(8,128)(2,1)}, bf16[2,128,16,128]{3,2,1,0:T(8,128)(2,1)S(1)}, u32[]{:S(2)}, u32[]{:S(2)}) collective-permute-start(bf16[2,128,16,128]{3,2,1,0:T(8,128)(2,1)} %get-tuple-element.72), channel_id=1, source_target_pairs={{0,12},{1,13},{2,14},{3,15},{4,0},{5,1},{6,2},{7,3},{8,4},{9,5},{1... | collective-permute-start | bytes 3145736 | tf_op jit(solution)/shard_map/ppermute | solution.py:414
  97.6 35.0 %collective-permute-start.11 = (bf16[128,16,128]{2,1,0:T(8,128)(2,1)S(1)}, bf16[128,16,128]{2,1,0:T(8,128)(2,1)S(1)}, u32[]{:S(2)}, u32[]{:S(2)}) collective-permute-start(bf16[128,16,128]{2,1,0:T(8,128)(2,1)S(1)} %fusion.3), channel_id=1, source_target_pairs={{0,12},{1,13},{2,14},{3,15},{4,0},{5,1},{6,2},{7,3},{8,4},{9,5},{1... | collective-permute-start | bytes 1572872 | tf_op jit(solution)/shard_map/ppermute | solution.py:414
  117.4 16.0 %collective-permute-start.10 = (bf16[128,16,128]{2,1,0:T(8,128)(2,1)S(1)}, bf16[128,16,128]{2,1,0:T(8,128)(2,1)S(1)}, u32[]{:S(2)}, u32[]{:S(2)}) collective-permute-start(bf16[128,16,128]{2,1,0:T(8,128)(2,1)S(1)} %fusion.2), channel_id=1, source_target_pairs={{0,4},{1,5},{2,6},{3,7},{4,8},{5,9},{6,10},{7,11},{8,12},{9,13},{1... | collective-permute-start | bytes 1572872 | tf_op jit(solution)/shard_map/ppermute | solution.py:414
  117.8 18.0 %collective-permute-start.9 = (bf16[128,16,128]{2,1,0:T(8,128)(2,1)S(1)}, bf16[128,16,128]{2,1,0:T(8,128)(2,1)S(1)}, u32[]{:S(2)}, u32[]{:S(2)}) collective-permute-start(bf16[128,16,128]{2,1,0:T(8,128)(2,1)S(1)} %fusion.1), channel_id=1, source_target_pairs={{0,3},{1,0},{2,1},{3,2},{4,7},{5,4},{6,5},{7,6},{8,11},{9,8},{10,9... | collective-permute-start | bytes 1572872 | tf_op jit(solution)/shard_map/ppermute | solution.py:414
  120.4 15.4 %collective-permute-start.8 = (bf16[128,16,128]{2,1,0:T(8,128)(2,1)S(1)}, bf16[128,16,128]{2,1,0:T(8,128)(2,1)S(1)}, u32[]{:S(2)}, u32[]{:S(2)}) collective-permute-start(bf16[128,16,128]{2,1,0:T(8,128)(2,1)S(1)} %fusion), channel_id=1, source_target_pairs={{0,1},{1,2},{2,3},{3,0},{4,5},{5,6},{6,7},{7,4},{8,9},{9,10},{10,1... | collective-permute-start | bytes 1572872 | tf_op jit(solution)/shard_map/ppermute | solution.py:414
  121.5 21.8 %collective-permute-start.19 = (bf16[128,16,128]{2,1,0:T(8,128)(2,1)S(1)}, bf16[128,16,128]{2,1,0:T(8,128)(2,1)S(1)}, u32[]{:S(2)}, u32[]{:S(2)}) collective-permute-start(bf16[128,16,128]{2,1,0:T(8,128)(2,1)S(1)} %fusion.7), channel_id=1, source_target_pairs={{0,12},{1,13},{2,14},{3,15},{4,0},{5,1},{6,2},{7,3},{8,4},{9,5},{1... | collective-permute-start | bytes 1572872 | tf_op jit(solution)/shard_map/ppermute | solution.py:414
  125.1 10.7 %copy-start.8 = (bf16[2,128,16,128]{3,2,1,0:T(8,128)(2,1)S(1)}, bf16[2,128,16,128]{3,2,1,0:T(8,128)(2,1)}, u32[]{:S(2)}) copy-start(bf16[2,128,16,128]{3,2,1,0:T(8,128)(2,1)} %get-tuple-element.52) | copy-start | bytes 3145732
  125.1 10.7 %copy-start.9 = (bf16[2,128,16,128]{3,2,1,0:T(8,128)(2,1)S(1)}, bf16[2,128,16,128]{3,2,1,0:T(8,128)(2,1)}, u32[]{:S(2)}) copy-start(bf16[2,128,16,128]{3,2,1,0:T(8,128)(2,1)} %get-tuple-element.83) | copy-start | bytes 3145732
  132.6 14.1 %collective-permute-start.18 = (bf16[128,16,128]{2,1,0:T(8,128)(2,1)S(1)}, bf16[128,16,128]{2,1,0:T(8,128)(2,1)S(1)}, u32[]{:S(2)}, u32[]{:S(2)}) collective-permute-start(bf16[128,16,128]{2,1,0:T(8,128)(2,1)S(1)} %fusion.6), channel_id=1, source_target_pairs={{0,4},{1,5},{2,6},{3,7},{4,8},{5,9},{6,10},{7,11},{8,12},{9,13},{1... | collective-permute-start | bytes 1572872 | tf_op jit(solution)/shard_map/ppermute | solution.py:414
  133.4 13.2 %collective-permute-start.17 = (bf16[128,16,128]{2,1,0:T(8,128)(2,1)S(1)}, bf16[128,16,128]{2,1,0:T(8,128)(2,1)S(1)}, u32[]{:S(2)}, u32[]{:S(2)}) collective-permute-start(bf16[128,16,128]{2,1,0:T(8,128)(2,1)S(1)} %fusion.5), channel_id=1, source_target_pairs={{0,3},{1,0},{2,1},{3,2},{4,7},{5,4},{6,5},{7,6},{8,11},{9,8},{10,9... | collective-permute-start | bytes 1572872 | tf_op jit(solution)/shard_map/ppermute | solution.py:414
  135.8 12.3 %collective-permute-start.16 = (bf16[128,16,128]{2,1,0:T(8,128)(2,1)S(1)}, bf16[128,16,128]{2,1,0:T(8,128)(2,1)S(1)}, u32[]{:S(2)}, u32[]{:S(2)}) collective-permute-start(bf16[128,16,128]{2,1,0:T(8,128)(2,1)S(1)} %fusion.4), channel_id=1, source_target_pairs={{0,1},{1,2},{2,3},{3,0},{4,5},{5,6},{6,7},{7,4},{8,9},{9,10},{10,1... | collective-permute-start | bytes 1572872 | tf_op jit(solution)/shard_map/ppermute | solution.py:414
  136.7 11.4 %copy-start.7 = (bf16[2,128,16,128]{3,2,1,0:T(8,128)(2,1)S(1)}, bf16[2,128,16,128]{3,2,1,0:T(8,128)(2,1)}, u32[]{:S(2)}) copy-start(bf16[2,128,16,128]{3,2,1,0:T(8,128)(2,1)} %get-tuple-element.85) | copy-start | bytes 3145732
  149.1 10.3 %collective-permute-start.23 = (bf16[2,2,32,16,128]{4,3,2,1,0:T(8,128)(2,1)S(1)}, bf16[2,2,32,16,128]{4,3,2,1,0:T(8,128)(2,1)S(1)}, u32[]{:S(2)}, u32[]{:S(2)}) collective-permute-start(bf16[2,2,32,16,128]{4,3,2,1,0:T(8,128)(2,1)S(1)} %maximum_maximum_fusion.3), channel_id=1, source_target_pairs={{0,3},{1,0},{2,1},{3,2},{4,7},{5,4},{6,5},{7,6},{8,11},{9,8},{10,9... | collective-permute-start | bytes 1572872 | tf_op jit(solution)/shard_map/ppermute | solution.py:414
  149.5 12.0 %collective-permute-start.22 = (bf16[2,2,32,16,128]{4,3,2,1,0:T(8,128)(2,1)S(1)}, bf16[2,2,32,16,128]{4,3,2,1,0:T(8,128)(2,1)S(1)}, u32[]{:S(2)}, u32[]{:S(2)}) collective-permute-start(bf16[2,2,32,16,128]{4,3,2,1,0:T(8,128)(2,1)S(1)} %maximum_maximum_fusion.2), channel_id=1, source_target_pairs={{0,1},{1,2},{2,3},{3,0},{4,5},{5,6},{6,7},{7,4},{8,9},{9,10},{10,1... | collective-permute-start | bytes 1572872 | tf_op jit(solution)/shard_map/ppermute | solution.py:414
  151.5 10.4 %collective-permute-start.21 = (bf16[2,2,32,16,128]{4,3,2,1,0:T(8,128)(2,1)S(1)}, bf16[2,2,32,16,128]{4,3,2,1,0:T(8,128)(2,1)S(1)}, u32[]{:S(2)}, u32[]{:S(2)}) collective-permute-start(bf16[2,2,32,16,128]{4,3,2,1,0:T(8,128)(2,1)S(1)} %maximum_maximum_fusion.1), channel_id=1, source_target_pairs={{0,12},{1,13},{2,14},{3,15},{4,0},{5,1},{6,2},{7,3},{8,4},{9,5},{1... | collective-permute-start | bytes 1572872 | tf_op jit(solution)/shard_map/ppermute | solution.py:414
  154.0 11.6 %collective-permute-start.20 = (bf16[2,2,32,16,128]{4,3,2,1,0:T(8,128)(2,1)S(1)}, bf16[2,2,32,16,128]{4,3,2,1,0:T(8,128)(2,1)S(1)}, u32[]{:S(2)}, u32[]{:S(2)}) collective-permute-start(bf16[2,2,32,16,128]{4,3,2,1,0:T(8,128)(2,1)S(1)} %maximum_maximum_fusion), channel_id=1, source_target_pairs={{0,4},{1,5},{2,6},{3,7},{4,8},{5,9},{6,10},{7,11},{8,12},{9,13},{1... | collective-permute-start | bytes 1572872 | tf_op jit(solution)/shard_map/ppermute | solution.py:414
  159.3 11.8 %copy-start.3 = (bf16[2,2,32,16,128]{4,3,2,1,0:T(8,128)(2,1)}, bf16[2,2,32,16,128]{4,3,2,1,0:T(8,128)(2,1)S(1)}, u32[]{:S(2)}) copy-start(bf16[2,2,32,16,128]{4,3,2,1,0:T(8,128)(2,1)S(1)} %collective-permute-done.23.refs_9_) | copy-start | bytes 1572868
  161.4 9.7 %copy-start.4 = (bf16[2,2,32,16,128]{4,3,2,1,0:T(8,128)(2,1)}, bf16[2,2,32,16,128]{4,3,2,1,0:T(8,128)(2,1)S(1)}, u32[]{:S(2)}) copy-start(bf16[2,2,32,16,128]{4,3,2,1,0:T(8,128)(2,1)S(1)} %collective-permute-done.22.refs_8_) | copy-start | bytes 1572868
  161.9 9.3 %copy-start.5 = (bf16[2,2,32,16,128]{4,3,2,1,0:T(8,128)(2,1)}, bf16[2,2,32,16,128]{4,3,2,1,0:T(8,128)(2,1)S(1)}, u32[]{:S(2)}) copy-start(bf16[2,2,32,16,128]{4,3,2,1,0:T(8,128)(2,1)S(1)} %collective-permute-done.21.refs_3_) | copy-start | bytes 1572868
  165.6 5.5 %copy-start.6 = (bf16[2,2,32,16,128]{4,3,2,1,0:T(8,128)(2,1)}, bf16[2,2,32,16,128]{4,3,2,1,0:T(8,128)(2,1)S(1)}, u32[]{:S(2)}) copy-start(bf16[2,2,32,16,128]{4,3,2,1,0:T(8,128)(2,1)S(1)} %collective-permute-done.20.refs_2_) | copy-start | bytes 1572868
  165.7 7.1 %collective-permute-start.27 = (bf16[2,32,16,128]{3,2,1,0:T(8,128)(2,1)S(1)}, bf16[2,32,16,128]{3,2,1,0:T(8,128)(2,1)S(1)}, u32[]{:S(2)}, u32[]{:S(2)}) collective-permute-start(bf16[2,32,16,128]{3,2,1,0:T(8,128)(2,1)S(1)} %fusion.8), channel_id=1, source_target_pairs={{0,3},{1,0},{2,1},{3,2},{4,7},{5,4},{6,5},{7,6},{8,11},{9,8},{10,9... | collective-permute-start | bytes 786440 | tf_op jit(solution)/shard_map/ppermute | solution.py:414
  167.6 7.7 %collective-permute-start.26 = (bf16[2,32,16,128]{3,2,1,0:T(8,128)(2,1)S(1)}, bf16[2,32,16,128]{3,2,1,0:T(8,128)(2,1)S(1)}, u32[]{:S(2)}, u32[]{:S(2)}) collective-permute-start(bf16[2,32,16,128]{3,2,1,0:T(8,128)(2,1)S(1)} %fusion.9), channel_id=1, source_target_pairs={{0,1},{1,2},{2,3},{3,0},{4,5},{5,6},{6,7},{7,4},{8,9},{9,10},{10,1... | collective-permute-start | bytes 786440 | tf_op jit(solution)/shard_map/ppermute | solution.py:414
  168.0 7.3 %collective-permute-start.25 = (bf16[2,32,16,128]{3,2,1,0:T(8,128)(2,1)S(1)}, bf16[2,32,16,128]{3,2,1,0:T(8,128)(2,1)S(1)}, u32[]{:S(2)}, u32[]{:S(2)}) collective-permute-start(bf16[2,32,16,128]{3,2,1,0:T(8,128)(2,1)S(1)} %fusion.10), channel_id=1, source_target_pairs={{0,12},{1,13},{2,14},{3,15},{4,0},{5,1},{6,2},{7,3},{8,4},{9,5},{1... | collective-permute-start | bytes 786440 | tf_op jit(solution)/shard_map/ppermute | solution.py:414
  169.1 7.7 %collective-permute-start.24 = (bf16[2,32,16,128]{3,2,1,0:T(8,128)(2,1)S(1)}, bf16[2,32,16,128]{3,2,1,0:T(8,128)(2,1)S(1)}, u32[]{:S(2)}, u32[]{:S(2)}) collective-permute-start(bf16[2,32,16,128]{3,2,1,0:T(8,128)(2,1)S(1)} %fusion.11), channel_id=1, source_target_pairs={{0,4},{1,5},{2,6},{3,7},{4,8},{5,9},{6,10},{7,11},{8,12},{9,13},{1... | collective-permute-start | bytes 786440 | tf_op jit(solution)/shard_map/ppermute | solution.py:414
  172.8 3.9 %copy-start.10 = (bf16[2,32,16,128]{3,2,1,0:T(8,128)(2,1)}, bf16[2,32,16,128]{3,2,1,0:T(8,128)(2,1)S(1)}, u32[]{:S(2)}) copy-start(bf16[2,32,16,128]{3,2,1,0:T(8,128)(2,1)S(1)} %collective-permute-done.27.refs_11_) | copy-start | bytes 786436
  175.3 1.5 copy-start.11
  175.3 1.5 copy-start.12
  176.8 0.7 copy-start.13

commit v5 on v4

--- a/solution.py
+++ b/solution.py
@@ -87,8 +87,15 @@
             weights[slot0 + i + j, BLOCK:, 128:] = at_low
 
 
-def product_kernel(a_ref, p_ref, q_out, left_ref, face_ref, couples, q, rows, weights, sems):
+def first_kernel(target_ref, a_ref, p_ref, ym_ref, yp_ref, zm_ref, zp_ref, *refs):
+    q_out, left_out, qh_out, *outs = refs[:13]
+    acc, stage, drain_sems, couples, q, rows, weights, left_ref, qh_ref, sems = refs[13:]
     step = pl.program_id(0)
+
+    @pl.when(step == 0)
+    def _clear():
+        clear(acc)
+
     start = pl.multiple_of(step * GROUP, GROUP)
     spread_weights(p_ref, start, rows, weights, start, left_ref)
     for k in range(PAIRS):
@@ -111,6 +118,9 @@
             span = pl.ds(n * GROUP, GROUP)
             return pltpu.make_async_copy(q.at[span], q_out.at[span], sems.at[n])
 
+        lefts_away = pltpu.make_async_copy(left_ref, left_out, sems.at[E_DEV // GROUP])
+        faces_away = pltpu.make_async_copy(qh_ref, qh_out, sems.at[E_DEV // GROUP + 1])
+        lefts_away.start()
         behind = plane // GROUP
 
         for z in range(EZ):
@@ -142,19 +152,41 @@
                         q[e, ROWS:, k * 128 : (k + 1) * 128] = own[:, 128:]
                     return 0
 
-                lax.fori_loop(0, GROUP, neighbour, 0, unroll=4)
+                lax.fori_loop(0, GROUP, neighbour, 0, unroll=8)
                 if base // GROUP >= behind:
                     copy(base // GROUP - behind).start()
         for n in range(E_DEV // GROUP - behind, E_DEV // GROUP):
             copy(n).start()
-        for n in range(FACE):
-            outer, x = divmod(n, EX)
-            face_ref[n] = couples[3, outer * plane + x]
-            face_ref[FACE + n] = couples[4, outer * plane + plane - EX + x]
-            face_ref[2 * FACE + n] = couples[5, n]
-            face_ref[3 * FACE + n] = couples[6, E_DEV - plane + n]
+
+        for f, ref in enumerate((ym_ref, yp_ref, zm_ref, zp_ref)):
+            for g in range(FACE // GROUP):
+                spread_weights(ref, g * GROUP, rows, weights, f * FACE + g * GROUP, None)
+
+        def face_pair(n, _):
+            column = n // EX * plane + n % EX
+            elements = (column, column + plane - EX, n, n + E_DEV - plane)
+            for f, e in enumerate(elements):
+                found = jnp.dot(
+                    couples[3 + f, e], weights[f * FACE + n], preferred_element_type=jnp.float32
+                ).astype(jnp.bfloat16)
+                qh_ref[f * FACE + n, :ROWS, :] = found[:, :128]
+                qh_ref[f * FACE + n, ROWS:, :] = found[:, 128:]
+            return 0
+
+        lax.fori_loop(0, FACE, face_pair, 0, unroll=8)
+        faces_away.start()
+
+        def terms(n, _):
+            add_face_terms(n, 0, target_ref, left_ref, qh_ref, acc)
+            add_terms(n, 0, target_ref, left_ref, q.at[pl.ds(n * GROUP, GROUP)], acc)
+            return 0
+
+        lax.fori_loop(0, E_DEV // GROUP, terms, 0)
+        drain(acc, stage, drain_sems, outs)
         for n in range(E_DEV // GROUP):
             copy(n).wait()
+        lefts_away.wait()
+        faces_away.wait()
 
 
 def add_terms(step, half, target_ref, lefts, q_ref, acc):
@@ -179,7 +211,7 @@
             acc[target] += terms[:, k * 128 : (k + 1) * 128]
         return 0
 
-    lax.fori_loop(0, GROUP, element, 0, unroll=4)
+    lax.fori_loop(0, GROUP, element, 0, unroll=8)
 
 
 def add_face_terms(step, half, target_ref, lefts, qh_ref, acc):
@@ -201,7 +233,7 @@
         acc[target_ref[e * PAIRS + 3 + face]] += term.astype(jnp.bfloat16).astype(jnp.float32)
         return 0
 
-    lax.fori_loop(0, GROUP, pair, 0, unroll=8)
+    lax.fori_loop(0, GROUP, pair, 0, unroll=16)
 
 
 def drain(acc, stage, sems, outs):
@@ -225,40 +257,6 @@
         copies.append(copy)
     for copy in copies[-BUFFERS:]:
         copy.wait()
-
-
-def first_kernel(target_ref, left_ref, q_ref, face_ref, ym_ref, yp_ref, zm_ref, zp_ref, *refs):
-    qh_ref, *outs = refs[:11]
-    acc, stage, sems, weights, rows = refs[11:]
-    step = pl.program_id(0)
-
-    @pl.when(step == 0)
-    def _clear():
-        clear(acc)
-
-    groups = FACE // GROUP
-    for f, ref in enumerate((ym_ref, yp_ref, zm_ref, zp_ref)):
-
-        @pl.when(step // groups == f)
-        def _weights():
-            base = pl.multiple_of(step % groups * GROUP, GROUP)
-            spread_weights(ref, base, rows, weights, 0, None)
-
-    def multiply(i, _):
-        n = step * GROUP + i
-        found = jnp.dot(face_ref[n], weights[i], preferred_element_type=jnp.float32)
-        found = found.astype(jnp.bfloat16)
-        qh_ref[n, :ROWS, :] = found[:, :128]
-        qh_ref[n, ROWS:, :] = found[:, 128:]
-        return 0
-
-    lax.fori_loop(0, GROUP, multiply, 0, unroll=8)
-    add_face_terms(step, 0, target_ref, left_ref, qh_ref, acc)
-    add_terms(step, 0, target_ref, left_ref, q_ref, acc)
-
-    @pl.when(step == pl.num_programs(0) - 1)
-    def _drain():
-        drain(acc, stage, sems, outs)
 
 
 def second_kernel(target_ref, left_ref, q_ref, qh_ref, *refs):
@@ -290,12 +288,11 @@
     pltpu.VMEM((BUFFERS, SLOT, HALF, 128), jnp.bfloat16),
     pltpu.SemaphoreType.DMA((BUFFERS,)),
 ]
-WEIGHTS = pltpu.VMEM((GROUP, 128, 256), jnp.bfloat16)
-
-
-def params():
+
+
+def params(megabytes):
     return pltpu.CompilerParams(
-        dimension_semantics=("arbitrary",), vmem_limit_bytes=48 * 1024 * 1024
+        dimension_semantics=("arbitrary",), vmem_limit_bytes=megabytes * 1024 * 1024
     )
 
 
@@ -303,43 +300,37 @@
     return pl.CostEstimate(flops=10**10, bytes_accessed=megabytes * 10**6, transcendentals=0)
 
 
-def local_products(a, p):
-    return pl.pallas_call(
-        product_kernel,
+def first_half(target, a, p, halos):
+    found = pl.pallas_call(
+        first_kernel,
         grid=(E_DEV // GROUP,),
-        in_specs=[pl.BlockSpec((PAIRS, GROUP, SQUARE), lambda i: (0, i, 0)), VMEM],
-        out_specs=[HBM, VMEM, VMEM],
+        in_specs=[
+            SMEM,
+            pl.BlockSpec((PAIRS, GROUP, SQUARE), lambda i: (0, i, 0)),
+            VMEM, VMEM, VMEM, VMEM, VMEM,
+        ],
+        out_specs=[HBM] * (3 + len(PACKS)),
         out_shape=[
             jax.ShapeDtypeStruct((E_DEV, BLOCK, PAIRS * 128), jnp.bfloat16),
             jax.ShapeDtypeStruct((E_DEV, BLOCK, BLOCK), jnp.bfloat16),
-            jax.ShapeDtypeStruct((4 * FACE, ROWS, 128), jnp.bfloat16),
-        ],
-        scratch_shapes=[
+            jax.ShapeDtypeStruct((4 * FACE, BLOCK, 128), jnp.bfloat16),
+        ]
+        + PACKS,
+        scratch_shapes=SUMS
+        + [
             pltpu.VMEM((PAIRS, E_DEV + 1, ROWS, 128), jnp.bfloat16),
             pltpu.VMEM((E_DEV + 1, BLOCK, PAIRS * 128), jnp.bfloat16),
             pltpu.VMEM((PAIRS * GROUP * PITCH + 8, 128), jnp.float32),
             pltpu.VMEM((E_DEV, 128, 256), jnp.bfloat16),
-            pltpu.SemaphoreType.DMA((E_DEV // GROUP,)),
+            pltpu.VMEM((E_DEV, BLOCK, BLOCK), jnp.bfloat16),
+            pltpu.VMEM((4 * FACE, BLOCK, 128), jnp.bfloat16),
+            pltpu.SemaphoreType.DMA((E_DEV // GROUP + 2,)),
         ],
-        compiler_params=params(),
-        cost_estimate=cost(60),
-        name="local_products",
-    )(a, p)
-
-
-def first_half(target, lefts, q, face, halos):
-    found = pl.pallas_call(
-        first_kernel,
-        grid=(E_DEV // GROUP,),
-        in_specs=[SMEM, VMEM, Q_SPEC, VMEM, VMEM, VMEM, VMEM, VMEM],
-        out_specs=[VMEM] + [HBM] * len(PACKS),
-        out_shape=[jax.ShapeDtypeStruct((4 * FACE, BLOCK, 128), jnp.bfloat16)] + PACKS,
-        scratch_shapes=SUMS + [WEIGHTS, pltpu.VMEM((GROUP * PITCH + 8, 128), jnp.float32)],
-        compiler_params=params(),
+        compiler_params=params(62),
         cost_estimate=cost(60),
         name="first_half",
-    )(target, lefts, q, face, *halos)
-    return found[0], found[1:]
+    )(target, a, p, *halos)
+    return found[0], found[1], found[2], found[3:]
 
 
 def second_half(target, lefts, q, qh):
@@ -350,7 +341,7 @@
         out_specs=[HBM] * len(PACKS),
         out_shape=PACKS,
         scratch_shapes=SUMS,
-        compiler_params=params(),
+        compiler_params=params(48),
         cost_estimate=cost(60),
         name="second_half",
     )(target, lefts, q, qh)
@@ -441,29 +432,24 @@
     found = []
     for (_, _, two), (right, left, keep_right, keep_left), (r1, l1) in zip(sets, kept, third):
         fourth = send((join(keep_right, r1[0]), join(keep_left, l1[0])), two)
-        found += [right, left, r1, l1, *fourth]
+        found += [added(right, l1[1]), added(left, r1[1]), *fourth]
     return found
 
 
 def finish_kernel(*refs):
     *ins, out_ref, scratch = refs
-    for which in range(2):
-        own_right, own_left, r1, l1, r2, l2 = ins[6 * which : 6 * which + 6]
+    for n in range(4):
+        base = ins[4 * (n // 2) + n % 2]
+        last = ins[4 * (n // 2) + 2 + n % 2]
         for half in range(2):
-            parts = (
-                (own_right[half], r2[half], l1[1, half]),
-                (own_left[half], r1[1, half], l2[half]),
-            )
-            for part, pieces in enumerate(parts):
-                total = added(*pieces)
-                for c in range(PART):
-                    scratch[c * FLAT_PITCH : c * FLAT_PITCH + HALF, :] = total[c]
-                rows = pl.ds((2 * which + part) * PART, PART)
-                for u in range(HALF):
-                    t = half * HALF + u
-                    out_ref[rows, t * 128 : (t + 1) * 128] = scratch[
-                        pl.ds(u, PART, stride=FLAT_PITCH), :
-                    ]
+            total = added(base[half], last[half])
+            for c in range(PART):
+                scratch[c * FLAT_PITCH : c * FLAT_PITCH + HALF, :] = total[c]
+            for u in range(HALF):
+                t = half * HALF + u
+                out_ref[n * PART : (n + 1) * PART, t * 128 : (t + 1) * 128] = scratch[
+                    pl.ds(u, PART, stride=FLAT_PITCH), :
+                ]
 
 
 def finish(parts):
@@ -480,8 +466,7 @@
 def on_device(a_blocks, p_blocks, dest_rank, dest_block):
     halos = faces(p_blocks)
     target = sum_places(dest_rank, dest_block)
-    q, lefts, face = local_products(jnp.swapaxes(a_blocks, 0, 1), p_blocks)
-    qh, first = first_half(target, lefts, q, face, halos)
+    q, lefts, qh, first = first_half(target, jnp.swapaxes(a_blocks, 0, 1), p_blocks, halos)
     second = second_half(target, lefts, q, qh)
     return finish(exchange((first, second)))
 

time: 183 us -> 172 us (0.940)
  Pallas kernels: 69.8 us -> 53.9 us
  waiting for transfers between devices: 52 us -> 55.8 us
    pallas_call x2 -> x1, Pallas kernels: 46.3 us -> 32.8 us  [first_half(): pl.pallas_call(first_kernel, grid=(E_DEV // GROUP,), in_specs=[SMEM, pl.B...]
    ppermute x4, waiting for transfers between devices: 0.01 us -> 4.25 us  [faces(): found += [lax.ppermute(last, axis, up), lax.ppermute(first, axis, down)]]
    convert_element_type x12, other arithmetic: 1.41 us -> 4.79 us  [join(): return added(keep, arrived).astype(jnp.bfloat16)]
    another operation x6 -> x2, other arithmetic: 5 us -> 1.66 us  [the longest x4 3.34 us: exchange(): jnp.stack([h[p][n] for h in parts])]
  transfers between devices with their start and end apart: 28 -> 28, of which waited for: 13 -> 16; matrix products, arithmetic and copies ran while one was open for 4% -> 4% of each run, Pallas kernels for 21% -> 10%
where the time goes in v5:
time: 172 us; the launch traced here: 170 us
  waiting for transfers between devices  55.8 us (32%)
  Pallas kernels  53.9 us (31%)
  starting transfers between devices  48.3 us (28%)
  other arithmetic  7.29 us (4%)
  local copies, waits for them, and re-layouts  4.29 us (2%)
    ppermute x24, waiting for transfers between devices, send(): return [lax.ppermute(v, 'dom', perm) for v, perm in zip(pair, perms)]  51.6 us
    ppermute x24, starting transfers between devices, send(): return [lax.ppermute(v, 'dom', perm) for v, perm in zip(pair, perms)]  38.1 us
    pallas_call x1, Pallas kernels, first_half(): pl.pallas_call(first_kernel, grid=(E_DEV // GROUP,), in_specs=[SMEM, pl.B...  32.8 us
    pallas_call x1, Pallas kernels, second_half(): pl.pallas_call(second_kernel, grid=(E_DEV // GROUP,), in_specs=[SMEM, VME...  17.7 us
    ppermute x4, starting transfers between devices, faces(): found += [lax.ppermute(last, axis, up), lax.ppermute(first, axis, down)]  10.2 us
    convert_element_type x12, other arithmetic, join(): return added(keep, arrived).astype(jnp.bfloat16)  4.79 us
    ppermute x4, waiting for transfers between devices, faces(): found += [lax.ppermute(last, axis, up), lax.ppermute(first, axis, down)]  4.25 us
    pallas_call x1, Pallas kernels, finish(): pl.pallas_call(finish_kernel, in_specs=[VMEM] * len(parts), out_specs=VME...  3.49 us
  transfers between devices with their start and end apart: 28, of which 16 were waited for; matrix products, arithmetic and copies ran while one was open for 4% of the time, Pallas kernels for 10%

profile of v5, /device:TPU:96, one launch (start us, length us, event | category | flops | bytes accessed | tf_op | source)
XLA Modules:
  0.0 170.1 jit_solution(12297492875035240621)
XLA Ops:
  0.0 1.1 slice_bitcast_fusion.8
  1.1 1.3 collective-permute-start.1
  2.4 4.6 %collective-permute-start = (bf16[32,4096]{1,0:T(8,128)(2,1)S(1)}, bf16[32,4096]{1,0:T(8,128)(2,1)S(1)}, u32[]{:S(2)}, u32[]{:S(2)}) collective-permute-start(bf16[32,4096]{1,0:T(8,128)(2,1)S(1)} %get-tuple-element.118), channel_id=1, source_target_pairs={{0,1},{1,2},{2,3},{3,4},{4,5},{5,6},{6,7},{7,8},{8,9},{9,10},{10,1... | collective-permute-start | bytes 786440 | tf_op jit(solution)/shard_map/ppermute | solution.py:360
  7.0 1.1 fusion.38
  8.0 1.9 %collective-permute-start.3 = (bf16[32,4096]{1,0:T(8,128)(2,1)S(1)}, bf16[32,4096]{1,0:T(8,128)(2,1)S(1)}, u32[]{:S(2)}, u32[]{:S(2)}) collective-permute-start(bf16[32,4096]{1,0:T(8,128)(2,1)S(1)} %get-tuple-element.115), channel_id=1, source_target_pairs={{16,0},{32,16},{48,32},{64,48},{80,64},{96,80},{112,96},{128,112},... | collective-permute-start | bytes 786440 | tf_op jit(solution)/shard_map/ppermute | solution.py:360
  10.0 2.4 %collective-permute-start.2 = (bf16[32,4096]{1,0:T(8,128)(2,1)S(1)}, bf16[32,4096]{1,0:T(8,128)(2,1)S(1)}, u32[]{:S(2)}, u32[]{:S(2)}) collective-permute-start(bf16[32,4096]{1,0:T(8,128)(2,1)S(1)} %get-tuple-element.116), channel_id=1, source_target_pairs={{0,16},{16,32},{32,48},{48,64},{64,80},{80,96},{96,112},{112,128},... | collective-permute-start | bytes 786440 | tf_op jit(solution)/shard_map/ppermute | solution.py:360
  12.8 0.6 fusion.26.target_ref
  13.8 3.8 %collective-permute-done.2.zm_ref = bf16[32,4096]{1,0:T(8,128)(2,1)S(1)} collective-permute-done((bf16[32,4096]{1,0:T(8,128)(2,1)S(1)}, bf16[32,4096]{1,0:T(8,128)(2,1)S(1)}, u32[]{:S(2)}, u32[]{:S(2)}) %collective-permute-start.2) | collective-permute-done | bytes 262176 | tf_op jit(solution)/shard_map/ppermute | solution.py:360
  17.7 0.7 copy-done.17
  18.4 32.8 %first_half.1 = (bf16[128,64,896]{2,1,0:T(8,128)(2,1)}, bf16[128,64,64]{2,1,0:T(8,128)(2,1)}, bf16[128,64,128]{2,1,0:T(8,128)(2,1)}, bf16[2,128,16,128]{3,2,1,0:...) custom-call(s32[896]{0:T(1024)} %fusion.26.target_ref, ...), custom_call_target="tpu_custom_call" | custom-call | flops 10000000000 | bytes 60000000 | tf_op jit(solution)/shard_map/first_half/pallas_call | solution.py:304
  51.1 1.6 collective-permute-start.4
  52.7 3.5 %collective-permute-start.5 = (bf16[2,128,16,128]{3,2,1,0:T(8,128)(2,1)}, bf16[2,128,16,128]{3,2,1,0:T(8,128)(2,1)S(1)}, u32[]{:S(2)}, u32[]{:S(2)}) collective-permute-start(bf16[2,128,16,128]{3,2,1,0:T(8,128)(2,1)} %get-tuple-element.51), channel_id=1, source_target_pairs={{0,3},{1,0},{2,1},{3,2},{4,7},{5,4},{6,5},{7,6},{8,11},{9,8},{10,9... | collective-permute-start | bytes 3145736 | tf_op jit(solution)/shard_map/ppermute | solution.py:405
  56.2 1.6 collective-permute-start.6
  57.7 1.7 collective-permute-start.7
  59.4 17.7 %second_half.1 = (bf16[2,128,16,128]{3,2,1,0:T(8,128)(2,1)S(1)}, bf16[2,128,16,128]{3,2,1,0:T(8,128)(2,1)S(1)}, bf16[1,128,16,128]{3,2,1,0:T(8,128)(2,1)S(1)}, b...) custom-call(s32[896]{0:T(1024)S(1)} %copy-done, ...), custom_call_target="tpu_custom_call" | custom-call | flops 10000000000 | bytes 60000000 | tf_op jit(solution)/shard_map/second_half/pallas_call | solution.py:337
  77.2 3.0 %collective-permute-done.4 = bf16[2,128,16,128]{3,2,1,0:T(8,128)(2,1)S(1)} collective-permute-done((bf16[2,128,16,128]{3,2,1,0:T(8,128)(2,1)}, bf16[2,128,16,128]{3,2,1,0:T(8,128)(2,1)S(1)}, u32[]{:S(2)}, u32[]{:S(2)}) %collective-permute-start.4) | collective-permute-done | bytes 1048608 | tf_op jit(solution)/shard_map/ppermute | solution.py:405
  80.2 2.1 %collective-permute-start.13 = (bf16[2,128,16,128]{3,2,1,0:T(8,128)(2,1)S(1)}, bf16[2,128,16,128]{3,2,1,0:T(8,128)(2,1)S(1)}, u32[]{:S(2)}, u32[]{:S(2)}) collective-permute-start(bf16[2,128,16,128]{3,2,1,0:T(8,128)(2,1)S(1)} %get-tuple-element.68), channel_id=1, source_target_pairs={{0,3},{1,0},{2,1},{3,2},{4,7},{5,4},{6,5},{7,6},{8,11},{9,8},{10,9... | collective-permute-start | bytes 3145736 | tf_op jit(solution)/shard_map/ppermute | solution.py:405
  82.3 1.6 collective-permute-start.14
  83.9 1.7 collective-permute-start.15
  85.7 0.7 collective-permute-start.11
  86.8 16.5 %collective-permute-done.12 = bf16[2,128,16,128]{3,2,1,0:T(8,128)(2,1)S(1)} collective-permute-done((bf16[2,128,16,128]{3,2,1,0:T(8,128)(2,1)S(1)}, bf16[2,128,16,128]{3,2,1,0:T(8,128)(2,1)S(1)}, u32[]{:S(2)}, u32[]{:S(2)}) %collective-permute-start.12) | collective-permute-done | bytes 1048608 | tf_op jit(solution)/shard_map/ppermute | solution.py:405
  103.4 1.0 collective-permute-start.10
  104.3 1.1 collective-permute-done.13
  105.5 2.8 %collective-permute-start.9 = (bf16[128,16,128]{2,1,0:T(8,128)(2,1)S(1)}, bf16[128,16,128]{2,1,0:T(8,128)(2,1)S(1)}, u32[]{:S(2)}, u32[]{:S(2)}) collective-permute-start(bf16[128,16,128]{2,1,0:T(8,128)(2,1)S(1)} %fusion.1), channel_id=1, source_target_pairs={{0,3},{1,0},{2,1},{3,2},{4,7},{5,4},{6,5},{7,6},{8,11},{9,8},{10,9... | collective-permute-start | bytes 1572872 | tf_op jit(solution)/shard_map/ppermute | solution.py:405
  108.3 1.5 collective-permute-done.14
  110.4 2.9 %collective-permute-start.19 = (bf16[128,16,128]{2,1,0:T(8,128)(2,1)S(1)}, bf16[128,16,128]{2,1,0:T(8,128)(2,1)S(1)}, u32[]{:S(2)}, u32[]{:S(2)}) collective-permute-start(bf16[128,16,128]{2,1,0:T(8,128)(2,1)S(1)} %fusion.7), channel_id=1, source_target_pairs={{0,12},{1,13},{2,14},{3,15},{4,0},{5,1},{6,2},{7,3},{8,4},{9,5},{1... | collective-permute-start | bytes 1572872 | tf_op jit(solution)/shard_map/ppermute | solution.py:405
  113.7 7.7 %collective-permute-done.11 = bf16[128,16,128]{2,1,0:T(8,128)(2,1)S(1)} collective-permute-done((bf16[128,16,128]{2,1,0:T(8,128)(2,1)S(1)}, bf16[128,16,128]{2,1,0:T(8,128)(2,1)S(1)}, u32[]{:S(2)}, u32[]{:S(2)}) %collective-permute-start.11) | collective-permute-done | bytes 524320 | tf_op jit(solution)/shard_map/ppermute | solution.py:405
  121.4 1.6 collective-permute-start.18
  123.0 1.1 collective-permute-start.17
  124.1 1.0 collective-permute-start.16
  125.1 0.8 fusion.30
  126.2 4.6 %collective-permute-done.19 = bf16[128,16,128]{2,1,0:T(8,128)(2,1)S(1)} collective-permute-done((bf16[128,16,128]{2,1,0:T(8,128)(2,1)S(1)}, bf16[128,16,128]{2,1,0:T(8,128)(2,1)S(1)}, u32[]{:S(2)}, u32[]{:S(2)}) %collective-permute-start.19) | collective-permute-done | bytes 524320 | tf_op jit(solution)/shard_map/ppermute | solution.py:405
  130.8 2.0 %collective-permute-done.18 = bf16[128,16,128]{2,1,0:T(8,128)(2,1)S(1)} collective-permute-done((bf16[128,16,128]{2,1,0:T(8,128)(2,1)S(1)}, bf16[128,16,128]{2,1,0:T(8,128)(2,1)S(1)}, u32[]{:S(2)}, u32[]{:S(2)}) %collective-permute-start.18) | collective-permute-done | bytes 524320 | tf_op jit(solution)/shard_map/ppermute | solution.py:405
  132.9 3.0 %collective-permute-done.16 = bf16[128,16,128]{2,1,0:T(8,128)(2,1)S(1)} collective-permute-done((bf16[128,16,128]{2,1,0:T(8,128)(2,1)S(1)}, bf16[128,16,128]{2,1,0:T(8,128)(2,1)S(1)}, u32[]{:S(2)}, u32[]{:S(2)}) %collective-permute-start.16) | collective-permute-done | bytes 524320 | tf_op jit(solution)/shard_map/ppermute | solution.py:405
  135.9 0.8 fusion.31
  137.5 3.2 %collective-permute-start.21 = (bf16[2,2,32,16,128]{4,3,2,1,0:T(8,128)(2,1)S(1)}, bf16[2,2,32,16,128]{4,3,2,1,0:T(8,128)(2,1)S(1)}, u32[]{:S(2)}, u32[]{:S(2)}) collective-permute-start(bf16[2,2,32,16,128]{4,3,2,1,0:T(8,128)(2,1)S(1)} %maximum_maximum_fusion.1), channel_id=1, source_target_pairs={{0,12},{1,13},{2,14},{3,15},{4,0},{5,1},{6,2},{7,3},{8,4},{9,5},{1... | collective-permute-start | bytes 1572872 | tf_op jit(solution)/shard_map/ppermute | solution.py:405
  140.9 3.3 %collective-permute-start.23 = (bf16[2,2,32,16,128]{4,3,2,1,0:T(8,128)(2,1)S(1)}, bf16[2,2,32,16,128]{4,3,2,1,0:T(8,128)(2,1)S(1)}, u32[]{:S(2)}, u32[]{:S(2)}) collective-permute-start(bf16[2,2,32,16,128]{4,3,2,1,0:T(8,128)(2,1)S(1)} %maximum_maximum_fusion.3), channel_id=1, source_target_pairs={{0,3},{1,0},{2,1},{3,2},{4,7},{5,4},{6,5},{7,6},{8,11},{9,8},{10,9... | collective-permute-start | bytes 1572872 | tf_op jit(solution)/shard_map/ppermute | solution.py:405
  144.2 3.7 %collective-permute-done.20 = bf16[2,2,32,16,128]{4,3,2,1,0:T(8,128)(2,1)S(1)} collective-permute-done((bf16[2,2,32,16,128]{4,3,2,1,0:T(8,128)(2,1)S(1)}, bf16[2,2,32,16,128]{4,3,2,1,0:T(8,128)(2,1)S(1)}, u32[]{:S(2)}, u32[]{:S(2)}) %collective-permute-start.20) | collective-permute-done | bytes 524320 | tf_op jit(solution)/shard_map/ppermute | solution.py:405
  148.0 3.9 %collective-permute-done.22 = bf16[2,2,32,16,128]{4,3,2,1,0:T(8,128)(2,1)S(1)} collective-permute-done((bf16[2,2,32,16,128]{4,3,2,1,0:T(8,128)(2,1)S(1)}, bf16[2,2,32,16,128]{4,3,2,1,0:T(8,128)(2,1)S(1)}, u32[]{:S(2)}, u32[]{:S(2)}) %collective-permute-start.22) | collective-permute-done | bytes 524320 | tf_op jit(solution)/shard_map/ppermute | solution.py:405
  151.9 0.9 fusion.9
  152.8 0.9 fusion.8
  153.7 3.2 %collective-permute-start.27 = (bf16[2,32,16,128]{3,2,1,0:T(8,128)(2,1)S(1)}, bf16[2,32,16,128]{3,2,1,0:T(8,128)(2,1)S(1)}, u32[]{:S(2)}, u32[]{:S(2)}) collective-permute-start(bf16[2,32,16,128]{3,2,1,0:T(8,128)(2,1)S(1)} %get-tuple-element.119), channel_id=1, source_target_pairs={{0,3},{1,0},{2,1},{3,2},{4,7},{5,4},{6,5},{7,6},{8,11},{9,8},{10,9... | collective-permute-start | bytes 786440 | tf_op jit(solution)/shard_map/ppermute | solution.py:405
  156.9 0.9 fusion.11
  157.9 0.9 fusion.10
  158.8 3.2 %collective-permute-start.25 = (bf16[2,32,16,128]{3,2,1,0:T(8,128)(2,1)S(1)}, bf16[2,32,16,128]{3,2,1,0:T(8,128)(2,1)S(1)}, u32[]{:S(2)}, u32[]{:S(2)}) collective-permute-start(bf16[2,32,16,128]{3,2,1,0:T(8,128)(2,1)S(1)} %get-tuple-element.135), channel_id=1, source_target_pairs={{0,12},{1,13},{2,14},{3,15},{4,0},{5,1},{6,2},{7,3},{8,4},{9,5},{1... | collective-permute-start | bytes 786440 | tf_op jit(solution)/shard_map/ppermute | solution.py:405
  162.0 3.4 %collective-permute-done.24.refs_2_ = bf16[2,32,16,128]{3,2,1,0:T(8,128)(2,1)S(1)} collective-permute-done((bf16[2,32,16,128]{3,2,1,0:T(8,128)(2,1)S(1)}, bf16[2,32,16,128]{3,2,1,0:T(8,128)(2,1)S(1)}, u32[]{:S(2)}, u32[]{:S(2)}) %collective-permute-start.24) | collective-permute-done | bytes 262176 | tf_op jit(solution)/shard_map/ppermute | solution.py:405
  165.4 0.5 collective-permute-done.25.refs_3_
  166.6 3.5 %finish.1 = f32[128,4096]{1,0:T(8,128)} custom-call(f32[2,32,16,128]{3,2,1,0:T(8,128)} %get-tuple-element.136.refs_0_, f32[2,32,16,128]{3,2,1,0:T(8,128)} %get-tuple-element.144.refs_1_, bf16[2,32,16,128]{3,2,1,0:T(8,128)(2,1)} %copy-done.10, bf16[2,32,16,128]{3,2,1,0:T(8,128)(2,1)} %copy-done.11, f32[2,32,16,128]{3,2,1,0:T(8,128)} %get-tuple-element.120.refs_4_, ...), custom_call_target="tpu_custom_call" | custom-call | tf_op jit(solution)/shard_map/finish/pallas_call | solution.py:456
  (87 shorter events, 4.3 us)
Async XLA Ops:
  0.0 12.4 %copy-start.13 = (s32[896,1]{0,1:T(1,128)S(1)}, s32[896,1]{0,1:T(1,128)}, u32[]{:S(2)}) copy-start(s32[896,1]{0,1:T(1,128)} %param.6) | copy-start | bytes 10756
  0.0 12.4 %copy-start.12 = (s32[128,7]{0,1:T(8,128)S(1)}, s32[128,7]{0,1:T(8,128)}, u32[]{:S(2)}) copy-start(s32[128,7]{0,1:T(8,128)} %param.7) | copy-start | bytes 10756
  1.1 12.3 %collective-permute-start.1 = (bf16[32,4096]{1,0:T(8,128)(2,1)S(1)}, bf16[32,4096]{1,0:T(8,128)(2,1)S(1)}, u32[]{:S(2)}, u32[]{:S(2)}) collective-permute-start(bf16[32,4096]{1,0:T(8,128)(2,1)S(1)} %get-tuple-element.117), channel_id=1, source_target_pairs={{1,0},{2,1},{3,2},{4,3},{5,4},{6,5},{7,6},{8,7},{9,8},{10,9},{11,1... | collective-permute-start | bytes 786440 | tf_op jit(solution)/shard_map/ppermute | solution.py:360
  2.4 11.0 %collective-permute-start = (bf16[32,4096]{1,0:T(8,128)(2,1)S(1)}, bf16[32,4096]{1,0:T(8,128)(2,1)S(1)}, u32[]{:S(2)}, u32[]{:S(2)}) collective-permute-start(bf16[32,4096]{1,0:T(8,128)(2,1)S(1)} %get-tuple-element.118), channel_id=1, source_target_pairs={{0,1},{1,2},{2,3},{3,4},{4,5},{5,6},{6,7},{7,8},{8,9},{9,10},{10,1... | collective-permute-start | bytes 786440 | tf_op jit(solution)/shard_map/ppermute | solution.py:360
  8.0 5.8 %collective-permute-start.3 = (bf16[32,4096]{1,0:T(8,128)(2,1)S(1)}, bf16[32,4096]{1,0:T(8,128)(2,1)S(1)}, u32[]{:S(2)}, u32[]{:S(2)}) collective-permute-start(bf16[32,4096]{1,0:T(8,128)(2,1)S(1)} %get-tuple-element.115), channel_id=1, source_target_pairs={{16,0},{32,16},{48,32},{64,48},{80,64},{96,80},{112,96},{128,112},... | collective-permute-start | bytes 786440 | tf_op jit(solution)/shard_map/ppermute | solution.py:360
  10.0 7.7 %collective-permute-start.2 = (bf16[32,4096]{1,0:T(8,128)(2,1)S(1)}, bf16[32,4096]{1,0:T(8,128)(2,1)S(1)}, u32[]{:S(2)}, u32[]{:S(2)}) collective-permute-start(bf16[32,4096]{1,0:T(8,128)(2,1)S(1)} %get-tuple-element.116), channel_id=1, source_target_pairs={{0,16},{16,32},{32,48},{48,64},{64,80},{80,96},{96,112},{112,128},... | collective-permute-start | bytes 786440 | tf_op jit(solution)/shard_map/ppermute | solution.py:360
  13.4 4.3 %copy-start.14 = (bf16[32,4096]{1,0:T(8,128)(2,1)}, bf16[32,4096]{1,0:T(8,128)(2,1)S(1)}, u32[]{:S(2)}) copy-start(bf16[32,4096]{1,0:T(8,128)(2,1)S(1)} %collective-permute-done.1.yp_ref) | copy-start | bytes 786436
  13.4 4.3 %copy-start.15 = (bf16[32,4096]{1,0:T(8,128)(2,1)}, bf16[32,4096]{1,0:T(8,128)(2,1)S(1)}, u32[]{:S(2)}) copy-start(bf16[32,4096]{1,0:T(8,128)(2,1)S(1)} %collective-permute-done.ym_ref) | copy-start | bytes 786436
  13.8 3.8 %copy-start.16 = (bf16[32,4096]{1,0:T(8,128)(2,1)}, bf16[32,4096]{1,0:T(8,128)(2,1)S(1)}, u32[]{:S(2)}) copy-start(bf16[32,4096]{1,0:T(8,128)(2,1)S(1)} %collective-permute-done.3.zp_ref) | copy-start | bytes 786436
  17.7 0.7 copy-start.17
  18.4 41.0 %copy-start = (s32[896]{0:T(1024)S(1)}, s32[896]{0:T(1024)}, u32[]{:S(2)}) copy-start(s32[896]{0:T(1024)} %fusion.26.target_ref) | copy-start | bytes 10756
  51.1 29.1 %collective-permute-start.4 = (bf16[2,128,16,128]{3,2,1,0:T(8,128)(2,1)}, bf16[2,128,16,128]{3,2,1,0:T(8,128)(2,1)S(1)}, u32[]{:S(2)}, u32[]{:S(2)}) collective-permute-start(bf16[2,128,16,128]{3,2,1,0:T(8,128)(2,1)} %get-tuple-element.50), channel_id=1, source_target_pairs={{0,1},{1,2},{2,3},{3,0},{4,5},{5,6},{6,7},{7,4},{8,9},{9,10},{10,1... | collective-permute-start | bytes 3145736 | tf_op jit(solution)/shard_map/ppermute | solution.py:405
  52.7 29.6 %collective-permute-start.5 = (bf16[2,128,16,128]{3,2,1,0:T(8,128)(2,1)}, bf16[2,128,16,128]{3,2,1,0:T(8,128)(2,1)S(1)}, u32[]{:S(2)}, u32[]{:S(2)}) collective-permute-start(bf16[2,128,16,128]{3,2,1,0:T(8,128)(2,1)} %get-tuple-element.51), channel_id=1, source_target_pairs={{0,3},{1,0},{2,1},{3,2},{4,7},{5,4},{6,5},{7,6},{8,11},{9,8},{10,9... | collective-permute-start | bytes 3145736 | tf_op jit(solution)/shard_map/ppermute | solution.py:405
  56.2 27.7 %collective-permute-start.6 = (bf16[2,128,16,128]{3,2,1,0:T(8,128)(2,1)}, bf16[2,128,16,128]{3,2,1,0:T(8,128)(2,1)S(1)}, u32[]{:S(2)}, u32[]{:S(2)}) collective-permute-start(bf16[2,128,16,128]{3,2,1,0:T(8,128)(2,1)} %get-tuple-element.52), channel_id=1, source_target_pairs={{0,4},{1,5},{2,6},{3,7},{4,8},{5,9},{6,10},{7,11},{8,12},{9,13},{1... | collective-permute-start | bytes 3145736 | tf_op jit(solution)/shard_map/ppermute | solution.py:405
  57.7 27.8 %collective-permute-start.7 = (bf16[2,128,16,128]{3,2,1,0:T(8,128)(2,1)}, bf16[2,128,16,128]{3,2,1,0:T(8,128)(2,1)S(1)}, u32[]{:S(2)}, u32[]{:S(2)}) collective-permute-start(bf16[2,128,16,128]{3,2,1,0:T(8,128)(2,1)} %get-tuple-element.53), channel_id=1, source_target_pairs={{0,12},{1,13},{2,14},{3,15},{4,0},{5,1},{6,2},{7,3},{8,4},{9,5},{1... | collective-permute-start | bytes 3145736 | tf_op jit(solution)/shard_map/ppermute | solution.py:405
  59.4 26.2 %copy-start.7 = (bf16[1,128,16,128]{3,2,1,0:T(8,128)(2,1)S(1)}, bf16[1,128,16,128]{3,2,1,0:T(8,128)(2,1)}, u32[]{:S(2)}) copy-start(bf16[1,128,16,128]{3,2,1,0:T(8,128)(2,1)} %get-tuple-element.59) | copy-start | bytes 1572868
  59.4 27.0 %copy-start.6 = (bf16[1,128,16,128]{3,2,1,0:T(8,128)(2,1)S(1)}, bf16[1,128,16,128]{3,2,1,0:T(8,128)(2,1)}, u32[]{:S(2)}) copy-start(bf16[1,128,16,128]{3,2,1,0:T(8,128)(2,1)} %get-tuple-element.49) | copy-start | bytes 1572868
  77.1 9.4 %copy-start.5 = (bf16[1,128,16,128]{3,2,1,0:T(8,128)(2,1)S(1)}, bf16[1,128,16,128]{3,2,1,0:T(8,128)(2,1)}, u32[]{:S(2)}) copy-start(bf16[1,128,16,128]{3,2,1,0:T(8,128)(2,1)} %get-tuple-element.55) | copy-start | bytes 1572868
  77.1 26.3 %collective-permute-start.12 = (bf16[2,128,16,128]{3,2,1,0:T(8,128)(2,1)S(1)}, bf16[2,128,16,128]{3,2,1,0:T(8,128)(2,1)S(1)}, u32[]{:S(2)}, u32[]{:S(2)}) collective-permute-start(bf16[2,128,16,128]{3,2,1,0:T(8,128)(2,1)S(1)} %get-tuple-element.67), channel_id=1, source_target_pairs={{0,1},{1,2},{2,3},{3,0},{4,5},{5,6},{6,7},{7,4},{8,9},{9,10},{10,1... | collective-permute-start | bytes 3145736 | tf_op jit(solution)/shard_map/ppermute | solution.py:405
  80.2 25.3 %collective-permute-start.13 = (bf16[2,128,16,128]{3,2,1,0:T(8,128)(2,1)S(1)}, bf16[2,128,16,128]{3,2,1,0:T(8,128)(2,1)S(1)}, u32[]{:S(2)}, u32[]{:S(2)}) collective-permute-start(bf16[2,128,16,128]{3,2,1,0:T(8,128)(2,1)S(1)} %get-tuple-element.68), channel_id=1, source_target_pairs={{0,3},{1,0},{2,1},{3,2},{4,7},{5,4},{6,5},{7,6},{8,11},{9,8},{10,9... | collective-permute-start | bytes 3145736 | tf_op jit(solution)/shard_map/ppermute | solution.py:405
  82.3 27.5 %collective-permute-start.14 = (bf16[2,128,16,128]{3,2,1,0:T(8,128)(2,1)}, bf16[2,128,16,128]{3,2,1,0:T(8,128)(2,1)S(1)}, u32[]{:S(2)}, u32[]{:S(2)}) collective-permute-start(bf16[2,128,16,128]{3,2,1,0:T(8,128)(2,1)} %get-tuple-element.69), channel_id=1, source_target_pairs={{0,4},{1,5},{2,6},{3,7},{4,8},{5,9},{6,10},{7,11},{8,12},{9,13},{1... | collective-permute-start | bytes 3145736 | tf_op jit(solution)/shard_map/ppermute | solution.py:405
  83.9 26.3 %collective-permute-start.15 = (bf16[2,128,16,128]{3,2,1,0:T(8,128)(2,1)}, bf16[2,128,16,128]{3,2,1,0:T(8,128)(2,1)S(1)}, u32[]{:S(2)}, u32[]{:S(2)}) collective-permute-start(bf16[2,128,16,128]{3,2,1,0:T(8,128)(2,1)} %get-tuple-element.70), channel_id=1, source_target_pairs={{0,12},{1,13},{2,14},{3,15},{4,0},{5,1},{6,2},{7,3},{8,4},{9,5},{1... | collective-permute-start | bytes 3145736 | tf_op jit(solution)/shard_map/ppermute | solution.py:405
  85.6 1.1 copy-start.4
  85.7 35.7 %collective-permute-start.11 = (bf16[128,16,128]{2,1,0:T(8,128)(2,1)S(1)}, bf16[128,16,128]{2,1,0:T(8,128)(2,1)S(1)}, u32[]{:S(2)}, u32[]{:S(2)}) collective-permute-start(bf16[128,16,128]{2,1,0:T(8,128)(2,1)S(1)} %fusion.3), channel_id=1, source_target_pairs={{0,12},{1,13},{2,14},{3,15},{4,0},{5,1},{6,2},{7,3},{8,4},{9,5},{1... | collective-permute-start | bytes 1572872 | tf_op jit(solution)/shard_map/ppermute | solution.py:405
  103.4 19.6 %collective-permute-start.10 = (bf16[128,16,128]{2,1,0:T(8,128)(2,1)S(1)}, bf16[128,16,128]{2,1,0:T(8,128)(2,1)S(1)}, u32[]{:S(2)}, u32[]{:S(2)}) collective-permute-start(bf16[128,16,128]{2,1,0:T(8,128)(2,1)S(1)} %fusion.2), channel_id=1, source_target_pairs={{0,4},{1,5},{2,6},{3,7},{4,8},{5,9},{6,10},{7,11},{8,12},{9,13},{1... | collective-permute-start | bytes 1572872 | tf_op jit(solution)/shard_map/ppermute | solution.py:405
  105.5 18.6 %collective-permute-start.9 = (bf16[128,16,128]{2,1,0:T(8,128)(2,1)S(1)}, bf16[128,16,128]{2,1,0:T(8,128)(2,1)S(1)}, u32[]{:S(2)}, u32[]{:S(2)}) collective-permute-start(bf16[128,16,128]{2,1,0:T(8,128)(2,1)S(1)} %fusion.1), channel_id=1, source_target_pairs={{0,3},{1,0},{2,1},{3,2},{4,7},{5,4},{6,5},{7,6},{8,11},{9,8},{10,9... | collective-permute-start | bytes 1572872 | tf_op jit(solution)/shard_map/ppermute | solution.py:405
  109.8 15.2 %collective-permute-start.8 = (bf16[128,16,128]{2,1,0:T(8,128)(2,1)S(1)}, bf16[128,16,128]{2,1,0:T(8,128)(2,1)S(1)}, u32[]{:S(2)}, u32[]{:S(2)}) collective-permute-start(bf16[128,16,128]{2,1,0:T(8,128)(2,1)S(1)} %fusion), channel_id=1, source_target_pairs={{0,1},{1,2},{2,3},{3,0},{4,5},{5,6},{6,7},{7,4},{8,9},{9,10},{10,1... | collective-permute-start | bytes 1572872 | tf_op jit(solution)/shard_map/ppermute | solution.py:405
  110.4 20.4 %collective-permute-start.19 = (bf16[128,16,128]{2,1,0:T(8,128)(2,1)S(1)}, bf16[128,16,128]{2,1,0:T(8,128)(2,1)S(1)}, u32[]{:S(2)}, u32[]{:S(2)}) collective-permute-start(bf16[128,16,128]{2,1,0:T(8,128)(2,1)S(1)} %fusion.7), channel_id=1, source_target_pairs={{0,12},{1,13},{2,14},{3,15},{4,0},{5,1},{6,2},{7,3},{8,4},{9,5},{1... | collective-permute-start | bytes 1572872 | tf_op jit(solution)/shard_map/ppermute | solution.py:405
  113.3 11.8 %copy-start.2 = (bf16[2,128,16,128]{3,2,1,0:T(8,128)(2,1)S(1)}, bf16[2,128,16,128]{3,2,1,0:T(8,128)(2,1)}, u32[]{:S(2)}) copy-start(bf16[2,128,16,128]{3,2,1,0:T(8,128)(2,1)} %get-tuple-element.48) | copy-start | bytes 3145732
  113.3 11.8 %copy-start.3 = (bf16[2,128,16,128]{3,2,1,0:T(8,128)(2,1)S(1)}, bf16[2,128,16,128]{3,2,1,0:T(8,128)(2,1)}, u32[]{:S(2)}) copy-start(bf16[2,128,16,128]{3,2,1,0:T(8,128)(2,1)} %get-tuple-element.81) | copy-start | bytes 3145732
  121.4 11.4 %collective-permute-start.18 = (bf16[128,16,128]{2,1,0:T(8,128)(2,1)S(1)}, bf16[128,16,128]{2,1,0:T(8,128)(2,1)S(1)}, u32[]{:S(2)}, u32[]{:S(2)}) collective-permute-start(bf16[128,16,128]{2,1,0:T(8,128)(2,1)S(1)} %fusion.6), channel_id=1, source_target_pairs={{0,4},{1,5},{2,6},{3,7},{4,8},{5,9},{6,10},{7,11},{8,12},{9,13},{1... | collective-permute-start | bytes 1572872 | tf_op jit(solution)/shard_map/ppermute | solution.py:405
  123.0 9.9 %collective-permute-start.17 = (bf16[128,16,128]{2,1,0:T(8,128)(2,1)S(1)}, bf16[128,16,128]{2,1,0:T(8,128)(2,1)S(1)}, u32[]{:S(2)}, u32[]{:S(2)}) collective-permute-start(bf16[128,16,128]{2,1,0:T(8,128)(2,1)S(1)} %fusion.5), channel_id=1, source_target_pairs={{0,3},{1,0},{2,1},{3,2},{4,7},{5,4},{6,5},{7,6},{8,11},{9,8},{10,9... | collective-permute-start | bytes 1572872 | tf_op jit(solution)/shard_map/ppermute | solution.py:405
  124.1 11.8 %collective-permute-start.16 = (bf16[128,16,128]{2,1,0:T(8,128)(2,1)S(1)}, bf16[128,16,128]{2,1,0:T(8,128)(2,1)S(1)}, u32[]{:S(2)}, u32[]{:S(2)}) collective-permute-start(bf16[128,16,128]{2,1,0:T(8,128)(2,1)S(1)} %fusion.4), channel_id=1, source_target_pairs={{0,1},{1,2},{2,3},{3,0},{4,5},{5,6},{6,7},{7,4},{8,9},{9,10},{10,1... | collective-permute-start | bytes 1572872 | tf_op jit(solution)/shard_map/ppermute | solution.py:405
  126.0 10.0 %copy-start.1 = (bf16[2,128,16,128]{3,2,1,0:T(8,128)(2,1)S(1)}, bf16[2,128,16,128]{3,2,1,0:T(8,128)(2,1)}, u32[]{:S(2)}) copy-start(bf16[2,128,16,128]{3,2,1,0:T(8,128)(2,1)} %get-tuple-element.83) | copy-start | bytes 3145732
  137.0 11.0 %collective-permute-start.20 = (bf16[2,2,32,16,128]{4,3,2,1,0:T(8,128)(2,1)S(1)}, bf16[2,2,32,16,128]{4,3,2,1,0:T(8,128)(2,1)S(1)}, u32[]{:S(2)}, u32[]{:S(2)}) collective-permute-start(bf16[2,2,32,16,128]{4,3,2,1,0:T(8,128)(2,1)S(1)} %maximum_maximum_fusion), channel_id=1, source_target_pairs={{0,4},{1,5},{2,6},{3,7},{4,8},{5,9},{6,10},{7,11},{8,12},{9,13},{1... | collective-permute-start | bytes 1572872 | tf_op jit(solution)/shard_map/ppermute | solution.py:405
  137.5 10.5 %collective-permute-start.21 = (bf16[2,2,32,16,128]{4,3,2,1,0:T(8,128)(2,1)S(1)}, bf16[2,2,32,16,128]{4,3,2,1,0:T(8,128)(2,1)S(1)}, u32[]{:S(2)}, u32[]{:S(2)}) collective-permute-start(bf16[2,2,32,16,128]{4,3,2,1,0:T(8,128)(2,1)S(1)} %maximum_maximum_fusion.1), channel_id=1, source_target_pairs={{0,12},{1,13},{2,14},{3,15},{4,0},{5,1},{6,2},{7,3},{8,4},{9,5},{1... | collective-permute-start | bytes 1572872 | tf_op jit(solution)/shard_map/ppermute | solution.py:405
  140.7 11.2 %collective-permute-start.22 = (bf16[2,2,32,16,128]{4,3,2,1,0:T(8,128)(2,1)S(1)}, bf16[2,2,32,16,128]{4,3,2,1,0:T(8,128)(2,1)S(1)}, u32[]{:S(2)}, u32[]{:S(2)}) collective-permute-start(bf16[2,2,32,16,128]{4,3,2,1,0:T(8,128)(2,1)S(1)} %maximum_maximum_fusion.2), channel_id=1, source_target_pairs={{0,1},{1,2},{2,3},{3,0},{4,5},{5,6},{6,7},{7,4},{8,9},{9,10},{10,1... | collective-permute-start | bytes 1572872 | tf_op jit(solution)/shard_map/ppermute | solution.py:405
  140.9 11.0 %collective-permute-start.23 = (bf16[2,2,32,16,128]{4,3,2,1,0:T(8,128)(2,1)S(1)}, bf16[2,2,32,16,128]{4,3,2,1,0:T(8,128)(2,1)S(1)}, u32[]{:S(2)}, u32[]{:S(2)}) collective-permute-start(bf16[2,2,32,16,128]{4,3,2,1,0:T(8,128)(2,1)S(1)} %maximum_maximum_fusion.3), channel_id=1, source_target_pairs={{0,3},{1,0},{2,1},{3,2},{4,7},{5,4},{6,5},{7,6},{8,11},{9,8},{10,9... | collective-permute-start | bytes 1572872 | tf_op jit(solution)/shard_map/ppermute | solution.py:405
  152.8 9.2 %collective-permute-start.26 = (bf16[2,32,16,128]{3,2,1,0:T(8,128)(2,1)S(1)}, bf16[2,32,16,128]{3,2,1,0:T(8,128)(2,1)S(1)}, u32[]{:S(2)}, u32[]{:S(2)}) collective-permute-start(bf16[2,32,16,128]{3,2,1,0:T(8,128)(2,1)S(1)} %get-tuple-element.127), channel_id=1, source_target_pairs={{0,1},{1,2},{2,3},{3,0},{4,5},{5,6},{6,7},{7,4},{8,9},{9,10},{10,1... | collective-permute-start | bytes 786440 | tf_op jit(solution)/shard_map/ppermute | solution.py:405
  153.7 8.3 %collective-permute-start.27 = (bf16[2,32,16,128]{3,2,1,0:T(8,128)(2,1)S(1)}, bf16[2,32,16,128]{3,2,1,0:T(8,128)(2,1)S(1)}, u32[]{:S(2)}, u32[]{:S(2)}) collective-permute-start(bf16[2,32,16,128]{3,2,1,0:T(8,128)(2,1)S(1)} %get-tuple-element.119), channel_id=1, source_target_pairs={{0,3},{1,0},{2,1},{3,2},{4,7},{5,4},{6,5},{7,6},{8,11},{9,8},{10,9... | collective-permute-start | bytes 786440 | tf_op jit(solution)/shard_map/ppermute | solution.py:405
  157.9 7.6 %collective-permute-start.24 = (bf16[2,32,16,128]{3,2,1,0:T(8,128)(2,1)S(1)}, bf16[2,32,16,128]{3,2,1,0:T(8,128)(2,1)S(1)}, u32[]{:S(2)}, u32[]{:S(2)}) collective-permute-start(bf16[2,32,16,128]{3,2,1,0:T(8,128)(2,1)S(1)} %get-tuple-element.143), channel_id=1, source_target_pairs={{0,4},{1,5},{2,6},{3,7},{4,8},{5,9},{6,10},{7,11},{8,12},{9,13},{1... | collective-permute-start | bytes 786440 | tf_op jit(solution)/shard_map/ppermute | solution.py:405
  158.8 7.1 %collective-permute-start.25 = (bf16[2,32,16,128]{3,2,1,0:T(8,128)(2,1)S(1)}, bf16[2,32,16,128]{3,2,1,0:T(8,128)(2,1)S(1)}, u32[]{:S(2)}, u32[]{:S(2)}) collective-permute-start(bf16[2,32,16,128]{3,2,1,0:T(8,128)(2,1)S(1)} %get-tuple-element.135), channel_id=1, source_target_pairs={{0,12},{1,13},{2,14},{3,15},{4,0},{5,1},{6,2},{7,3},{8,4},{9,5},{1... | collective-permute-start | bytes 786440 | tf_op jit(solution)/shard_map/ppermute | solution.py:405
  162.0 3.9 %copy-start.8 = (bf16[2,32,16,128]{3,2,1,0:T(8,128)(2,1)}, bf16[2,32,16,128]{3,2,1,0:T(8,128)(2,1)S(1)}, u32[]{:S(2)}) copy-start(bf16[2,32,16,128]{3,2,1,0:T(8,128)(2,1)S(1)} %collective-permute-done.26.refs_6_) | copy-start | bytes 786436
  162.0 3.9 %copy-start.9 = (bf16[2,32,16,128]{3,2,1,0:T(8,128)(2,1)}, bf16[2,32,16,128]{3,2,1,0:T(8,128)(2,1)S(1)}, u32[]{:S(2)}) copy-start(bf16[2,32,16,128]{3,2,1,0:T(8,128)(2,1)S(1)} %collective-permute-done.27.refs_7_) | copy-start | bytes 786436
  165.4 0.7 copy-start.10
  165.9 0.7 copy-start.11

commit v6 on v5

--- a/solution.py
+++ b/solution.py
@@ -25,7 +25,7 @@
 SLOT = SIDE * PART
 SLOTS = OWNERS * CB_DEV // SLOT
 BUFFERS = 4
-SLOT_OF = 0x53201476
+SLOT_OF = 0x35204176
 
 
 def spread_rows(flat, scratch, base):
@@ -87,9 +87,9 @@
             weights[slot0 + i + j, BLOCK:, 128:] = at_low
 
 
-def first_kernel(target_ref, a_ref, p_ref, ym_ref, yp_ref, zm_ref, zp_ref, *refs):
-    q_out, left_out, qh_out, *outs = refs[:13]
-    acc, stage, drain_sems, couples, q, rows, weights, left_ref, qh_ref, sems = refs[13:]
+def first_kernel(target_ref, odd_ref, a_ref, p_ref, *refs):
+    halos, (q_out, left_out, qh_out), outs = refs[:4], refs[4:7], refs[7:17]
+    acc, stage, drain_sems, couples, q, rows, weights, left_ref, qh_ref, sems = refs[17:]
     step = pl.program_id(0)
 
     @pl.when(step == 0)
@@ -158,7 +158,9 @@
         for n in range(E_DEV // GROUP - behind, E_DEV // GROUP):
             copy(n).start()
 
-        for f, ref in enumerate((ym_ref, yp_ref, zm_ref, zp_ref)):
+        dom_odd, slab_odd = odd_ref[0], odd_ref[1]
+        sides = (1 - dom_odd, dom_odd, 3 - slab_odd, 2 + slab_odd)
+        for f, ref in zip(sides, halos):
             for g in range(FACE // GROUP):
                 spread_weights(ref, g * GROUP, rows, weights, f * FACE + g * GROUP, None)
 
@@ -300,11 +302,12 @@
     return pl.CostEstimate(flops=10**10, bytes_accessed=megabytes * 10**6, transcendentals=0)
 
 
-def first_half(target, a, p, halos):
+def first_half(target, odd, a, p, halos):
     found = pl.pallas_call(
         first_kernel,
         grid=(E_DEV // GROUP,),
         in_specs=[
+            SMEM,
             SMEM,
             pl.BlockSpec((PAIRS, GROUP, SQUARE), lambda i: (0, i, 0)),
             VMEM, VMEM, VMEM, VMEM, VMEM,
@@ -329,7 +332,7 @@
         compiler_params=params(62),
         cost_estimate=cost(60),
         name="first_half",
-    )(target, a, p, *halos)
+    )(target, odd, a, p, *halos)
     return found[0], found[1], found[2], found[3:]
 
 
@@ -352,38 +355,36 @@
     found = []
     for axis, dim in (("dom", 1), ("slab", 0)):
         size = lax.axis_size(axis)
-        up = [(i, i + 1) for i in range(size - 1)]
-        down = [(j, i) for i, j in up]
+        even = lax.axis_index(axis) % 2 == 0
         length = brick.shape[dim]
         last = lax.slice_in_dim(brick, length - 1, length, axis=dim).reshape(FACE, SQUARE)
         first = lax.slice_in_dim(brick, 0, 1, axis=dim).reshape(FACE, SQUARE)
-        found += [lax.ppermute(last, axis, up), lax.ppermute(first, axis, down)]
+        near = [(i, i ^ 1) for i in range(size)]
+        far = [(i, (i + 1 ^ 1) - 1) for i in range(1, size - 1)]
+        found.append(lax.ppermute(jnp.where(even, last, first), axis, near))
+        found.append(lax.ppermute(jnp.where(even, first, last), axis, far))
     return found
 
 
 def sum_places(dest_rank, dest_block):
     me = lax.axis_index("dom")
-    rank = dest_rank.reshape(-1)
+    away = dest_rank.reshape(-1) ^ me
     block = dest_block.reshape(-1)
-    dx = (rank - me) % SIDE
-    dy = (rank // SIDE - me // SIDE) % SIDE
+    dx = away % SIDE
+    dy = away // SIDE
     which = block // (2 * PART)
     part = (block // PART) % 2
-    hops = jnp.where(which == 0, dx, dy)
+    place = jnp.where(which == 0, dx, dy)
     other = jnp.where(which == 0, dy, dx)
-    slot = (SLOT_OF >> (4 * (2 * hops + part))) & 7
+    slot = (SLOT_OF >> (4 * (2 * place + part))) & 7
     return ((which * (SLOTS // 2) + slot) * SIDE + other) * PART + block % PART
 
 
-def ring_perms():
-    def moved(dx, dy):
-        return [
-            (y * SIDE + x, (y + dy) % SIDE * SIDE + (x + dx) % SIDE)
-            for y in range(SIDE)
-            for x in range(SIDE)
-        ]
-
-    return (moved(1, 0), moved(-1, 0)), (moved(0, 1), moved(0, -1))
+def pair_perms():
+    return [
+        [[(i, i ^ (swap * stride)) for i in range(OWNERS)] for swap in (1, 3)]
+        for stride in (1, SIDE)
+    ]
 
 
 def added(*parts):
@@ -398,7 +399,7 @@
 
 
 def exchange(halves):
-    along_x, along_y = ring_perms()
+    along_x, along_y = pair_perms()
     sets = ((0, along_x, along_y), (5, along_y, along_x))
 
     def send(pair, perms):
@@ -411,28 +412,34 @@
     second = []
     for packs, arrived in zip(halves, first):
         row = []
-        for (at, one, _), (r1, l1) in zip(sets, arrived):
-            row.append(send((join(packs[at + 2][0], r1[0]), join(packs[at + 3][0], l1[0])), one))
+        for (at, one, _), (near, far) in zip(sets, arrived):
+            joined = join(packs[at + 2][0], far[0]), join(packs[at + 3][0], near[0])
+            row.append(send(joined, one))
         second.append(lax.optimization_barrier(row))
     shape = (SIDE, PART, HALF, 128)
     sums = [[], []]
     for packs, one, two in zip(halves, first, second):
-        for n, ((at, _, _), (r1, l1), (r2, l2)) in enumerate(zip(sets, one, two)):
+        for n, ((at, _, _), (n1, f1), (n2, f2)) in enumerate(zip(sets, one, two)):
             own = packs[at + 4]
             sums[n].append(
-                (added(own[0], r2, l1[1]).reshape(shape), added(own[1], r1[1], l2).reshape(shape))
+                (added(own[0], n1[1], f2).reshape(shape), added(own[1], f1[1], n2).reshape(shape))
             )
     third, kept = [], []
     for (_, _, two), parts in zip(sets, sums):
-        r, l = ([jnp.stack([h[p][n] for h in parts]) for n in range(SIDE)] for p in range(2))
-        r16, l16 = ([v.astype(jnp.bfloat16) for v in w] for w in (r, l))
-        kept.append((r[0], l[0], r16[1], l16[3]))
-        third.append(send((jnp.stack([r16[2], l16[1]]), jnp.stack([l16[2], r16[3]])), two))
+        p0, p1 = ([jnp.stack([h[p][n] for h in parts]) for n in range(SIDE)] for p in range(2))
+        q0, q1 = ([v.astype(jnp.bfloat16) for v in w] for w in (p0, p1))
+        kept.append((p0[0], p1[0], q1[1], q0[3]))
+        third.append(send((jnp.stack([q0[2], q0[1]]), jnp.stack([q1[2], q1[3]])), two))
     third = lax.optimization_barrier(third)
+    joined = [
+        (join(keep_near, far[0]), join(keep_far, near[0]))
+        for (_, _, keep_near, keep_far), (near, far) in zip(kept, third)
+    ]
+    joined, third = lax.optimization_barrier((joined, third))
     found = []
-    for (_, _, two), (right, left, keep_right, keep_left), (r1, l1) in zip(sets, kept, third):
-        fourth = send((join(keep_right, r1[0]), join(keep_left, l1[0])), two)
-        found += [added(right, l1[1]), added(left, r1[1]), *fourth]
+    for (_, _, two), (own0, own1, _, _), (n1, f1), pair in zip(sets, kept, third, joined):
+        n2, f2 = send(pair, two)
+        found += [added(own0, n1[1]), added(own1, f1[1]), f2, n2]
     return found
 
 
@@ -466,7 +473,9 @@
 def on_device(a_blocks, p_blocks, dest_rank, dest_block):
     halos = faces(p_blocks)
     target = sum_places(dest_rank, dest_block)
-    q, lefts, qh, first = first_half(target, jnp.swapaxes(a_blocks, 0, 1), p_blocks, halos)
+    odd = jnp.stack([lax.axis_index(axis) % 2 for axis in ("dom", "slab")])
+    a = jnp.swapaxes(a_blocks, 0, 1)
+    q, lefts, qh, first = first_half(target, odd, a, p_blocks, halos)
     second = second_half(target, lefts, q, qh)
     return finish(exchange((first, second)))
 

time: 172 us -> 165 us (0.959)
  starting transfers between devices: 48.3 us -> 41.5 us
  other arithmetic: 7.29 us -> 10.1 us
  local copies, waits for them, and re-layouts: 4.29 us -> 2.46 us
    ppermute x24, starting transfers between devices: 38.1 us -> 31.3 us  [send(): return [lax.ppermute(v, 'dom', perm) for v, perm in zip(pair, perms)]]
    ppermute x4, waiting for transfers between devices: 4.25 us -> 0.85 us  [the longest x2 0.84 us: faces(): found.append(lax.ppermute(jnp.where(even, first, last), axis, far))]
    add x0 -> x4, other arithmetic: none -> 3.4 us  [added(): total = total + part.astype(jnp.float32)]
    convert_element_type x12, other arithmetic: 4.79 us -> 1.41 us  [join(): return added(keep, arrived).astype(jnp.bfloat16)]
    select_n x0 -> x2, other arithmetic: none -> 2.16 us  [faces(): found.append(lax.ppermute(jnp.where(even, first, last), axis, far))]
    ppermute x24, waiting for transfers between devices: 51.6 us -> 53.6 us  [send(): return [lax.ppermute(v, 'dom', perm) for v, perm in zip(pair, perms)]]
  transfers between devices with their start and end apart: 28 -> 28, of which waited for: 16 -> 20; matrix products, arithmetic and copies ran while one was open for 4% -> 5% of each run, Pallas kernels for 10% -> 11%
where the time goes in v6:
time: 165 us; the launch traced here: 163 us
  waiting for transfers between devices  54.5 us (33%)
  Pallas kernels  54 us (33%)
  starting transfers between devices  41.5 us (25%)
  other arithmetic  10.1 us (6%)
  local copies, waits for them, and re-layouts  2.46 us (1%)
    ppermute x24, waiting for transfers between devices, send(): return [lax.ppermute(v, 'dom', perm) for v, perm in zip(pair, perms)]  53.6 us
    pallas_call x1, Pallas kernels, first_half(): pl.pallas_call(first_kernel, grid=(E_DEV // GROUP,), in_specs=[SMEM, SMEM...  32.8 us
    ppermute x24, starting transfers between devices, send(): return [lax.ppermute(v, 'dom', perm) for v, perm in zip(pair, perms)]  31.3 us
    pallas_call x1, Pallas kernels, second_half(): pl.pallas_call(second_kernel, grid=(E_DEV // GROUP,), in_specs=[SMEM, VME...  17.7 us
    ppermute x2, starting transfers between devices, faces(): found.append(lax.ppermute(jnp.where(even, last, first), axis, near))  7.62 us
    pallas_call x1, Pallas kernels, finish(): pl.pallas_call(finish_kernel, in_specs=[VMEM] * len(parts), out_specs=VME...  3.49 us
    add x4, other arithmetic, added(): total = total + part.astype(jnp.float32)  3.4 us
  transfers between devices with their start and end apart: 28, of which 20 were waited for; matrix products, arithmetic and copies ran while one was open for 5% of the time, Pallas kernels for 11%

profile of v6, /device:TPU:96, one launch (start us, length us, event | category | flops | bytes accessed | tf_op | source)
XLA Modules:
  0.0 162.9 jit_solution(10631577613598344935)
XLA Ops:
  0.0 1.1 select_bitcast_fusion
  1.1 0.7 collective-permute-start.1
  1.8 4.3 %collective-permute-start = (bf16[32,4096]{1,0:T(8,128)(2,1)S(1)}, bf16[32,4096]{1,0:T(8,128)(2,1)S(1)}, u32[]{:S(2)}, u32[]{:S(2)}) collective-permute-start(bf16[32,4096]{1,0:T(8,128)(2,1)S(1)} %get-tuple-element.134), channel_id=1, source_target_pairs={{0,1},{1,0},{2,3},{3,2},{4,5},{5,4},{6,7},{7,6},{8,9},{9,8},{10,11... | collective-permute-start | bytes 786440 | tf_op jit(solution)/shard_map/ppermute | solution.py:364
  6.1 1.1 broadcast_select_fusion
  7.2 1.9 %collective-permute-start.3 = (bf16[32,4096]{1,0:T(8,128)(2,1)S(1)}, bf16[32,4096]{1,0:T(8,128)(2,1)S(1)}, u32[]{:S(2)}, u32[]{:S(2)}) collective-permute-start(bf16[32,4096]{1,0:T(8,128)(2,1)S(1)} %get-tuple-element.131), channel_id=1, source_target_pairs={{16,32},{32,16},{48,64},{64,48},{80,96},{96,80},{112,128},{128,112... | collective-permute-start | bytes 786440 | tf_op jit(solution)/shard_map/ppermute | solution.py:365
  9.1 3.3 %collective-permute-start.2 = (bf16[32,4096]{1,0:T(8,128)(2,1)S(1)}, bf16[32,4096]{1,0:T(8,128)(2,1)S(1)}, u32[]{:S(2)}, u32[]{:S(2)}) collective-permute-start(bf16[32,4096]{1,0:T(8,128)(2,1)S(1)} %get-tuple-element.132), channel_id=1, source_target_pairs={{0,16},{16,0},{32,48},{48,32},{64,80},{80,64},{96,112},{112,96},{1... | collective-permute-start | bytes 786440 | tf_op jit(solution)/shard_map/ppermute | solution.py:364
  13.4 0.6 fusion.22.target_ref
  14.0 0.8 collective-permute-done.3.refs_3_
  14.9 0.7 copy-done.16
  15.6 32.8 %first_half.1 = (bf16[128,64,896]{2,1,0:T(8,128)(2,1)}, bf16[128,64,64]{2,1,0:T(8,128)(2,1)}, bf16[128,64,128]{2,1,0:T(8,128)(2,1)}, bf16[2,128,16,128]{3,2,1,0:...) custom-call(s32[896]{0:T(1024)} %fusion.22.target_ref, ...), custom_call_target="tpu_custom_call" | custom-call | flops 10000000000 | bytes 60000000 | tf_op jit(solution)/shard_map/first_half/pallas_call | solution.py:306
  48.5 3.3 %collective-permute-start.5 = (bf16[2,128,16,128]{3,2,1,0:T(8,128)(2,1)}, bf16[2,128,16,128]{3,2,1,0:T(8,128)(2,1)S(1)}, u32[]{:S(2)}, u32[]{:S(2)}) collective-permute-start(bf16[2,128,16,128]{3,2,1,0:T(8,128)(2,1)} %get-tuple-element.58), channel_id=1, source_target_pairs={{0,3},{1,2},{2,1},{3,0},{4,7},{5,6},{6,5},{7,4},{8,11},{9,10},{10,... | collective-permute-start | bytes 3145736 | tf_op jit(solution)/shard_map/ppermute | solution.py:406
  51.8 1.6 collective-permute-start.6
  53.4 1.9 %collective-permute-start.7 = (bf16[2,128,16,128]{3,2,1,0:T(8,128)(2,1)}, bf16[2,128,16,128]{3,2,1,0:T(8,128)(2,1)S(1)}, u32[]{:S(2)}, u32[]{:S(2)}) collective-permute-start(bf16[2,128,16,128]{3,2,1,0:T(8,128)(2,1)} %get-tuple-element.60), channel_id=1, source_target_pairs={{0,12},{1,13},{2,14},{3,15},{4,8},{5,9},{6,10},{7,11},{8,4},{9,5},... | collective-permute-start | bytes 3145736 | tf_op jit(solution)/shard_map/ppermute | solution.py:406
  55.3 17.7 %second_half.1 = (bf16[2,128,16,128]{3,2,1,0:T(8,128)(2,1)S(1)}, bf16[2,128,16,128]{3,2,1,0:T(8,128)(2,1)S(1)}, bf16[1,128,16,128]{3,2,1,0:T(8,128)(2,1)S(1)}, b...) custom-call(s32[896]{0:T(1024)S(1)} %copy-done, ...), custom_call_target="tpu_custom_call" | custom-call | flops 10000000000 | bytes 60000000 | tf_op jit(solution)/shard_map/second_half/pallas_call | solution.py:340
  73.1 1.2 collective-permute-done.4
  74.3 1.0 collective-permute-start.13
  75.6 3.4 %collective-permute-start.14 = (bf16[2,128,16,128]{3,2,1,0:T(8,128)(2,1)}, bf16[2,128,16,128]{3,2,1,0:T(8,128)(2,1)S(1)}, u32[]{:S(2)}, u32[]{:S(2)}) collective-permute-start(bf16[2,128,16,128]{3,2,1,0:T(8,128)(2,1)} %get-tuple-element.76), channel_id=1, source_target_pairs={{0,4},{1,5},{2,6},{3,7},{4,0},{5,1},{6,2},{7,3},{8,12},{9,13},{10,... | collective-permute-start | bytes 3145736 | tf_op jit(solution)/shard_map/ppermute | solution.py:406
  79.0 2.2 %collective-permute-start.15 = (bf16[2,128,16,128]{3,2,1,0:T(8,128)(2,1)}, bf16[2,128,16,128]{3,2,1,0:T(8,128)(2,1)S(1)}, u32[]{:S(2)}, u32[]{:S(2)}) collective-permute-start(bf16[2,128,16,128]{3,2,1,0:T(8,128)(2,1)} %get-tuple-element.77), channel_id=1, source_target_pairs={{0,12},{1,13},{2,14},{3,15},{4,8},{5,9},{6,10},{7,11},{8,4},{9,5},... | collective-permute-start | bytes 3145736 | tf_op jit(solution)/shard_map/ppermute | solution.py:406
  81.3 1.4 collective-permute-start.11
  83.1 15.4 %collective-permute-done.12 = bf16[2,128,16,128]{3,2,1,0:T(8,128)(2,1)S(1)} collective-permute-done((bf16[2,128,16,128]{3,2,1,0:T(8,128)(2,1)S(1)}, bf16[2,128,16,128]{3,2,1,0:T(8,128)(2,1)S(1)}, u32[]{:S(2)}, u32[]{:S(2)}) %collective-permute-start.12) | collective-permute-done | bytes 1048608 | tf_op jit(solution)/shard_map/ppermute | solution.py:406
  98.8 2.4 %collective-permute-done.13 = bf16[2,128,16,128]{3,2,1,0:T(8,128)(2,1)S(1)} collective-permute-done((bf16[2,128,16,128]{3,2,1,0:T(8,128)(2,1)S(1)}, bf16[2,128,16,128]{3,2,1,0:T(8,128)(2,1)S(1)}, u32[]{:S(2)}, u32[]{:S(2)}) %collective-permute-start.13) | collective-permute-done | bytes 1048608 | tf_op jit(solution)/shard_map/ppermute | solution.py:406
  101.2 2.0 %collective-permute-done.14 = bf16[2,128,16,128]{3,2,1,0:T(8,128)(2,1)S(1)} collective-permute-done((bf16[2,128,16,128]{3,2,1,0:T(8,128)(2,1)}, bf16[2,128,16,128]{3,2,1,0:T(8,128)(2,1)S(1)}, u32[]{:S(2)}, u32[]{:S(2)}) %collective-permute-start.14) | collective-permute-done | bytes 1048608 | tf_op jit(solution)/shard_map/ppermute | solution.py:406
  103.1 2.1 %collective-permute-start.9 = (bf16[128,16,128]{2,1,0:T(8,128)(2,1)S(1)}, bf16[128,16,128]{2,1,0:T(8,128)(2,1)S(1)}, u32[]{:S(2)}, u32[]{:S(2)}) collective-permute-start(bf16[128,16,128]{2,1,0:T(8,128)(2,1)S(1)} %fusion.1), channel_id=1, source_target_pairs={{0,3},{1,2},{2,1},{3,0},{4,7},{5,6},{6,5},{7,4},{8,11},{9,10},{10,... | collective-permute-start | bytes 1572872 | tf_op jit(solution)/shard_map/ppermute | solution.py:406
  105.2 1.2 collective-permute-done.15
  106.6 2.3 %collective-permute-start.19 = (bf16[128,16,128]{2,1,0:T(8,128)(2,1)S(1)}, bf16[128,16,128]{2,1,0:T(8,128)(2,1)S(1)}, u32[]{:S(2)}, u32[]{:S(2)}) collective-permute-start(bf16[128,16,128]{2,1,0:T(8,128)(2,1)S(1)} %fusion.7), channel_id=1, source_target_pairs={{0,12},{1,13},{2,14},{3,15},{4,8},{5,9},{6,10},{7,11},{8,4},{9,5},... | collective-permute-start | bytes 1572872 | tf_op jit(solution)/shard_map/ppermute | solution.py:406
  109.3 8.4 %collective-permute-done.11 = bf16[128,16,128]{2,1,0:T(8,128)(2,1)S(1)} collective-permute-done((bf16[128,16,128]{2,1,0:T(8,128)(2,1)S(1)}, bf16[128,16,128]{2,1,0:T(8,128)(2,1)S(1)}, u32[]{:S(2)}, u32[]{:S(2)}) %collective-permute-start.11) | collective-permute-done | bytes 524320 | tf_op jit(solution)/shard_map/ppermute | solution.py:406
  117.7 1.7 %collective-permute-start.17 = (bf16[128,16,128]{2,1,0:T(8,128)(2,1)S(1)}, bf16[128,16,128]{2,1,0:T(8,128)(2,1)S(1)}, u32[]{:S(2)}, u32[]{:S(2)}) collective-permute-start(bf16[128,16,128]{2,1,0:T(8,128)(2,1)S(1)} %fusion.5), channel_id=1, source_target_pairs={{0,3},{1,2},{2,1},{3,0},{4,7},{5,6},{6,5},{7,4},{8,11},{9,10},{10,... | collective-permute-start | bytes 1572872 | tf_op jit(solution)/shard_map/ppermute | solution.py:406
  119.4 0.8 fusion.28
  120.5 7.3 %collective-permute-done.19 = bf16[128,16,128]{2,1,0:T(8,128)(2,1)S(1)} collective-permute-done((bf16[128,16,128]{2,1,0:T(8,128)(2,1)S(1)}, bf16[128,16,128]{2,1,0:T(8,128)(2,1)S(1)}, u32[]{:S(2)}, u32[]{:S(2)}) %collective-permute-start.19) | collective-permute-done | bytes 524320 | tf_op jit(solution)/shard_map/ppermute | solution.py:406
  127.8 1.6 collective-permute-done.18
  129.3 0.8 collective-permute-done.16
  130.1 1.3 collective-permute-done.17
  131.4 0.8 fusion.29
  132.5 2.1 %collective-permute-start.21 = (bf16[2,2,32,16,128]{4,3,2,1,0:T(8,128)(2,1)S(1)}, bf16[2,2,32,16,128]{4,3,2,1,0:T(8,128)(2,1)S(1)}, u32[]{:S(2)}, u32[]{:S(2)}) collective-permute-start(bf16[2,2,32,16,128]{4,3,2,1,0:T(8,128)(2,1)S(1)} %maximum_maximum_fusion.1), channel_id=1, source_target_pairs={{0,12},{1,13},{2,14},{3,15},{4,8},{5,9},{6,10},{7,11},{8,4},{9,5},... | collective-permute-start | bytes 1572872 | tf_op jit(solution)/shard_map/ppermute | solution.py:406
  134.7 0.9 collective-permute-start.20
  136.1 2.3 %collective-permute-start.23 = (bf16[2,2,32,16,128]{4,3,2,1,0:T(8,128)(2,1)S(1)}, bf16[2,2,32,16,128]{4,3,2,1,0:T(8,128)(2,1)S(1)}, u32[]{:S(2)}, u32[]{:S(2)}) collective-permute-start(bf16[2,2,32,16,128]{4,3,2,1,0:T(8,128)(2,1)S(1)} %maximum_maximum_fusion.3), channel_id=1, source_target_pairs={{0,3},{1,2},{2,1},{3,0},{4,7},{5,6},{6,5},{7,4},{8,11},{9,10},{10,... | collective-permute-start | bytes 1572872 | tf_op jit(solution)/shard_map/ppermute | solution.py:406
  138.4 6.8 %collective-permute-done.21 = bf16[2,2,32,16,128]{4,3,2,1,0:T(8,128)(2,1)S(1)} collective-permute-done((bf16[2,2,32,16,128]{4,3,2,1,0:T(8,128)(2,1)S(1)}, bf16[2,2,32,16,128]{4,3,2,1,0:T(8,128)(2,1)S(1)}, u32[]{:S(2)}, u32[]{:S(2)}) %collective-permute-start.21) | collective-permute-done | bytes 524320 | tf_op jit(solution)/shard_map/ppermute | solution.py:406
  146.0 1.4 collective-permute-done.23
  147.7 1.6 %collective-permute-start.24 = (bf16[2,32,16,128]{3,2,1,0:T(8,128)(2,1)S(1)}, bf16[2,32,16,128]{3,2,1,0:T(8,128)(2,1)S(1)}, u32[]{:S(2)}, u32[]{:S(2)}) collective-permute-start(bf16[2,32,16,128]{3,2,1,0:T(8,128)(2,1)S(1)} %fusion.10), channel_id=1, source_target_pairs={{0,12},{1,13},{2,14},{3,15},{4,8},{5,9},{6,10},{7,11},{8,4},{9,5},... | collective-permute-start | bytes 786440 | tf_op jit(solution)/shard_map/ppermute | solution.py:406
  149.3 1.1 collective-permute-start.25
  150.4 1.7 %collective-permute-start.26 = (bf16[2,32,16,128]{3,2,1,0:T(8,128)(2,1)S(1)}, bf16[2,32,16,128]{3,2,1,0:T(8,128)(2,1)S(1)}, u32[]{:S(2)}, u32[]{:S(2)}) collective-permute-start(bf16[2,32,16,128]{3,2,1,0:T(8,128)(2,1)S(1)} %fusion.8), channel_id=1, source_target_pairs={{0,3},{1,2},{2,1},{3,0},{4,7},{5,6},{6,5},{7,4},{8,11},{9,10},{10,... | collective-permute-start | bytes 786440 | tf_op jit(solution)/shard_map/ppermute | solution.py:406
  152.1 0.8 maximum_add_fusion.3.refs_5_
  152.9 0.8 maximum_add_fusion.2.refs_4_
  153.8 0.9 maximum_add_fusion.refs_0_
  154.6 0.9 maximum_add_fusion.1.refs_1_
  155.7 2.3 %collective-permute-done.26.refs_6_ = bf16[2,32,16,128]{3,2,1,0:T(8,128)(2,1)S(1)} collective-permute-done((bf16[2,32,16,128]{3,2,1,0:T(8,128)(2,1)S(1)}, bf16[2,32,16,128]{3,2,1,0:T(8,128)(2,1)S(1)}, u32[]{:S(2)}, u32[]{:S(2)}) %collective-permute-start.26) | collective-permute-done | bytes 262176 | tf_op jit(solution)/shard_map/ppermute | solution.py:406
  158.7 0.7 copy-done.11
  159.4 3.5 %finish.1 = f32[128,4096]{1,0:T(8,128)} custom-call(f32[2,32,16,128]{3,2,1,0:T(8,128)} %maximum_add_fusion.refs_0_, f32[2,32,16,128]{3,2,1,0:T(8,128)} %maximum_add_fusion.1.refs_1_, bf16[2,32,16,128]{3,2,1,0:T(8,128)(2,1)} %copy-done.8, bf16[2,32,16,128]{3,2,1,0:T(8,128)(2,1)} %copy-done.9, f32[2,32,16,128]{3,2,1,0:T(8,128)} %maximum_add_fusion.2.refs_4_, ...), custom_call_target="tpu_custom_call" | custom-call | tf_op jit(solution)/shard_map/finish/pallas_call | solution.py:463
  (92 shorter events, 5.8 us)
Async XLA Ops:
  0.0 12.4 %copy-start.13 = (s32[896,1]{0,1:T(1,128)S(1)}, s32[896,1]{0,1:T(1,128)}, u32[]{:S(2)}) copy-start(s32[896,1]{0,1:T(1,128)} %param.6) | copy-start | bytes 10756
  0.0 13.0 %copy-start.12 = (s32[128,7]{0,1:T(8,128)S(1)}, s32[128,7]{0,1:T(8,128)}, u32[]{:S(2)}) copy-start(s32[128,7]{0,1:T(8,128)} %param.7) | copy-start | bytes 10756
  1.1 12.9 %collective-permute-start.1 = (bf16[32,4096]{1,0:T(8,128)(2,1)S(1)}, bf16[32,4096]{1,0:T(8,128)(2,1)S(1)}, u32[]{:S(2)}, u32[]{:S(2)}) collective-permute-start(bf16[32,4096]{1,0:T(8,128)(2,1)S(1)} %get-tuple-element.133), channel_id=1, source_target_pairs={{1,2},{2,1},{3,4},{4,3},{5,6},{6,5},{7,8},{8,7},{9,10},{10,9},{11,... | collective-permute-start | bytes 786440 | tf_op jit(solution)/shard_map/ppermute | solution.py:365
  1.8 12.2 %collective-permute-start = (bf16[32,4096]{1,0:T(8,128)(2,1)S(1)}, bf16[32,4096]{1,0:T(8,128)(2,1)S(1)}, u32[]{:S(2)}, u32[]{:S(2)}) collective-permute-start(bf16[32,4096]{1,0:T(8,128)(2,1)S(1)} %get-tuple-element.134), channel_id=1, source_target_pairs={{0,1},{1,0},{2,3},{3,2},{4,5},{5,4},{6,7},{7,6},{8,9},{9,8},{10,11... | collective-permute-start | bytes 786440 | tf_op jit(solution)/shard_map/ppermute | solution.py:364
  7.2 7.7 %collective-permute-start.3 = (bf16[32,4096]{1,0:T(8,128)(2,1)S(1)}, bf16[32,4096]{1,0:T(8,128)(2,1)S(1)}, u32[]{:S(2)}, u32[]{:S(2)}) collective-permute-start(bf16[32,4096]{1,0:T(8,128)(2,1)S(1)} %get-tuple-element.131), channel_id=1, source_target_pairs={{16,32},{32,16},{48,64},{64,48},{80,96},{96,80},{112,128},{128,112... | collective-permute-start | bytes 786440 | tf_op jit(solution)/shard_map/ppermute | solution.py:365
  9.1 5.8 %collective-permute-start.2 = (bf16[32,4096]{1,0:T(8,128)(2,1)S(1)}, bf16[32,4096]{1,0:T(8,128)(2,1)S(1)}, u32[]{:S(2)}, u32[]{:S(2)}) collective-permute-start(bf16[32,4096]{1,0:T(8,128)(2,1)S(1)} %get-tuple-element.132), channel_id=1, source_target_pairs={{0,16},{16,0},{32,48},{48,32},{64,80},{80,64},{96,112},{112,96},{1... | collective-permute-start | bytes 786440 | tf_op jit(solution)/shard_map/ppermute | solution.py:364
  14.0 0.9 copy-start.14
  14.0 0.9 copy-start.15
  14.8 0.7 copy-start.16
  14.9 0.8 copy-start.17
  15.6 39.6 %copy-start = (s32[896]{0:T(1024)S(1)}, s32[896]{0:T(1024)}, u32[]{:S(2)}) copy-start(s32[896]{0:T(1024)} %fusion.22.target_ref) | copy-start | bytes 10756
  48.4 25.9 %collective-permute-start.4 = (bf16[2,128,16,128]{3,2,1,0:T(8,128)(2,1)}, bf16[2,128,16,128]{3,2,1,0:T(8,128)(2,1)S(1)}, u32[]{:S(2)}, u32[]{:S(2)}) collective-permute-start(bf16[2,128,16,128]{3,2,1,0:T(8,128)(2,1)} %get-tuple-element.57), channel_id=1, source_target_pairs={{0,1},{1,0},{2,3},{3,2},{4,5},{5,4},{6,7},{7,6},{8,9},{9,8},{10,11... | collective-permute-start | bytes 3145736 | tf_op jit(solution)/shard_map/ppermute | solution.py:406
  48.5 27.1 %collective-permute-start.5 = (bf16[2,128,16,128]{3,2,1,0:T(8,128)(2,1)}, bf16[2,128,16,128]{3,2,1,0:T(8,128)(2,1)S(1)}, u32[]{:S(2)}, u32[]{:S(2)}) collective-permute-start(bf16[2,128,16,128]{3,2,1,0:T(8,128)(2,1)} %get-tuple-element.58), channel_id=1, source_target_pairs={{0,3},{1,2},{2,1},{3,0},{4,7},{5,6},{6,5},{7,4},{8,11},{9,10},{10,... | collective-permute-start | bytes 3145736 | tf_op jit(solution)/shard_map/ppermute | solution.py:406
  51.8 27.2 %collective-permute-start.6 = (bf16[2,128,16,128]{3,2,1,0:T(8,128)(2,1)}, bf16[2,128,16,128]{3,2,1,0:T(8,128)(2,1)S(1)}, u32[]{:S(2)}, u32[]{:S(2)}) collective-permute-start(bf16[2,128,16,128]{3,2,1,0:T(8,128)(2,1)} %get-tuple-element.59), channel_id=1, source_target_pairs={{0,4},{1,5},{2,6},{3,7},{4,0},{5,1},{6,2},{7,3},{8,12},{9,13},{10,... | collective-permute-start | bytes 3145736 | tf_op jit(solution)/shard_map/ppermute | solution.py:406
  53.4 27.8 %collective-permute-start.7 = (bf16[2,128,16,128]{3,2,1,0:T(8,128)(2,1)}, bf16[2,128,16,128]{3,2,1,0:T(8,128)(2,1)S(1)}, u32[]{:S(2)}, u32[]{:S(2)}) collective-permute-start(bf16[2,128,16,128]{3,2,1,0:T(8,128)(2,1)} %get-tuple-element.60), channel_id=1, source_target_pairs={{0,12},{1,13},{2,14},{3,15},{4,8},{5,9},{6,10},{7,11},{8,4},{9,5},... | collective-permute-start | bytes 3145736 | tf_op jit(solution)/shard_map/ppermute | solution.py:406
  55.3 25.9 %copy-start.7 = (bf16[1,128,16,128]{3,2,1,0:T(8,128)(2,1)S(1)}, bf16[1,128,16,128]{3,2,1,0:T(8,128)(2,1)}, u32[]{:S(2)}) copy-start(bf16[1,128,16,128]{3,2,1,0:T(8,128)(2,1)} %get-tuple-element.67) | copy-start | bytes 1572868
  55.3 27.4 %copy-start.6 = (bf16[1,128,16,128]{3,2,1,0:T(8,128)(2,1)S(1)}, bf16[1,128,16,128]{3,2,1,0:T(8,128)(2,1)}, u32[]{:S(2)}) copy-start(bf16[1,128,16,128]{3,2,1,0:T(8,128)(2,1)} %get-tuple-element.64) | copy-start | bytes 1572868
  73.0 9.8 %copy-start.5 = (bf16[1,128,16,128]{3,2,1,0:T(8,128)(2,1)S(1)}, bf16[1,128,16,128]{3,2,1,0:T(8,128)(2,1)}, u32[]{:S(2)}) copy-start(bf16[1,128,16,128]{3,2,1,0:T(8,128)(2,1)} %get-tuple-element.62) | copy-start | bytes 1572868
  73.0 25.5 %collective-permute-start.12 = (bf16[2,128,16,128]{3,2,1,0:T(8,128)(2,1)S(1)}, bf16[2,128,16,128]{3,2,1,0:T(8,128)(2,1)S(1)}, u32[]{:S(2)}, u32[]{:S(2)}) collective-permute-start(bf16[2,128,16,128]{3,2,1,0:T(8,128)(2,1)S(1)} %get-tuple-element.74), channel_id=1, source_target_pairs={{0,1},{1,0},{2,3},{3,2},{4,5},{5,4},{6,7},{7,6},{8,9},{9,8},{10,11... | collective-permute-start | bytes 3145736 | tf_op jit(solution)/shard_map/ppermute | solution.py:406
  74.3 26.9 %collective-permute-start.13 = (bf16[2,128,16,128]{3,2,1,0:T(8,128)(2,1)S(1)}, bf16[2,128,16,128]{3,2,1,0:T(8,128)(2,1)S(1)}, u32[]{:S(2)}, u32[]{:S(2)}) collective-permute-start(bf16[2,128,16,128]{3,2,1,0:T(8,128)(2,1)S(1)} %get-tuple-element.75), channel_id=1, source_target_pairs={{0,3},{1,2},{2,1},{3,0},{4,7},{5,6},{6,5},{7,4},{8,11},{9,10},{10,... | collective-permute-start | bytes 3145736 | tf_op jit(solution)/shard_map/ppermute | solution.py:406
  75.6 27.5 %collective-permute-start.14 = (bf16[2,128,16,128]{3,2,1,0:T(8,128)(2,1)}, bf16[2,128,16,128]{3,2,1,0:T(8,128)(2,1)S(1)}, u32[]{:S(2)}, u32[]{:S(2)}) collective-permute-start(bf16[2,128,16,128]{3,2,1,0:T(8,128)(2,1)} %get-tuple-element.76), channel_id=1, source_target_pairs={{0,4},{1,5},{2,6},{3,7},{4,0},{5,1},{6,2},{7,3},{8,12},{9,13},{10,... | collective-permute-start | bytes 3145736 | tf_op jit(solution)/shard_map/ppermute | solution.py:406
  79.0 27.5 %collective-permute-start.15 = (bf16[2,128,16,128]{3,2,1,0:T(8,128)(2,1)}, bf16[2,128,16,128]{3,2,1,0:T(8,128)(2,1)S(1)}, u32[]{:S(2)}, u32[]{:S(2)}) collective-permute-start(bf16[2,128,16,128]{3,2,1,0:T(8,128)(2,1)} %get-tuple-element.77), channel_id=1, source_target_pairs={{0,12},{1,13},{2,14},{3,15},{4,8},{5,9},{6,10},{7,11},{8,4},{9,5},... | collective-permute-start | bytes 3145736 | tf_op jit(solution)/shard_map/ppermute | solution.py:406
  81.2 1.8 %copy-start.4 = (bf16[1,128,16,128]{3,2,1,0:T(8,128)(2,1)S(1)}, bf16[1,128,16,128]{3,2,1,0:T(8,128)(2,1)}, u32[]{:S(2)}) copy-start(bf16[1,128,16,128]{3,2,1,0:T(8,128)(2,1)} %get-tuple-element.65) | copy-start | bytes 1572868
  81.3 36.4 %collective-permute-start.11 = (bf16[128,16,128]{2,1,0:T(8,128)(2,1)S(1)}, bf16[128,16,128]{2,1,0:T(8,128)(2,1)S(1)}, u32[]{:S(2)}, u32[]{:S(2)}) collective-permute-start(bf16[128,16,128]{2,1,0:T(8,128)(2,1)S(1)} %fusion.3), channel_id=1, source_target_pairs={{0,12},{1,13},{2,14},{3,15},{4,8},{5,9},{6,10},{7,11},{8,4},{9,5},... | collective-permute-start | bytes 1572872 | tf_op jit(solution)/shard_map/ppermute | solution.py:406
  98.6 19.1 %collective-permute-start.10 = (bf16[128,16,128]{2,1,0:T(8,128)(2,1)S(1)}, bf16[128,16,128]{2,1,0:T(8,128)(2,1)S(1)}, u32[]{:S(2)}, u32[]{:S(2)}) collective-permute-start(bf16[128,16,128]{2,1,0:T(8,128)(2,1)S(1)} %fusion.2), channel_id=1, source_target_pairs={{0,4},{1,5},{2,6},{3,7},{4,0},{5,1},{6,2},{7,3},{8,12},{9,13},{10,... | collective-permute-start | bytes 1572872 | tf_op jit(solution)/shard_map/ppermute | solution.py:406
  101.2 16.5 %collective-permute-start.8 = (bf16[128,16,128]{2,1,0:T(8,128)(2,1)S(1)}, bf16[128,16,128]{2,1,0:T(8,128)(2,1)S(1)}, u32[]{:S(2)}, u32[]{:S(2)}) collective-permute-start(bf16[128,16,128]{2,1,0:T(8,128)(2,1)S(1)} %fusion), channel_id=1, source_target_pairs={{0,1},{1,0},{2,3},{3,2},{4,5},{5,4},{6,7},{7,6},{8,9},{9,8},{10,11... | collective-permute-start | bytes 1572872 | tf_op jit(solution)/shard_map/ppermute | solution.py:406
  103.1 16.3 %collective-permute-start.9 = (bf16[128,16,128]{2,1,0:T(8,128)(2,1)S(1)}, bf16[128,16,128]{2,1,0:T(8,128)(2,1)S(1)}, u32[]{:S(2)}, u32[]{:S(2)}) collective-permute-start(bf16[128,16,128]{2,1,0:T(8,128)(2,1)S(1)} %fusion.1), channel_id=1, source_target_pairs={{0,3},{1,2},{2,1},{3,0},{4,7},{5,6},{6,5},{7,4},{8,11},{9,10},{10,... | collective-permute-start | bytes 1572872 | tf_op jit(solution)/shard_map/ppermute | solution.py:406
  106.6 21.2 %collective-permute-start.19 = (bf16[128,16,128]{2,1,0:T(8,128)(2,1)S(1)}, bf16[128,16,128]{2,1,0:T(8,128)(2,1)S(1)}, u32[]{:S(2)}, u32[]{:S(2)}) collective-permute-start(bf16[128,16,128]{2,1,0:T(8,128)(2,1)S(1)} %fusion.7), channel_id=1, source_target_pairs={{0,12},{1,13},{2,14},{3,15},{4,8},{5,9},{6,10},{7,11},{8,4},{9,5},... | collective-permute-start | bytes 1572872 | tf_op jit(solution)/shard_map/ppermute | solution.py:406
  108.8 10.6 %copy-start.2 = (bf16[2,128,16,128]{3,2,1,0:T(8,128)(2,1)S(1)}, bf16[2,128,16,128]{3,2,1,0:T(8,128)(2,1)}, u32[]{:S(2)}) copy-start(bf16[2,128,16,128]{3,2,1,0:T(8,128)(2,1)} %get-tuple-element.56) | copy-start | bytes 3145732
  108.8 10.6 %copy-start.3 = (bf16[2,128,16,128]{3,2,1,0:T(8,128)(2,1)S(1)}, bf16[2,128,16,128]{3,2,1,0:T(8,128)(2,1)}, u32[]{:S(2)}) copy-start(bf16[2,128,16,128]{3,2,1,0:T(8,128)(2,1)} %get-tuple-element.89) | copy-start | bytes 3145732
  117.7 11.6 %collective-permute-start.18 = (bf16[128,16,128]{2,1,0:T(8,128)(2,1)S(1)}, bf16[128,16,128]{2,1,0:T(8,128)(2,1)S(1)}, u32[]{:S(2)}, u32[]{:S(2)}) collective-permute-start(bf16[128,16,128]{2,1,0:T(8,128)(2,1)S(1)} %fusion.6), channel_id=1, source_target_pairs={{0,4},{1,5},{2,6},{3,7},{4,0},{5,1},{6,2},{7,3},{8,12},{9,13},{10,... | collective-permute-start | bytes 1572872 | tf_op jit(solution)/shard_map/ppermute | solution.py:406
  117.7 12.4 %collective-permute-start.16 = (bf16[128,16,128]{2,1,0:T(8,128)(2,1)S(1)}, bf16[128,16,128]{2,1,0:T(8,128)(2,1)S(1)}, u32[]{:S(2)}, u32[]{:S(2)}) collective-permute-start(bf16[128,16,128]{2,1,0:T(8,128)(2,1)S(1)} %fusion.4), channel_id=1, source_target_pairs={{0,1},{1,0},{2,3},{3,2},{4,5},{5,4},{6,7},{7,6},{8,9},{9,8},{10,11... | collective-permute-start | bytes 1572872 | tf_op jit(solution)/shard_map/ppermute | solution.py:406
  117.7 13.7 %collective-permute-start.17 = (bf16[128,16,128]{2,1,0:T(8,128)(2,1)S(1)}, bf16[128,16,128]{2,1,0:T(8,128)(2,1)S(1)}, u32[]{:S(2)}, u32[]{:S(2)}) collective-permute-start(bf16[128,16,128]{2,1,0:T(8,128)(2,1)S(1)} %fusion.5), channel_id=1, source_target_pairs={{0,3},{1,2},{2,1},{3,0},{4,7},{5,6},{6,5},{7,4},{8,11},{9,10},{10,... | collective-permute-start | bytes 1572872 | tf_op jit(solution)/shard_map/ppermute | solution.py:406
  120.3 11.1 %copy-start.1 = (bf16[2,128,16,128]{3,2,1,0:T(8,128)(2,1)S(1)}, bf16[2,128,16,128]{3,2,1,0:T(8,128)(2,1)}, u32[]{:S(2)}) copy-start(bf16[2,128,16,128]{3,2,1,0:T(8,128)(2,1)} %get-tuple-element.91) | copy-start | bytes 3145732
  132.5 12.8 %collective-permute-start.21 = (bf16[2,2,32,16,128]{4,3,2,1,0:T(8,128)(2,1)S(1)}, bf16[2,2,32,16,128]{4,3,2,1,0:T(8,128)(2,1)S(1)}, u32[]{:S(2)}, u32[]{:S(2)}) collective-permute-start(bf16[2,2,32,16,128]{4,3,2,1,0:T(8,128)(2,1)S(1)} %maximum_maximum_fusion.1), channel_id=1, source_target_pairs={{0,12},{1,13},{2,14},{3,15},{4,8},{5,9},{6,10},{7,11},{8,4},{9,5},... | collective-permute-start | bytes 1572872 | tf_op jit(solution)/shard_map/ppermute | solution.py:406
  134.7 10.8 %collective-permute-start.20 = (bf16[2,2,32,16,128]{4,3,2,1,0:T(8,128)(2,1)S(1)}, bf16[2,2,32,16,128]{4,3,2,1,0:T(8,128)(2,1)S(1)}, u32[]{:S(2)}, u32[]{:S(2)}) collective-permute-start(bf16[2,2,32,16,128]{4,3,2,1,0:T(8,128)(2,1)S(1)} %maximum_maximum_fusion), channel_id=1, source_target_pairs={{0,4},{1,5},{2,6},{3,7},{4,0},{5,1},{6,2},{7,3},{8,12},{9,13},{10,... | collective-permute-start | bytes 1572872 | tf_op jit(solution)/shard_map/ppermute | solution.py:406
  135.7 10.3 %collective-permute-start.22 = (bf16[2,2,32,16,128]{4,3,2,1,0:T(8,128)(2,1)S(1)}, bf16[2,2,32,16,128]{4,3,2,1,0:T(8,128)(2,1)S(1)}, u32[]{:S(2)}, u32[]{:S(2)}) collective-permute-start(bf16[2,2,32,16,128]{4,3,2,1,0:T(8,128)(2,1)S(1)} %maximum_maximum_fusion.2), channel_id=1, source_target_pairs={{0,1},{1,0},{2,3},{3,2},{4,5},{5,4},{6,7},{7,6},{8,9},{9,8},{10,11... | collective-permute-start | bytes 1572872 | tf_op jit(solution)/shard_map/ppermute | solution.py:406
  136.1 11.2 %collective-permute-start.23 = (bf16[2,2,32,16,128]{4,3,2,1,0:T(8,128)(2,1)S(1)}, bf16[2,2,32,16,128]{4,3,2,1,0:T(8,128)(2,1)S(1)}, u32[]{:S(2)}, u32[]{:S(2)}) collective-permute-start(bf16[2,2,32,16,128]{4,3,2,1,0:T(8,128)(2,1)S(1)} %maximum_maximum_fusion.3), channel_id=1, source_target_pairs={{0,3},{1,2},{2,1},{3,0},{4,7},{5,6},{6,5},{7,4},{8,11},{9,10},{10,... | collective-permute-start | bytes 1572872 | tf_op jit(solution)/shard_map/ppermute | solution.py:406
  147.7 7.9 %collective-permute-start.24 = (bf16[2,32,16,128]{3,2,1,0:T(8,128)(2,1)S(1)}, bf16[2,32,16,128]{3,2,1,0:T(8,128)(2,1)S(1)}, u32[]{:S(2)}, u32[]{:S(2)}) collective-permute-start(bf16[2,32,16,128]{3,2,1,0:T(8,128)(2,1)S(1)} %fusion.10), channel_id=1, source_target_pairs={{0,12},{1,13},{2,14},{3,15},{4,8},{5,9},{6,10},{7,11},{8,4},{9,5},... | collective-permute-start | bytes 786440 | tf_op jit(solution)/shard_map/ppermute | solution.py:406
  149.3 6.4 %collective-permute-start.25 = (bf16[2,32,16,128]{3,2,1,0:T(8,128)(2,1)S(1)}, bf16[2,32,16,128]{3,2,1,0:T(8,128)(2,1)S(1)}, u32[]{:S(2)}, u32[]{:S(2)}) collective-permute-start(bf16[2,32,16,128]{3,2,1,0:T(8,128)(2,1)S(1)} %fusion.11), channel_id=1, source_target_pairs={{0,4},{1,5},{2,6},{3,7},{4,0},{5,1},{6,2},{7,3},{8,12},{9,13},{10,... | collective-permute-start | bytes 786440 | tf_op jit(solution)/shard_map/ppermute | solution.py:406
  150.4 7.6 %collective-permute-start.26 = (bf16[2,32,16,128]{3,2,1,0:T(8,128)(2,1)S(1)}, bf16[2,32,16,128]{3,2,1,0:T(8,128)(2,1)S(1)}, u32[]{:S(2)}, u32[]{:S(2)}) collective-permute-start(bf16[2,32,16,128]{3,2,1,0:T(8,128)(2,1)S(1)} %fusion.8), channel_id=1, source_target_pairs={{0,3},{1,2},{2,1},{3,0},{4,7},{5,6},{6,5},{7,4},{8,11},{9,10},{10,... | collective-permute-start | bytes 786440 | tf_op jit(solution)/shard_map/ppermute | solution.py:406
  152.1 6.4 %collective-permute-start.27 = (bf16[2,32,16,128]{3,2,1,0:T(8,128)(2,1)S(1)}, bf16[2,32,16,128]{3,2,1,0:T(8,128)(2,1)S(1)}, u32[]{:S(2)}, u32[]{:S(2)}) collective-permute-start(bf16[2,32,16,128]{3,2,1,0:T(8,128)(2,1)S(1)} %fusion.9), channel_id=1, source_target_pairs={{0,1},{1,0},{2,3},{3,2},{4,5},{5,4},{6,7},{7,6},{8,9},{9,8},{10,11... | collective-permute-start | bytes 786440 | tf_op jit(solution)/shard_map/ppermute | solution.py:406
  155.6 2.9 %copy-start.8 = (bf16[2,32,16,128]{3,2,1,0:T(8,128)(2,1)}, bf16[2,32,16,128]{3,2,1,0:T(8,128)(2,1)S(1)}, u32[]{:S(2)}) copy-start(bf16[2,32,16,128]{3,2,1,0:T(8,128)(2,1)S(1)} %collective-permute-done.24.refs_2_) | copy-start | bytes 786436
  155.7 2.8 %copy-start.9 = (bf16[2,32,16,128]{3,2,1,0:T(8,128)(2,1)}, bf16[2,32,16,128]{3,2,1,0:T(8,128)(2,1)S(1)}, u32[]{:S(2)}) copy-start(bf16[2,32,16,128]{3,2,1,0:T(8,128)(2,1)S(1)} %collective-permute-done.25.refs_3_) | copy-start | bytes 786436
  158.0 0.7 copy-start.10
  158.7 0.7 copy-start.11

commit v7 on v6

--- a/solution.py
+++ b/solution.py
@@ -89,11 +89,18 @@
 
 def first_kernel(target_ref, odd_ref, a_ref, p_ref, *refs):
     halos, (q_out, left_out, qh_out), outs = refs[:4], refs[4:7], refs[7:17]
-    acc, stage, drain_sems, couples, q, rows, weights, left_ref, qh_ref, sems = refs[17:]
+    acc, stage, drain_sems, couples, q, rows, weights, left_ref, qh_ref, near, sems = refs[17:]
     step = pl.program_id(0)
+
+    fetches = [
+        pltpu.make_async_copy(ref, near.at[f], sems.at[E_DEV // GROUP + 2 + f])
+        for f, ref in enumerate(halos)
+    ]
 
     @pl.when(step == 0)
     def _clear():
+        for fetch in fetches:
+            fetch.start()
         clear(acc)
 
     start = pl.multiple_of(step * GROUP, GROUP)
@@ -152,7 +159,7 @@
                         q[e, ROWS:, k * 128 : (k + 1) * 128] = own[:, 128:]
                     return 0
 
-                lax.fori_loop(0, GROUP, neighbour, 0, unroll=8)
+                lax.fori_loop(0, GROUP, neighbour, 0, unroll=GROUP)
                 if base // GROUP >= behind:
                     copy(base // GROUP - behind).start()
         for n in range(E_DEV // GROUP - behind, E_DEV // GROUP):
@@ -160,9 +167,10 @@
 
         dom_odd, slab_odd = odd_ref[0], odd_ref[1]
         sides = (1 - dom_odd, dom_odd, 3 - slab_odd, 2 + slab_odd)
-        for f, ref in zip(sides, halos):
+        for n, f in enumerate(sides):
+            fetches[n].wait()
             for g in range(FACE // GROUP):
-                spread_weights(ref, g * GROUP, rows, weights, f * FACE + g * GROUP, None)
+                spread_weights(near.at[n], g * GROUP, rows, weights, f * FACE + g * GROUP, None)
 
         def face_pair(n, _):
             column = n // EX * plane + n % EX
@@ -213,7 +221,7 @@
             acc[target] += terms[:, k * 128 : (k + 1) * 128]
         return 0
 
-    lax.fori_loop(0, GROUP, element, 0, unroll=8)
+    lax.fori_loop(0, GROUP, element, 0, unroll=GROUP)
 
 
 def add_face_terms(step, half, target_ref, lefts, qh_ref, acc):
@@ -235,7 +243,7 @@
         acc[target_ref[e * PAIRS + 3 + face]] += term.astype(jnp.bfloat16).astype(jnp.float32)
         return 0
 
-    lax.fori_loop(0, GROUP, pair, 0, unroll=16)
+    lax.fori_loop(0, GROUP, pair, 0, unroll=GROUP)
 
 
 def drain(acc, stage, sems, outs):
@@ -261,21 +269,27 @@
         copy.wait()
 
 
-def second_kernel(target_ref, left_ref, q_ref, qh_ref, *refs):
+def second_kernel(target_ref, left_in, q_ref, qh_in, *refs):
     outs = refs[:10]
-    acc, stage, sems = refs[10:]
+    acc, stage, drain_sems, left_ref, qh_ref, sems = refs[10:]
     step = pl.program_id(0)
 
     @pl.when(step == 0)
     def _clear():
+        lefts = pltpu.make_async_copy(left_in, left_ref, sems.at[0])
+        faces = pltpu.make_async_copy(qh_in, qh_ref, sems.at[1])
+        lefts.start()
+        faces.start()
         clear(acc)
+        lefts.wait()
+        faces.wait()
 
     add_face_terms(step, 1, target_ref, left_ref, qh_ref, acc)
     add_terms(step, 1, target_ref, left_ref, q_ref, acc)
 
     @pl.when(step == pl.num_programs(0) - 1)
     def _drain():
-        drain(acc, stage, sems, outs)
+        drain(acc, stage, drain_sems, outs)
 
 
 VMEM = pl.BlockSpec(memory_space=pltpu.VMEM)
@@ -310,7 +324,7 @@
             SMEM,
             SMEM,
             pl.BlockSpec((PAIRS, GROUP, SQUARE), lambda i: (0, i, 0)),
-            VMEM, VMEM, VMEM, VMEM, VMEM,
+            VMEM, HBM, HBM, HBM, HBM,
         ],
         out_specs=[HBM] * (3 + len(PACKS)),
         out_shape=[
@@ -327,7 +341,8 @@
             pltpu.VMEM((E_DEV, 128, 256), jnp.bfloat16),
             pltpu.VMEM((E_DEV, BLOCK, BLOCK), jnp.bfloat16),
             pltpu.VMEM((4 * FACE, BLOCK, 128), jnp.bfloat16),
-            pltpu.SemaphoreType.DMA((E_DEV // GROUP + 2,)),
+            pltpu.VMEM((4, FACE, SQUARE), jnp.bfloat16),
+            pltpu.SemaphoreType.DMA((E_DEV // GROUP + 6,)),
         ],
         compiler_params=params(62),
         cost_estimate=cost(60),
@@ -340,10 +355,15 @@
     return pl.pallas_call(
         second_kernel,
         grid=(E_DEV // GROUP,),
-        in_specs=[SMEM, VMEM, Q_SPEC, VMEM],
+        in_specs=[SMEM, HBM, Q_SPEC, HBM],
         out_specs=[HBM] * len(PACKS),
         out_shape=PACKS,
-        scratch_shapes=SUMS,
+        scratch_shapes=SUMS
+        + [
+            pltpu.VMEM((E_DEV, BLOCK, BLOCK), jnp.bfloat16),
+            pltpu.VMEM((4 * FACE, BLOCK, 128), jnp.bfloat16),
+            pltpu.SemaphoreType.DMA((2,)),
+        ],
         compiler_params=params(48),
         cost_estimate=cost(60),
         name="second_half",
@@ -444,28 +464,45 @@
 
 
 def finish_kernel(*refs):
-    *ins, out_ref, scratch = refs
-    for n in range(4):
-        base = ins[4 * (n // 2) + n % 2]
-        last = ins[4 * (n // 2) + 2 + n % 2]
+    *ins, out_ref, scratch, bases, flat, in_sems, out_sems = refs
+    places = [4 * (n // 2) + n % 2 for n in range(4)]
+    fetches = [
+        pltpu.make_async_copy(ins[at], bases.at[n], in_sems.at[n]) for n, at in enumerate(places)
+    ]
+    for fetch in fetches:
+        fetch.start()
+    stores = []
+    for n, at in enumerate(places):
+        fetches[n].wait()
         for half in range(2):
-            total = added(base[half], last[half])
+            total = added(bases[n, half], ins[at + 2][half])
             for c in range(PART):
                 scratch[c * FLAT_PITCH : c * FLAT_PITCH + HALF, :] = total[c]
             for u in range(HALF):
                 t = half * HALF + u
-                out_ref[n * PART : (n + 1) * PART, t * 128 : (t + 1) * 128] = scratch[
-                    pl.ds(u, PART, stride=FLAT_PITCH), :
-                ]
+                flat[n, :, t * 128 : (t + 1) * 128] = scratch[pl.ds(u, PART, stride=FLAT_PITCH), :]
+        store = pltpu.make_async_copy(
+            flat.at[n], out_ref.at[pl.ds(n * PART, PART)], out_sems.at[n]
+        )
+        store.start()
+        stores.append(store)
+    for store in stores:
+        store.wait()
 
 
 def finish(parts):
     return pl.pallas_call(
         finish_kernel,
-        in_specs=[VMEM] * len(parts),
-        out_specs=VMEM,
+        in_specs=[HBM, HBM, VMEM, VMEM] * 2,
+        out_specs=HBM,
         out_shape=jax.ShapeDtypeStruct((CB_DEV, SQUARE), jnp.float32),
-        scratch_shapes=[pltpu.VMEM((PART * FLAT_PITCH + 8, 128), jnp.float32)],
+        scratch_shapes=[
+            pltpu.VMEM((PART * FLAT_PITCH + 8, 128), jnp.float32),
+            pltpu.VMEM((4, 2, PART, HALF, 128), jnp.float32),
+            pltpu.VMEM((4, PART, SQUARE), jnp.float32),
+            pltpu.SemaphoreType.DMA((4,)),
+            pltpu.SemaphoreType.DMA((4,)),
+        ],
         name="finish",
     )(*parts)
 

time: 165 us -> 160 us (0.970)
  Pallas kernels: 54 us -> 48.2 us
    pallas_call x1, Pallas kernels: 32.8 us -> 28.1 us  [first_half(): pl.pallas_call(first_kernel, grid=(E_DEV // GROUP,), in_specs=[SMEM, SMEM...]
  transfers between devices with their start and end apart: 28 -> 28, of which waited for: 20 -> 20; matrix products, arithmetic and copies ran while one was open for 5% -> 5% of each run, Pallas kernels for 11% -> 10%
where the time goes in v7:
time: 160 us; the launch traced here: 159 us
  waiting for transfers between devices  54.9 us (34%)
  Pallas kernels  48.2 us (30%)
  starting transfers between devices  42.3 us (26%)
  other arithmetic  10.1 us (6%)
  local copies, waits for them, and re-layouts  2.49 us (2%)
    ppermute x24, waiting for transfers between devices, send(): return [lax.ppermute(v, 'dom', perm) for v, perm in zip(pair, perms)]  54.1 us
    ppermute x24, starting transfers between devices, send(): return [lax.ppermute(v, 'dom', perm) for v, perm in zip(pair, perms)]  32.1 us
    pallas_call x1, Pallas kernels, first_half(): pl.pallas_call(first_kernel, grid=(E_DEV // GROUP,), in_specs=[SMEM, SMEM...  28.1 us
    pallas_call x1, Pallas kernels, second_half(): pl.pallas_call(second_kernel, grid=(E_DEV // GROUP,), in_specs=[SMEM, HBM...  16.4 us
    ppermute x2, starting transfers between devices, faces(): found.append(lax.ppermute(jnp.where(even, last, first), axis, near))  7.62 us
    pallas_call x1, Pallas kernels, finish(): pl.pallas_call(finish_kernel, in_specs=[HBM, HBM, VMEM, VMEM] * 2, out_sp...  3.7 us
    add x4, other arithmetic, added(): total = total + part.astype(jnp.float32)  3.4 us
  transfers between devices with their start and end apart: 28, of which 20 were waited for; matrix products, arithmetic and copies ran while one was open for 5% of the time, Pallas kernels for 10%

profile of v7, /device:TPU:96, one launch (start us, length us, event | category | flops | bytes accessed | tf_op | source)
XLA Modules:
  0.0 158.6 jit_solution(18202598857022834722)
XLA Ops:
  0.0 1.1 select_bitcast_fusion
  1.1 0.7 collective-permute-start.1
  1.8 4.3 %collective-permute-start = (bf16[32,4096]{1,0:T(8,128)(2,1)S(1)}, bf16[32,4096]{1,0:T(8,128)(2,1)S(1)}, u32[]{:S(2)}, u32[]{:S(2)}) collective-permute-start(bf16[32,4096]{1,0:T(8,128)(2,1)S(1)} %get-tuple-element.134), channel_id=1, source_target_pairs={{0,1},{1,0},{2,3},{3,2},{4,5},{5,4},{6,7},{7,6},{8,9},{9,8},{10,11... | collective-permute-start | bytes 786440 | tf_op jit(solution)/shard_map/ppermute | solution.py:384
  6.1 1.1 broadcast_select_fusion
  7.2 1.9 %collective-permute-start.3 = (bf16[32,4096]{1,0:T(8,128)(2,1)S(1)}, bf16[32,4096]{1,0:T(8,128)(2,1)S(1)}, u32[]{:S(2)}, u32[]{:S(2)}) collective-permute-start(bf16[32,4096]{1,0:T(8,128)(2,1)S(1)} %get-tuple-element.131), channel_id=1, source_target_pairs={{16,32},{32,16},{48,64},{64,48},{80,96},{96,80},{112,128},{128,112... | collective-permute-start | bytes 786440 | tf_op jit(solution)/shard_map/ppermute | solution.py:385
  9.1 3.3 %collective-permute-start.2 = (bf16[32,4096]{1,0:T(8,128)(2,1)S(1)}, bf16[32,4096]{1,0:T(8,128)(2,1)S(1)}, u32[]{:S(2)}, u32[]{:S(2)}) collective-permute-start(bf16[32,4096]{1,0:T(8,128)(2,1)S(1)} %get-tuple-element.132), channel_id=1, source_target_pairs={{0,16},{16,0},{32,48},{48,32},{64,80},{80,64},{96,112},{112,96},{1... | collective-permute-start | bytes 786440 | tf_op jit(solution)/shard_map/ppermute | solution.py:384
  14.0 0.8 collective-permute-done.3.refs_3_
  14.9 0.7 copy-done.16
  15.6 28.1 %first_half.1 = (bf16[128,64,896]{2,1,0:T(8,128)(2,1)}, bf16[128,64,64]{2,1,0:T(8,128)(2,1)}, bf16[128,64,128]{2,1,0:T(8,128)(2,1)}, bf16[2,128,16,128]{3,2,1,0:...) custom-call(s32[896]{0:T(1024)} %fusion.22.target_ref, ...), custom_call_target="tpu_custom_call" | custom-call | flops 10000000000 | bytes 60000000 | tf_op jit(solution)/shard_map/first_half/pallas_call | solution.py:320
  43.9 3.3 %collective-permute-start.5 = (bf16[2,128,16,128]{3,2,1,0:T(8,128)(2,1)}, bf16[2,128,16,128]{3,2,1,0:T(8,128)(2,1)S(1)}, u32[]{:S(2)}, u32[]{:S(2)}) collective-permute-start(bf16[2,128,16,128]{3,2,1,0:T(8,128)(2,1)} %get-tuple-element.58), channel_id=1, source_target_pairs={{0,3},{1,2},{2,1},{3,0},{4,7},{5,6},{6,5},{7,4},{8,11},{9,10},{10,... | collective-permute-start | bytes 3145736 | tf_op jit(solution)/shard_map/ppermute | solution.py:426
  47.1 1.6 collective-permute-start.6
  48.7 1.9 %collective-permute-start.7 = (bf16[2,128,16,128]{3,2,1,0:T(8,128)(2,1)}, bf16[2,128,16,128]{3,2,1,0:T(8,128)(2,1)S(1)}, u32[]{:S(2)}, u32[]{:S(2)}) collective-permute-start(bf16[2,128,16,128]{3,2,1,0:T(8,128)(2,1)} %get-tuple-element.60), channel_id=1, source_target_pairs={{0,12},{1,13},{2,14},{3,15},{4,8},{5,9},{6,10},{7,11},{8,4},{9,5},... | collective-permute-start | bytes 3145736 | tf_op jit(solution)/shard_map/ppermute | solution.py:426
  50.6 16.4 %second_half.1 = (bf16[2,128,16,128]{3,2,1,0:T(8,128)(2,1)S(1)}, bf16[2,128,16,128]{3,2,1,0:T(8,128)(2,1)S(1)}, bf16[1,128,16,128]{3,2,1,0:T(8,128)(2,1)S(1)}, b...) custom-call(s32[896]{0:T(1024)S(1)} %copy-done, ...), custom_call_target="tpu_custom_call" | custom-call | flops 10000000000 | bytes 60000000 | tf_op jit(solution)/shard_map/second_half/pallas_call | solution.py:355
  67.1 2.5 %collective-permute-done.4 = bf16[2,128,16,128]{3,2,1,0:T(8,128)(2,1)S(1)} collective-permute-done((bf16[2,128,16,128]{3,2,1,0:T(8,128)(2,1)}, bf16[2,128,16,128]{3,2,1,0:T(8,128)(2,1)S(1)}, u32[]{:S(2)}, u32[]{:S(2)}) %collective-permute-start.4) | collective-permute-done | bytes 1048608 | tf_op jit(solution)/shard_map/ppermute | solution.py:426
  69.6 1.0 collective-permute-start.13
  70.9 3.4 %collective-permute-start.14 = (bf16[2,128,16,128]{3,2,1,0:T(8,128)(2,1)}, bf16[2,128,16,128]{3,2,1,0:T(8,128)(2,1)S(1)}, u32[]{:S(2)}, u32[]{:S(2)}) collective-permute-start(bf16[2,128,16,128]{3,2,1,0:T(8,128)(2,1)} %get-tuple-element.76), channel_id=1, source_target_pairs={{0,4},{1,5},{2,6},{3,7},{4,0},{5,1},{6,2},{7,3},{8,12},{9,13},{10,... | collective-permute-start | bytes 3145736 | tf_op jit(solution)/shard_map/ppermute | solution.py:426
  74.3 2.2 %collective-permute-start.15 = (bf16[2,128,16,128]{3,2,1,0:T(8,128)(2,1)}, bf16[2,128,16,128]{3,2,1,0:T(8,128)(2,1)S(1)}, u32[]{:S(2)}, u32[]{:S(2)}) collective-permute-start(bf16[2,128,16,128]{3,2,1,0:T(8,128)(2,1)} %get-tuple-element.77), channel_id=1, source_target_pairs={{0,12},{1,13},{2,14},{3,15},{4,8},{5,9},{6,10},{7,11},{8,4},{9,5},... | collective-permute-start | bytes 3145736 | tf_op jit(solution)/shard_map/ppermute | solution.py:426
  76.6 1.4 collective-permute-start.11
  78.4 14.2 %collective-permute-done.12 = bf16[2,128,16,128]{3,2,1,0:T(8,128)(2,1)S(1)} collective-permute-done((bf16[2,128,16,128]{3,2,1,0:T(8,128)(2,1)S(1)}, bf16[2,128,16,128]{3,2,1,0:T(8,128)(2,1)S(1)}, u32[]{:S(2)}, u32[]{:S(2)}) %collective-permute-start.12) | collective-permute-done | bytes 1048608 | tf_op jit(solution)/shard_map/ppermute | solution.py:426
  92.6 1.1 collective-permute-start.10
  93.7 2.8 %collective-permute-done.13 = bf16[2,128,16,128]{3,2,1,0:T(8,128)(2,1)S(1)} collective-permute-done((bf16[2,128,16,128]{3,2,1,0:T(8,128)(2,1)S(1)}, bf16[2,128,16,128]{3,2,1,0:T(8,128)(2,1)S(1)}, u32[]{:S(2)}, u32[]{:S(2)}) %collective-permute-start.13) | collective-permute-done | bytes 1048608 | tf_op jit(solution)/shard_map/ppermute | solution.py:426
  96.5 2.0 %collective-permute-done.14 = bf16[2,128,16,128]{3,2,1,0:T(8,128)(2,1)S(1)} collective-permute-done((bf16[2,128,16,128]{3,2,1,0:T(8,128)(2,1)}, bf16[2,128,16,128]{3,2,1,0:T(8,128)(2,1)S(1)}, u32[]{:S(2)}, u32[]{:S(2)}) %collective-permute-start.14) | collective-permute-done | bytes 1048608 | tf_op jit(solution)/shard_map/ppermute | solution.py:426
  98.4 2.1 %collective-permute-start.9 = (bf16[128,16,128]{2,1,0:T(8,128)(2,1)S(1)}, bf16[128,16,128]{2,1,0:T(8,128)(2,1)S(1)}, u32[]{:S(2)}, u32[]{:S(2)}) collective-permute-start(bf16[128,16,128]{2,1,0:T(8,128)(2,1)S(1)} %fusion.1), channel_id=1, source_target_pairs={{0,3},{1,2},{2,1},{3,0},{4,7},{5,6},{6,5},{7,4},{8,11},{9,10},{10,... | collective-permute-start | bytes 1572872 | tf_op jit(solution)/shard_map/ppermute | solution.py:426
  100.6 1.2 collective-permute-done.15
  101.9 2.3 %collective-permute-start.19 = (bf16[128,16,128]{2,1,0:T(8,128)(2,1)S(1)}, bf16[128,16,128]{2,1,0:T(8,128)(2,1)S(1)}, u32[]{:S(2)}, u32[]{:S(2)}) collective-permute-start(bf16[128,16,128]{2,1,0:T(8,128)(2,1)S(1)} %fusion.7), channel_id=1, source_target_pairs={{0,12},{1,13},{2,14},{3,15},{4,8},{5,9},{6,10},{7,11},{8,4},{9,5},... | collective-permute-start | bytes 1572872 | tf_op jit(solution)/shard_map/ppermute | solution.py:426
  104.6 8.4 %collective-permute-done.11 = bf16[128,16,128]{2,1,0:T(8,128)(2,1)S(1)} collective-permute-done((bf16[128,16,128]{2,1,0:T(8,128)(2,1)S(1)}, bf16[128,16,128]{2,1,0:T(8,128)(2,1)S(1)}, u32[]{:S(2)}, u32[]{:S(2)}) %collective-permute-start.11) | collective-permute-done | bytes 524320 | tf_op jit(solution)/shard_map/ppermute | solution.py:426
  113.0 1.7 %collective-permute-start.17 = (bf16[128,16,128]{2,1,0:T(8,128)(2,1)S(1)}, bf16[128,16,128]{2,1,0:T(8,128)(2,1)S(1)}, u32[]{:S(2)}, u32[]{:S(2)}) collective-permute-start(bf16[128,16,128]{2,1,0:T(8,128)(2,1)S(1)} %fusion.5), channel_id=1, source_target_pairs={{0,3},{1,2},{2,1},{3,0},{4,7},{5,6},{6,5},{7,4},{8,11},{9,10},{10,... | collective-permute-start | bytes 1572872 | tf_op jit(solution)/shard_map/ppermute | solution.py:426
  114.7 0.8 fusion.28
  115.8 7.3 %collective-permute-done.19 = bf16[128,16,128]{2,1,0:T(8,128)(2,1)S(1)} collective-permute-done((bf16[128,16,128]{2,1,0:T(8,128)(2,1)S(1)}, bf16[128,16,128]{2,1,0:T(8,128)(2,1)S(1)}, u32[]{:S(2)}, u32[]{:S(2)}) %collective-permute-start.19) | collective-permute-done | bytes 524320 | tf_op jit(solution)/shard_map/ppermute | solution.py:426
  123.1 1.6 collective-permute-done.18
  124.6 0.8 collective-permute-done.16
  125.4 1.3 collective-permute-done.17
  126.7 0.8 fusion.29
  127.8 2.1 %collective-permute-start.21 = (bf16[2,2,32,16,128]{4,3,2,1,0:T(8,128)(2,1)S(1)}, bf16[2,2,32,16,128]{4,3,2,1,0:T(8,128)(2,1)S(1)}, u32[]{:S(2)}, u32[]{:S(2)}) collective-permute-start(bf16[2,2,32,16,128]{4,3,2,1,0:T(8,128)(2,1)S(1)} %maximum_maximum_fusion.1), channel_id=1, source_target_pairs={{0,12},{1,13},{2,14},{3,15},{4,8},{5,9},{6,10},{7,11},{8,4},{9,5},... | collective-permute-start | bytes 1572872 | tf_op jit(solution)/shard_map/ppermute | solution.py:426
  130.0 1.2 collective-permute-start.20
  131.6 2.2 %collective-permute-start.23 = (bf16[2,2,32,16,128]{4,3,2,1,0:T(8,128)(2,1)S(1)}, bf16[2,2,32,16,128]{4,3,2,1,0:T(8,128)(2,1)S(1)}, u32[]{:S(2)}, u32[]{:S(2)}) collective-permute-start(bf16[2,2,32,16,128]{4,3,2,1,0:T(8,128)(2,1)S(1)} %maximum_maximum_fusion.3), channel_id=1, source_target_pairs={{0,3},{1,2},{2,1},{3,0},{4,7},{5,6},{6,5},{7,4},{8,11},{9,10},{10,... | collective-permute-start | bytes 1572872 | tf_op jit(solution)/shard_map/ppermute | solution.py:426
  134.0 6.7 %collective-permute-done.21 = bf16[2,2,32,16,128]{4,3,2,1,0:T(8,128)(2,1)S(1)} collective-permute-done((bf16[2,2,32,16,128]{4,3,2,1,0:T(8,128)(2,1)S(1)}, bf16[2,2,32,16,128]{4,3,2,1,0:T(8,128)(2,1)S(1)}, u32[]{:S(2)}, u32[]{:S(2)}) %collective-permute-start.21) | collective-permute-done | bytes 524320 | tf_op jit(solution)/shard_map/ppermute | solution.py:426
  141.5 1.4 collective-permute-done.23
  143.2 1.8 %collective-permute-start.24 = (bf16[2,32,16,128]{3,2,1,0:T(8,128)(2,1)S(1)}, bf16[2,32,16,128]{3,2,1,0:T(8,128)(2,1)S(1)}, u32[]{:S(2)}, u32[]{:S(2)}) collective-permute-start(bf16[2,32,16,128]{3,2,1,0:T(8,128)(2,1)S(1)} %fusion.10), channel_id=1, source_target_pairs={{0,12},{1,13},{2,14},{3,15},{4,8},{5,9},{6,10},{7,11},{8,4},{9,5},... | collective-permute-start | bytes 786440 | tf_op jit(solution)/shard_map/ppermute | solution.py:426
  145.0 0.8 collective-permute-start.25
  145.8 1.6 %collective-permute-start.26 = (bf16[2,32,16,128]{3,2,1,0:T(8,128)(2,1)S(1)}, bf16[2,32,16,128]{3,2,1,0:T(8,128)(2,1)S(1)}, u32[]{:S(2)}, u32[]{:S(2)}) collective-permute-start(bf16[2,32,16,128]{3,2,1,0:T(8,128)(2,1)S(1)} %fusion.8), channel_id=1, source_target_pairs={{0,3},{1,2},{2,1},{3,0},{4,7},{5,6},{6,5},{7,4},{8,11},{9,10},{10,... | collective-permute-start | bytes 786440 | tf_op jit(solution)/shard_map/ppermute | solution.py:426
  147.4 0.8 maximum_add_fusion.3.refs_5_
  148.2 0.8 maximum_add_fusion.2.refs_4_
  149.1 0.9 maximum_add_fusion.refs_0_
  149.9 0.9 maximum_add_fusion.1.refs_1_
  151.4 2.0 %collective-permute-done.26.refs_6_ = bf16[2,32,16,128]{3,2,1,0:T(8,128)(2,1)S(1)} collective-permute-done((bf16[2,32,16,128]{3,2,1,0:T(8,128)(2,1)S(1)}, bf16[2,32,16,128]{3,2,1,0:T(8,128)(2,1)S(1)}, u32[]{:S(2)}, u32[]{:S(2)}) %collective-permute-start.26) | collective-permute-done | bytes 262176 | tf_op jit(solution)/shard_map/ppermute | solution.py:426
  154.1 0.7 copy-done.11
  154.8 3.7 %finish.1 = f32[128,4096]{1,0:T(8,128)} custom-call(f32[2,32,16,128]{3,2,1,0:T(8,128)} %maximum_add_fusion.refs_0_, f32[2,32,16,128]{3,2,1,0:T(8,128)} %maximum_add_fusion.1.refs_1_, bf16[2,32,16,128]{3,2,1,0:T(8,128)(2,1)} %copy-done.8, bf16[2,32,16,128]{3,2,1,0:T(8,128)(2,1)} %copy-done.9, f32[2,32,16,128]{3,2,1,0:T(8,128)} %maximum_add_fusion.2.refs_4_, ...), custom_call_target="tpu_custom_call" | custom-call | tf_op jit(solution)/shard_map/finish/pallas_call | solution.py:494
  (92 shorter events, 6.8 us)
Async XLA Ops:
  0.0 12.4 %copy-start.13 = (s32[896,1]{0,1:T(1,128)S(1)}, s32[896,1]{0,1:T(1,128)}, u32[]{:S(2)}) copy-start(s32[896,1]{0,1:T(1,128)} %param.6) | copy-start | bytes 10756
  0.0 13.0 %copy-start.12 = (s32[128,7]{0,1:T(8,128)S(1)}, s32[128,7]{0,1:T(8,128)}, u32[]{:S(2)}) copy-start(s32[128,7]{0,1:T(8,128)} %param.7) | copy-start | bytes 10756
  1.1 12.9 %collective-permute-start.1 = (bf16[32,4096]{1,0:T(8,128)(2,1)S(1)}, bf16[32,4096]{1,0:T(8,128)(2,1)S(1)}, u32[]{:S(2)}, u32[]{:S(2)}) collective-permute-start(bf16[32,4096]{1,0:T(8,128)(2,1)S(1)} %get-tuple-element.133), channel_id=1, source_target_pairs={{1,2},{2,1},{3,4},{4,3},{5,6},{6,5},{7,8},{8,7},{9,10},{10,9},{11,... | collective-permute-start | bytes 786440 | tf_op jit(solution)/shard_map/ppermute | solution.py:385
  1.8 12.2 %collective-permute-start = (bf16[32,4096]{1,0:T(8,128)(2,1)S(1)}, bf16[32,4096]{1,0:T(8,128)(2,1)S(1)}, u32[]{:S(2)}, u32[]{:S(2)}) collective-permute-start(bf16[32,4096]{1,0:T(8,128)(2,1)S(1)} %get-tuple-element.134), channel_id=1, source_target_pairs={{0,1},{1,0},{2,3},{3,2},{4,5},{5,4},{6,7},{7,6},{8,9},{9,8},{10,11... | collective-permute-start | bytes 786440 | tf_op jit(solution)/shard_map/ppermute | solution.py:384
  7.2 7.7 %collective-permute-start.3 = (bf16[32,4096]{1,0:T(8,128)(2,1)S(1)}, bf16[32,4096]{1,0:T(8,128)(2,1)S(1)}, u32[]{:S(2)}, u32[]{:S(2)}) collective-permute-start(bf16[32,4096]{1,0:T(8,128)(2,1)S(1)} %get-tuple-element.131), channel_id=1, source_target_pairs={{16,32},{32,16},{48,64},{64,48},{80,96},{96,80},{112,128},{128,112... | collective-permute-start | bytes 786440 | tf_op jit(solution)/shard_map/ppermute | solution.py:385
  9.1 5.8 %collective-permute-start.2 = (bf16[32,4096]{1,0:T(8,128)(2,1)S(1)}, bf16[32,4096]{1,0:T(8,128)(2,1)S(1)}, u32[]{:S(2)}, u32[]{:S(2)}) collective-permute-start(bf16[32,4096]{1,0:T(8,128)(2,1)S(1)} %get-tuple-element.132), channel_id=1, source_target_pairs={{0,16},{16,0},{32,48},{48,32},{64,80},{80,64},{96,112},{112,96},{1... | collective-permute-start | bytes 786440 | tf_op jit(solution)/shard_map/ppermute | solution.py:384
  14.0 0.9 copy-start.14
  14.0 0.9 copy-start.15
  14.8 0.7 copy-start.16
  14.9 0.8 copy-start.17
  15.6 34.9 %copy-start = (s32[896]{0:T(1024)S(1)}, s32[896]{0:T(1024)}, u32[]{:S(2)}) copy-start(s32[896]{0:T(1024)} %fusion.22.target_ref) | copy-start | bytes 10756
  43.7 25.9 %collective-permute-start.4 = (bf16[2,128,16,128]{3,2,1,0:T(8,128)(2,1)}, bf16[2,128,16,128]{3,2,1,0:T(8,128)(2,1)S(1)}, u32[]{:S(2)}, u32[]{:S(2)}) collective-permute-start(bf16[2,128,16,128]{3,2,1,0:T(8,128)(2,1)} %get-tuple-element.57), channel_id=1, source_target_pairs={{0,1},{1,0},{2,3},{3,2},{4,5},{5,4},{6,7},{7,6},{8,9},{9,8},{10,11... | collective-permute-start | bytes 3145736 | tf_op jit(solution)/shard_map/ppermute | solution.py:426
  43.9 27.0 %collective-permute-start.5 = (bf16[2,128,16,128]{3,2,1,0:T(8,128)(2,1)}, bf16[2,128,16,128]{3,2,1,0:T(8,128)(2,1)S(1)}, u32[]{:S(2)}, u32[]{:S(2)}) collective-permute-start(bf16[2,128,16,128]{3,2,1,0:T(8,128)(2,1)} %get-tuple-element.58), channel_id=1, source_target_pairs={{0,3},{1,2},{2,1},{3,0},{4,7},{5,6},{6,5},{7,4},{8,11},{9,10},{10,... | collective-permute-start | bytes 3145736 | tf_op jit(solution)/shard_map/ppermute | solution.py:426
  47.1 27.1 %collective-permute-start.6 = (bf16[2,128,16,128]{3,2,1,0:T(8,128)(2,1)}, bf16[2,128,16,128]{3,2,1,0:T(8,128)(2,1)S(1)}, u32[]{:S(2)}, u32[]{:S(2)}) collective-permute-start(bf16[2,128,16,128]{3,2,1,0:T(8,128)(2,1)} %get-tuple-element.59), channel_id=1, source_target_pairs={{0,4},{1,5},{2,6},{3,7},{4,0},{5,1},{6,2},{7,3},{8,12},{9,13},{10,... | collective-permute-start | bytes 3145736 | tf_op jit(solution)/shard_map/ppermute | solution.py:426
  48.7 27.8 %collective-permute-start.7 = (bf16[2,128,16,128]{3,2,1,0:T(8,128)(2,1)}, bf16[2,128,16,128]{3,2,1,0:T(8,128)(2,1)S(1)}, u32[]{:S(2)}, u32[]{:S(2)}) collective-permute-start(bf16[2,128,16,128]{3,2,1,0:T(8,128)(2,1)} %get-tuple-element.60), channel_id=1, source_target_pairs={{0,12},{1,13},{2,14},{3,15},{4,8},{5,9},{6,10},{7,11},{8,4},{9,5},... | collective-permute-start | bytes 3145736 | tf_op jit(solution)/shard_map/ppermute | solution.py:426
  50.6 25.9 %copy-start.7 = (bf16[1,128,16,128]{3,2,1,0:T(8,128)(2,1)S(1)}, bf16[1,128,16,128]{3,2,1,0:T(8,128)(2,1)}, u32[]{:S(2)}) copy-start(bf16[1,128,16,128]{3,2,1,0:T(8,128)(2,1)} %get-tuple-element.67) | copy-start | bytes 1572868
  50.6 27.4 %copy-start.6 = (bf16[1,128,16,128]{3,2,1,0:T(8,128)(2,1)S(1)}, bf16[1,128,16,128]{3,2,1,0:T(8,128)(2,1)}, u32[]{:S(2)}) copy-start(bf16[1,128,16,128]{3,2,1,0:T(8,128)(2,1)} %get-tuple-element.64) | copy-start | bytes 1572868
  67.0 11.1 %copy-start.5 = (bf16[1,128,16,128]{3,2,1,0:T(8,128)(2,1)S(1)}, bf16[1,128,16,128]{3,2,1,0:T(8,128)(2,1)}, u32[]{:S(2)}) copy-start(bf16[1,128,16,128]{3,2,1,0:T(8,128)(2,1)} %get-tuple-element.62) | copy-start | bytes 1572868
  67.0 25.6 %collective-permute-start.12 = (bf16[2,128,16,128]{3,2,1,0:T(8,128)(2,1)S(1)}, bf16[2,128,16,128]{3,2,1,0:T(8,128)(2,1)S(1)}, u32[]{:S(2)}, u32[]{:S(2)}) collective-permute-start(bf16[2,128,16,128]{3,2,1,0:T(8,128)(2,1)S(1)} %get-tuple-element.74), channel_id=1, source_target_pairs={{0,1},{1,0},{2,3},{3,2},{4,5},{5,4},{6,7},{7,6},{8,9},{9,8},{10,11... | collective-permute-start | bytes 3145736 | tf_op jit(solution)/shard_map/ppermute | solution.py:426
  69.6 26.9 %collective-permute-start.13 = (bf16[2,128,16,128]{3,2,1,0:T(8,128)(2,1)S(1)}, bf16[2,128,16,128]{3,2,1,0:T(8,128)(2,1)S(1)}, u32[]{:S(2)}, u32[]{:S(2)}) collective-permute-start(bf16[2,128,16,128]{3,2,1,0:T(8,128)(2,1)S(1)} %get-tuple-element.75), channel_id=1, source_target_pairs={{0,3},{1,2},{2,1},{3,0},{4,7},{5,6},{6,5},{7,4},{8,11},{9,10},{10,... | collective-permute-start | bytes 3145736 | tf_op jit(solution)/shard_map/ppermute | solution.py:426
  70.9 27.5 %collective-permute-start.14 = (bf16[2,128,16,128]{3,2,1,0:T(8,128)(2,1)}, bf16[2,128,16,128]{3,2,1,0:T(8,128)(2,1)S(1)}, u32[]{:S(2)}, u32[]{:S(2)}) collective-permute-start(bf16[2,128,16,128]{3,2,1,0:T(8,128)(2,1)} %get-tuple-element.76), channel_id=1, source_target_pairs={{0,4},{1,5},{2,6},{3,7},{4,0},{5,1},{6,2},{7,3},{8,12},{9,13},{10,... | collective-permute-start | bytes 3145736 | tf_op jit(solution)/shard_map/ppermute | solution.py:426
  74.3 27.5 %collective-permute-start.15 = (bf16[2,128,16,128]{3,2,1,0:T(8,128)(2,1)}, bf16[2,128,16,128]{3,2,1,0:T(8,128)(2,1)S(1)}, u32[]{:S(2)}, u32[]{:S(2)}) collective-permute-start(bf16[2,128,16,128]{3,2,1,0:T(8,128)(2,1)} %get-tuple-element.77), channel_id=1, source_target_pairs={{0,12},{1,13},{2,14},{3,15},{4,8},{5,9},{6,10},{7,11},{8,4},{9,5},... | collective-permute-start | bytes 3145736 | tf_op jit(solution)/shard_map/ppermute | solution.py:426
  76.5 1.8 %copy-start.4 = (bf16[1,128,16,128]{3,2,1,0:T(8,128)(2,1)S(1)}, bf16[1,128,16,128]{3,2,1,0:T(8,128)(2,1)}, u32[]{:S(2)}) copy-start(bf16[1,128,16,128]{3,2,1,0:T(8,128)(2,1)} %get-tuple-element.65) | copy-start | bytes 1572868
  76.6 36.3 %collective-permute-start.11 = (bf16[128,16,128]{2,1,0:T(8,128)(2,1)S(1)}, bf16[128,16,128]{2,1,0:T(8,128)(2,1)S(1)}, u32[]{:S(2)}, u32[]{:S(2)}) collective-permute-start(bf16[128,16,128]{2,1,0:T(8,128)(2,1)S(1)} %fusion.3), channel_id=1, source_target_pairs={{0,12},{1,13},{2,14},{3,15},{4,8},{5,9},{6,10},{7,11},{8,4},{9,5},... | collective-permute-start | bytes 1572872 | tf_op jit(solution)/shard_map/ppermute | solution.py:426
  92.6 20.4 %collective-permute-start.10 = (bf16[128,16,128]{2,1,0:T(8,128)(2,1)S(1)}, bf16[128,16,128]{2,1,0:T(8,128)(2,1)S(1)}, u32[]{:S(2)}, u32[]{:S(2)}) collective-permute-start(bf16[128,16,128]{2,1,0:T(8,128)(2,1)S(1)} %fusion.2), channel_id=1, source_target_pairs={{0,4},{1,5},{2,6},{3,7},{4,0},{5,1},{6,2},{7,3},{8,12},{9,13},{10,... | collective-permute-start | bytes 1572872 | tf_op jit(solution)/shard_map/ppermute | solution.py:426
  96.5 16.5 %collective-permute-start.8 = (bf16[128,16,128]{2,1,0:T(8,128)(2,1)S(1)}, bf16[128,16,128]{2,1,0:T(8,128)(2,1)S(1)}, u32[]{:S(2)}, u32[]{:S(2)}) collective-permute-start(bf16[128,16,128]{2,1,0:T(8,128)(2,1)S(1)} %fusion), channel_id=1, source_target_pairs={{0,1},{1,0},{2,3},{3,2},{4,5},{5,4},{6,7},{7,6},{8,9},{9,8},{10,11... | collective-permute-start | bytes 1572872 | tf_op jit(solution)/shard_map/ppermute | solution.py:426
  98.4 16.3 %collective-permute-start.9 = (bf16[128,16,128]{2,1,0:T(8,128)(2,1)S(1)}, bf16[128,16,128]{2,1,0:T(8,128)(2,1)S(1)}, u32[]{:S(2)}, u32[]{:S(2)}) collective-permute-start(bf16[128,16,128]{2,1,0:T(8,128)(2,1)S(1)} %fusion.1), channel_id=1, source_target_pairs={{0,3},{1,2},{2,1},{3,0},{4,7},{5,6},{6,5},{7,4},{8,11},{9,10},{10,... | collective-permute-start | bytes 1572872 | tf_op jit(solution)/shard_map/ppermute | solution.py:426
  101.9 21.2 %collective-permute-start.19 = (bf16[128,16,128]{2,1,0:T(8,128)(2,1)S(1)}, bf16[128,16,128]{2,1,0:T(8,128)(2,1)S(1)}, u32[]{:S(2)}, u32[]{:S(2)}) collective-permute-start(bf16[128,16,128]{2,1,0:T(8,128)(2,1)S(1)} %fusion.7), channel_id=1, source_target_pairs={{0,12},{1,13},{2,14},{3,15},{4,8},{5,9},{6,10},{7,11},{8,4},{9,5},... | collective-permute-start | bytes 1572872 | tf_op jit(solution)/shard_map/ppermute | solution.py:426
  104.2 10.5 %copy-start.2 = (bf16[2,128,16,128]{3,2,1,0:T(8,128)(2,1)S(1)}, bf16[2,128,16,128]{3,2,1,0:T(8,128)(2,1)}, u32[]{:S(2)}) copy-start(bf16[2,128,16,128]{3,2,1,0:T(8,128)(2,1)} %get-tuple-element.56) | copy-start | bytes 3145732
  104.2 10.5 %copy-start.3 = (bf16[2,128,16,128]{3,2,1,0:T(8,128)(2,1)S(1)}, bf16[2,128,16,128]{3,2,1,0:T(8,128)(2,1)}, u32[]{:S(2)}) copy-start(bf16[2,128,16,128]{3,2,1,0:T(8,128)(2,1)} %get-tuple-element.89) | copy-start | bytes 3145732
  113.0 11.6 %collective-permute-start.18 = (bf16[128,16,128]{2,1,0:T(8,128)(2,1)S(1)}, bf16[128,16,128]{2,1,0:T(8,128)(2,1)S(1)}, u32[]{:S(2)}, u32[]{:S(2)}) collective-permute-start(bf16[128,16,128]{2,1,0:T(8,128)(2,1)S(1)} %fusion.6), channel_id=1, source_target_pairs={{0,4},{1,5},{2,6},{3,7},{4,0},{5,1},{6,2},{7,3},{8,12},{9,13},{10,... | collective-permute-start | bytes 1572872 | tf_op jit(solution)/shard_map/ppermute | solution.py:426
  113.0 12.4 %collective-permute-start.16 = (bf16[128,16,128]{2,1,0:T(8,128)(2,1)S(1)}, bf16[128,16,128]{2,1,0:T(8,128)(2,1)S(1)}, u32[]{:S(2)}, u32[]{:S(2)}) collective-permute-start(bf16[128,16,128]{2,1,0:T(8,128)(2,1)S(1)} %fusion.4), channel_id=1, source_target_pairs={{0,1},{1,0},{2,3},{3,2},{4,5},{5,4},{6,7},{7,6},{8,9},{9,8},{10,11... | collective-permute-start | bytes 1572872 | tf_op jit(solution)/shard_map/ppermute | solution.py:426
  113.0 13.7 %collective-permute-start.17 = (bf16[128,16,128]{2,1,0:T(8,128)(2,1)S(1)}, bf16[128,16,128]{2,1,0:T(8,128)(2,1)S(1)}, u32[]{:S(2)}, u32[]{:S(2)}) collective-permute-start(bf16[128,16,128]{2,1,0:T(8,128)(2,1)S(1)} %fusion.5), channel_id=1, source_target_pairs={{0,3},{1,2},{2,1},{3,0},{4,7},{5,6},{6,5},{7,4},{8,11},{9,10},{10,... | collective-permute-start | bytes 1572872 | tf_op jit(solution)/shard_map/ppermute | solution.py:426
  115.6 11.1 %copy-start.1 = (bf16[2,128,16,128]{3,2,1,0:T(8,128)(2,1)S(1)}, bf16[2,128,16,128]{3,2,1,0:T(8,128)(2,1)}, u32[]{:S(2)}) copy-start(bf16[2,128,16,128]{3,2,1,0:T(8,128)(2,1)} %get-tuple-element.91) | copy-start | bytes 3145732
  127.8 12.8 %collective-permute-start.21 = (bf16[2,2,32,16,128]{4,3,2,1,0:T(8,128)(2,1)S(1)}, bf16[2,2,32,16,128]{4,3,2,1,0:T(8,128)(2,1)S(1)}, u32[]{:S(2)}, u32[]{:S(2)}) collective-permute-start(bf16[2,2,32,16,128]{4,3,2,1,0:T(8,128)(2,1)S(1)} %maximum_maximum_fusion.1), channel_id=1, source_target_pairs={{0,12},{1,13},{2,14},{3,15},{4,8},{5,9},{6,10},{7,11},{8,4},{9,5},... | collective-permute-start | bytes 1572872 | tf_op jit(solution)/shard_map/ppermute | solution.py:426
  130.0 11.0 %collective-permute-start.20 = (bf16[2,2,32,16,128]{4,3,2,1,0:T(8,128)(2,1)S(1)}, bf16[2,2,32,16,128]{4,3,2,1,0:T(8,128)(2,1)S(1)}, u32[]{:S(2)}, u32[]{:S(2)}) collective-permute-start(bf16[2,2,32,16,128]{4,3,2,1,0:T(8,128)(2,1)S(1)} %maximum_maximum_fusion), channel_id=1, source_target_pairs={{0,4},{1,5},{2,6},{3,7},{4,0},{5,1},{6,2},{7,3},{8,12},{9,13},{10,... | collective-permute-start | bytes 1572872 | tf_op jit(solution)/shard_map/ppermute | solution.py:426
  131.2 10.3 %collective-permute-start.22 = (bf16[2,2,32,16,128]{4,3,2,1,0:T(8,128)(2,1)S(1)}, bf16[2,2,32,16,128]{4,3,2,1,0:T(8,128)(2,1)S(1)}, u32[]{:S(2)}, u32[]{:S(2)}) collective-permute-start(bf16[2,2,32,16,128]{4,3,2,1,0:T(8,128)(2,1)S(1)} %maximum_maximum_fusion.2), channel_id=1, source_target_pairs={{0,1},{1,0},{2,3},{3,2},{4,5},{5,4},{6,7},{7,6},{8,9},{9,8},{10,11... | collective-permute-start | bytes 1572872 | tf_op jit(solution)/shard_map/ppermute | solution.py:426
  131.6 11.3 %collective-permute-start.23 = (bf16[2,2,32,16,128]{4,3,2,1,0:T(8,128)(2,1)S(1)}, bf16[2,2,32,16,128]{4,3,2,1,0:T(8,128)(2,1)S(1)}, u32[]{:S(2)}, u32[]{:S(2)}) collective-permute-start(bf16[2,2,32,16,128]{4,3,2,1,0:T(8,128)(2,1)S(1)} %maximum_maximum_fusion.3), channel_id=1, source_target_pairs={{0,3},{1,2},{2,1},{3,0},{4,7},{5,6},{6,5},{7,4},{8,11},{9,10},{10,... | collective-permute-start | bytes 1572872 | tf_op jit(solution)/shard_map/ppermute | solution.py:426
  143.2 7.7 %collective-permute-start.24 = (bf16[2,32,16,128]{3,2,1,0:T(8,128)(2,1)S(1)}, bf16[2,32,16,128]{3,2,1,0:T(8,128)(2,1)S(1)}, u32[]{:S(2)}, u32[]{:S(2)}) collective-permute-start(bf16[2,32,16,128]{3,2,1,0:T(8,128)(2,1)S(1)} %fusion.10), channel_id=1, source_target_pairs={{0,12},{1,13},{2,14},{3,15},{4,8},{5,9},{6,10},{7,11},{8,4},{9,5},... | collective-permute-start | bytes 786440 | tf_op jit(solution)/shard_map/ppermute | solution.py:426
  145.0 6.4 %collective-permute-start.25 = (bf16[2,32,16,128]{3,2,1,0:T(8,128)(2,1)S(1)}, bf16[2,32,16,128]{3,2,1,0:T(8,128)(2,1)S(1)}, u32[]{:S(2)}, u32[]{:S(2)}) collective-permute-start(bf16[2,32,16,128]{3,2,1,0:T(8,128)(2,1)S(1)} %fusion.11), channel_id=1, source_target_pairs={{0,4},{1,5},{2,6},{3,7},{4,0},{5,1},{6,2},{7,3},{8,12},{9,13},{10,... | collective-permute-start | bytes 786440 | tf_op jit(solution)/shard_map/ppermute | solution.py:426
  145.8 7.6 %collective-permute-start.26 = (bf16[2,32,16,128]{3,2,1,0:T(8,128)(2,1)S(1)}, bf16[2,32,16,128]{3,2,1,0:T(8,128)(2,1)S(1)}, u32[]{:S(2)}, u32[]{:S(2)}) collective-permute-start(bf16[2,32,16,128]{3,2,1,0:T(8,128)(2,1)S(1)} %fusion.8), channel_id=1, source_target_pairs={{0,3},{1,2},{2,1},{3,0},{4,7},{5,6},{6,5},{7,4},{8,11},{9,10},{10,... | collective-permute-start | bytes 786440 | tf_op jit(solution)/shard_map/ppermute | solution.py:426
  147.4 6.4 %collective-permute-start.27 = (bf16[2,32,16,128]{3,2,1,0:T(8,128)(2,1)S(1)}, bf16[2,32,16,128]{3,2,1,0:T(8,128)(2,1)S(1)}, u32[]{:S(2)}, u32[]{:S(2)}) collective-permute-start(bf16[2,32,16,128]{3,2,1,0:T(8,128)(2,1)S(1)} %fusion.9), channel_id=1, source_target_pairs={{0,1},{1,0},{2,3},{3,2},{4,5},{5,4},{6,7},{7,6},{8,9},{9,8},{10,11... | collective-permute-start | bytes 786440 | tf_op jit(solution)/shard_map/ppermute | solution.py:426
  150.9 2.9 %copy-start.8 = (bf16[2,32,16,128]{3,2,1,0:T(8,128)(2,1)}, bf16[2,32,16,128]{3,2,1,0:T(8,128)(2,1)S(1)}, u32[]{:S(2)}) copy-start(bf16[2,32,16,128]{3,2,1,0:T(8,128)(2,1)S(1)} %collective-permute-done.24.refs_2_) | copy-start | bytes 786436
  151.4 2.4 %copy-start.9 = (bf16[2,32,16,128]{3,2,1,0:T(8,128)(2,1)}, bf16[2,32,16,128]{3,2,1,0:T(8,128)(2,1)S(1)}, u32[]{:S(2)}) copy-start(bf16[2,32,16,128]{3,2,1,0:T(8,128)(2,1)S(1)} %collective-permute-done.25.refs_3_) | copy-start | bytes 786436
  153.4 0.7 copy-start.10
  154.1 0.7 copy-start.11

commit v8 on v7

--- a/solution.py
+++ b/solution.py
@@ -25,6 +25,7 @@
 SLOT = SIDE * PART
 SLOTS = OWNERS * CB_DEV // SLOT
 BUFFERS = 4
+PLACES = 4096
 SLOT_OF = 0x35204176
 
 
@@ -87,7 +88,7 @@
             weights[slot0 + i + j, BLOCK:, 128:] = at_low
 
 
-def first_kernel(target_ref, odd_ref, a_ref, p_ref, *refs):
+def first_kernel(target_ref, a_ref, p_ref, *refs):
     halos, (q_out, left_out, qh_out), outs = refs[:4], refs[4:7], refs[7:17]
     acc, stage, drain_sems, couples, q, rows, weights, left_ref, qh_ref, near, sems = refs[17:]
     step = pl.program_id(0)
@@ -165,7 +166,8 @@
         for n in range(E_DEV // GROUP - behind, E_DEV // GROUP):
             copy(n).start()
 
-        dom_odd, slab_odd = odd_ref[0], odd_ref[1]
+        odd = target_ref[0] // PLACES
+        dom_odd, slab_odd = odd % 2, odd // 2
         sides = (1 - dom_odd, dom_odd, 3 - slab_odd, 2 + slab_odd)
         for n, f in enumerate(sides):
             fetches[n].wait()
@@ -215,7 +217,7 @@
         terms = jnp.where(low, both[:HALF], both[HALF:])
         terms = terms.astype(jnp.bfloat16).astype(jnp.float32)
         for k in range(PAIRS):
-            target = target_ref[e * PAIRS + k]
+            target = target_ref[e * PAIRS + k] % PLACES
             if inside[k] is not None:
                 target = jnp.where(inside[k], target, OWNERS * CB_DEV)
             acc[target] += terms[:, k * 128 : (k + 1) * 128]
@@ -240,7 +242,8 @@
             preferred_element_type=jnp.float32,
         )
         term = jnp.where(low, both[:HALF], both[HALF:])
-        acc[target_ref[e * PAIRS + 3 + face]] += term.astype(jnp.bfloat16).astype(jnp.float32)
+        target = target_ref[e * PAIRS + 3 + face] % PLACES
+        acc[target] += term.astype(jnp.bfloat16).astype(jnp.float32)
         return 0
 
     lax.fori_loop(0, GROUP, pair, 0, unroll=GROUP)
@@ -316,12 +319,11 @@
     return pl.CostEstimate(flops=10**10, bytes_accessed=megabytes * 10**6, transcendentals=0)
 
 
-def first_half(target, odd, a, p, halos):
+def first_half(target, a, p, halos):
     found = pl.pallas_call(
         first_kernel,
         grid=(E_DEV // GROUP,),
         in_specs=[
-            SMEM,
             SMEM,
             pl.BlockSpec((PAIRS, GROUP, SQUARE), lambda i: (0, i, 0)),
             VMEM, HBM, HBM, HBM, HBM,
@@ -344,10 +346,10 @@
             pltpu.VMEM((4, FACE, SQUARE), jnp.bfloat16),
             pltpu.SemaphoreType.DMA((E_DEV // GROUP + 6,)),
         ],
-        compiler_params=params(62),
+        compiler_params=params(58),
         cost_estimate=cost(60),
         name="first_half",
-    )(target, odd, a, p, *halos)
+    )(target, a, p, *halos)
     return found[0], found[1], found[2], found[3:]
 
 
@@ -388,6 +390,7 @@
 
 def sum_places(dest_rank, dest_block):
     me = lax.axis_index("dom")
+    odd = me % 2 + 2 * (lax.axis_index("slab") % 2)
     away = dest_rank.reshape(-1) ^ me
     block = dest_block.reshape(-1)
     dx = away % SIDE
@@ -397,7 +400,8 @@
     place = jnp.where(which == 0, dx, dy)
     other = jnp.where(which == 0, dy, dx)
     slot = (SLOT_OF >> (4 * (2 * place + part))) & 7
-    return ((which * (SLOTS // 2) + slot) * SIDE + other) * PART + block % PART
+    found = ((which * (SLOTS // 2) + slot) * SIDE + other) * PART + block % PART
+    return found + odd * PLACES
 
 
 def pair_perms():
@@ -445,21 +449,28 @@
                 (added(own[0], n1[1], f2).reshape(shape), added(own[1], f1[1], n2).reshape(shape))
             )
     third, kept = [], []
-    for (_, _, two), parts in zip(sets, sums):
-        p0, p1 = ([jnp.stack([h[p][n] for h in parts]) for n in range(SIDE)] for p in range(2))
-        q0, q1 = ([v.astype(jnp.bfloat16) for v in w] for w in (p0, p1))
-        kept.append((p0[0], p1[0], q1[1], q0[3]))
-        third.append(send((jnp.stack([q0[2], q0[1]]), jnp.stack([q1[2], q1[3]])), two))
-    third = lax.optimization_barrier(third)
-    joined = [
-        (join(keep_near, far[0]), join(keep_far, near[0]))
-        for (_, _, keep_near, keep_far), (near, far) in zip(kept, third)
-    ]
+    for half in range(2):
+        row, keep = [], []
+        for (_, _, two), parts in zip(sets, sums):
+            p0, p1 = parts[half]
+            q0, q1 = p0.astype(jnp.bfloat16), p1.astype(jnp.bfloat16)
+            keep.append((p0[0], p1[0], q1[1], q0[3]))
+            row.append(send((jnp.stack([q0[2], q0[1]]), jnp.stack([q1[2], q1[3]])), two))
+        third.append(lax.optimization_barrier(row))
+        kept.append(keep)
+    joined = []
+    for n in range(2):
+        near = [join(keep[n][2], row[n][1][0]) for keep, row in zip(kept, third)]
+        far = [join(keep[n][3], row[n][0][0]) for keep, row in zip(kept, third)]
+        joined.append((jnp.stack(near), jnp.stack(far)))
     joined, third = lax.optimization_barrier((joined, third))
     found = []
-    for (_, _, two), (own0, own1, _, _), (n1, f1), pair in zip(sets, kept, third, joined):
+    for n, ((_, _, two), pair) in enumerate(zip(sets, joined)):
         n2, f2 = send(pair, two)
-        found += [added(own0, n1[1]), added(own1, f1[1]), f2, n2]
+        for part in range(2):
+            base = [added(keep[n][part], row[n][part][1]) for keep, row in zip(kept, third)]
+            found.append(jnp.stack(base))
+        found += [f2, n2]
     return found
 
 
@@ -510,9 +521,8 @@
 def on_device(a_blocks, p_blocks, dest_rank, dest_block):
     halos = faces(p_blocks)
     target = sum_places(dest_rank, dest_block)
-    odd = jnp.stack([lax.axis_index(axis) % 2 for axis in ("dom", "slab")])
     a = jnp.swapaxes(a_blocks, 0, 1)
-    q, lefts, qh, first = first_half(target, odd, a, p_blocks, halos)
+    q, lefts, qh, first = first_half(target, a, p_blocks, halos)
     second = second_half(target, lefts, q, qh)
     return finish(exchange((first, second)))
 

time: 160 us -> 161 us (level)
  starting transfers between devices: 42.3 us -> 46.7 us
  waiting for transfers between devices: 54.9 us -> 50.8 us
    ppermute x24 -> x28, waiting for transfers between devices: 54.1 us -> 49.3 us  [send(): return [lax.ppermute(v, 'dom', perm) for v, perm in zip(pair, perms)]]
    ppermute x24 -> x28, starting transfers between devices: 32.1 us -> 36.5 us  [send(): return [lax.ppermute(v, 'dom', perm) for v, perm in zip(pair, perms)]]
    add x4, other arithmetic: 3.4 us -> 0.22 us  [added(): total = total + part.astype(jnp.float32)]
    convert_element_type x0 -> x4, other arithmetic: none -> 1.65 us  [exchange(): q0, q1 = (p0.astype(jnp.bfloat16), p1.astype(jnp.bfloat16))]
    another operation x5 -> x8, other arithmetic: 2.38 us -> 3.49 us  [the longest x4 3.38 us: exchange(): found.append(jnp.stack(base))]
  transfers between devices with their start and end apart: 28 -> 32, of which waited for: 20 -> 18; matrix products, arithmetic and copies ran while one was open for 5% -> 5% of each run, Pallas kernels for 10% -> 10%
where the time goes in v8:
time: 161 us; the launch traced here: 160 us
  waiting for transfers between devices  50.8 us (32%)
  Pallas kernels  48.7 us (30%)
  starting transfers between devices  46.7 us (29%)
  other arithmetic  9.69 us (6%)
  local copies, waits for them, and re-layouts  3.48 us (2%)
    ppermute x28, waiting for transfers between devices, send(): return [lax.ppermute(v, 'dom', perm) for v, perm in zip(pair, perms)]  49.3 us
    ppermute x28, starting transfers between devices, send(): return [lax.ppermute(v, 'dom', perm) for v, perm in zip(pair, perms)]  36.5 us
    pallas_call x1, Pallas kernels, first_half(): pl.pallas_call(first_kernel, grid=(E_DEV // GROUP,), in_specs=[SMEM, pl.B...  28.4 us
    pallas_call x1, Pallas kernels, second_half(): pl.pallas_call(second_kernel, grid=(E_DEV // GROUP,), in_specs=[SMEM, HBM...  16.6 us
    ppermute x2, starting transfers between devices, faces(): found.append(lax.ppermute(jnp.where(even, last, first), axis, near))  7.62 us
    pallas_call x1, Pallas kernels, finish(): pl.pallas_call(finish_kernel, in_specs=[HBM, HBM, VMEM, VMEM] * 2, out_sp...  3.7 us
    another operation x4, other arithmetic, exchange(): found.append(jnp.stack(base))  3.38 us
  transfers between devices with their start and end apart: 32, of which 18 were waited for; matrix products, arithmetic and copies ran while one was open for 5% of the time, Pallas kernels for 10%

profile of v8, /device:TPU:96, one launch (start us, length us, event | category | flops | bytes accessed | tf_op | source)
XLA Modules:
  0.0 160.1 jit_solution(11404227606795262300)
XLA Ops:
  0.0 1.1 select_bitcast_fusion
  1.1 0.7 collective-permute-start.1
  1.8 4.3 %collective-permute-start = (bf16[32,4096]{1,0:T(8,128)(2,1)S(1)}, bf16[32,4096]{1,0:T(8,128)(2,1)S(1)}, u32[]{:S(2)}, u32[]{:S(2)}) collective-permute-start(bf16[32,4096]{1,0:T(8,128)(2,1)S(1)} %get-tuple-element.150), channel_id=1, source_target_pairs={{0,1},{1,0},{2,3},{3,2},{4,5},{5,4},{6,7},{7,6},{8,9},{9,8},{10,11... | collective-permute-start | bytes 786440 | tf_op jit(solution)/shard_map/ppermute | solution.py:386
  6.1 1.1 broadcast_select_fusion
  7.2 1.9 %collective-permute-start.3 = (bf16[32,4096]{1,0:T(8,128)(2,1)S(1)}, bf16[32,4096]{1,0:T(8,128)(2,1)S(1)}, u32[]{:S(2)}, u32[]{:S(2)}) collective-permute-start(bf16[32,4096]{1,0:T(8,128)(2,1)S(1)} %get-tuple-element.147), channel_id=1, source_target_pairs={{16,32},{32,16},{48,64},{64,48},{80,96},{96,80},{112,128},{128,112... | collective-permute-start | bytes 786440 | tf_op jit(solution)/shard_map/ppermute | solution.py:387
  9.1 3.3 %collective-permute-start.2 = (bf16[32,4096]{1,0:T(8,128)(2,1)S(1)}, bf16[32,4096]{1,0:T(8,128)(2,1)S(1)}, u32[]{:S(2)}, u32[]{:S(2)}) collective-permute-start(bf16[32,4096]{1,0:T(8,128)(2,1)S(1)} %get-tuple-element.148), channel_id=1, source_target_pairs={{0,16},{16,0},{32,48},{48,32},{64,80},{80,64},{96,112},{112,96},{1... | collective-permute-start | bytes 786440 | tf_op jit(solution)/shard_map/ppermute | solution.py:386
  13.4 1.4 collective-permute-done.3.refs_3_
  14.9 0.7 copy-done.16
  15.6 28.4 %first_half.1 = (bf16[128,64,896]{2,1,0:T(8,128)(2,1)}, bf16[128,64,64]{2,1,0:T(8,128)(2,1)}, bf16[128,64,128]{2,1,0:T(8,128)(2,1)}, bf16[2,128,16,128]{3,2,1,0:...) custom-call(s32[896]{0:T(1024)} %fusion.35.target_ref, ...), custom_call_target="tpu_custom_call" | custom-call | flops 10000000000 | bytes 60000000 | tf_op jit(solution)/shard_map/first_half/pallas_call | solution.py:323
  44.2 3.3 %collective-permute-start.5 = (bf16[2,128,16,128]{3,2,1,0:T(8,128)(2,1)}, bf16[2,128,16,128]{3,2,1,0:T(8,128)(2,1)S(1)}, u32[]{:S(2)}, u32[]{:S(2)}) collective-permute-start(bf16[2,128,16,128]{3,2,1,0:T(8,128)(2,1)} %get-tuple-element.66), channel_id=1, source_target_pairs={{0,3},{1,2},{2,1},{3,0},{4,7},{5,6},{6,5},{7,4},{8,11},{9,10},{10,... | collective-permute-start | bytes 3145736 | tf_op jit(solution)/shard_map/ppermute | solution.py:430
  47.5 1.6 collective-permute-start.6
  49.1 1.9 %collective-permute-start.7 = (bf16[2,128,16,128]{3,2,1,0:T(8,128)(2,1)}, bf16[2,128,16,128]{3,2,1,0:T(8,128)(2,1)S(1)}, u32[]{:S(2)}, u32[]{:S(2)}) collective-permute-start(bf16[2,128,16,128]{3,2,1,0:T(8,128)(2,1)} %get-tuple-element.68), channel_id=1, source_target_pairs={{0,12},{1,13},{2,14},{3,15},{4,8},{5,9},{6,10},{7,11},{8,4},{9,5},... | collective-permute-start | bytes 3145736 | tf_op jit(solution)/shard_map/ppermute | solution.py:430
  51.0 16.6 %second_half.1 = (bf16[2,128,16,128]{3,2,1,0:T(8,128)(2,1)S(1)}, bf16[2,128,16,128]{3,2,1,0:T(8,128)(2,1)S(1)}, bf16[1,128,16,128]{3,2,1,0:T(8,128)(2,1)S(1)}, b...) custom-call(s32[896]{0:T(1024)S(1)} %copy-done, ...), custom_call_target="tpu_custom_call" | custom-call | flops 10000000000 | bytes 60000000 | tf_op jit(solution)/shard_map/second_half/pallas_call | solution.py:357
  67.7 2.3 %collective-permute-done.4 = bf16[2,128,16,128]{3,2,1,0:T(8,128)(2,1)S(1)} collective-permute-done((bf16[2,128,16,128]{3,2,1,0:T(8,128)(2,1)}, bf16[2,128,16,128]{3,2,1,0:T(8,128)(2,1)S(1)}, u32[]{:S(2)}, u32[]{:S(2)}) %collective-permute-start.4) | collective-permute-done | bytes 1048608 | tf_op jit(solution)/shard_map/ppermute | solution.py:430
  69.9 1.0 collective-permute-start.17
  71.3 3.4 %collective-permute-start.18 = (bf16[2,128,16,128]{3,2,1,0:T(8,128)(2,1)}, bf16[2,128,16,128]{3,2,1,0:T(8,128)(2,1)S(1)}, u32[]{:S(2)}, u32[]{:S(2)}) collective-permute-start(bf16[2,128,16,128]{3,2,1,0:T(8,128)(2,1)} %get-tuple-element.89), channel_id=1, source_target_pairs={{0,4},{1,5},{2,6},{3,7},{4,0},{5,1},{6,2},{7,3},{8,12},{9,13},{10,... | collective-permute-start | bytes 3145736 | tf_op jit(solution)/shard_map/ppermute | solution.py:430
  74.6 2.2 %collective-permute-start.19 = (bf16[2,128,16,128]{3,2,1,0:T(8,128)(2,1)}, bf16[2,128,16,128]{3,2,1,0:T(8,128)(2,1)S(1)}, u32[]{:S(2)}, u32[]{:S(2)}) collective-permute-start(bf16[2,128,16,128]{3,2,1,0:T(8,128)(2,1)} %get-tuple-element.90), channel_id=1, source_target_pairs={{0,12},{1,13},{2,14},{3,15},{4,8},{5,9},{6,10},{7,11},{8,4},{9,5},... | collective-permute-start | bytes 3145736 | tf_op jit(solution)/shard_map/ppermute | solution.py:430
  77.0 1.3 collective-permute-start.11
  78.8 14.3 %collective-permute-done.16 = bf16[2,128,16,128]{3,2,1,0:T(8,128)(2,1)S(1)} collective-permute-done((bf16[2,128,16,128]{3,2,1,0:T(8,128)(2,1)S(1)}, bf16[2,128,16,128]{3,2,1,0:T(8,128)(2,1)S(1)}, u32[]{:S(2)}, u32[]{:S(2)}) %collective-permute-start.16) | collective-permute-done | bytes 1048608 | tf_op jit(solution)/shard_map/ppermute | solution.py:430
  93.1 0.9 collective-permute-start.10
  94.0 2.8 %collective-permute-done.17 = bf16[2,128,16,128]{3,2,1,0:T(8,128)(2,1)S(1)} collective-permute-done((bf16[2,128,16,128]{3,2,1,0:T(8,128)(2,1)S(1)}, bf16[2,128,16,128]{3,2,1,0:T(8,128)(2,1)S(1)}, u32[]{:S(2)}, u32[]{:S(2)}) %collective-permute-start.17) | collective-permute-done | bytes 1048608 | tf_op jit(solution)/shard_map/ppermute | solution.py:430
  96.8 2.0 %collective-permute-done.18 = bf16[2,128,16,128]{3,2,1,0:T(8,128)(2,1)S(1)} collective-permute-done((bf16[2,128,16,128]{3,2,1,0:T(8,128)(2,1)}, bf16[2,128,16,128]{3,2,1,0:T(8,128)(2,1)S(1)}, u32[]{:S(2)}, u32[]{:S(2)}) %collective-permute-start.18) | collective-permute-done | bytes 1048608 | tf_op jit(solution)/shard_map/ppermute | solution.py:430
  98.8 2.1 %collective-permute-start.9 = (bf16[128,16,128]{2,1,0:T(8,128)(2,1)S(1)}, bf16[128,16,128]{2,1,0:T(8,128)(2,1)S(1)}, u32[]{:S(2)}, u32[]{:S(2)}) collective-permute-start(bf16[128,16,128]{2,1,0:T(8,128)(2,1)S(1)} %fusion.1), channel_id=1, source_target_pairs={{0,3},{1,2},{2,1},{3,0},{4,7},{5,6},{6,5},{7,4},{8,11},{9,10},{10,... | collective-permute-start | bytes 1572872 | tf_op jit(solution)/shard_map/ppermute | solution.py:430
  100.9 1.2 collective-permute-done.19
  102.3 2.3 %collective-permute-start.23 = (bf16[128,16,128]{2,1,0:T(8,128)(2,1)S(1)}, bf16[128,16,128]{2,1,0:T(8,128)(2,1)S(1)}, u32[]{:S(2)}, u32[]{:S(2)}) collective-permute-start(bf16[128,16,128]{2,1,0:T(8,128)(2,1)S(1)} %fusion.7), channel_id=1, source_target_pairs={{0,12},{1,13},{2,14},{3,15},{4,8},{5,9},{6,10},{7,11},{8,4},{9,5},... | collective-permute-start | bytes 1572872 | tf_op jit(solution)/shard_map/ppermute | solution.py:430
  105.0 8.4 %collective-permute-done.11 = bf16[128,16,128]{2,1,0:T(8,128)(2,1)S(1)} collective-permute-done((bf16[128,16,128]{2,1,0:T(8,128)(2,1)S(1)}, bf16[128,16,128]{2,1,0:T(8,128)(2,1)S(1)}, u32[]{:S(2)}, u32[]{:S(2)}) %collective-permute-start.11) | collective-permute-done | bytes 524320 | tf_op jit(solution)/shard_map/ppermute | solution.py:430
  113.4 1.6 %collective-permute-start.21 = (bf16[128,16,128]{2,1,0:T(8,128)(2,1)S(1)}, bf16[128,16,128]{2,1,0:T(8,128)(2,1)S(1)}, u32[]{:S(2)}, u32[]{:S(2)}) collective-permute-start(bf16[128,16,128]{2,1,0:T(8,128)(2,1)S(1)} %fusion.5), channel_id=1, source_target_pairs={{0,3},{1,2},{2,1},{3,0},{4,7},{5,6},{6,5},{7,4},{8,11},{9,10},{10,... | collective-permute-start | bytes 1572872 | tf_op jit(solution)/shard_map/ppermute | solution.py:430
  115.4 0.8 copy-done.2
  116.8 2.1 %collective-permute-start.12 = (bf16[2,32,16,128]{3,2,1,0:T(8,128)(2,1)S(1)}, bf16[2,32,16,128]{3,2,1,0:T(8,128)(2,1)S(1)}, u32[]{:S(2)}, u32[]{:S(2)}) collective-permute-start(bf16[2,32,16,128]{3,2,1,0:T(8,128)(2,1)S(1)} %pad_maximum_fusion.4), channel_id=1, source_target_pairs={{0,4},{1,5},{2,6},{3,7},{4,0},{5,1},{6,2},{7,3},{8,12},{9,13},{10,... | collective-permute-start | bytes 786440 | tf_op jit(solution)/shard_map/ppermute | solution.py:430
  118.9 4.5 %collective-permute-done.23 = bf16[128,16,128]{2,1,0:T(8,128)(2,1)S(1)} collective-permute-done((bf16[128,16,128]{2,1,0:T(8,128)(2,1)S(1)}, bf16[128,16,128]{2,1,0:T(8,128)(2,1)S(1)}, u32[]{:S(2)}, u32[]{:S(2)}) %collective-permute-start.23) | collective-permute-done | bytes 524320 | tf_op jit(solution)/shard_map/ppermute | solution.py:430
  123.7 4.1 %collective-permute-done.22 = bf16[128,16,128]{2,1,0:T(8,128)(2,1)S(1)} collective-permute-done((bf16[128,16,128]{2,1,0:T(8,128)(2,1)S(1)}, bf16[128,16,128]{2,1,0:T(8,128)(2,1)S(1)}, u32[]{:S(2)}, u32[]{:S(2)}) %collective-permute-start.22) | collective-permute-done | bytes 524320 | tf_op jit(solution)/shard_map/ppermute | solution.py:430
  127.8 2.3 %collective-permute-start.13 = (bf16[2,32,16,128]{3,2,1,0:T(8,128)(2,1)S(1)}, bf16[2,32,16,128]{3,2,1,0:T(8,128)(2,1)S(1)}, u32[]{:S(2)}, u32[]{:S(2)}) collective-permute-start(bf16[2,32,16,128]{3,2,1,0:T(8,128)(2,1)S(1)} %bitcast.152), channel_id=1, source_target_pairs={{0,12},{1,13},{2,14},{3,15},{4,8},{5,9},{6,10},{7,11},{8,4},{9,5},... | collective-permute-start | bytes 786440 | tf_op jit(solution)/shard_map/ppermute | solution.py:430
  130.1 2.0 %collective-permute-start.15 = (bf16[2,32,16,128]{3,2,1,0:T(8,128)(2,1)S(1)}, bf16[2,32,16,128]{3,2,1,0:T(8,128)(2,1)S(1)}, u32[]{:S(2)}, u32[]{:S(2)}) collective-permute-start(bf16[2,32,16,128]{3,2,1,0:T(8,128)(2,1)S(1)} %bitcast.151), channel_id=1, source_target_pairs={{0,3},{1,2},{2,1},{3,0},{4,7},{5,6},{6,5},{7,4},{8,11},{9,10},{10,... | collective-permute-start | bytes 786440 | tf_op jit(solution)/shard_map/ppermute | solution.py:430
  133.4 3.4 %collective-permute-start.25 = (bf16[2,32,16,128]{3,2,1,0:T(8,128)(2,1)S(1)}, bf16[2,32,16,128]{3,2,1,0:T(8,128)(2,1)S(1)}, u32[]{:S(2)}, u32[]{:S(2)}) collective-permute-start(bf16[2,32,16,128]{3,2,1,0:T(8,128)(2,1)S(1)} %bitcast.154), channel_id=1, source_target_pairs={{0,12},{1,13},{2,14},{3,15},{4,8},{5,9},{6,10},{7,11},{8,4},{9,5},... | collective-permute-start | bytes 786440 | tf_op jit(solution)/shard_map/ppermute | solution.py:430
  136.8 0.9 collective-permute-start.27
  137.7 1.0 collective-permute-done.15
  139.8 1.4 collective-permute-done.25
  141.1 3.2 %collective-permute-done.27 = bf16[2,32,16,128]{3,2,1,0:T(8,128)(2,1)S(1)} collective-permute-done((bf16[2,32,16,128]{3,2,1,0:T(8,128)(2,1)S(1)}, bf16[2,32,16,128]{3,2,1,0:T(8,128)(2,1)S(1)}, u32[]{:S(2)}, u32[]{:S(2)}) %collective-permute-start.27) | collective-permute-done | bytes 262176 | tf_op jit(solution)/shard_map/ppermute | solution.py:430
  144.7 1.8 %collective-permute-start.28 = (bf16[2,32,16,128]{3,2,1,0:T(8,128)(2,1)S(1)}, bf16[2,32,16,128]{3,2,1,0:T(8,128)(2,1)S(1)}, u32[]{:S(2)}, u32[]{:S(2)}) collective-permute-start(bf16[2,32,16,128]{3,2,1,0:T(8,128)(2,1)S(1)} %pad_maximum_fusion.9), channel_id=1, source_target_pairs={{0,12},{1,13},{2,14},{3,15},{4,8},{5,9},{6,10},{7,11},{8,4},{9,5},... | collective-permute-start | bytes 786440 | tf_op jit(solution)/shard_map/ppermute | solution.py:430
  146.4 0.8 collective-permute-start.29
  147.2 1.1 collective-permute-start.30
  148.4 0.8 pad_maximum_fusion.3.refs_5_
  149.4 0.8 pad_maximum_fusion.1.refs_1_
  150.2 0.9 pad_maximum_fusion.refs_0_
  151.1 0.8 pad_maximum_fusion.2.refs_4_
  152.8 2.0 %collective-permute-done.30.refs_6_ = bf16[2,32,16,128]{3,2,1,0:T(8,128)(2,1)S(1)} collective-permute-done((bf16[2,32,16,128]{3,2,1,0:T(8,128)(2,1)S(1)}, bf16[2,32,16,128]{3,2,1,0:T(8,128)(2,1)S(1)}, u32[]{:S(2)}, u32[]{:S(2)}) %collective-permute-start.30) | collective-permute-done | bytes 262176 | tf_op jit(solution)/shard_map/ppermute | solution.py:430
  155.5 0.7 copy-done.11
  156.2 3.7 %finish.1 = f32[128,4096]{1,0:T(8,128)} custom-call(f32[2,32,16,128]{3,2,1,0:T(8,128)} %pad_maximum_fusion.refs_0_, f32[2,32,16,128]{3,2,1,0:T(8,128)} %pad_maximum_fusion.1.refs_1_, bf16[2,32,16,128]{3,2,1,0:T(8,128)(2,1)} %copy-done.8, bf16[2,32,16,128]{3,2,1,0:T(8,128)(2,1)} %copy-done.9, f32[2,32,16,128]{3,2,1,0:T(8,128)} %pad_maximum_fusion.2.refs_4_, ...), custom_call_target="tpu_custom_call" | custom-call | tf_op jit(solution)/shard_map/finish/pallas_call | solution.py:505
  (105 shorter events, 8.2 us)
Async XLA Ops:
  0.0 12.4 %copy-start.13 = (s32[896,1]{0,1:T(1,128)S(1)}, s32[896,1]{0,1:T(1,128)}, u32[]{:S(2)}) copy-start(s32[896,1]{0,1:T(1,128)} %param.6) | copy-start | bytes 10756
  0.0 12.4 %copy-start.12 = (s32[128,7]{0,1:T(8,128)S(1)}, s32[128,7]{0,1:T(8,128)}, u32[]{:S(2)}) copy-start(s32[128,7]{0,1:T(8,128)} %param.7) | copy-start | bytes 10756
  1.1 12.3 %collective-permute-start.1 = (bf16[32,4096]{1,0:T(8,128)(2,1)S(1)}, bf16[32,4096]{1,0:T(8,128)(2,1)S(1)}, u32[]{:S(2)}, u32[]{:S(2)}) collective-permute-start(bf16[32,4096]{1,0:T(8,128)(2,1)S(1)} %get-tuple-element.149), channel_id=1, source_target_pairs={{1,2},{2,1},{3,4},{4,3},{5,6},{6,5},{7,8},{8,7},{9,10},{10,9},{11,... | collective-permute-start | bytes 786440 | tf_op jit(solution)/shard_map/ppermute | solution.py:387
  1.8 11.6 %collective-permute-start = (bf16[32,4096]{1,0:T(8,128)(2,1)S(1)}, bf16[32,4096]{1,0:T(8,128)(2,1)S(1)}, u32[]{:S(2)}, u32[]{:S(2)}) collective-permute-start(bf16[32,4096]{1,0:T(8,128)(2,1)S(1)} %get-tuple-element.150), channel_id=1, source_target_pairs={{0,1},{1,0},{2,3},{3,2},{4,5},{5,4},{6,7},{7,6},{8,9},{9,8},{10,11... | collective-permute-start | bytes 786440 | tf_op jit(solution)/shard_map/ppermute | solution.py:386
  7.2 7.7 %collective-permute-start.3 = (bf16[32,4096]{1,0:T(8,128)(2,1)S(1)}, bf16[32,4096]{1,0:T(8,128)(2,1)S(1)}, u32[]{:S(2)}, u32[]{:S(2)}) collective-permute-start(bf16[32,4096]{1,0:T(8,128)(2,1)S(1)} %get-tuple-element.147), channel_id=1, source_target_pairs={{16,32},{32,16},{48,64},{64,48},{80,96},{96,80},{112,128},{128,112... | collective-permute-start | bytes 786440 | tf_op jit(solution)/shard_map/ppermute | solution.py:387
  9.1 5.8 %collective-permute-start.2 = (bf16[32,4096]{1,0:T(8,128)(2,1)S(1)}, bf16[32,4096]{1,0:T(8,128)(2,1)S(1)}, u32[]{:S(2)}, u32[]{:S(2)}) collective-permute-start(bf16[32,4096]{1,0:T(8,128)(2,1)S(1)} %get-tuple-element.148), channel_id=1, source_target_pairs={{0,16},{16,0},{32,48},{48,32},{64,80},{80,64},{96,112},{112,96},{1... | collective-permute-start | bytes 786440 | tf_op jit(solution)/shard_map/ppermute | solution.py:386
  13.4 1.5 copy-start.14
  13.4 1.5 copy-start.15
  14.8 0.7 copy-start.16
  14.9 0.8 copy-start.17
  15.6 35.3 %copy-start = (s32[896]{0:T(1024)S(1)}, s32[896]{0:T(1024)}, u32[]{:S(2)}) copy-start(s32[896]{0:T(1024)} %fusion.35.target_ref) | copy-start | bytes 10756
  44.1 25.9 %collective-permute-start.4 = (bf16[2,128,16,128]{3,2,1,0:T(8,128)(2,1)}, bf16[2,128,16,128]{3,2,1,0:T(8,128)(2,1)S(1)}, u32[]{:S(2)}, u32[]{:S(2)}) collective-permute-start(bf16[2,128,16,128]{3,2,1,0:T(8,128)(2,1)} %get-tuple-element.65), channel_id=1, source_target_pairs={{0,1},{1,0},{2,3},{3,2},{4,5},{5,4},{6,7},{7,6},{8,9},{9,8},{10,11... | collective-permute-start | bytes 3145736 | tf_op jit(solution)/shard_map/ppermute | solution.py:430
  44.2 27.0 %collective-permute-start.5 = (bf16[2,128,16,128]{3,2,1,0:T(8,128)(2,1)}, bf16[2,128,16,128]{3,2,1,0:T(8,128)(2,1)S(1)}, u32[]{:S(2)}, u32[]{:S(2)}) collective-permute-start(bf16[2,128,16,128]{3,2,1,0:T(8,128)(2,1)} %get-tuple-element.66), channel_id=1, source_target_pairs={{0,3},{1,2},{2,1},{3,0},{4,7},{5,6},{6,5},{7,4},{8,11},{9,10},{10,... | collective-permute-start | bytes 3145736 | tf_op jit(solution)/shard_map/ppermute | solution.py:430
  47.5 27.2 %collective-permute-start.6 = (bf16[2,128,16,128]{3,2,1,0:T(8,128)(2,1)}, bf16[2,128,16,128]{3,2,1,0:T(8,128)(2,1)S(1)}, u32[]{:S(2)}, u32[]{:S(2)}) collective-permute-start(bf16[2,128,16,128]{3,2,1,0:T(8,128)(2,1)} %get-tuple-element.67), channel_id=1, source_target_pairs={{0,4},{1,5},{2,6},{3,7},{4,0},{5,1},{6,2},{7,3},{8,12},{9,13},{10,... | collective-permute-start | bytes 3145736 | tf_op jit(solution)/shard_map/ppermute | solution.py:430
  49.1 27.8 %collective-permute-start.7 = (bf16[2,128,16,128]{3,2,1,0:T(8,128)(2,1)}, bf16[2,128,16,128]{3,2,1,0:T(8,128)(2,1)S(1)}, u32[]{:S(2)}, u32[]{:S(2)}) collective-permute-start(bf16[2,128,16,128]{3,2,1,0:T(8,128)(2,1)} %get-tuple-element.68), channel_id=1, source_target_pairs={{0,12},{1,13},{2,14},{3,15},{4,8},{5,9},{6,10},{7,11},{8,4},{9,5},... | collective-permute-start | bytes 3145736 | tf_op jit(solution)/shard_map/ppermute | solution.py:430
  50.9 25.9 %copy-start.7 = (bf16[1,128,16,128]{3,2,1,0:T(8,128)(2,1)S(1)}, bf16[1,128,16,128]{3,2,1,0:T(8,128)(2,1)}, u32[]{:S(2)}) copy-start(bf16[1,128,16,128]{3,2,1,0:T(8,128)(2,1)} %get-tuple-element.75) | copy-start | bytes 1572868
  51.0 27.4 %copy-start.6 = (bf16[1,128,16,128]{3,2,1,0:T(8,128)(2,1)S(1)}, bf16[1,128,16,128]{3,2,1,0:T(8,128)(2,1)}, u32[]{:S(2)}) copy-start(bf16[1,128,16,128]{3,2,1,0:T(8,128)(2,1)} %get-tuple-element.72) | copy-start | bytes 1572868
  67.6 10.9 %copy-start.5 = (bf16[1,128,16,128]{3,2,1,0:T(8,128)(2,1)S(1)}, bf16[1,128,16,128]{3,2,1,0:T(8,128)(2,1)}, u32[]{:S(2)}) copy-start(bf16[1,128,16,128]{3,2,1,0:T(8,128)(2,1)} %get-tuple-element.70) | copy-start | bytes 1572868
  67.6 25.5 %collective-permute-start.16 = (bf16[2,128,16,128]{3,2,1,0:T(8,128)(2,1)S(1)}, bf16[2,128,16,128]{3,2,1,0:T(8,128)(2,1)S(1)}, u32[]{:S(2)}, u32[]{:S(2)}) collective-permute-start(bf16[2,128,16,128]{3,2,1,0:T(8,128)(2,1)S(1)} %get-tuple-element.87), channel_id=1, source_target_pairs={{0,1},{1,0},{2,3},{3,2},{4,5},{5,4},{6,7},{7,6},{8,9},{9,8},{10,11... | collective-permute-start | bytes 3145736 | tf_op jit(solution)/shard_map/ppermute | solution.py:430
  69.9 26.9 %collective-permute-start.17 = (bf16[2,128,16,128]{3,2,1,0:T(8,128)(2,1)S(1)}, bf16[2,128,16,128]{3,2,1,0:T(8,128)(2,1)S(1)}, u32[]{:S(2)}, u32[]{:S(2)}) collective-permute-start(bf16[2,128,16,128]{3,2,1,0:T(8,128)(2,1)S(1)} %get-tuple-element.88), channel_id=1, source_target_pairs={{0,3},{1,2},{2,1},{3,0},{4,7},{5,6},{6,5},{7,4},{8,11},{9,10},{10,... | collective-permute-start | bytes 3145736 | tf_op jit(solution)/shard_map/ppermute | solution.py:430
  71.3 27.5 %collective-permute-start.18 = (bf16[2,128,16,128]{3,2,1,0:T(8,128)(2,1)}, bf16[2,128,16,128]{3,2,1,0:T(8,128)(2,1)S(1)}, u32[]{:S(2)}, u32[]{:S(2)}) collective-permute-start(bf16[2,128,16,128]{3,2,1,0:T(8,128)(2,1)} %get-tuple-element.89), channel_id=1, source_target_pairs={{0,4},{1,5},{2,6},{3,7},{4,0},{5,1},{6,2},{7,3},{8,12},{9,13},{10,... | collective-permute-start | bytes 3145736 | tf_op jit(solution)/shard_map/ppermute | solution.py:430
  74.6 27.5 %collective-permute-start.19 = (bf16[2,128,16,128]{3,2,1,0:T(8,128)(2,1)}, bf16[2,128,16,128]{3,2,1,0:T(8,128)(2,1)S(1)}, u32[]{:S(2)}, u32[]{:S(2)}) collective-permute-start(bf16[2,128,16,128]{3,2,1,0:T(8,128)(2,1)} %get-tuple-element.90), channel_id=1, source_target_pairs={{0,12},{1,13},{2,14},{3,15},{4,8},{5,9},{6,10},{7,11},{8,4},{9,5},... | collective-permute-start | bytes 3145736 | tf_op jit(solution)/shard_map/ppermute | solution.py:430
  76.8 1.8 %copy-start.4 = (bf16[1,128,16,128]{3,2,1,0:T(8,128)(2,1)S(1)}, bf16[1,128,16,128]{3,2,1,0:T(8,128)(2,1)}, u32[]{:S(2)}) copy-start(bf16[1,128,16,128]{3,2,1,0:T(8,128)(2,1)} %get-tuple-element.73) | copy-start | bytes 1572868
  77.0 36.4 %collective-permute-start.11 = (bf16[128,16,128]{2,1,0:T(8,128)(2,1)S(1)}, bf16[128,16,128]{2,1,0:T(8,128)(2,1)S(1)}, u32[]{:S(2)}, u32[]{:S(2)}) collective-permute-start(bf16[128,16,128]{2,1,0:T(8,128)(2,1)S(1)} %fusion.3), channel_id=1, source_target_pairs={{0,12},{1,13},{2,14},{3,15},{4,8},{5,9},{6,10},{7,11},{8,4},{9,5},... | collective-permute-start | bytes 1572872 | tf_op jit(solution)/shard_map/ppermute | solution.py:430
  93.1 20.2 %collective-permute-start.10 = (bf16[128,16,128]{2,1,0:T(8,128)(2,1)S(1)}, bf16[128,16,128]{2,1,0:T(8,128)(2,1)S(1)}, u32[]{:S(2)}, u32[]{:S(2)}) collective-permute-start(bf16[128,16,128]{2,1,0:T(8,128)(2,1)S(1)} %fusion.2), channel_id=1, source_target_pairs={{0,4},{1,5},{2,6},{3,7},{4,0},{5,1},{6,2},{7,3},{8,12},{9,13},{10,... | collective-permute-start | bytes 1572872 | tf_op jit(solution)/shard_map/ppermute | solution.py:430
  96.8 18.1 %collective-permute-start.8 = (bf16[128,16,128]{2,1,0:T(8,128)(2,1)S(1)}, bf16[128,16,128]{2,1,0:T(8,128)(2,1)S(1)}, u32[]{:S(2)}, u32[]{:S(2)}) collective-permute-start(bf16[128,16,128]{2,1,0:T(8,128)(2,1)S(1)} %fusion), channel_id=1, source_target_pairs={{0,1},{1,0},{2,3},{3,2},{4,5},{5,4},{6,7},{7,6},{8,9},{9,8},{10,11... | collective-permute-start | bytes 1572872 | tf_op jit(solution)/shard_map/ppermute | solution.py:430
  98.8 16.2 %collective-permute-start.9 = (bf16[128,16,128]{2,1,0:T(8,128)(2,1)S(1)}, bf16[128,16,128]{2,1,0:T(8,128)(2,1)S(1)}, u32[]{:S(2)}, u32[]{:S(2)}) collective-permute-start(bf16[128,16,128]{2,1,0:T(8,128)(2,1)S(1)} %fusion.1), channel_id=1, source_target_pairs={{0,3},{1,2},{2,1},{3,0},{4,7},{5,6},{6,5},{7,4},{8,11},{9,10},{10,... | collective-permute-start | bytes 1572872 | tf_op jit(solution)/shard_map/ppermute | solution.py:430
  102.3 21.2 %collective-permute-start.23 = (bf16[128,16,128]{2,1,0:T(8,128)(2,1)S(1)}, bf16[128,16,128]{2,1,0:T(8,128)(2,1)S(1)}, u32[]{:S(2)}, u32[]{:S(2)}) collective-permute-start(bf16[128,16,128]{2,1,0:T(8,128)(2,1)S(1)} %fusion.7), channel_id=1, source_target_pairs={{0,12},{1,13},{2,14},{3,15},{4,8},{5,9},{6,10},{7,11},{8,4},{9,5},... | collective-permute-start | bytes 1572872 | tf_op jit(solution)/shard_map/ppermute | solution.py:430
  104.5 10.4 %copy-start.3 = (bf16[2,128,16,128]{3,2,1,0:T(8,128)(2,1)S(1)}, bf16[2,128,16,128]{3,2,1,0:T(8,128)(2,1)}, u32[]{:S(2)}) copy-start(bf16[2,128,16,128]{3,2,1,0:T(8,128)(2,1)} %get-tuple-element.64) | copy-start | bytes 3145732
  113.3 14.5 %collective-permute-start.22 = (bf16[128,16,128]{2,1,0:T(8,128)(2,1)S(1)}, bf16[128,16,128]{2,1,0:T(8,128)(2,1)S(1)}, u32[]{:S(2)}, u32[]{:S(2)}) collective-permute-start(bf16[128,16,128]{2,1,0:T(8,128)(2,1)S(1)} %fusion.6), channel_id=1, source_target_pairs={{0,4},{1,5},{2,6},{3,7},{4,0},{5,1},{6,2},{7,3},{8,12},{9,13},{10,... | collective-permute-start | bytes 1572872 | tf_op jit(solution)/shard_map/ppermute | solution.py:430
  113.4 16.8 %collective-permute-start.21 = (bf16[128,16,128]{2,1,0:T(8,128)(2,1)S(1)}, bf16[128,16,128]{2,1,0:T(8,128)(2,1)S(1)}, u32[]{:S(2)}, u32[]{:S(2)}) collective-permute-start(bf16[128,16,128]{2,1,0:T(8,128)(2,1)S(1)} %fusion.5), channel_id=1, source_target_pairs={{0,3},{1,2},{2,1},{3,0},{4,7},{5,6},{6,5},{7,4},{8,11},{9,10},{10,... | collective-permute-start | bytes 1572872 | tf_op jit(solution)/shard_map/ppermute | solution.py:430
  115.0 17.2 %collective-permute-start.20 = (bf16[128,16,128]{2,1,0:T(8,128)(2,1)S(1)}, bf16[128,16,128]{2,1,0:T(8,128)(2,1)S(1)}, u32[]{:S(2)}, u32[]{:S(2)}) collective-permute-start(bf16[128,16,128]{2,1,0:T(8,128)(2,1)S(1)} %fusion.4), channel_id=1, source_target_pairs={{0,1},{1,0},{2,3},{3,2},{4,5},{5,4},{6,7},{7,6},{8,9},{9,8},{10,11... | collective-permute-start | bytes 1572872 | tf_op jit(solution)/shard_map/ppermute | solution.py:430
  115.0 1.2 copy-start.2
  116.6 15.5 %copy-start.1 = (bf16[2,128,16,128]{3,2,1,0:T(8,128)(2,1)S(1)}, bf16[2,128,16,128]{3,2,1,0:T(8,128)(2,1)}, u32[]{:S(2)}) copy-start(bf16[2,128,16,128]{3,2,1,0:T(8,128)(2,1)} %get-tuple-element.101) | copy-start | bytes 3145732
  116.8 16.5 %collective-permute-start.12 = (bf16[2,32,16,128]{3,2,1,0:T(8,128)(2,1)S(1)}, bf16[2,32,16,128]{3,2,1,0:T(8,128)(2,1)S(1)}, u32[]{:S(2)}, u32[]{:S(2)}) collective-permute-start(bf16[2,32,16,128]{3,2,1,0:T(8,128)(2,1)S(1)} %pad_maximum_fusion.4), channel_id=1, source_target_pairs={{0,4},{1,5},{2,6},{3,7},{4,0},{5,1},{6,2},{7,3},{8,12},{9,13},{10,... | collective-permute-start | bytes 786440 | tf_op jit(solution)/shard_map/ppermute | solution.py:430
  123.4 10.0 %collective-permute-start.14 = (bf16[2,32,16,128]{3,2,1,0:T(8,128)(2,1)S(1)}, bf16[2,32,16,128]{3,2,1,0:T(8,128)(2,1)S(1)}, u32[]{:S(2)}, u32[]{:S(2)}) collective-permute-start(bf16[2,32,16,128]{3,2,1,0:T(8,128)(2,1)S(1)} %pad_maximum_fusion.5), channel_id=1, source_target_pairs={{0,1},{1,0},{2,3},{3,2},{4,5},{5,4},{6,7},{7,6},{8,9},{9,8},{10,11... | collective-permute-start | bytes 786440 | tf_op jit(solution)/shard_map/ppermute | solution.py:430
  127.8 9.0 %collective-permute-start.13 = (bf16[2,32,16,128]{3,2,1,0:T(8,128)(2,1)S(1)}, bf16[2,32,16,128]{3,2,1,0:T(8,128)(2,1)S(1)}, u32[]{:S(2)}, u32[]{:S(2)}) collective-permute-start(bf16[2,32,16,128]{3,2,1,0:T(8,128)(2,1)S(1)} %bitcast.152), channel_id=1, source_target_pairs={{0,12},{1,13},{2,14},{3,15},{4,8},{5,9},{6,10},{7,11},{8,4},{9,5},... | collective-permute-start | bytes 786440 | tf_op jit(solution)/shard_map/ppermute | solution.py:430
  130.1 8.6 %collective-permute-start.15 = (bf16[2,32,16,128]{3,2,1,0:T(8,128)(2,1)S(1)}, bf16[2,32,16,128]{3,2,1,0:T(8,128)(2,1)S(1)}, u32[]{:S(2)}, u32[]{:S(2)}) collective-permute-start(bf16[2,32,16,128]{3,2,1,0:T(8,128)(2,1)S(1)} %bitcast.151), channel_id=1, source_target_pairs={{0,3},{1,2},{2,1},{3,0},{4,7},{5,6},{6,5},{7,4},{8,11},{9,10},{10,... | collective-permute-start | bytes 786440 | tf_op jit(solution)/shard_map/ppermute | solution.py:430
  133.1 6.5 %collective-permute-start.24 = (bf16[2,32,16,128]{3,2,1,0:T(8,128)(2,1)S(1)}, bf16[2,32,16,128]{3,2,1,0:T(8,128)(2,1)S(1)}, u32[]{:S(2)}, u32[]{:S(2)}) collective-permute-start(bf16[2,32,16,128]{3,2,1,0:T(8,128)(2,1)S(1)} %pad_maximum_fusion.6), channel_id=1, source_target_pairs={{0,4},{1,5},{2,6},{3,7},{4,0},{5,1},{6,2},{7,3},{8,12},{9,13},{10,... | collective-permute-start | bytes 786440 | tf_op jit(solution)/shard_map/ppermute | solution.py:430
  133.3 6.5 %collective-permute-start.26 = (bf16[2,32,16,128]{3,2,1,0:T(8,128)(2,1)S(1)}, bf16[2,32,16,128]{3,2,1,0:T(8,128)(2,1)S(1)}, u32[]{:S(2)}, u32[]{:S(2)}) collective-permute-start(bf16[2,32,16,128]{3,2,1,0:T(8,128)(2,1)S(1)} %pad_maximum_fusion.7), channel_id=1, source_target_pairs={{0,1},{1,0},{2,3},{3,2},{4,5},{5,4},{6,7},{7,6},{8,9},{9,8},{10,11... | collective-permute-start | bytes 786440 | tf_op jit(solution)/shard_map/ppermute | solution.py:430
  133.4 7.7 %collective-permute-start.25 = (bf16[2,32,16,128]{3,2,1,0:T(8,128)(2,1)S(1)}, bf16[2,32,16,128]{3,2,1,0:T(8,128)(2,1)S(1)}, u32[]{:S(2)}, u32[]{:S(2)}) collective-permute-start(bf16[2,32,16,128]{3,2,1,0:T(8,128)(2,1)S(1)} %bitcast.154), channel_id=1, source_target_pairs={{0,12},{1,13},{2,14},{3,15},{4,8},{5,9},{6,10},{7,11},{8,4},{9,5},... | collective-permute-start | bytes 786440 | tf_op jit(solution)/shard_map/ppermute | solution.py:430
  136.8 7.6 %collective-permute-start.27 = (bf16[2,32,16,128]{3,2,1,0:T(8,128)(2,1)S(1)}, bf16[2,32,16,128]{3,2,1,0:T(8,128)(2,1)S(1)}, u32[]{:S(2)}, u32[]{:S(2)}) collective-permute-start(bf16[2,32,16,128]{3,2,1,0:T(8,128)(2,1)S(1)} %bitcast.153), channel_id=1, source_target_pairs={{0,3},{1,2},{2,1},{3,0},{4,7},{5,6},{6,5},{7,4},{8,11},{9,10},{10,... | collective-permute-start | bytes 786440 | tf_op jit(solution)/shard_map/ppermute | solution.py:430
  144.7 7.7 %collective-permute-start.28 = (bf16[2,32,16,128]{3,2,1,0:T(8,128)(2,1)S(1)}, bf16[2,32,16,128]{3,2,1,0:T(8,128)(2,1)S(1)}, u32[]{:S(2)}, u32[]{:S(2)}) collective-permute-start(bf16[2,32,16,128]{3,2,1,0:T(8,128)(2,1)S(1)} %pad_maximum_fusion.9), channel_id=1, source_target_pairs={{0,12},{1,13},{2,14},{3,15},{4,8},{5,9},{6,10},{7,11},{8,4},{9,5},... | collective-permute-start | bytes 786440 | tf_op jit(solution)/shard_map/ppermute | solution.py:430
  146.4 6.4 %collective-permute-start.29 = (bf16[2,32,16,128]{3,2,1,0:T(8,128)(2,1)S(1)}, bf16[2,32,16,128]{3,2,1,0:T(8,128)(2,1)S(1)}, u32[]{:S(2)}, u32[]{:S(2)}) collective-permute-start(bf16[2,32,16,128]{3,2,1,0:T(8,128)(2,1)S(1)} %pad_maximum_fusion.8), channel_id=1, source_target_pairs={{0,4},{1,5},{2,6},{3,7},{4,0},{5,1},{6,2},{7,3},{8,12},{9,13},{10,... | collective-permute-start | bytes 786440 | tf_op jit(solution)/shard_map/ppermute | solution.py:430
  147.2 7.6 %collective-permute-start.30 = (bf16[2,32,16,128]{3,2,1,0:T(8,128)(2,1)S(1)}, bf16[2,32,16,128]{3,2,1,0:T(8,128)(2,1)S(1)}, u32[]{:S(2)}, u32[]{:S(2)}) collective-permute-start(bf16[2,32,16,128]{3,2,1,0:T(8,128)(2,1)S(1)} %pad_maximum_fusion.11), channel_id=1, source_target_pairs={{0,3},{1,2},{2,1},{3,0},{4,7},{5,6},{6,5},{7,4},{8,11},{9,10},{10,... | collective-permute-start | bytes 786440 | tf_op jit(solution)/shard_map/ppermute | solution.py:430
  148.3 6.5 %collective-permute-start.31 = (bf16[2,32,16,128]{3,2,1,0:T(8,128)(2,1)S(1)}, bf16[2,32,16,128]{3,2,1,0:T(8,128)(2,1)S(1)}, u32[]{:S(2)}, u32[]{:S(2)}) collective-permute-start(bf16[2,32,16,128]{3,2,1,0:T(8,128)(2,1)S(1)} %pad_maximum_fusion.10), channel_id=1, source_target_pairs={{0,1},{1,0},{2,3},{3,2},{4,5},{5,4},{6,7},{7,6},{8,9},{9,8},{10,11... | collective-permute-start | bytes 786440 | tf_op jit(solution)/shard_map/ppermute | solution.py:430
  152.4 2.4 %copy-start.8 = (bf16[2,32,16,128]{3,2,1,0:T(8,128)(2,1)}, bf16[2,32,16,128]{3,2,1,0:T(8,128)(2,1)S(1)}, u32[]{:S(2)}) copy-start(bf16[2,32,16,128]{3,2,1,0:T(8,128)(2,1)S(1)} %collective-permute-done.28.refs_2_) | copy-start | bytes 786436
  152.8 2.0 %copy-start.9 = (bf16[2,32,16,128]{3,2,1,0:T(8,128)(2,1)}, bf16[2,32,16,128]{3,2,1,0:T(8,128)(2,1)S(1)}, u32[]{:S(2)}) copy-start(bf16[2,32,16,128]{3,2,1,0:T(8,128)(2,1)S(1)} %collective-permute-done.29.refs_3_) | copy-start | bytes 786436
  (2 other events, 1.4 us)
